TPU v7x, 32 devices: a whole 2x2x4 slice. The times are simulated.
32 devices in a mesh: dom: 8 (over z, y), rel: 4 (over x, core).
Axes of the slice: x: 2, y: 2, z: 4, core: 2. Of those that a mesh axis runs over, the one named last changes fastest.
Arguments:
- partitions: bfloat16 [4096, 400], P('dom'), may hold values from -1.5 to 1.5
- remainder: bfloat16 [256, 400], replicated, may hold values from -1.5 to 1.5
- relations: float32 [2560, 400], replicated, may hold values from -4 to 4
- counts: int32 [8, 8, 4], P('dom', None, 'rel'), may hold values from 0 to 1, as said below
- lhs_rows: int32 [8, 8, 4, 128], P('dom', None, 'rel'), may hold values from 0 to 511
- lhs_rems: int32 [8, 8, 4, 128], P('dom', None, 'rel'), may hold values from 0 to 255
- rel_ids: int32 [8, 8, 4, 128], P('dom', None, 'rel'), may hold values from 0 to 2559
- rhs_rows: int32 [8, 8, 4, 128], P('dom', None, 'rel'), may hold values from 0 to 511
- rhs_rems: int32 [8, 8, 4, 128], P('dom', None, 'rel'), may hold values from 0 to 255
- neg_rows: int32 [8, 8, 4, 128], P('dom', None, 'rel'), may hold values from 0 to 511
- neg_rems: int32 [8, 8, 4, 128], P('dom', None, 'rel'), may hold values from 0 to 255
Outputs:
- grad_partitions: float32 [4096, 400], P('dom')
- grad_remainder: float32 [256, 400], replicated
- grad_relations: float32 [2560, 400], replicated
Inputs may be any that keep to these rules, and one draw needn't show every extreme that they name: In every bucket (p, t) some device j of rel has counts[p, t, j] = 1.
All inputs are finite; a program needn't handle non-finite values.
Results may differ from a plain program's by a relative error of at most 0.009.
Values may be sent and summed in bfloat16 or wider, within the bound.
No kernel may reach another device: no remote copies, remote signals or barrier semaphores. Data moves between devices by JAX's collectives and lax.ppermute only.
A program may use at most 128 MiB of HBM per device.

v0:
```python
import jax
import jax.numpy as jnp
from jax import lax
from jax.sharding import PartitionSpec as P


def shifted(value, axis, by):
    length = lax.axis_size(axis)
    return lax.ppermute(value, axis, [(i, (i + by) % length) for i in range(length)])


def complex_product(left, right):
    half = left.shape[-1] // 2
    left_re, left_im = (left[..., :half], left[..., half:])
    right_re, right_im = (right[..., :half], right[..., half:])
    return jnp.concatenate(
        [left_re * right_re - left_im * right_im, left_re * right_im + left_im * right_re], -1
    )


def conjugate_product(grad, other):
    half = grad.shape[-1] // 2
    grad_re, grad_im = (grad[..., :half], grad[..., half:])
    other_re, other_im = (other[..., :half], other[..., half:])
    return jnp.concatenate(
        [grad_re * other_re + grad_im * other_im, grad_im * other_re - grad_re * other_im], -1
    )


def edge_terms(lhs, rel_vec, cand, width):
    high = lax.Precision.HIGHEST
    total = cand.shape[0]
    u_vec = complex_product(lhs, rel_vec)
    rhs = cand[:width]
    positive = jnp.sum(u_vec * rhs, -1)
    negative = lax.dot_general(
        u_vec, cand, (((1,), (1,)), ((), ())), precision=high, preferred_element_type=jnp.float32
    )
    keep = 1.0 - jnp.eye(width, total, dtype=jnp.float32)
    grad_pos = -jax.nn.sigmoid(-positive)
    grad_neg = jax.nn.sigmoid(negative) * keep / total
    grad_u = grad_pos[:, None] * rhs + jnp.dot(
        grad_neg, cand, precision=high, preferred_element_type=jnp.float32
    )
    extra = jnp.concatenate(
        [grad_pos[:, None] * u_vec, jnp.zeros((total - width, u_vec.shape[1]), jnp.float32)], 0
    )
    grad_cand = (
        lax.dot_general(
            grad_neg,
            u_vec,
            (((0,), (0,)), ((), ())),
            precision=high,
            preferred_element_type=jnp.float32,
        )
        + extra
    )
    grad_lhs = conjugate_product(grad_u, rel_vec)
    grad_rel = conjugate_product(grad_u, lhs)
    return (grad_lhs, grad_rel, grad_cand)


def block_update(lhs_tab, rhs_tab, remainder, relations, labels, grads):
    lhs_row, lhs_rem, rel_row, rhs_row, rhs_rem, neg_row, neg_rem = labels
    rhs_grad, lhs_grad, rem_grad, rel_grad = grads
    cand_row = jnp.concatenate([rhs_row, neg_row])
    cand_rem = jnp.concatenate([rhs_rem, neg_rem])
    lhs = jnp.take(lhs_tab, lhs_row, axis=0).astype(jnp.float32) + jnp.take(
        remainder, lhs_rem, axis=0
    ).astype(jnp.float32)
    cand = jnp.take(rhs_tab, cand_row, axis=0).astype(jnp.float32) + jnp.take(
        remainder, cand_rem, axis=0
    ).astype(jnp.float32)
    rel_vec = jnp.take(relations, rel_row, axis=0)
    grad_lhs, grad_rel, grad_cand = edge_terms(lhs, rel_vec, cand, lhs_row.shape[0])
    lhs_grad = lhs_grad.at[lhs_row].add(grad_lhs)
    rhs_grad = rhs_grad.at[cand_row].add(grad_cand)
    rem_grad = rem_grad.at[lhs_rem].add(grad_lhs).at[cand_rem].add(grad_cand)
    rel_grad = rel_grad.at[rel_row].add(grad_rel)
    return (rhs_grad, lhs_grad, rem_grad, rel_grad)


def body(
    partitions,
    remainder,
    relations,
    counts,
    lhs_rows,
    lhs_rems,
    rel_ids,
    rhs_rows,
    rhs_rems,
    neg_rows,
    neg_rems,
):
    prows, width = partitions.shape
    stops = lax.axis_size("dom")
    own_lists = (
        lhs_rows[0],
        lhs_rems[0],
        rel_ids[0],
        rhs_rows[0],
        rhs_rems[0],
        neg_rows[0],
        neg_rems[0],
    )
    own_loads = counts[0, :, 0]

    def share(stop):
        return own_loads[stop]

    def labels_for(stop, turn):
        return tuple((table[stop, turn] for table in own_lists))

    def run_stop(stop, rhs_tab, grads):

        def block_step(turn, inner):
            return block_update(
                partitions, rhs_tab, remainder, relations, labels_for(stop, turn), inner
            )

        return lax.fori_loop(0, share(stop), block_step, grads)

    zero_part = jnp.zeros((prows, width), jnp.float32)
    zero_rem = jnp.zeros((remainder.shape[0], width), jnp.float32)
    zero_rel = jnp.zeros((relations.shape[0], width), jnp.float32)

    def stop_carry(stop, carry):
        rhs_tab, rhs_grad, lhs_grad, rem_grad, rel_grad = carry
        rhs_grad, lhs_grad, rem_grad, rel_grad = run_stop(
            stop, rhs_tab, (rhs_grad, lhs_grad, rem_grad, rel_grad)
        )
        rhs_tab = shifted(rhs_tab, "dom", 1)
        rhs_grad = shifted(rhs_grad, "dom", 1)
        return (rhs_tab, rhs_grad, lhs_grad, rem_grad, rel_grad)

    start = (partitions, zero_part, zero_part, zero_rem, zero_rel)
    unused_tab, home_grad, lhs_grad, rem_grad, rel_grad = lax.fori_loop(0, stops, stop_carry, start)
    grad_partitions = lax.psum(lhs_grad + home_grad, "rel")
    grad_relations, grad_remainder = lax.psum((rel_grad, rem_grad), ("dom", "rel"))
    return (grad_partitions, grad_remainder, grad_relations)


def solution(mesh):
    in_specs = (
        P("dom", None),
        P(),
        P(),
        P("dom", None, "rel"),
        P("dom", None, "rel", None),
        P("dom", None, "rel", None),
        P("dom", None, "rel", None),
        P("dom", None, "rel", None),
        P("dom", None, "rel", None),
        P("dom", None, "rel", None),
        P("dom", None, "rel", None),
    )
    out_specs = (P("dom", None), P(), P())
    return jax.shard_map(body, mesh=mesh, in_specs=in_specs, out_specs=out_specs, check_vma=False)
```

profile of v0, /device:TPU:0, one launch (start us, length us, event | category | flops | bytes accessed | tf_op | source)
XLA Modules:
  0.0 852.4 jit_solution(10569515848723063246)
XLA Ops:
  9.2 5.6 copy.32
  20.1 626.6 %while.61 = (s32[]{:T(128)}, bf16[512,400]{1,0:T(8,128)(2,1)}, f32[512,400]{0,1:T(8,128)S(1)}, f32[512,400]{1,0:T(8,128)}, f32[256,400]{1,0:T(8,128)}, /*index=5...) while((s32[]{:T(128)}, bf16[512,400]{1,0:T(8,128)(2,1)}, ...), condition=%wide.region_9.10_spmd, body=%wide.region_0.9_spmd.sunk | while | flops 475323904 | bytes 29682108 | solution.py:138
  35.8 30.8 %while.62 = (s32[]{:T(128)}, f32[512,400]{1,0:T(8,128)}, f32[512,400]{1,0:T(8,128)}, f32[256,400]{1,0:T(8,128)}, f32[2560,400]{1,0:T(8,128)}, /*index=5*/s32[]{:...) while((s32[]{:T(128)}, f32[512,400]{1,0:T(8,128)}, ...), condition=%wide.region_8.8_spmd, body=%wide.region_2.7_spmd.sunk | while | flops 1959170 | bytes 14077645 | solution.py:122
  44.6 6.2 scatter_custom_fusion.29
  68.3 35.5 %collective-permute-done = bf16[512,400]{1,0:T(8,128)(2,1)} collective-permute-done((bf16[512,400]{1,0:T(8,128)(2,1)S(1)}, bf16[512,400]{1,0:T(8,128)(2,1)}, u32[]{:S(2)}, u32[]{:S(2)}) %collective-permute-start) | collective-permute-done | bytes 409632 | tf_op jit(solution)/shard_map/while/body/eval_jaxpr/ppermute | solution.py:9
  119.5 30.8 %while.62 = (s32[]{:T(128)}, f32[512,400]{1,0:T(8,128)}, f32[512,400]{1,0:T(8,128)}, f32[256,400]{1,0:T(8,128)}, f32[2560,400]{1,0:T(8,128)}, /*index=5*/s32[]{:...) while((s32[]{:T(128)}, f32[512,400]{1,0:T(8,128)}, ...), condition=%wide.region_8.8_spmd, body=%wide.region_2.7_spmd.sunk | while | flops 1959170 | bytes 14077645 | solution.py:122
  128.3 6.2 scatter_custom_fusion.29
  152.0 25.5 %collective-permute-done = bf16[512,400]{1,0:T(8,128)(2,1)} collective-permute-done((bf16[512,400]{1,0:T(8,128)(2,1)S(1)}, bf16[512,400]{1,0:T(8,128)(2,1)}, u32[]{:S(2)}, u32[]{:S(2)}) %collective-permute-start) | collective-permute-done | bytes 409632 | tf_op jit(solution)/shard_map/while/body/eval_jaxpr/ppermute | solution.py:9
  193.3 30.8 %while.62 = (s32[]{:T(128)}, f32[512,400]{1,0:T(8,128)}, f32[512,400]{1,0:T(8,128)}, f32[256,400]{1,0:T(8,128)}, f32[2560,400]{1,0:T(8,128)}, /*index=5*/s32[]{:...) while((s32[]{:T(128)}, f32[512,400]{1,0:T(8,128)}, ...), condition=%wide.region_8.8_spmd, body=%wide.region_2.7_spmd.sunk | while | flops 1959170 | bytes 14077645 | solution.py:122
  202.0 6.2 scatter_custom_fusion.29
  229.5 18.5 %collective-permute-done = bf16[512,400]{1,0:T(8,128)(2,1)} collective-permute-done((bf16[512,400]{1,0:T(8,128)(2,1)S(1)}, bf16[512,400]{1,0:T(8,128)(2,1)}, u32[]{:S(2)}, u32[]{:S(2)}) %collective-permute-start) | collective-permute-done | bytes 409632 | tf_op jit(solution)/shard_map/while/body/eval_jaxpr/ppermute | solution.py:9
  265.9 27.2 %collective-permute-start.1 = (f32[512,400]{0,1:T(8,128)S(1)}, f32[512,400]{0,1:T(8,128)S(1)}, u32[]{:S(2)}, u32[]{:S(2)}) collective-permute-start(f32[512,400]{0,1:T(8,128)S(1)} %copy.41), channel_id=1, source_target_pairs={{0,4},{4,8},{8,12},{12,16},{16,20},{20,24},{24,28},{28,0},{1,5},{5... | collective-permute-start | bytes 2457608 | tf_op jit(solution)/shard_map/while/body/eval_jaxpr/ppermute | solution.py:9
  293.1 38.0 %collective-permute-done = bf16[512,400]{1,0:T(8,128)(2,1)} collective-permute-done((bf16[512,400]{1,0:T(8,128)(2,1)S(1)}, bf16[512,400]{1,0:T(8,128)(2,1)}, u32[]{:S(2)}, u32[]{:S(2)}) %collective-permute-start) | collective-permute-done | bytes 409632 | tf_op jit(solution)/shard_map/while/body/eval_jaxpr/ppermute | solution.py:9
  346.9 30.8 %while.62 = (s32[]{:T(128)}, f32[512,400]{1,0:T(8,128)}, f32[512,400]{1,0:T(8,128)}, f32[256,400]{1,0:T(8,128)}, f32[2560,400]{1,0:T(8,128)}, /*index=5*/s32[]{:...) while((s32[]{:T(128)}, f32[512,400]{1,0:T(8,128)}, ...), condition=%wide.region_8.8_spmd, body=%wide.region_2.7_spmd.sunk | while | flops 1959170 | bytes 14077645 | solution.py:122
  355.6 6.2 scatter_custom_fusion.29
  379.4 30.9 %collective-permute-done = bf16[512,400]{1,0:T(8,128)(2,1)} collective-permute-done((bf16[512,400]{1,0:T(8,128)(2,1)S(1)}, bf16[512,400]{1,0:T(8,128)(2,1)}, u32[]{:S(2)}, u32[]{:S(2)}) %collective-permute-start) | collective-permute-done | bytes 409632 | tf_op jit(solution)/shard_map/while/body/eval_jaxpr/ppermute | solution.py:9
  428.2 24.9 %collective-permute-done = bf16[512,400]{1,0:T(8,128)(2,1)} collective-permute-done((bf16[512,400]{1,0:T(8,128)(2,1)S(1)}, bf16[512,400]{1,0:T(8,128)(2,1)}, u32[]{:S(2)}, u32[]{:S(2)}) %collective-permute-start) | collective-permute-done | bytes 409632 | tf_op jit(solution)/shard_map/while/body/eval_jaxpr/ppermute | solution.py:9
  471.1 36.5 %collective-permute-start.1 = (f32[512,400]{0,1:T(8,128)S(1)}, f32[512,400]{0,1:T(8,128)S(1)}, u32[]{:S(2)}, u32[]{:S(2)}) collective-permute-start(f32[512,400]{0,1:T(8,128)S(1)} %copy.41), channel_id=1, source_target_pairs={{0,4},{4,8},{8,12},{12,16},{16,20},{20,24},{24,28},{28,0},{1,5},{5... | collective-permute-start | bytes 2457608 | tf_op jit(solution)/shard_map/while/body/eval_jaxpr/ppermute | solution.py:9
  507.7 59.6 %collective-permute-done = bf16[512,400]{1,0:T(8,128)(2,1)} collective-permute-done((bf16[512,400]{1,0:T(8,128)(2,1)S(1)}, bf16[512,400]{1,0:T(8,128)(2,1)}, u32[]{:S(2)}, u32[]{:S(2)}) %collective-permute-start) | collective-permute-done | bytes 409632 | tf_op jit(solution)/shard_map/while/body/eval_jaxpr/ppermute | solution.py:9
  583.0 30.8 %while.62 = (s32[]{:T(128)}, f32[512,400]{1,0:T(8,128)}, f32[512,400]{1,0:T(8,128)}, f32[256,400]{1,0:T(8,128)}, f32[2560,400]{1,0:T(8,128)}, /*index=5*/s32[]{:...) while((s32[]{:T(128)}, f32[512,400]{1,0:T(8,128)}, ...), condition=%wide.region_8.8_spmd, body=%wide.region_2.7_spmd.sunk | while | flops 1959170 | bytes 14077645 | solution.py:122
  591.7 6.2 scatter_custom_fusion.29
  615.5 31.3 %collective-permute-done = bf16[512,400]{1,0:T(8,128)(2,1)} collective-permute-done((bf16[512,400]{1,0:T(8,128)(2,1)S(1)}, bf16[512,400]{1,0:T(8,128)(2,1)}, u32[]{:S(2)}, u32[]{:S(2)}) %collective-permute-start) | collective-permute-done | bytes 409632 | tf_op jit(solution)/shard_map/while/body/eval_jaxpr/ppermute | solution.py:9
  655.9 30.8 %all-reduce.5.cloned.1.call-done = f32[512,400]{0,1:T(8,128)} async-done(((f32[512,400]{0,1:T(8,128)}), f32[512,400]{0,1:T(8,128)}) %all-reduce.5.cloned.1.call-update) | async-done | bytes 819216 | tf_op jit(solution)/shard_map/psum | solution.py:139
  686.7 150.7 %all-reduce.7.cloned.1.call-done = (f32[256,400]{0,1:T(8,128)}, f32[2560,400]{0,1:T(8,128)}) async-done(((f32[256,400]{0,1:T(8,128)}, f32[2560,400]{0,1:T(8,128)}), (f32[256,400]{0,1:T(8,128)}, f32[2560,400]{0,1:T(8,128)})) %all-reduce.7.cloned.1.call-update) | async-done | bytes 4505616 | tf_op jit(solution)/shard_map/psum | solution.py:140
  (472 shorter events, 284.1 us)
Async XLA Ops:
  7.2 679.5 %all-reduce.5.cloned.1.call-start = ((), (), s32[]{:S(2)}) async-start(), calls=%async_computation | async-start | bytes 1638400 | tf_op jit(solution)/shard_map/psum | solution.py:139
  8.4 6.5 copy-start.1
  14.9 5.2 copy-start.2
  68.2 35.6 %collective-permute-start.1 = (f32[512,400]{0,1:T(8,128)S(1)}, f32[512,400]{0,1:T(8,128)S(1)}, u32[]{:S(2)}, u32[]{:S(2)}) collective-permute-start(f32[512,400]{0,1:T(8,128)S(1)} %copy.41), channel_id=1, source_target_pairs={{0,4},{4,8},{8,12},{12,16},{16,20},{20,24},{24,28},{28,0},{1,5},{5... | collective-permute-start | bytes 2457608 | tf_op jit(solution)/shard_map/while/body/eval_jaxpr/ppermute | solution.py:9
  68.2 35.6 %collective-permute-start = (bf16[512,400]{1,0:T(8,128)(2,1)S(1)}, bf16[512,400]{1,0:T(8,128)(2,1)}, u32[]{:S(2)}, u32[]{:S(2)}) collective-permute-start(bf16[512,400]{1,0:T(8,128)(2,1)S(1)} %get-tuple-element.1406), channel_id=1, source_target_pairs={{0,4},{4,8},{8,12},{12,16},{16,20},{20,24},{24,28},{28,0},{1,5},{5... | collective-permute-start | bytes 1228808 | tf_op jit(solution)/shard_map/while/body/eval_jaxpr/ppermute | solution.py:9
  151.9 25.6 %collective-permute-start.1 = (f32[512,400]{0,1:T(8,128)S(1)}, f32[512,400]{0,1:T(8,128)S(1)}, u32[]{:S(2)}, u32[]{:S(2)}) collective-permute-start(f32[512,400]{0,1:T(8,128)S(1)} %copy.41), channel_id=1, source_target_pairs={{0,4},{4,8},{8,12},{12,16},{16,20},{20,24},{24,28},{28,0},{1,5},{5... | collective-permute-start | bytes 2457608 | tf_op jit(solution)/shard_map/while/body/eval_jaxpr/ppermute | solution.py:9
  152.0 25.6 %collective-permute-start = (bf16[512,400]{1,0:T(8,128)(2,1)S(1)}, bf16[512,400]{1,0:T(8,128)(2,1)}, u32[]{:S(2)}, u32[]{:S(2)}) collective-permute-start(bf16[512,400]{1,0:T(8,128)(2,1)S(1)} %get-tuple-element.1406), channel_id=1, source_target_pairs={{0,4},{4,8},{8,12},{12,16},{16,20},{20,24},{24,28},{28,0},{1,5},{5... | collective-permute-start | bytes 1228808 | tf_op jit(solution)/shard_map/while/body/eval_jaxpr/ppermute | solution.py:9
  225.7 22.3 %collective-permute-start.1 = (f32[512,400]{0,1:T(8,128)S(1)}, f32[512,400]{0,1:T(8,128)S(1)}, u32[]{:S(2)}, u32[]{:S(2)}) collective-permute-start(f32[512,400]{0,1:T(8,128)S(1)} %copy.41), channel_id=1, source_target_pairs={{0,4},{4,8},{8,12},{12,16},{16,20},{20,24},{24,28},{28,0},{1,5},{5... | collective-permute-start | bytes 2457608 | tf_op jit(solution)/shard_map/while/body/eval_jaxpr/ppermute | solution.py:9
  225.7 22.3 %collective-permute-start = (bf16[512,400]{1,0:T(8,128)(2,1)S(1)}, bf16[512,400]{1,0:T(8,128)(2,1)}, u32[]{:S(2)}, u32[]{:S(2)}) collective-permute-start(bf16[512,400]{1,0:T(8,128)(2,1)S(1)} %get-tuple-element.1406), channel_id=1, source_target_pairs={{0,4},{4,8},{8,12},{12,16},{16,20},{20,24},{24,28},{28,0},{1,5},{5... | collective-permute-start | bytes 1228808 | tf_op jit(solution)/shard_map/while/body/eval_jaxpr/ppermute | solution.py:9
  265.9 65.2 %collective-permute-start.1 = (f32[512,400]{0,1:T(8,128)S(1)}, f32[512,400]{0,1:T(8,128)S(1)}, u32[]{:S(2)}, u32[]{:S(2)}) collective-permute-start(f32[512,400]{0,1:T(8,128)S(1)} %copy.41), channel_id=1, source_target_pairs={{0,4},{4,8},{8,12},{12,16},{16,20},{20,24},{24,28},{28,0},{1,5},{5... | collective-permute-start | bytes 2457608 | tf_op jit(solution)/shard_map/while/body/eval_jaxpr/ppermute | solution.py:9
  293.1 38.0 %collective-permute-start = (bf16[512,400]{1,0:T(8,128)(2,1)S(1)}, bf16[512,400]{1,0:T(8,128)(2,1)}, u32[]{:S(2)}, u32[]{:S(2)}) collective-permute-start(bf16[512,400]{1,0:T(8,128)(2,1)S(1)} %get-tuple-element.1406), channel_id=1, source_target_pairs={{0,4},{4,8},{8,12},{12,16},{16,20},{20,24},{24,28},{28,0},{1,5},{5... | collective-permute-start | bytes 1228808 | tf_op jit(solution)/shard_map/while/body/eval_jaxpr/ppermute | solution.py:9
  379.2 31.0 %collective-permute-start.1 = (f32[512,400]{0,1:T(8,128)S(1)}, f32[512,400]{0,1:T(8,128)S(1)}, u32[]{:S(2)}, u32[]{:S(2)}) collective-permute-start(f32[512,400]{0,1:T(8,128)S(1)} %copy.41), channel_id=1, source_target_pairs={{0,4},{4,8},{8,12},{12,16},{16,20},{20,24},{24,28},{28,0},{1,5},{5... | collective-permute-start | bytes 2457608 | tf_op jit(solution)/shard_map/while/body/eval_jaxpr/ppermute | solution.py:9
  379.3 30.9 %collective-permute-start = (bf16[512,400]{1,0:T(8,128)(2,1)S(1)}, bf16[512,400]{1,0:T(8,128)(2,1)}, u32[]{:S(2)}, u32[]{:S(2)}) collective-permute-start(bf16[512,400]{1,0:T(8,128)(2,1)S(1)} %get-tuple-element.1406), channel_id=1, source_target_pairs={{0,4},{4,8},{8,12},{12,16},{16,20},{20,24},{24,28},{28,0},{1,5},{5... | collective-permute-start | bytes 1228808 | tf_op jit(solution)/shard_map/while/body/eval_jaxpr/ppermute | solution.py:9
  428.1 25.1 %collective-permute-start.1 = (f32[512,400]{0,1:T(8,128)S(1)}, f32[512,400]{0,1:T(8,128)S(1)}, u32[]{:S(2)}, u32[]{:S(2)}) collective-permute-start(f32[512,400]{0,1:T(8,128)S(1)} %copy.41), channel_id=1, source_target_pairs={{0,4},{4,8},{8,12},{12,16},{16,20},{20,24},{24,28},{28,0},{1,5},{5... | collective-permute-start | bytes 2457608 | tf_op jit(solution)/shard_map/while/body/eval_jaxpr/ppermute | solution.py:9
  428.2 25.0 %collective-permute-start = (bf16[512,400]{1,0:T(8,128)(2,1)S(1)}, bf16[512,400]{1,0:T(8,128)(2,1)}, u32[]{:S(2)}, u32[]{:S(2)}) collective-permute-start(bf16[512,400]{1,0:T(8,128)(2,1)S(1)} %get-tuple-element.1406), channel_id=1, source_target_pairs={{0,4},{4,8},{8,12},{12,16},{16,20},{20,24},{24,28},{28,0},{1,5},{5... | collective-permute-start | bytes 1228808 | tf_op jit(solution)/shard_map/while/body/eval_jaxpr/ppermute | solution.py:9
  471.1 96.1 %collective-permute-start.1 = (f32[512,400]{0,1:T(8,128)S(1)}, f32[512,400]{0,1:T(8,128)S(1)}, u32[]{:S(2)}, u32[]{:S(2)}) collective-permute-start(f32[512,400]{0,1:T(8,128)S(1)} %copy.41), channel_id=1, source_target_pairs={{0,4},{4,8},{8,12},{12,16},{16,20},{20,24},{24,28},{28,0},{1,5},{5... | collective-permute-start | bytes 2457608 | tf_op jit(solution)/shard_map/while/body/eval_jaxpr/ppermute | solution.py:9
  507.6 59.6 %collective-permute-start = (bf16[512,400]{1,0:T(8,128)(2,1)S(1)}, bf16[512,400]{1,0:T(8,128)(2,1)}, u32[]{:S(2)}, u32[]{:S(2)}) collective-permute-start(bf16[512,400]{1,0:T(8,128)(2,1)S(1)} %get-tuple-element.1406), channel_id=1, source_target_pairs={{0,4},{4,8},{8,12},{12,16},{16,20},{20,24},{24,28},{28,0},{1,5},{5... | collective-permute-start | bytes 1228808 | tf_op jit(solution)/shard_map/while/body/eval_jaxpr/ppermute | solution.py:9
  615.3 31.4 %collective-permute-start.1 = (f32[512,400]{0,1:T(8,128)S(1)}, f32[512,400]{0,1:T(8,128)S(1)}, u32[]{:S(2)}, u32[]{:S(2)}) collective-permute-start(f32[512,400]{0,1:T(8,128)S(1)} %copy.41), channel_id=1, source_target_pairs={{0,4},{4,8},{8,12},{12,16},{16,20},{20,24},{24,28},{28,0},{1,5},{5... | collective-permute-start | bytes 2457608 | tf_op jit(solution)/shard_map/while/body/eval_jaxpr/ppermute | solution.py:9
  615.4 31.3 %collective-permute-start = (bf16[512,400]{1,0:T(8,128)(2,1)S(1)}, bf16[512,400]{1,0:T(8,128)(2,1)}, u32[]{:S(2)}, u32[]{:S(2)}) collective-permute-start(bf16[512,400]{1,0:T(8,128)(2,1)S(1)} %get-tuple-element.1406), channel_id=1, source_target_pairs={{0,4},{4,8},{8,12},{12,16},{16,20},{20,24},{24,28},{28,0},{1,5},{5... | collective-permute-start | bytes 1228808 | tf_op jit(solution)/shard_map/while/body/eval_jaxpr/ppermute | solution.py:9
  649.3 5.7 copy-start
  649.3 188.0 %all-reduce.7.cloned.1.call-start = ((), (), s32[]{:S(2)}) async-start(), calls=%async_computation.1 | async-start | bytes 9011200 | tf_op jit(solution)/shard_map/psum | solution.py:140
Sparse Core Ops, SparseCore 0:
  649.4 37.1 all-reduce.4
  693.0 144.2 all-reduce.6
where the time goes:
time: 849 us; the launch traced here: 852 us
  waiting for transfers between devices  446 us (53%)
  local copies, waits for them, and re-layouts  172 us (20%)
  other arithmetic  129 us (15%)
  starting transfers between devices  68.2 us (8%)
  matrix products  14.2 us (2%)
  between operations  14.1 us (2%)
  loops' own time  10.2 us (1%)
    ppermute x16, waiting for transfers between devices, shifted(): lax.ppermute(value, axis, [(i, (i + by) % length) for i in range(length)])  264 us
    psum x1, waiting for transfers between devices, body(): lax.psum((rel_grad, rem_grad), ('dom', 'rel'))  151 us
    ppermute x16, starting transfers between devices, shifted(): lax.ppermute(value, axis, [(i, (i + by) % length) for i in range(length)])  68.1 us
    gather x13, local copies, waits for them, and re-layouts, block_update(): rel_vec = jnp.take(relations, rel_row, axis=0)  43.7 us
    scatter-add x10, other arithmetic, block_update(): rem_grad = rem_grad.at[lhs_rem].add(grad_lhs).at[cand_rem].add(grad_cand)  35.6 us
    scatter-add x5, other arithmetic, block_update(): rel_grad = rel_grad.at[rel_row].add(grad_rel)  31 us
    psum x1, waiting for transfers between devices, body(): grad_partitions = lax.psum(lhs_grad + home_grad, 'rel')  30.8 us
    while x16, local copies, waits for them, and re-layouts, run_stop(): return lax.fori_loop(0, share(stop), block_step, grads)  22.7 us
  transfers between devices with their start and end apart: 18, of which 10 were waited for; matrix products, arithmetic and copies ran while one was open for 1% of the time, Pallas kernels for 0%

commit v1 on v0

v1 whole, which is shorter than its diff:
```python
import functools

import jax
import jax.numpy as jnp
from jax import lax
from jax.experimental import pallas as pl
from jax.experimental.pallas import tpu as pltpu
from jax.sharding import PartitionSpec as P

F32 = jnp.float32
BF16 = jnp.bfloat16
LANES = 128
VMEM_LIMIT = 56 * 2**20
NT = (((1,), (1,)), ((), ()))
NN = (((1,), (0,)), ((), ()))
TN = (((0,), (0,)), ((), ()))


def params():
    return pltpu.CompilerParams(vmem_limit_bytes=VMEM_LIMIT)


def bits_of(count):
    return count.bit_length() - 1


def reverse_bits(value, count):
    out = 0
    for bit in range(bits_of(count)):
        out = out * 2 + ((value >> bit) & 1)
    return out


def split(value):
    high = value.astype(BF16)
    low = (value - high.astype(F32)).astype(BF16)
    return high, low


def dot(left, right, dims):
    return lax.dot_general(left, right, dims, preferred_element_type=F32)


def dot3(left, right, dims):
    left_high, left_low = split(left)
    right_high, right_low = split(right)
    return (
        dot(left_high, right_high, dims)
        + dot(left_high, right_low, dims)
        + dot(left_low, right_high, dims)
    )


def one_hot(ids, rows, base=0):
    place = lax.broadcasted_iota(jnp.int32, (rows, ids.shape[1]), 0)
    return jnp.where(place == ids - base, 1.0, 0.0).astype(BF16)


def store_split(ref, cols, value):
    high, low = split(value)
    depth = value.shape[0]
    ref[0:depth, cols] = high
    ref[depth : 2 * depth, cols] = low


def folded(value):
    depth = value.shape[0] // 2
    return value[:depth] + value[depth:]


def quantized(value):
    top = jnp.max(jnp.abs(value), axis=0, keepdims=True)
    exponent = jnp.floor(jnp.log2(jnp.maximum(top, 1e-30))) + 1.0
    scaled = jnp.round(value * jnp.exp2(15.0 - exponent))
    return jnp.clip(scaled, -32767.0, 32767.0), exponent


def to_words(value):
    return value.astype(jnp.int32).astype(jnp.int16)


def from_words(words):
    return words.astype(jnp.int32).astype(F32)


def pack_table(value):
    scaled, exponent = quantized(value)
    tail = jnp.broadcast_to(exponent, (16, value.shape[1]))
    return to_words(jnp.concatenate([scaled, tail], axis=0))


def unpack_table(words):
    depth = words.shape[0] - 16
    value = from_words(words)
    return value[:depth] * jnp.exp2(value[depth : depth + 1] - 15.0)


def pack_chunk(value):
    scaled, exponent = quantized(value)
    rows = value.shape[0]
    place = lax.broadcasted_iota(jnp.int32, value.shape, 0)
    return to_words(jnp.where(place >= rows - 8, exponent, scaled))


def unpack_chunk(words):
    value = from_words(words)
    rows = value.shape[0]
    place = lax.broadcasted_iota(jnp.int32, value.shape, 0)
    scale = jnp.exp2(value[rows - 1 : rows] - 15.0)
    return jnp.where(place >= rows - 8, 0.0, value * scale)


class Plan:
    def __init__(self, doms, rels, prows, width, rems, nrels, maxb):
        self.doms, self.rels, self.maxb = doms, rels, maxb
        self.devices = doms * rels
        self.prows, self.width, self.rems, self.nrels = prows, width, rems, nrels
        self.buckets = doms // rels
        self.slots = rels * maxb
        self.bucket_edges = self.slots * LANES
        self.edges = self.buckets * self.bucket_edges
        self.part_lanes = prows // rels
        self.half_rel, self.half_rem = nrels // 2, rems // 2
        self.half_lanes = self.half_rel + self.half_rem
        self.subs = width // 8
        self.units = (self.half_lanes // LANES) * self.subs
        self.half_chunks = self.devices // 2
        self.chunk_units = -(-self.units // self.half_chunks)
        self.chunk_rows = (self.chunk_units + 2) // 2 * 16
        rel_bits = bits_of(rels)
        all_bits = rel_bits + bits_of(doms)
        self.groups = [
            [0],
            list(range(1, rel_bits + 1)),
            list(range(rel_bits + 1, all_bits)),
        ]
        self.masks = [self.group_masks(bits) for bits in self.groups]
        order = [bit for group in self.groups for bit in reversed(group)]
        self.place = {bit: all_bits - 1 - at for at, bit in enumerate(order)}

    @staticmethod
    def group_masks(bits):
        masks = []
        for index in range(2 ** len(bits)):
            masks.append(sum(((index >> at) & 1) << bit for at, bit in enumerate(bits)))
        return masks

    def me(self):
        return lax.axis_index("dom") * self.rels + lax.axis_index("rel")

    def low_chunk(self, device):
        return device >> 1

    def position(self, chunk, me):
        relative = chunk ^ (me >> 1)
        out = 0
        for bit, at in self.place.items():
            if bit:
                out = out + (((relative >> (bit - 1)) & 1) << at)
        return out

    def bucket_mask(self, rel, bucket):
        return reverse_bits(rel, self.rels) * self.buckets + bucket

    def dynamic_mask(self, rel, bucket):
        out = 0
        width = bits_of(self.rels)
        for bit in range(width):
            out = out + (((rel >> bit) & 1) << (width - 1 - bit))
        return out * self.buckets + bucket


def send(value, plan, target):
    pairs = [(device, target(device)) for device in range(plan.devices)]
    return lax.ppermute(value, ("dom", "rel"), pairs)


def lists_kernel(plan, *refs):
    tables, counts, outs = refs[:7], refs[7], refs[8:]
    source = lax.axis_index("dom")
    rel = lax.axis_index("rel")
    for mask, out in enumerate(outs):
        for bucket in range(plan.buckets):
            target = source ^ plan.dynamic_mask(rel ^ mask, bucket)
            stop = lax.rem(source - target + plan.doms, plan.doms)
            for turn in range(plan.maxb):
                block = bucket * plan.maxb + turn
                for at, table in enumerate(tables):
                    out[block, at : at + 1, :] = table[0, stop, turn : turn + 1, :]
                live = jnp.where(turn < counts[stop], 1, 0)
                out[block, 7:8, :] = jnp.full((1, LANES), live, jnp.int32)


def prep_kernel(plan, *refs):
    labels = refs[: plan.rels]
    own, rem, relations, lhs_out, rel_out, u_out, rem_out, rel_split = refs[plan.rels :]
    depth, half = plan.width, plan.width // 2
    high, low = split(relations[...])
    rel_split[0:depth, :] = high
    rel_split[depth : 2 * depth, :] = low
    for bucket in range(plan.buckets):
        for pair in range(0, plan.slots, 2):
            blocks = [divmod(slot, plan.maxb) for slot in range(pair, min(pair + 2, plan.slots))]
            row = lambda at: jnp.concatenate(
                [
                    labels[mask][bucket * plan.maxb + turn, at : at + 1, :]
                    for mask, turn in blocks
                ],
                axis=1,
            )
            start = bucket * plan.bucket_edges + pair * LANES
            wide = len(blocks) * LANES
            cols = slice(start, start + wide)
            lhs = dot(own[...], one_hot(row(0), plan.prows), NN) + dot(
                rem[...], one_hot(row(1), plan.rems), NN
            )
            vec = folded(dot(rel_split[...], one_hot(row(2), plan.nrels), NN))
            lhs_out[:, cols] = lhs
            rel_out[:, cols] = vec
            u_out[0:half, cols] = lhs[:half] * vec[:half] - lhs[half:] * vec[half:]
            u_out[half:, cols] = lhs[:half] * vec[half:] + lhs[half:] * vec[:half]
            for at, (mask, turn) in enumerate(blocks):
                block = labels[mask]
                place = bucket * plan.maxb + turn
                ids = jnp.concatenate([block[place, 4:5, :], block[place, 6:7, :]], axis=1)
                begin = 2 * (start + at * LANES)
                rem_out[:, begin : begin + 2 * LANES] = dot(
                    rem[...], one_hot(ids, plan.rems), NN
                ).astype(BF16)


def conjugate_parts(grad, other):
    half = grad.shape[0] // 2
    grad_re, grad_im = grad[:half], grad[half:]
    other_re, other_im = other[:half], other[half:]
    return jnp.concatenate(
        [grad_re * other_re + grad_im * other_im, grad_im * other_re - grad_re * other_im], 0
    )


def bucket_kernel(plan, bucket, packed, *refs):
    labels = refs[: plan.rels]
    target, lhs_in, rel_in, u_in, rem_in = refs[plan.rels : plan.rels + 5]
    lhs_out, rel_out, cand_out, part_out = refs[plan.rels + 5 :]
    total = 2 * LANES
    blocks = [
        (labels[mask], bucket * plan.maxb + turn)
        for mask, turn in (divmod(slot, plan.maxb) for slot in range(plan.slots))
    ]
    edge = lax.broadcasted_iota(jnp.int32, (LANES, total), 0)
    column = lax.broadcasted_iota(jnp.int32, (LANES, total), 1)
    keep = jnp.where(edge == column, 0.0, 1.0 / total)
    cand_ids = [
        jnp.concatenate([label[at, 3:4, :], label[at, 5:6, :]], axis=1) for label, at in blocks
    ]
    for slot, (label, at) in enumerate(blocks):
        cols = slice(slot * LANES, (slot + 1) * LANES)
        wide = slice(slot * total, (slot + 1) * total)
        cand = dot(target[...], one_hot(cand_ids[slot], plan.prows), NN) + rem_in[
            :, wide
        ].astype(F32)
        rhs = cand[:, :LANES]
        u_vec = u_in[:, cols]
        live = label[at, 7:8, :].astype(F32)
        positive = jnp.sum(u_vec * rhs, axis=0, keepdims=True)
        negative = dot3(u_vec, cand, TN)
        grad_pos = -jax.nn.sigmoid(-positive) * live
        grad_neg = jax.nn.sigmoid(negative) * keep * live[0:1, 0:1]
        grad_u = grad_pos * rhs + dot3(cand, grad_neg, NT)
        from_neg = dot3(u_vec, grad_neg, NN)
        grad_cand = jnp.concatenate(
            [from_neg[:, :LANES] + grad_pos * u_vec, from_neg[:, LANES:]], axis=1
        )
        store_split(lhs_out, cols, conjugate_parts(grad_u, rel_in[:, cols]))
        store_split(rel_out, cols, conjugate_parts(grad_u, lhs_in[:, cols]))
        store_split(cand_out, wide, grad_cand)
    ids = jnp.concatenate(cand_ids, axis=1) ^ (lax.axis_index("rel") * plan.part_lanes)
    part = folded(dot(cand_out[...], one_hot(ids, plan.prows), NT))
    part_out[...] = pack_table(part) if packed else part


def reduce_kernel(plan, away, *refs):
    labels = refs[: plan.rels]
    grads = refs[plan.rels : plan.rels + 3 * plan.buckets]
    out, table = refs[plan.rels + 3 * plan.buckets :]
    me = plan.me()
    half = (me & 1) ^ (1 if away else 0)
    blocks = lambda bucket: [
        (labels[mask], bucket * plan.maxb + turn)
        for mask, turn in (divmod(slot, plan.maxb) for slot in range(plan.slots))
    ]
    row = lambda bucket, at: jnp.concatenate(
        [label[place, at : at + 1, :] for label, place in blocks(bucket)], axis=1
    )
    pairs = lambda bucket, first, second: jnp.concatenate(
        [
            label[place, at : at + 1, :]
            for label, place in blocks(bucket)
            for at in (first, second)
        ],
        axis=1,
    )
    depth = plan.width
    step = 2 * LANES if plan.half_rel % (2 * LANES) == 0 else LANES
    for start in range(0, plan.half_rel, step):
        total = 0.0
        for bucket in range(plan.buckets):
            hot = one_hot(row(bucket, 2), step, half * plan.half_rel + start)
            total = total + dot(grads[3 * bucket + 1][...], hot, NT)
        table[:, start : start + step] = folded(total)
    total = 0.0
    base = half * plan.half_rem
    for bucket in range(plan.buckets):
        hot = one_hot(row(bucket, 1), plan.half_rem, base)
        total = total + dot(grads[3 * bucket][...], hot, NT)
        hot = one_hot(pairs(bucket, 4, 6), plan.half_rem, base)
        total = total + dot(grads[3 * bucket + 2][...], hot, NT)
    table[:, plan.half_rel :] = folded(total)
    for chunk in range(plan.half_chunks):
        parts = []
        for unit in range(chunk * plan.chunk_units, (chunk + 1) * plan.chunk_units):
            if unit < plan.units:
                lane, sub = divmod(unit, plan.subs)
                parts.append(table[8 * sub : 8 * sub + 8, lane * LANES : (lane + 1) * LANES])
            else:
                parts.append(jnp.zeros((8, LANES), F32))
        spare = plan.chunk_rows - 8 * plan.chunk_units
        parts.append(jnp.zeros((spare, LANES), F32))
        value = jnp.concatenate(parts, axis=0)
        out[plan.position(chunk, me)] = pack_chunk(value) if away else value


def combine_kernel(group, last, *refs):
    keep, arrived = refs[0], refs[1:group]
    outs = refs[group:]
    count = keep.shape[0]
    share = count // len(outs)
    for at in range(count):
        value = keep[at]
        for ref in arrived:
            value = value + unpack_chunk(ref[at])
        which, place = divmod(at, share)
        outs[which][place] = pack_chunk(value) if (which or last) else value


def spread_kernel(plan, count, *refs):
    pieces, (rel_out, rem_out, held) = refs[:count], refs[count:]
    at = 0
    for piece in pieces:
        held[at : at + piece.shape[0]] = piece[...]
        at += piece.shape[0]
    me = plan.me()
    core = me & 1
    for half in range(2):
        first = (half ^ core) * plan.half_chunks
        for chunk in range(plan.half_chunks):
            value = unpack_chunk(held[first + plan.position(chunk, me)])
            for index in range(plan.chunk_units):
                unit = chunk * plan.chunk_units + index
                if unit >= plan.units:
                    break
                lane, sub = divmod(unit, plan.subs)
                lane = lane * LANES
                rows = slice(8 * sub, 8 * sub + 8)
                block = value[8 * index : 8 * index + 8]
                if lane < plan.half_rel:
                    lane += half * plan.half_rel
                    rel_out[rows, lane : lane + LANES] = block
                else:
                    lane += half * plan.half_rem - plan.half_rel
                    rem_out[rows, lane : lane + LANES] = block


def add_pack_kernel(*refs):
    value = refs[0][...]
    for ref in refs[1:-1]:
        value = value + unpack_table(ref[...])
    refs[-1][...] = pack_table(value)


def source_kernel(plan, *refs):
    labels = refs[: plan.rels]
    grads, out = refs[plan.rels : -1], refs[-1]
    shift = lax.axis_index("rel") * plan.part_lanes
    total = 0.0
    for bucket in range(plan.buckets):
        ids = jnp.concatenate(
            [
                labels[mask][bucket * plan.maxb + turn, 0:1, :]
                for mask, turn in (divmod(slot, plan.maxb) for slot in range(plan.slots))
            ],
            axis=1,
        )
        total = total + dot(grads[bucket][...], one_hot(ids ^ shift, plan.prows), NT)
    out[...] = folded(total)


def share_kernel(plan, table, arrived, keep, *outs):
    value = table[...] + unpack_table(arrived[...])
    lanes = plan.part_lanes
    keep[...] = value[:, :lanes]
    for at, out in enumerate(outs):
        out[...] = pack_table(value[:, (at + 1) * lanes : (at + 2) * lanes])


def part_out_kernel(plan, *refs):
    out = refs[-1]
    rel = lax.axis_index("rel")
    lanes = plan.part_lanes
    for mask, ref in enumerate(refs[:-1]):
        if lanes % LANES:
            out[:, mask * lanes : (mask + 1) * lanes] = unpack_table(ref[...])
        else:
            start = pl.multiple_of((rel ^ mask) * lanes, lanes)
            out[:, pl.ds(start, lanes)] = unpack_table(ref[...])


def shape(extent, kind):
    return jax.ShapeDtypeStruct(extent, kind)


def call(kernel, outs, args, scratch=(), in_specs=None, name=None):
    return pl.pallas_call(
        kernel,
        out_shape=outs,
        in_specs=in_specs or [pl.BlockSpec(memory_space=pltpu.VMEM)] * len(args),
        out_specs=[pl.BlockSpec(memory_space=pltpu.VMEM)] * len(outs),
        scratch_shapes=list(scratch),
        compiler_params=params(),
        name=name,
    )(*args)


def body(
    partitions,
    remainder,
    relations,
    counts,
    lhs_rows,
    lhs_rems,
    rel_ids,
    rhs_rows,
    rhs_rems,
    neg_rows,
    neg_rems,
):
    prows, width = partitions.shape
    plan = Plan(
        lax.axis_size("dom"),
        lax.axis_size("rel"),
        prows,
        width,
        remainder.shape[0],
        relations.shape[0],
        lhs_rows.shape[2],
    )
    vmem = pl.BlockSpec(memory_space=pltpu.VMEM)
    smem = pl.BlockSpec(memory_space=pltpu.SMEM)
    own, rem, rels = partitions.T, remainder.T, relations.T
    edges, lanes = plan.edges, plan.bucket_edges

    targets = [send(own, plan, lambda d: d ^ (plan.bucket_mask(d % plan.rels, 0) * plan.rels))]
    for bucket in range(1, plan.buckets):
        targets.append(send(targets[0], plan, lambda d, b=bucket: d ^ (b * plan.rels)))

    tables = [lhs_rows, lhs_rems, rel_ids, rhs_rows, rhs_rems, neg_rows, neg_rems]
    labels = call(
        functools.partial(lists_kernel, plan),
        [shape((plan.buckets * plan.maxb, 8, LANES), jnp.int32)] * plan.rels,
        tables + [counts.reshape(-1)],
        in_specs=[vmem] * 7 + [smem],
        name="lists",
    )
    labels = [labels[0]] + [
        send(labels[mask], plan, lambda d, m=mask: d ^ m) for mask in range(1, plan.rels)
    ]

    lhs, vec, u_vec, cand_rem = call(
        functools.partial(prep_kernel, plan),
        [
            shape((width, edges), F32),
            shape((width, edges), F32),
            shape((width, edges), F32),
            shape((width, 2 * edges), BF16),
        ],
        labels + [own, rem, rels],
        scratch=[pltpu.VMEM((2 * width, plan.nrels), BF16)],
        name="prep",
    )

    grads, parts = [], []
    for bucket in range(plan.buckets):
        packed = bucket > 0
        one = pl.BlockSpec((width, lanes), lambda i, b=bucket: (0, b))
        two = pl.BlockSpec((width, 2 * lanes), lambda i, b=bucket: (0, b))
        whole = lambda extent: pl.BlockSpec(extent, lambda i: (0,) * len(extent))
        outs = [
            shape((2 * width, lanes), BF16),
            shape((2 * width, lanes), BF16),
            shape((2 * width, 2 * lanes), BF16),
            shape((width + 16, prows), jnp.int16) if packed else shape((width, prows), F32),
        ]
        made = pl.pallas_call(
            functools.partial(bucket_kernel, plan, bucket, packed),
            grid=(1,),
            out_shape=outs,
            in_specs=[whole(label.shape) for label in labels]
            + [whole(own.shape), one, one, one, two],
            out_specs=[whole(out.shape) for out in outs],
            compiler_params=params(),
            name="bucket",
        )(*labels, targets[bucket], lhs, vec, u_vec, cand_rem)
        grads += made[:3]
        parts.append(made[3])

    chunk = (plan.half_chunks, plan.chunk_rows, LANES)
    half_args = labels + grads
    table = [pltpu.VMEM((width, plan.half_lanes), F32)]
    (away,) = call(
        functools.partial(reduce_kernel, plan, True),
        [shape(chunk, jnp.int16)],
        half_args,
        scratch=table,
        name="reduce_away",
    )
    arrived = [send(away, plan, lambda d: d ^ 1)]
    near = [
        send(parts[bucket], plan, lambda d, b=bucket: d ^ (b * plan.rels))
        for bucket in range(1, plan.buckets)
    ]
    (keep,) = call(
        functools.partial(reduce_kernel, plan, False),
        [shape(chunk, F32)],
        half_args,
        scratch=table,
        name="reduce_home",
    )
    (far,) = call(
        add_pack_kernel, [shape((width + 16, prows), jnp.int16)], [parts[0]] + near, name="far"
    )
    far = send(far, plan, lambda d: d ^ (plan.bucket_mask(d % plan.rels, 0) * plan.rels))
    (source,) = call(
        functools.partial(source_kernel, plan),
        [shape((width, prows), F32)],
        labels + grads[0::3],
        name="source",
    )

    count = plan.half_chunks
    for level, masks in enumerate(plan.masks[1:]):
        size = len(masks)
        count //= size
        outs = [shape((count,) + chunk[1:], F32)] + [
            shape((count,) + chunk[1:], jnp.int16)
        ] * (size - 1)
        made = call(
            functools.partial(combine_kernel, 1 + len(arrived), False),
            outs,
            [keep] + arrived,
            name="combine",
        )
        keep = made[0]
        arrived = [
            send(value, plan, lambda d, m=mask: d ^ m)
            for value, mask in zip(made[1:], masks[1:])
        ]
    (total,) = call(
        functools.partial(combine_kernel, 1 + len(arrived), True),
        [shape((1,) + chunk[1:], jnp.int16)],
        [keep] + arrived,
        name="total",
    )

    lanes = plan.part_lanes
    shares = call(
        functools.partial(share_kernel, plan),
        [shape((width, lanes), F32)]
        + [shape((width + 16, lanes), jnp.int16)] * (plan.rels - 1),
        [source, far],
        name="share",
    )
    mine = [shares[0]] + [
        send(value, plan, lambda d, m=mask: d ^ m)
        for mask, value in zip(range(1, plan.rels), shares[1:])
    ]
    (mine,) = call(
        add_pack_kernel, [shape((width + 16, lanes), jnp.int16)], mine, name="mine"
    )

    pieces = [total]
    for masks in reversed(plan.masks[1:]):
        whole_piece = jnp.concatenate(pieces, axis=0)
        pieces = [whole_piece] + [
            send(whole_piece, plan, lambda d, m=mask: d ^ m) for mask in masks[1:]
        ]
    pieces += [send(piece, plan, lambda d: d ^ 1) for piece in pieces]

    owners = [mine] + [
        send(mine, plan, lambda d, m=mask: d ^ m) for mask in range(1, plan.rels)
    ]
    (grad_partitions,) = call(
        functools.partial(part_out_kernel, plan),
        [shape((width, prows), F32)],
        owners,
        name="part_out",
    )
    if lanes % LANES:
        order = jnp.arange(plan.rels) ^ lax.axis_index("rel")
        split_lanes = grad_partitions.reshape(width, plan.rels, lanes)
        grad_partitions = jnp.take(split_lanes, order, axis=1).reshape(width, prows)
    grad_relations, grad_remainder = call(
        functools.partial(spread_kernel, plan, len(pieces)),
        [shape((width, plan.nrels), F32), shape((width, plan.rems), F32)],
        pieces,
        scratch=[pltpu.VMEM((plan.devices,) + chunk[1:], jnp.int16)],
        name="spread",
    )
    return grad_partitions.T, grad_remainder.T, grad_relations.T


def solution(mesh):
    edge = P("dom", None, "rel", None)
    in_specs = (P("dom", None), P(), P(), P("dom", None, "rel")) + (edge,) * 7
    out_specs = (P("dom", None), P(), P())
    return jax.shard_map(body, mesh=mesh, in_specs=in_specs, out_specs=out_specs, check_vma=False)
```

time: 849 us -> 155 us (0.18)
  waiting for transfers between devices: 446 us -> 36.3 us
  local copies, waits for them, and re-layouts: 172 us -> 8.15 us
  other arithmetic: 129 us -> 0.91 us
  Pallas kernels: 0 us -> 67.4 us
  starting transfers between devices: 68.2 us -> 41.4 us
  matrix products: 14.2 us -> 0 us
  between operations: 14.1 us -> 0.77 us
  loops' own time: 10.2 us -> 0 us
    ppermute x16 -> x30, waiting for transfers between devices: 264 us -> 36.3 us  [send(): return lax.ppermute(value, ('dom', 'rel'), pairs)]
    psum x2 -> x0, waiting for transfers between devices: 181 us -> none  [the longest x1 151 us: body(): lax.psum((rel_grad, rem_grad), ('dom', 'rel'))]
    scatter-add x25 -> x0, other arithmetic: 106 us -> none  [the longest x10 35.6 us: block_update(): rem_grad = rem_grad.at[lhs_rem].add(grad_lhs).at[cand_rem].add(grad_cand)]
    gather x65 -> x0, local copies, waits for them, and re-layouts: 95.7 us -> none  [the longest x13 43.7 us: block_update(): rel_vec = jnp.take(relations, rel_row, axis=0)]
    pallas_call x0 -> x15, Pallas kernels: none -> 67.4 us  [the longest x13 51.6 us: call(): pl.pallas_call(kernel, out_shape=outs, in_specs=in_specs or [pl.BlockSpec...]
    while x22 -> x0, local copies, waits for them, and re-layouts: 37.7 us -> none  [the longest x16 22.7 us: run_stop(): return lax.fori_loop(0, share(stop), block_step, grads)]
    ppermute x16 -> x30, starting transfers between devices: 68.1 us -> 41.4 us  [send(): return lax.ppermute(value, ('dom', 'rel'), pairs)]
    dot_general x24 -> x0, matrix products: 14.2 us -> none  [the longest x8 5.49 us: edge_terms(): lax.dot_general(grad_neg, u_vec, (((0,), (0,)), ((), ())), precision=high...]
  transfers between devices with their start and end apart: 18 -> 30, of which waited for: 10 -> 16; matrix products, arithmetic and copies ran while one was open for 1% -> 1% of each run, Pallas kernels for 0% -> 30%
where the time goes in v1:
time: 155 us
  Pallas kernels  67.4 us (43%)
  starting transfers between devices  41.4 us (27%)
  waiting for transfers between devices  36.3 us (23%)
  local copies, waits for them, and re-layouts  8.15 us (5%)
    pallas_call x13, Pallas kernels, call(): pl.pallas_call(kernel, out_shape=outs, in_specs=in_specs or [pl.BlockSpec...  51.6 us
    ppermute x30, starting transfers between devices, send(): return lax.ppermute(value, ('dom', 'rel'), pairs)  41.4 us
    ppermute x30, waiting for transfers between devices, send(): return lax.ppermute(value, ('dom', 'rel'), pairs)  36.3 us
    pallas_call x2, Pallas kernels, body(): pl.pallas_call(functools.partial(bucket_kernel, plan, bucket, packed), gr...  15.8 us
    unnamed x58, local copies, waits for them, and re-layouts  8.15 us
  transfers between devices with their start and end apart: 30, of which 16 were waited for; matrix products, arithmetic and copies ran while one was open for 1% of the time, Pallas kernels for 30%

profile of v1, /device:TPU:0, one launch (start us, length us, event | category | flops | bytes accessed | tf_op | source)
XLA Modules:
  0.0 154.9 jit_solution(2815334893238327377)
XLA Ops:
  2.3 3.0 %collective-permute-start.4 = (bf16[400,512]{1,0:T(8,128)(2,1)S(1)}, bf16[400,512]{1,0:T(8,128)(2,1)S(1)}, u32[]{:S(2)}, u32[]{:S(2)}) collective-permute-start(bf16[400,512]{1,0:T(8,128)(2,1)S(1)} %collective-permute-done.3.refs_4_), channel_id=1, source_target_pairs={{0,4},{1,5},{2,6},{3,7},{4,0},{5,1},{6,2},{7,3},{8,12},{9,13},{10,... | collective-permute-start | bytes 1228808 | tf_op jit(solution)/shard_map/ppermute | solution.py:175
  6.7 12.1 %collective-permute-start = (s32[2,8,128]{2,1,0:T(8,128)}, s32[2,8,128]{2,1,0:T(8,128)S(1)}, u32[]{:S(2)}, u32[]{:S(2)}) collective-permute-start(s32[2,8,128]{2,1,0:T(8,128)} %get-tuple-element.34), channel_id=1, source_target_pairs={{0,1},{1,0},{2,3},{3,2},{4,5},{5,4},{6,7},{7,6},{8,9},{9,8},{10,11... | collective-permute-start | bytes 24584 | tf_op jit(solution)/shard_map/ppermute | solution.py:175
  18.8 2.3 %collective-permute-start.1 = (s32[2,8,128]{2,1,0:T(8,128)}, s32[2,8,128]{2,1,0:T(8,128)S(1)}, u32[]{:S(2)}, u32[]{:S(2)}) collective-permute-start(s32[2,8,128]{2,1,0:T(8,128)} %get-tuple-element.35), channel_id=1, source_target_pairs={{0,2},{1,3},{2,0},{3,1},{4,6},{5,7},{6,4},{7,5},{8,10},{9,11},{10,... | collective-permute-start | bytes 24584 | tf_op jit(solution)/shard_map/ppermute | solution.py:175
  25.0 10.3 %prep.1 = (f32[400,1024]{1,0:T(8,128)}, f32[400,1024]{1,0:T(8,128)}, f32[400,1024]{1,0:T(8,128)}, bf16[400,2048]{1,0:T(8,128)(2,1)}) custom-call(s32[2,8,128]{2,1,0:T(8,128)} %get-tuple-element.33.refs_0_, s32[2,8,128]{2,1,0:T(8,128)} %copy-done.16, s32[2,8,128]{2,1,0:T(8,128)} %copy-done.17, s32[2,8,128]{2,1,0:T(8,128)} %copy-done.18, ...), custom_call_target="tpu_custom_call" | custom-call | tf_op jit(solution)/shard_map/prep/pallas_call | solution.py:423
  35.2 7.9 %bucket.2 = (bf16[800,512]{1,0:T(8,128)(2,1)}, bf16[800,512]{1,0:T(8,128)(2,1)}, bf16[800,1024]{1,0:T(8,128)(2,1)}, f32[400,512]{1,0:T(8,128)}) custom-call(s32[2,8,128]{2,1,0:T(8,128)} %get-tuple-element.33.refs_0_, s32[2,8,128]{2,1,0:T(8,128)} %copy-done.16, s32[2,8,128]{2,1,0:T(8,128)} %copy-done.17, s32[2,8,128]{2,1,0:T(8,128)} %copy-done.18, ...), custom_call_target="tpu_custom_call" | custom-call | tf_op jit(solution)/shard_map/bucket/pallas_call | solution.py:503
  43.8 7.9 %bucket.3 = (bf16[800,512]{1,0:T(8,128)(2,1)}, bf16[800,512]{1,0:T(8,128)(2,1)}, bf16[800,1024]{1,0:T(8,128)(2,1)}, s16[416,512]{1,0:T(8,128)(2,1)}) custom-call(s32[2,8,128]{2,1,0:T(8,128)} %get-tuple-element.33.refs_0_, s32[2,8,128]{2,1,0:T(8,128)} %copy-done.16, s32[2,8,128]{2,1,0:T(8,128)} %copy-done.17, s32[2,8,128]{2,1,0:T(8,128)} %copy-done.18, ...), custom_call_target="tpu_custom_call" | custom-call | tf_op jit(solution)/shard_map/bucket/pallas_call | solution.py:503
  51.8 7.8 %reduce_away.1 = s16[16,288,128]{2,1,0:T(8,128)(2,1)} custom-call(s32[2,8,128]{2,1,0:T(8,128)} %get-tuple-element.33.refs_0_, s32[2,8,128]{2,1,0:T(8,128)} %copy-done.16, s32[2,8,128]{2,1,0:T(8,128)} %copy-done.17, s32[2,8,128]{2,1,0:T(8,128)} %copy-done.18, bf16[800,512]{1,0:T(8,128)(2,1)} %get-tuple-element.41.refs_4_, ...), custom_call_target="tpu_custom_call" | custom-call | tf_op jit(solution)/shard_map/reduce_away/pallas_call | solution.py:423
  60.3 8.1 %reduce_home.1.refs_0_ = f32[16,288,128]{2,1,0:T(8,128)} custom-call(s32[2,8,128]{2,1,0:T(8,128)} %get-tuple-element.33.refs_0_, s32[2,8,128]{2,1,0:T(8,128)} %copy-done.16, s32[2,8,128]{2,1,0:T(8,128)} %copy-done.17, s32[2,8,128]{2,1,0:T(8,128)} %copy-done.18, bf16[800,512]{1,0:T(8,128)(2,1)} %get-tuple-element.41.refs_4_, ...), custom_call_target="tpu_custom_call" | custom-call | tf_op jit(solution)/shard_map/reduce_home/pallas_call | solution.py:423
  69.4 3.5 %combine.2 = (f32[4,288,128]{2,1,0:T(8,128)}, s16[4,288,128]{2,1,0:T(8,128)(2,1)}, s16[4,288,128]{2,1,0:T(8,128)(2,1)}, s16[4,288,128]{2,1,0:T(8,128)(2,1)}) custom-call(f32[16,288,128]{2,1,0:T(8,128)} %reduce_home.1.refs_0_, s16[16,288,128]{2,1,0:T(8,128)(2,1)} %copy-done.1), custom_call_target="tpu_custom_call" | custom-call | tf_op jit(solution)/shard_map/combine/pallas_call | solution.py:423
  77.2 2.3 %far.1 = s16[416,512]{1,0:T(8,128)(2,1)} custom-call(f32[400,512]{1,0:T(8,128)} %get-tuple-element.43.refs_0_, s16[416,512]{1,0:T(8,128)(2,1)} %copy-done.3), custom_call_target="tpu_custom_call" | custom-call | tf_op jit(solution)/shard_map/far/pallas_call | solution.py:423
  83.0 4.9 %collective-permute-done.15.refs_2_ = s16[4,288,128]{2,1,0:T(8,128)(2,1)S(1)} collective-permute-done((s16[4,288,128]{2,1,0:T(8,128)(2,1)}, s16[4,288,128]{2,1,0:T(8,128)(2,1)S(1)}, u32[]{:S(2)}, u32[]{:S(2)}) %collective-permute-start.15) | collective-permute-done | bytes 294944 | tf_op jit(solution)/shard_map/ppermute | solution.py:175
  90.1 2.3 %combine.3 = (f32[1,288,128]{2,1,0:T(8,128)}, s16[1,288,128]{2,1,0:T(8,128)(2,1)}, s16[1,288,128]{2,1,0:T(8,128)(2,1)}, s16[1,288,128]{2,1,0:T(8,128)(2,1)}) custom-call(f32[4,288,128]{2,1,0:T(8,128)} %get-tuple-element.53.refs_0_, s16[4,288,128]{2,1,0:T(8,128)(2,1)} %copy-done.13, s16[4,288,128]{2,1,0:T(8,128)(2,1)} %copy-done.14, ...), custom_call_target="tpu_custom_call" | custom-call | tf_op jit(solution)/shard_map/combine/pallas_call | solution.py:423
  93.2 3.5 %collective-permute-start.18 = (s16[1,288,128]{2,1,0:T(8,128)(2,1)}, s16[1,288,128]{2,1,0:T(8,128)(2,1)S(1)}, u32[]{:S(2)}, u32[]{:S(2)}) collective-permute-start(s16[1,288,128]{2,1,0:T(8,128)(2,1)} %get-tuple-element.59), channel_id=1, source_target_pairs={{0,16},{1,17},{2,18},{3,19},{4,20},{5,21},{6,22},{7,23},{8,24},{9,... | collective-permute-start | bytes 221192 | tf_op jit(solution)/shard_map/ppermute | solution.py:175
  97.6 3.7 %collective-permute-done.18.refs_2_ = s16[1,288,128]{2,1,0:T(8,128)(2,1)S(1)} collective-permute-done((s16[1,288,128]{2,1,0:T(8,128)(2,1)}, s16[1,288,128]{2,1,0:T(8,128)(2,1)S(1)}, u32[]{:S(2)}, u32[]{:S(2)}) %collective-permute-start.18) | collective-permute-done | bytes 73760 | tf_op jit(solution)/shard_map/ppermute | solution.py:175
  107.0 2.8 %collective-permute-start.20 = (s16[1,288,128]{2,1,0:T(8,128)(2,1)}, s16[1,288,128]{2,1,0:T(8,128)(2,1)S(1)}, u32[]{:S(2)}, u32[]{:S(2)}) collective-permute-start(s16[1,288,128]{2,1,0:T(8,128)(2,1)} %total.1), channel_id=1, source_target_pairs={{0,8},{1,9},{2,10},{3,11},{4,12},{5,13},{6,14},{7,15},{8,0},{9,1},... | collective-permute-start | bytes 221192 | tf_op jit(solution)/shard_map/ppermute | solution.py:175
  109.8 2.0 %collective-permute-done.22 = s16[1,288,128]{2,1,0:T(8,128)(2,1)S(1)} collective-permute-done((s16[1,288,128]{2,1,0:T(8,128)(2,1)}, s16[1,288,128]{2,1,0:T(8,128)(2,1)S(1)}, u32[]{:S(2)}, u32[]{:S(2)}) %collective-permute-start.22) | collective-permute-done | bytes 73760 | tf_op jit(solution)/shard_map/ppermute | solution.py:175
  114.2 1.9 %collective-permute-start.25 = (s16[4,288,128]{2,1,0:T(8,128)(2,1)S(1)}, s16[4,288,128]{2,1,0:T(8,128)(2,1)S(1)}, u32[]{:S(2)}, u32[]{:S(2)}) collective-permute-start(s16[4,288,128]{2,1,0:T(8,128)(2,1)S(1)} %pad_add_fusion.refs_0_), channel_id=1, source_target_pairs={{0,6},{1,7},{2,4},{3,5},{4,2},{5,3},{6,0},{7,1},{8,14},{9,15},{10,... | collective-permute-start | bytes 884744 | tf_op jit(solution)/shard_map/ppermute | solution.py:175
  117.8 3.4 %source.1.table = f32[400,512]{1,0:T(8,128)} custom-call(s32[2,8,128]{2,1,0:T(8,128)} %get-tuple-element.33.refs_0_, s32[2,8,128]{2,1,0:T(8,128)} %copy-done.16, s32[2,8,128]{2,1,0:T(8,128)} %copy-done.17, s32[2,8,128]{2,1,0:T(8,128)} %copy-done.18, bf16[800,512]{1,0:T(8,128)(2,1)} %get-tuple-element.41.refs_4_, ...), custom_call_target="tpu_custom_call" | custom-call | tf_op jit(solution)/shard_map/source/pallas_call | solution.py:423
  122.0 2.2 %share.1 = (f32[400,128]{1,0:T(8,128)}, s16[416,128]{1,0:T(8,128)(2,1)}, s16[416,128]{1,0:T(8,128)(2,1)}, s16[416,128]{1,0:T(8,128)(2,1)}) custom-call(f32[400,512]{1,0:T(8,128)} %source.1.table, s16[416,512]{1,0:T(8,128)(2,1)} %copy-done.2), custom_call_target="tpu_custom_call" | custom-call | tf_op jit(solution)/shard_map/share/pallas_call | solution.py:423
  126.3 3.8 %collective-permute-done.8.refs_2_ = s16[416,128]{1,0:T(8,128)(2,1)S(1)} collective-permute-done((s16[416,128]{1,0:T(8,128)(2,1)}, s16[416,128]{1,0:T(8,128)(2,1)S(1)}, u32[]{:S(2)}, u32[]{:S(2)}) %collective-permute-start.8) | collective-permute-done | bytes 106528 | tf_op jit(solution)/shard_map/ppermute | solution.py:175
  135.9 3.4 %collective-permute-done.12.refs_3_ = s16[416,128]{1,0:T(8,128)(2,1)S(1)} collective-permute-done((s16[416,128]{1,0:T(8,128)(2,1)}, s16[416,128]{1,0:T(8,128)(2,1)S(1)}, u32[]{:S(2)}, u32[]{:S(2)}) %collective-permute-start.12) | collective-permute-done | bytes 106528 | tf_op jit(solution)/shard_map/ppermute | solution.py:175
  140.2 4.3 %collective-permute-done.11.refs_2_ = s16[416,128]{1,0:T(8,128)(2,1)S(1)} collective-permute-done((s16[416,128]{1,0:T(8,128)(2,1)}, s16[416,128]{1,0:T(8,128)(2,1)S(1)}, u32[]{:S(2)}, u32[]{:S(2)}) %collective-permute-start.11) | collective-permute-done | bytes 106528 | tf_op jit(solution)/shard_map/ppermute | solution.py:175
  146.7 2.1 %part_out.1 = f32[400,512]{1,0:T(8,128)} custom-call(s16[416,128]{1,0:T(8,128)(2,1)} %mine.1.refs_0_, s16[416,128]{1,0:T(8,128)(2,1)} %copy-done.24, s16[416,128]{1,0:T(8,128)(2,1)} %copy-done.23, s16[416,128]{1,0:T(8,128)(2,1)} %copy-done.19), custom_call_target="tpu_custom_call" | custom-call | tf_op jit(solution)/shard_map/part_out/pallas_call | solution.py:423
  150.4 4.5 %spread.1 = (f32[400,2560]{1,0:T(8,128)}, f32[400,256]{1,0:T(8,128)}) custom-call(s16[4,288,128]{2,1,0:T(8,128)(2,1)} %copy-done, s16[4,288,128]{2,1,0:T(8,128)(2,1)} %copy-done.8, s16[4,288,128]{2,1,0:T(8,128)(2,1)} %copy-done.7, s16[4,288,128]{2,1,0:T(8,128)(2,1)} %copy-done.6, s16[4,288,128]{2,1,0:T(8,128)(2,1)} %copy-done.9, ...), custom_call_target="tpu_custom_call" | custom-call | tf_op jit(solution)/shard_map/spread/pallas_call | solution.py:423
  (110 shorter events, 44.3 us)
Async XLA Ops:
  2.3 40.8 %collective-permute-start.4 = (bf16[400,512]{1,0:T(8,128)(2,1)S(1)}, bf16[400,512]{1,0:T(8,128)(2,1)S(1)}, u32[]{:S(2)}, u32[]{:S(2)}) collective-permute-start(bf16[400,512]{1,0:T(8,128)(2,1)S(1)} %collective-permute-done.3.refs_4_), channel_id=1, source_target_pairs={{0,4},{1,5},{2,6},{3,7},{4,0},{5,1},{6,2},{7,3},{8,12},{9,13},{10,... | collective-permute-start | bytes 1228808 | tf_op jit(solution)/shard_map/ppermute | solution.py:175
  6.7 14.4 %collective-permute-start = (s32[2,8,128]{2,1,0:T(8,128)}, s32[2,8,128]{2,1,0:T(8,128)S(1)}, u32[]{:S(2)}, u32[]{:S(2)}) collective-permute-start(s32[2,8,128]{2,1,0:T(8,128)} %get-tuple-element.34), channel_id=1, source_target_pairs={{0,1},{1,0},{2,3},{3,2},{4,5},{5,4},{6,7},{7,6},{8,9},{9,8},{10,11... | collective-permute-start | bytes 24584 | tf_op jit(solution)/shard_map/ppermute | solution.py:175
  59.6 8.7 %collective-permute-start.13 = (s16[16,288,128]{2,1,0:T(8,128)(2,1)}, s16[16,288,128]{2,1,0:T(8,128)(2,1)S(1)}, u32[]{:S(2)}, u32[]{:S(2)}) collective-permute-start(s16[16,288,128]{2,1,0:T(8,128)(2,1)} %reduce_away.1), channel_id=1, source_target_pairs={{0,1},{1,0},{2,3},{3,2},{4,5},{5,4},{6,7},{7,6},{8,9},{9,8},{10,11... | collective-permute-start | bytes 3538952 | tf_op jit(solution)/shard_map/ppermute | solution.py:175
  59.8 16.7 %collective-permute-start.5 = (s16[416,512]{1,0:T(8,128)(2,1)S(1)}, s16[416,512]{1,0:T(8,128)(2,1)S(1)}, u32[]{:S(2)}, u32[]{:S(2)}) collective-permute-start(s16[416,512]{1,0:T(8,128)(2,1)S(1)} %copy-done.28), channel_id=1, source_target_pairs={{0,4},{1,5},{2,6},{3,7},{4,0},{5,1},{6,2},{7,3},{8,12},{9,13},{10,... | collective-permute-start | bytes 1277960 | tf_op jit(solution)/shard_map/ppermute | solution.py:175
  73.0 10.1 %collective-permute-start.14 = (s16[4,288,128]{2,1,0:T(8,128)(2,1)}, s16[4,288,128]{2,1,0:T(8,128)(2,1)S(1)}, u32[]{:S(2)}, u32[]{:S(2)}) collective-permute-start(s16[4,288,128]{2,1,0:T(8,128)(2,1)} %get-tuple-element.54), channel_id=1, source_target_pairs={{0,2},{1,3},{2,0},{3,1},{4,6},{5,7},{6,4},{7,5},{8,10},{9,11},{10,... | collective-permute-start | bytes 884744 | tf_op jit(solution)/shard_map/ppermute | solution.py:175
  73.5 14.4 %collective-permute-start.15 = (s16[4,288,128]{2,1,0:T(8,128)(2,1)}, s16[4,288,128]{2,1,0:T(8,128)(2,1)S(1)}, u32[]{:S(2)}, u32[]{:S(2)}) collective-permute-start(s16[4,288,128]{2,1,0:T(8,128)(2,1)} %get-tuple-element.55), channel_id=1, source_target_pairs={{0,4},{1,5},{2,6},{3,7},{4,0},{5,1},{6,2},{7,3},{8,12},{9,13},{10,... | collective-permute-start | bytes 884744 | tf_op jit(solution)/shard_map/ppermute | solution.py:175
  75.1 14.3 %collective-permute-start.16 = (s16[4,288,128]{2,1,0:T(8,128)(2,1)}, s16[4,288,128]{2,1,0:T(8,128)(2,1)S(1)}, u32[]{:S(2)}, u32[]{:S(2)}) collective-permute-start(s16[4,288,128]{2,1,0:T(8,128)(2,1)} %get-tuple-element.56), channel_id=1, source_target_pairs={{0,6},{1,7},{2,4},{3,5},{4,2},{5,3},{6,0},{7,1},{8,14},{9,15},{10,... | collective-permute-start | bytes 884744 | tf_op jit(solution)/shard_map/ppermute | solution.py:175
  79.5 41.7 %collective-permute-start.6 = (s16[416,512]{1,0:T(8,128)(2,1)}, s16[416,512]{1,0:T(8,128)(2,1)S(1)}, u32[]{:S(2)}, u32[]{:S(2)}) collective-permute-start(s16[416,512]{1,0:T(8,128)(2,1)} %far.1), channel_id=1, source_target_pairs={{0,0},{1,17},{2,10},{3,27},{4,4},{5,21},{6,14},{7,31},{8,8},{9,25}... | collective-permute-start | bytes 1277960 | tf_op jit(solution)/shard_map/ppermute | solution.py:175
  93.2 8.2 %collective-permute-start.18 = (s16[1,288,128]{2,1,0:T(8,128)(2,1)}, s16[1,288,128]{2,1,0:T(8,128)(2,1)S(1)}, u32[]{:S(2)}, u32[]{:S(2)}) collective-permute-start(s16[1,288,128]{2,1,0:T(8,128)(2,1)} %get-tuple-element.59), channel_id=1, source_target_pairs={{0,16},{1,17},{2,18},{3,19},{4,20},{5,21},{6,22},{7,23},{8,24},{9,... | collective-permute-start | bytes 221192 | tf_op jit(solution)/shard_map/ppermute | solution.py:175
  96.6 6.4 %collective-permute-start.19 = (s16[1,288,128]{2,1,0:T(8,128)(2,1)}, s16[1,288,128]{2,1,0:T(8,128)(2,1)S(1)}, u32[]{:S(2)}, u32[]{:S(2)}) collective-permute-start(s16[1,288,128]{2,1,0:T(8,128)(2,1)} %get-tuple-element.60), channel_id=1, source_target_pairs={{0,24},{1,25},{2,26},{3,27},{4,28},{5,29},{6,30},{7,31},{8,16},{9,... | collective-permute-start | bytes 221192 | tf_op jit(solution)/shard_map/ppermute | solution.py:175
  105.4 6.4 %collective-permute-start.22 = (s16[1,288,128]{2,1,0:T(8,128)(2,1)}, s16[1,288,128]{2,1,0:T(8,128)(2,1)S(1)}, u32[]{:S(2)}, u32[]{:S(2)}) collective-permute-start(s16[1,288,128]{2,1,0:T(8,128)(2,1)} %total.1), channel_id=1, source_target_pairs={{0,24},{1,25},{2,26},{3,27},{4,28},{5,29},{6,30},{7,31},{8,16},{9,... | collective-permute-start | bytes 221192 | tf_op jit(solution)/shard_map/ppermute | solution.py:175
  107.0 6.4 %collective-permute-start.21 = (s16[1,288,128]{2,1,0:T(8,128)(2,1)}, s16[1,288,128]{2,1,0:T(8,128)(2,1)S(1)}, u32[]{:S(2)}, u32[]{:S(2)}) collective-permute-start(s16[1,288,128]{2,1,0:T(8,128)(2,1)} %total.1), channel_id=1, source_target_pairs={{0,16},{1,17},{2,18},{3,19},{4,20},{5,21},{6,22},{7,23},{8,24},{9,... | collective-permute-start | bytes 221192 | tf_op jit(solution)/shard_map/ppermute | solution.py:175
  107.0 6.4 %collective-permute-start.20 = (s16[1,288,128]{2,1,0:T(8,128)(2,1)}, s16[1,288,128]{2,1,0:T(8,128)(2,1)S(1)}, u32[]{:S(2)}, u32[]{:S(2)}) collective-permute-start(s16[1,288,128]{2,1,0:T(8,128)(2,1)} %total.1), channel_id=1, source_target_pairs={{0,8},{1,9},{2,10},{3,11},{4,12},{5,13},{6,14},{7,15},{8,0},{9,1},... | collective-permute-start | bytes 221192 | tf_op jit(solution)/shard_map/ppermute | solution.py:175
  114.2 20.9 %collective-permute-start.25 = (s16[4,288,128]{2,1,0:T(8,128)(2,1)S(1)}, s16[4,288,128]{2,1,0:T(8,128)(2,1)S(1)}, u32[]{:S(2)}, u32[]{:S(2)}) collective-permute-start(s16[4,288,128]{2,1,0:T(8,128)(2,1)S(1)} %pad_add_fusion.refs_0_), channel_id=1, source_target_pairs={{0,6},{1,7},{2,4},{3,5},{4,2},{5,3},{6,0},{7,1},{8,14},{9,15},{10,... | collective-permute-start | bytes 884744 | tf_op jit(solution)/shard_map/ppermute | solution.py:175
  116.1 19.2 %collective-permute-start.24 = (s16[4,288,128]{2,1,0:T(8,128)(2,1)S(1)}, s16[4,288,128]{2,1,0:T(8,128)(2,1)S(1)}, u32[]{:S(2)}, u32[]{:S(2)}) collective-permute-start(s16[4,288,128]{2,1,0:T(8,128)(2,1)S(1)} %pad_add_fusion.refs_0_), channel_id=1, source_target_pairs={{0,4},{1,5},{2,6},{3,7},{4,0},{5,1},{6,2},{7,3},{8,12},{9,13},{10,... | collective-permute-start | bytes 884744 | tf_op jit(solution)/shard_map/ppermute | solution.py:175
  116.7 19.0 %collective-permute-start.23 = (s16[4,288,128]{2,1,0:T(8,128)(2,1)S(1)}, s16[4,288,128]{2,1,0:T(8,128)(2,1)S(1)}, u32[]{:S(2)}, u32[]{:S(2)}) collective-permute-start(s16[4,288,128]{2,1,0:T(8,128)(2,1)S(1)} %pad_add_fusion.refs_0_), channel_id=1, source_target_pairs={{0,2},{1,3},{2,0},{3,1},{4,6},{5,7},{6,4},{7,5},{8,10},{9,11},{10,... | collective-permute-start | bytes 884744 | tf_op jit(solution)/shard_map/ppermute | solution.py:175
  124.1 6.0 %collective-permute-start.8 = (s16[416,128]{1,0:T(8,128)(2,1)}, s16[416,128]{1,0:T(8,128)(2,1)S(1)}, u32[]{:S(2)}, u32[]{:S(2)}) collective-permute-start(s16[416,128]{1,0:T(8,128)(2,1)} %get-tuple-element.47), channel_id=1, source_target_pairs={{0,2},{1,3},{2,0},{3,1},{4,6},{5,7},{6,4},{7,5},{8,10},{9,11},{10,... | collective-permute-start | bytes 319496 | tf_op jit(solution)/shard_map/ppermute | solution.py:175
  125.6 6.0 %collective-permute-start.9 = (s16[416,128]{1,0:T(8,128)(2,1)}, s16[416,128]{1,0:T(8,128)(2,1)S(1)}, u32[]{:S(2)}, u32[]{:S(2)}) collective-permute-start(s16[416,128]{1,0:T(8,128)(2,1)} %get-tuple-element.48), channel_id=1, source_target_pairs={{0,3},{1,2},{2,1},{3,0},{4,7},{5,6},{6,5},{7,4},{8,11},{9,10},{10,... | collective-permute-start | bytes 319496 | tf_op jit(solution)/shard_map/ppermute | solution.py:175
  134.1 5.2 %collective-permute-start.12 = (s16[416,128]{1,0:T(8,128)(2,1)}, s16[416,128]{1,0:T(8,128)(2,1)S(1)}, u32[]{:S(2)}, u32[]{:S(2)}) collective-permute-start(s16[416,128]{1,0:T(8,128)(2,1)} %mine.1.refs_0_), channel_id=1, source_target_pairs={{0,3},{1,2},{2,1},{3,0},{4,7},{5,6},{6,5},{7,4},{8,11},{9,10},{10,... | collective-permute-start | bytes 319496 | tf_op jit(solution)/shard_map/ppermute | solution.py:175
  134.8 13.9 %collective-permute-start.26 = (s16[4,288,128]{2,1,0:T(8,128)(2,1)S(1)}, s16[4,288,128]{2,1,0:T(8,128)(2,1)S(1)}, u32[]{:S(2)}, u32[]{:S(2)}) collective-permute-start(s16[4,288,128]{2,1,0:T(8,128)(2,1)S(1)} %pad_add_fusion.refs_0_), channel_id=1, source_target_pairs={{0,1},{1,0},{2,3},{3,2},{4,5},{5,4},{6,7},{7,6},{8,9},{9,8},{10,11... | collective-permute-start | bytes 884744 | tf_op jit(solution)/shard_map/ppermute | solution.py:175
  135.2 13.6 %collective-permute-start.29 = (s16[4,288,128]{2,1,0:T(8,128)(2,1)S(1)}, s16[4,288,128]{2,1,0:T(8,128)(2,1)S(1)}, u32[]{:S(2)}, u32[]{:S(2)}) collective-permute-start(s16[4,288,128]{2,1,0:T(8,128)(2,1)S(1)} %collective-permute-done.25.refs_3_), channel_id=1, source_target_pairs={{0,1},{1,0},{2,3},{3,2},{4,5},{5,4},{6,7},{7,6},{8,9},{9,8},{10,11... | collective-permute-start | bytes 884744 | tf_op jit(solution)/shard_map/ppermute | solution.py:175
  135.4 13.4 %collective-permute-start.28 = (s16[4,288,128]{2,1,0:T(8,128)(2,1)S(1)}, s16[4,288,128]{2,1,0:T(8,128)(2,1)S(1)}, u32[]{:S(2)}, u32[]{:S(2)}) collective-permute-start(s16[4,288,128]{2,1,0:T(8,128)(2,1)S(1)} %collective-permute-done.24.refs_2_), channel_id=1, source_target_pairs={{0,1},{1,0},{2,3},{3,2},{4,5},{5,4},{6,7},{7,6},{8,9},{9,8},{10,11... | collective-permute-start | bytes 884744 | tf_op jit(solution)/shard_map/ppermute | solution.py:175
  135.7 13.1 %collective-permute-start.27 = (s16[4,288,128]{2,1,0:T(8,128)(2,1)S(1)}, s16[4,288,128]{2,1,0:T(8,128)(2,1)S(1)}, u32[]{:S(2)}, u32[]{:S(2)}) collective-permute-start(s16[4,288,128]{2,1,0:T(8,128)(2,1)S(1)} %collective-permute-done.23.refs_1_), channel_id=1, source_target_pairs={{0,1},{1,0},{2,3},{3,2},{4,5},{5,4},{6,7},{7,6},{8,9},{9,8},{10,11... | collective-permute-start | bytes 884744 | tf_op jit(solution)/shard_map/ppermute | solution.py:175
  139.3 5.2 %collective-permute-start.11 = (s16[416,128]{1,0:T(8,128)(2,1)}, s16[416,128]{1,0:T(8,128)(2,1)S(1)}, u32[]{:S(2)}, u32[]{:S(2)}) collective-permute-start(s16[416,128]{1,0:T(8,128)(2,1)} %mine.1.refs_0_), channel_id=1, source_target_pairs={{0,2},{1,3},{2,0},{3,1},{4,6},{5,7},{6,4},{7,5},{8,10},{9,11},{10,... | collective-permute-start | bytes 319496 | tf_op jit(solution)/shard_map/ppermute | solution.py:175
  (35 other events, 164.1 us)

commit v2 on v1

v2 whole, which is shorter than its diff:
```python
import functools

import jax
import jax.numpy as jnp
from jax import lax
from jax.experimental import pallas as pl
from jax.experimental.pallas import tpu as pltpu
from jax.sharding import PartitionSpec as P

F32 = jnp.float32
BF16 = jnp.bfloat16
LANES = 128
NT = (((1,), (1,)), ((), ()))
NN = (((1,), (0,)), ((), ()))
TN = (((0,), (0,)), ((), ()))


def bits_of(count):
    return count.bit_length() - 1


def reverse_bits(value, count):
    out = 0
    for bit in range(bits_of(count)):
        out = out * 2 + ((value >> bit) & 1)
    return out


def split(value):
    high = value.astype(BF16)
    low = (value - high.astype(F32)).astype(BF16)
    return high, low


def dot(left, right, dims):
    return lax.dot_general(left, right, dims, preferred_element_type=F32)


def dot3(left, right, dims):
    left_high, left_low = split(left)
    right_high, right_low = split(right)
    return (
        dot(left_high, right_high, dims)
        + dot(left_high, right_low, dims)
        + dot(left_low, right_high, dims)
    )


def one_hot(ids, rows, base=0):
    place = lax.broadcasted_iota(jnp.int32, (rows, ids.shape[1]), 0)
    return jnp.where(place == ids - base, 1.0, 0.0).astype(BF16)


def store_split(ref, cols, value):
    high, low = split(value)
    depth = value.shape[0]
    ref[0:depth, cols] = high
    ref[depth : 2 * depth, cols] = low


def folded(value):
    depth = value.shape[0] // 2
    return value[:depth] + value[depth:]


def quantized(value):
    top = jnp.max(jnp.abs(value), axis=0, keepdims=True)
    exponent = jnp.floor(jnp.log2(jnp.maximum(top, 1e-30))) + 1.0
    scaled = jnp.round(value * jnp.exp2(15.0 - exponent))
    return jnp.clip(scaled, -32767.0, 32767.0), exponent


def to_words(value):
    return value.astype(jnp.int32).astype(jnp.int16)


def from_words(words):
    return words.astype(jnp.int32).astype(F32)


def pack_table(value):
    scaled, exponent = quantized(value)
    tail = jnp.broadcast_to(exponent, (16, value.shape[1]))
    return to_words(jnp.concatenate([scaled, tail], axis=0))


def unpack_table(words):
    depth = words.shape[0] - 16
    value = from_words(words)
    return value[:depth] * jnp.exp2(value[depth : depth + 1] - 15.0)


def pack_chunk(value):
    scaled, exponent = quantized(value)
    rows = value.shape[0]
    place = lax.broadcasted_iota(jnp.int32, value.shape, 0)
    return to_words(jnp.where(place >= rows - 8, exponent, scaled))


def unpack_chunk(words):
    value = from_words(words)
    rows = value.shape[0]
    place = lax.broadcasted_iota(jnp.int32, value.shape, 0)
    scale = jnp.exp2(value[rows - 1 : rows] - 15.0)
    return jnp.where(place >= rows - 8, 0.0, value * scale)


class Plan:
    def __init__(self, doms, rels, prows, width, rems, nrels, maxb):
        self.doms, self.rels, self.maxb = doms, rels, maxb
        self.devices = doms * rels
        self.prows, self.width, self.rems, self.nrels = prows, width, rems, nrels
        self.buckets = doms // rels
        self.slots = rels * maxb
        self.bucket_edges = self.slots * LANES
        self.edges = self.buckets * self.bucket_edges
        self.part_lanes = prows // rels
        self.half_rel, self.half_rem = nrels // 2, rems // 2
        self.half_lanes = self.half_rel + self.half_rem
        self.subs = width // 8
        self.units = (self.half_lanes // LANES) * self.subs
        self.half_chunks = self.devices // 2
        self.chunk_units = -(-self.units // self.half_chunks)
        self.chunk_rows = (self.chunk_units + 2) // 2 * 16
        rel_bits = bits_of(rels)
        all_bits = rel_bits + bits_of(doms)
        self.groups = [
            [0],
            list(range(1, rel_bits + 1)),
            list(range(rel_bits + 1, all_bits)),
        ]
        self.masks = [self.group_masks(bits) for bits in self.groups]
        order = [bit for group in self.groups for bit in reversed(group)]
        self.place = {bit: all_bits - 1 - at for at, bit in enumerate(order)}

    @staticmethod
    def group_masks(bits):
        masks = []
        for index in range(2 ** len(bits)):
            masks.append(sum(((index >> at) & 1) << bit for at, bit in enumerate(bits)))
        return masks

    def row(self, labels, bucket, kinds, first, count):
        rows = []
        for slot in range(first, first + count):
            mask, turn = divmod(slot, self.maxb)
            block = bucket * self.maxb + turn
            rows += [labels[mask][block, kind : kind + 1, :] for kind in kinds]
        return jnp.concatenate(rows, axis=1) if len(rows) > 1 else rows[0]

    def whole_row(self, labels, kinds):
        rows = [
            self.row(labels, bucket, kinds, 0, self.slots) for bucket in range(self.buckets)
        ]
        return jnp.concatenate(rows, axis=1) if len(rows) > 1 else rows[0]

    def me(self):
        return lax.axis_index("dom") * self.rels + lax.axis_index("rel")

    def low_chunk(self, device):
        return device >> 1

    def position(self, chunk, me):
        relative = chunk ^ (me >> 1)
        out = 0
        for bit, at in self.place.items():
            if bit:
                out = out + (((relative >> (bit - 1)) & 1) << at)
        return out

    def bucket_mask(self, rel, bucket):
        return reverse_bits(rel, self.rels) * self.buckets + bucket

    def dynamic_mask(self, rel, bucket):
        out = 0
        width = bits_of(self.rels)
        for bit in range(width):
            out = out + (((rel >> bit) & 1) << (width - 1 - bit))
        return out * self.buckets + bucket


def send(value, plan, target):
    pairs = [(device, target(device)) for device in range(plan.devices)]
    return lax.ppermute(value, ("dom", "rel"), pairs)


def lists_kernel(plan, *refs):
    tables, counts, outs = refs[:7], refs[7], refs[8:]
    source = lax.axis_index("dom")
    rel = lax.axis_index("rel")
    for mask, out in enumerate(outs):
        for bucket in range(plan.buckets):
            target = source ^ plan.dynamic_mask(rel ^ mask, bucket)
            stop = lax.rem(source - target + plan.doms, plan.doms)
            for turn in range(plan.maxb):
                block = bucket * plan.maxb + turn
                for at, table in enumerate(tables):
                    out[block, at : at + 1, :] = table[0, stop, turn : turn + 1, :]
                live = jnp.where(turn < counts[stop], 1, 0)
                out[block, 7:8, :] = jnp.full((1, LANES), live, jnp.int32)


def prep_kernel(plan, *refs):
    labels = refs[: plan.rels]
    own, rem, relations, lhs_out, rel_out, rem_out, rel_split = refs[plan.rels :]
    depth = plan.width
    high, low = split(relations[...])
    rel_split[0:depth, :] = high
    rel_split[depth : 2 * depth, :] = low
    for bucket in range(plan.buckets):
        for pair in range(0, plan.slots, 2):
            count = min(2, plan.slots - pair)
            row = lambda at: plan.row(labels, bucket, (at,), pair, count)
            start = bucket * plan.bucket_edges + pair * LANES
            cols = slice(start, start + count * LANES)
            lhs_out[:, cols] = dot(own[...], one_hot(row(0), plan.prows), NN) + dot(
                rem[...], one_hot(row(1), plan.rems), NN
            )
            rel_out[:, cols] = folded(dot(rel_split[...], one_hot(row(2), plan.nrels), NN))
            ids = plan.row(labels, bucket, (4, 6), pair, count)
            rem_out[:, 2 * start : 2 * (start + count * LANES)] = dot(
                rem[...], one_hot(ids, plan.rems), NN
            ).astype(BF16)


def conjugate_parts(grad, other):
    half = grad.shape[0] // 2
    grad_re, grad_im = grad[:half], grad[half:]
    other_re, other_im = other[:half], other[half:]
    return jnp.concatenate(
        [grad_re * other_re + grad_im * other_im, grad_im * other_re - grad_re * other_im], 0
    )


def complex_product(left, right):
    half = left.shape[0] // 2
    left_re, left_im = left[:half], left[half:]
    right_re, right_im = right[:half], right[half:]
    return jnp.concatenate(
        [left_re * right_re - left_im * right_im, left_re * right_im + left_im * right_re], 0
    )


def bucket_grads(plan, bucket, labels, target, lhs_in, rel_in, rem_in, lhs_out, rel_out, cand_out, base):
    total = 2 * LANES
    edge = lax.broadcasted_iota(jnp.int32, (LANES, total), 0)
    column = lax.broadcasted_iota(jnp.int32, (LANES, total), 1)
    keep = jnp.where(edge == column, 0.0, 1.0 / total)
    for slot in range(plan.slots):
        cols = slice(slot * LANES, (slot + 1) * LANES)
        wide = slice(slot * total, (slot + 1) * total)
        ids = plan.row(labels, bucket, (3, 5), slot, 1)
        cand = dot(target[...], one_hot(ids, plan.prows), NN) + rem_in[:, wide].astype(F32)
        rhs = cand[:, :LANES]
        lhs, vec = lhs_in[:, cols], rel_in[:, cols]
        u_vec = complex_product(lhs, vec)
        live = plan.row(labels, bucket, (7,), slot, 1).astype(F32)
        positive = jnp.sum(u_vec * rhs, axis=0, keepdims=True)
        negative = dot3(u_vec, cand, TN)
        grad_pos = -jax.nn.sigmoid(-positive) * live
        grad_neg = jax.nn.sigmoid(negative) * keep * live[0:1, 0:1]
        grad_u = grad_pos * rhs + dot3(cand, grad_neg, NT)
        from_neg = dot3(u_vec, grad_neg, NN)
        grad_cand = jnp.concatenate(
            [from_neg[:, :LANES] + grad_pos * u_vec, from_neg[:, LANES:]], axis=1
        )
        at = base + slot
        cols = slice(at * LANES, (at + 1) * LANES)
        wide = slice(at * total, (at + 1) * total)
        store_split(lhs_out, cols, conjugate_parts(grad_u, vec))
        store_split(rel_out, cols, conjugate_parts(grad_u, lhs))
        store_split(cand_out, wide, grad_cand)


def bucket_kernel(plan, bucket, *refs):
    bucket_grads(plan, bucket, refs[: plan.rels], *refs[plan.rels :], 0)


def last_kernel(plan, *refs):
    labels = refs[: plan.rels]
    before = refs[plan.rels : plan.rels + 3 * (plan.buckets - 1)]
    refs = refs[plan.rels + 3 * (plan.buckets - 1) :]
    target, lhs_in, rel_in, rem_in = refs[:4]
    away, outs, helds, table, sems = refs[4], refs[5:8], refs[8:11], refs[11], refs[12]
    edges = plan.bucket_edges
    loads = []
    for at, ref in enumerate(before):
        wide = edges * (2 if at % 3 == 2 else 1)
        start = (at // 3) * wide
        loads.append(
            pltpu.make_async_copy(ref, helds[at % 3].at[:, start : start + wide], sems.at[at])
        )
        loads[-1].start()
    base = (plan.buckets - 1) * plan.slots
    bucket_grads(plan, plan.buckets - 1, labels, target, lhs_in, rel_in, rem_in, *helds, base)
    for load in loads:
        load.wait()
    stores = [
        pltpu.make_async_copy(held, out, sems.at[len(loads) + at])
        for at, (held, out) in enumerate(zip(helds, outs))
    ]
    for store in stores:
        store.start()
    reduce_half(plan, True, labels, helds, table, away)
    for store in stores:
        store.wait()


def reduce_half(plan, away, labels, grads, table, out):
    lhs_grads, rel_grads, cand_grads = grads
    me = plan.me()
    half = (me & 1) ^ (1 if away else 0)
    step = 2 * LANES if plan.half_rel % (2 * LANES) == 0 else LANES
    ids = plan.whole_row(labels, (2,)) - half * plan.half_rel
    for start in range(0, plan.half_rel, step):
        hot = one_hot(ids, step, start)
        table[:, start : start + step] = folded(dot(rel_grads[...], hot, NT))
    base = half * plan.half_rem
    first = one_hot(plan.whole_row(labels, (1,)), plan.half_rem, base)
    second = one_hot(plan.whole_row(labels, (4, 6)), plan.half_rem, base)
    table[:, plan.half_rel :] = folded(
        dot(lhs_grads[...], first, NT) + dot(cand_grads[...], second, NT)
    )
    for chunk in range(plan.half_chunks):
        parts = []
        for unit in range(chunk * plan.chunk_units, (chunk + 1) * plan.chunk_units):
            if unit < plan.units:
                lane, sub = divmod(unit, plan.subs)
                parts.append(table[8 * sub : 8 * sub + 8, lane * LANES : (lane + 1) * LANES])
            else:
                parts.append(jnp.zeros((8, LANES), F32))
        spare = plan.chunk_rows - 8 * plan.chunk_units
        parts.append(jnp.zeros((spare, LANES), F32))
        value = jnp.concatenate(parts, axis=0)
        out[plan.position(chunk, me)] = pack_chunk(value) if away else value


def part_sum(plan, labels, bucket, grads):
    ids = plan.row(labels, bucket, (3, 5), 0, plan.slots)
    shift = lax.axis_index("rel") * plan.part_lanes
    return folded(dot(grads, one_hot(ids ^ shift, plan.prows), NT))


def near_kernel(plan, bucket, *refs):
    labels = refs[: plan.rels]
    grads, out = refs[plan.rels :]
    out[...] = pack_table(part_sum(plan, labels, bucket, grads[...]))


def home_kernel(plan, after, *refs):
    labels = refs[: plan.rels]
    grads = refs[plan.rels : plan.rels + 3]
    keep, part, source, table = refs[plan.rels + 3 + after :]
    reduce_half(plan, False, labels, grads, table, keep)
    part[...] = part_sum(plan, labels, 0, grads[2][:, : 2 * plan.bucket_edges])
    ids = plan.whole_row(labels, (0,)) ^ (lax.axis_index("rel") * plan.part_lanes)
    source[...] = folded(dot(grads[0][...], one_hot(ids, plan.prows), NT))


def combine(keep, arrived, outs, last=False):
    count = keep.shape[0]
    share = count // len(outs)
    for at in range(count):
        value = keep[at]
        for ref in arrived:
            value = value + unpack_chunk(ref[at])
        which, place = divmod(at, share)
        outs[which][place] = pack_chunk(value) if (which or last) else value


def stage_one_kernel(plan, *refs):
    keep, core, part = refs[:3]
    near = refs[3 : 2 + plan.buckets]
    outs, far = refs[2 + plan.buckets : -1], refs[-1]
    combine(keep, [core], outs)
    value = part[...]
    for ref in near:
        value = value + unpack_table(ref[...])
    far[...] = pack_table(value)


def stage_two_kernel(plan, *refs):
    size, later = len(plan.masks[1]), len(plan.masks[2])
    keep, arrived, (source, far) = refs[0], refs[1:size], refs[size : size + 2]
    outs = refs[size + 2 : size + 2 + later]
    mine, shares = refs[size + 2 + later], refs[size + 3 + later :]
    combine(keep, arrived, outs)
    lanes = plan.part_lanes
    value = source[...] + unpack_table(far[...])
    mine[...] = value[:, :lanes]
    for at, out in enumerate(shares):
        out[...] = pack_table(value[:, (at + 1) * lanes : (at + 2) * lanes])


def stage_three_kernel(plan, *refs):
    size = len(plan.masks[2])
    keep, arrived = refs[0], refs[1:size]
    mine, shares = refs[size], refs[size + 1 : size + plan.rels]
    total, part = refs[size + plan.rels :]
    combine(keep, arrived, [total], True)
    value = mine[...]
    for ref in shares:
        value = value + unpack_table(ref[...])
    part[...] = pack_table(value)


def spread_kernel(plan, other, count, core, *refs):
    pieces, (rel_out, rem_out, held) = refs[:count], refs[-3:]
    at = 0
    for piece in pieces:
        held[at : at + piece.shape[0]] = piece[...]
        at += piece.shape[0]
    me = plan.me()
    for chunk in range(plan.half_chunks):
        value = unpack_chunk(held[plan.position(chunk, me)])
        for index in range(plan.chunk_units):
            unit = chunk * plan.chunk_units + index
            if unit >= plan.units:
                break
            lane, sub = divmod(unit, plan.subs)
            lane = lane * LANES
            rows = slice(8 * sub, 8 * sub + 8)
            block = value[8 * index : 8 * index + 8]
            if lane < plan.half_rel:
                rel_out[rows, lane : lane + LANES] = block
            else:
                lane -= plan.half_rel
                rem_out[rows, lane : lane + LANES] = block


def relay_kernel(*refs):
    pass


def part_out_kernel(plan, *refs):
    out = refs[-1]
    rel = lax.axis_index("rel")
    lanes = plan.part_lanes
    for mask, ref in enumerate(refs[:-1]):
        if lanes % LANES:
            out[:, mask * lanes : (mask + 1) * lanes] = unpack_table(ref[...])
        else:
            start = pl.multiple_of((rel ^ mask) * lanes, lanes)
            out[:, pl.ds(start, lanes)] = unpack_table(ref[...])


def shape(extent, kind):
    return jax.ShapeDtypeStruct(extent, kind)


VMEM = pl.BlockSpec(memory_space=pltpu.VMEM)
ANY = pl.BlockSpec(memory_space=pl.ANY)


def call(kernel, outs, args, name, cost, limit=48, scratch=(), in_specs=None, out_specs=None, **more):
    work = pl.CostEstimate(flops=int(cost * 1e9), bytes_accessed=int(cost * 3e6), transcendentals=0)
    return pl.pallas_call(
        kernel,
        out_shape=outs,
        in_specs=in_specs or [VMEM] * len(args),
        out_specs=out_specs or [VMEM] * len(outs),
        scratch_shapes=list(scratch),
        compiler_params=pltpu.CompilerParams(vmem_limit_bytes=limit * 2**20),
        cost_estimate=work,
        name=name,
        **more,
    )(*args)


def body(
    partitions,
    remainder,
    relations,
    counts,
    lhs_rows,
    lhs_rems,
    rel_ids,
    rhs_rows,
    rhs_rems,
    neg_rows,
    neg_rems,
):
    prows, width = partitions.shape
    plan = Plan(
        lax.axis_size("dom"),
        lax.axis_size("rel"),
        prows,
        width,
        remainder.shape[0],
        relations.shape[0],
        lhs_rows.shape[2],
    )
    smem = pl.BlockSpec(memory_space=pltpu.SMEM)
    own, rem, rels = partitions.T, remainder.T, relations.T
    edges, wide = plan.edges, plan.bucket_edges
    buckets = plan.buckets
    afar = lambda d: d ^ (plan.bucket_mask(d % plan.rels, 0) * plan.rels)
    i16 = jnp.int16

    first = send(own, plan, afar)
    tables = [lhs_rows, lhs_rems, rel_ids, rhs_rows, rhs_rems, neg_rows, neg_rems]
    labels = call(
        functools.partial(lists_kernel, plan),
        [shape((buckets * plan.maxb, 8, LANES), jnp.int32)] * plan.rels,
        tables + [counts.reshape(-1)],
        "lists",
        1.0,
        8,
        in_specs=[VMEM] * 7 + [smem],
    )
    labels = [labels[0]] + [
        send(labels[mask], plan, lambda d, m=mask: d ^ m) for mask in range(1, plan.rels)
    ]
    lhs, vec, cand_rem = call(
        functools.partial(prep_kernel, plan),
        [shape((width, edges), F32), shape((width, edges), F32), shape((width, 2 * edges), BF16)],
        labels + [own, rem, rels],
        "prep",
        10.0,
        scratch=[pltpu.VMEM((2 * width, plan.nrels), BF16)],
    )
    (first,) = call(
        relay_kernel,
        [shape((width, prows), BF16)],
        [first, cand_rem],
        "relay",
        0.1,
        1,
        in_specs=[ANY, ANY],
        out_specs=[ANY],
        input_output_aliases={0: 0},
    )
    targets = [first] + [
        send(first, plan, lambda d, b=bucket: d ^ (b * plan.rels)) for bucket in range(1, buckets)
    ]

    grad_shapes = lambda count: [
        shape((2 * width, count), BF16),
        shape((2 * width, count), BF16),
        shape((2 * width, 2 * count), BF16),
    ]
    one = lambda b: pl.BlockSpec((width, wide), lambda i: (0, b))
    two = lambda b: pl.BlockSpec((width, 2 * wide), lambda i: (0, b))
    whole = lambda extent: pl.BlockSpec(extent, lambda i: (0,) * len(extent))
    label_specs = [whole(label.shape) for label in labels]
    grads = []
    for bucket in range(buckets - 1):
        outs = grad_shapes(wide)
        grads += call(
            functools.partial(bucket_kernel, plan, bucket),
            outs,
            labels + [targets[bucket], lhs, vec, cand_rem],
            "bucket",
            7.0,
            grid=(1,),
            in_specs=label_specs + [whole(own.shape), one(bucket), one(bucket), two(bucket)],
            out_specs=[whole(out.shape) for out in outs],
        )
    last = buckets - 1
    chunk = (plan.half_chunks, plan.chunk_rows, LANES)
    table = [pltpu.VMEM((width, plan.half_lanes), F32)]
    made = call(
        functools.partial(last_kernel, plan),
        [shape(chunk, i16)] + grad_shapes(edges),
        labels + grads + [targets[last], lhs, vec, cand_rem],
        "last",
        14.0,
        grid=(1,),
        in_specs=label_specs
        + [ANY] * len(grads)
        + [whole(own.shape), one(last), one(last), two(last)],
        out_specs=[whole(chunk)] + [ANY] * 3,
        scratch=[pltpu.VMEM(held.shape, BF16) for held in grad_shapes(edges)]
        + table
        + [pltpu.SemaphoreType.DMA((len(grads) + 3,))],
    )
    away, grads = made[0], list(made[1:])
    core = send(away, plan, lambda d: d ^ 1)

    near, packed = [], []
    for bucket in range(1, buckets):
        packed += call(
            functools.partial(near_kernel, plan, bucket),
            [shape((width + 16, prows), i16)],
            labels + [grads[2]],
            "near",
            2.5,
            grid=(1,),
            in_specs=label_specs
            + [pl.BlockSpec((2 * width, 2 * wide), lambda i, b=bucket: (0, b))],
            out_specs=[whole((width + 16, prows))],
        )
        near.append(send(packed[-1], plan, lambda d, b=bucket: d ^ (b * plan.rels)))
    keep, part, source = call(
        functools.partial(home_kernel, plan, len(packed) + 1),
        [shape(chunk, F32), shape((width, prows), F32), shape((width, prows), F32)],
        labels + grads + packed + [away],
        "home",
        11.0,
        in_specs=[VMEM] * (len(labels) + 3) + [ANY] * (len(packed) + 1),
        scratch=table,
    )

    def shares(count, size):
        extent = (count // size,) + chunk[1:]
        return [shape(extent, F32)] + [shape(extent, i16)] * (size - 1)

    def exchanged(values, masks):
        return [
            send(value, plan, lambda d, m=mask: d ^ m) for value, mask in zip(values, masks[1:])
        ]

    size, later = len(plan.masks[1]), len(plan.masks[2])
    made = call(
        functools.partial(stage_one_kernel, plan),
        shares(chunk[0], size) + [shape((width + 16, prows), i16)],
        [keep, core, part] + near,
        "stage_one",
        4.0,
        16,
    )
    keep, arrived = made[0], exchanged(made[1:-1], plan.masks[1])
    far = send(made[-1], plan, afar)

    lanes = plan.part_lanes
    made = call(
        functools.partial(stage_two_kernel, plan),
        shares(chunk[0] // size, later)
        + [shape((width, lanes), F32)]
        + [shape((width + 16, lanes), i16)] * (plan.rels - 1),
        [keep] + arrived + [source, far],
        "stage_two",
        3.0,
        16,
    )
    keep, arrived = made[0], exchanged(made[1:later], plan.masks[2])
    mine = [made[later]] + exchanged(made[later + 1 :], range(plan.rels))

    total, part = call(
        functools.partial(stage_three_kernel, plan),
        [shape((1,) + chunk[1:], i16), shape((width + 16, lanes), i16)],
        [keep] + arrived + mine,
        "stage_three",
        2.0,
        16,
    )
    pieces = [total] + exchanged([total] * (later - 1), plan.masks[2])
    owners = [part] + exchanged([part] * (plan.rels - 1), range(plan.rels))
    block = jnp.concatenate(pieces, axis=0)
    pieces = [block] + exchanged([block] * (size - 1), plan.masks[1])
    (grad_partitions,) = call(
        functools.partial(part_out_kernel, plan),
        [shape((width, prows), F32)],
        owners,
        "part_out",
        2.0,
        16,
    )
    if lanes % LANES:
        order = jnp.arange(plan.rels) ^ lax.axis_index("rel")
        split_lanes = grad_partitions.reshape(width, plan.rels, lanes)
        grad_partitions = jnp.take(split_lanes, order, axis=1).reshape(width, prows)

    others = [send(piece, plan, lambda d: d ^ 1) for piece in pieces]
    side = lax.axis_index("rel") & 1
    outs = [shape((width, plan.nrels), F32), shape((width, plan.rems), F32)]
    held = pltpu.VMEM(chunk, i16)
    for turn, group in enumerate([pieces, others]):
        base = [] if turn == 0 else list(outs_made)
        spec = lambda lanes: pl.BlockSpec((width, lanes), lambda i, half: (0, half[0]))
        work = pl.CostEstimate(flops=int(2e9), bytes_accessed=int(6e6), transcendentals=0)
        outs_made = pl.pallas_call(
            functools.partial(spread_kernel, plan, turn, len(group)),
            out_shape=outs,
            grid_spec=pltpu.PrefetchScalarGridSpec(
                num_scalar_prefetch=1,
                grid=(1,),
                in_specs=[
                    pl.BlockSpec(piece.shape, lambda i, half: (0, 0, 0)) for piece in group
                ]
                + [ANY] * len(base),
                out_specs=[spec(plan.half_rel), spec(plan.half_rem)],
                scratch_shapes=[held],
            ),
            input_output_aliases={1 + len(group) + at: at for at in range(len(base))},
            compiler_params=pltpu.CompilerParams(vmem_limit_bytes=24 * 2**20),
            cost_estimate=work,
            name="spread",
        )((side ^ turn).reshape(1), *group, *base)
    grad_relations, grad_remainder = outs_made
    return grad_partitions.T, grad_remainder.T, grad_relations.T


def solution(mesh):
    edge = P("dom", None, "rel", None)
    in_specs = (P("dom", None), P(), P(), P("dom", None, "rel")) + (edge,) * 7
    out_specs = (P("dom", None), P(), P())
    return jax.shard_map(body, mesh=mesh, in_specs=in_specs, out_specs=out_specs, check_vma=False)
```

time: 155 us -> 131 us (0.85)
  Pallas kernels: 67.4 us -> 41.2 us
  starting transfers between devices: 41.4 us -> 34.6 us
  waiting for transfers between devices: 36.3 us -> 41.7 us
  local copies, waits for them, and re-layouts: 8.15 us -> 11.4 us
    pallas_call x15 -> x13, Pallas kernels: 67.4 us -> 41.2 us  [the longest x11 37.9 us: call(): pl.pallas_call(kernel, out_shape=outs, in_specs=in_specs or [VMEM] * len(...]
    ppermute x30, starting transfers between devices: 41.4 us -> 34.6 us  [send(): return lax.ppermute(value, ('dom', 'rel'), pairs)]
    ppermute x30, waiting for transfers between devices: 36.3 us -> 41.7 us  [send(): return lax.ppermute(value, ('dom', 'rel'), pairs)]
    unnamed x58 -> x35, local copies, waits for them, and re-layouts: 8.15 us -> 11.4 us
  transfers between devices with their start and end apart: 30 -> 30, of which waited for: 16 -> 10; matrix products, arithmetic and copies ran while one was open for 1% -> 0% of each run, Pallas kernels for 30% -> 20%
where the time goes in v2:
time: 131 us; the launch traced here: 130 us
  waiting for transfers between devices  41.7 us (32%)
  Pallas kernels  41.2 us (31%)
  starting transfers between devices  34.6 us (26%)
  local copies, waits for them, and re-layouts  11.4 us (9%)
    ppermute x30, waiting for transfers between devices, send(): return lax.ppermute(value, ('dom', 'rel'), pairs)  41.7 us
    pallas_call x11, Pallas kernels, call(): pl.pallas_call(kernel, out_shape=outs, in_specs=in_specs or [VMEM] * len(...  37.9 us
    ppermute x30, starting transfers between devices, send(): return lax.ppermute(value, ('dom', 'rel'), pairs)  34.6 us
    unnamed x35, local copies, waits for them, and re-layouts  11.4 us
    pallas_call x2, Pallas kernels, body(): pl.pallas_call(functools.partial(spread_kernel, plan, turn, len(group)),...  3.32 us
  transfers between devices with their start and end apart: 30, of which 10 were waited for; matrix products, arithmetic and copies ran while one was open for 0% of the time, Pallas kernels for 20%

profile of v2, /device:TPU:0, one launch (start us, length us, event | category | flops | bytes accessed | tf_op | source)
XLA Modules:
  0.0 129.8 jit_solution(3310623829949768648)
XLA Ops:
  7.2 2.6 %collective-permute-start.1 = (s32[2,8,128]{2,1,0:T(8,128)S(1)}, s32[2,8,128]{2,1,0:T(8,128)S(1)}, u32[]{:S(2)}, u32[]{:S(2)}) collective-permute-start(s32[2,8,128]{2,1,0:T(8,128)S(1)} %get-tuple-element.41), channel_id=1, source_target_pairs={{0,2},{1,3},{2,0},{3,1},{4,6},{5,7},{6,4},{7,5},{8,10},{9,11},{10,... | collective-permute-start | bytes 24584 | tf_op jit(solution)/shard_map/ppermute | solution.py:184
  12.9 7.6 %prep.1 = (f32[400,1024]{1,0:T(8,128)S(1)}, f32[400,1024]{1,0:T(8,128)S(1)}, bf16[400,2048]{1,0:T(8,128)(2,1)S(1)}) custom-call(s32[2,8,128]{2,1,0:T(8,128)S(1)} %get-tuple-element.39.refs_0_, s32[2,8,128]{2,1,0:T(8,128)S(1)} %collective-permute-done.refs_1_, s32[2,8,128]{2,1,0:T(8,128)S(1)} %collective-permute-done.1.refs_2_, ...), custom_call_target="tpu_custom_call" | custom-call | flops 10000000000 | bytes 30000000 | tf_op jit(solution)/shard_map/prep/pallas_call | solution.py:457
  21.7 1.6 %collective-permute-start.4 = (bf16[400,512]{1,0:T(8,128)(2,1)S(1)}, bf16[400,512]{1,0:T(8,128)(2,1)S(1)}, u32[]{:S(2)}, u32[]{:S(2)}) collective-permute-start(bf16[400,512]{1,0:T(8,128)(2,1)S(1)} %relay.1.refs_4_), channel_id=1, source_target_pairs={{0,4},{1,5},{2,6},{3,7},{4,0},{5,1},{6,2},{7,3},{8,12},{9,13},{10,... | collective-permute-start | bytes 1228808 | tf_op jit(solution)/shard_map/ppermute | solution.py:184
  23.3 5.5 %bucket.1 = (bf16[800,512]{1,0:T(8,128)(2,1)S(1)}, bf16[800,512]{1,0:T(8,128)(2,1)S(1)}, bf16[800,1024]{1,0:T(8,128)(2,1)S(1)}) custom-call(s32[2,8,128]{2,1,0:T(8,128)S(1)} %get-tuple-element.39.refs_0_, s32[2,8,128]{2,1,0:T(8,128)S(1)} %collective-permute-done.refs_1_, s32[2,8,128]{2,1,0:T(8,128)S(1)} %collective-permute-done.1.refs_2_, ...), custom_call_target="tpu_custom_call" | custom-call | flops 7000000000 | bytes 21000000 | tf_op jit(solution)/shard_map/bucket/pallas_call | solution.py:457
  30.0 2.4 %collective-permute-done.4.refs_7_ = bf16[400,512]{1,0:T(8,128)(2,1)S(1)} collective-permute-done((bf16[400,512]{1,0:T(8,128)(2,1)S(1)}, bf16[400,512]{1,0:T(8,128)(2,1)S(1)}, u32[]{:S(2)}, u32[]{:S(2)}) %collective-permute-start.4) | collective-permute-done | bytes 409632 | tf_op jit(solution)/shard_map/ppermute | solution.py:184
  32.4 11.7 %last.1 = (s16[16,288,128]{2,1,0:T(8,128)(2,1)S(1)}, bf16[800,1024]{1,0:T(8,128)(2,1)S(1)}, bf16[800,1024]{1,0:T(8,128)(2,1)}, bf16[800,2048]{1,0:T(8,128)(2,1)}) custom-call(s32[2,8,128]{2,1,0:T(8,128)S(1)} %get-tuple-element.39.refs_0_, s32[2,8,128]{2,1,0:T(8,128)S(1)} %collective-permute-done.refs_1_, s32[2,8,128]{2,1,0:T(8,128)S(1)} %collective-permute-done.1.refs_2_, ...), custom_call_target="tpu_custom_call" | custom-call | flops 14000000000 | bytes 42000000 | tf_op jit(solution)/shard_map/last/pallas_call | solution.py:457
  44.1 1.6 %collective-permute-start.5 = (s16[16,288,128]{2,1,0:T(8,128)(2,1)S(1)}, s16[16,288,128]{2,1,0:T(8,128)(2,1)S(1)}, u32[]{:S(2)}, u32[]{:S(2)}) collective-permute-start(s16[16,288,128]{2,1,0:T(8,128)(2,1)S(1)} %get-tuple-element.52.refs_8_), channel_id=1, source_target_pairs={{0,1},{1,0},{2,3},{3,2},{4,5},{5,4},{6,7},{7,6},{8,9},{9,8},{10,11... | collective-permute-start | bytes 3538952 | tf_op jit(solution)/shard_map/ppermute | solution.py:184
  45.7 1.9 %copy-done.11 = bf16[800,2048]{1,0:T(8,128)(2,1)S(1)} copy-done((bf16[800,2048]{1,0:T(8,128)(2,1)S(1)}, bf16[800,2048]{1,0:T(8,128)(2,1)}, u32[]{:S(2)}) %copy-start.11) | copy-done | bytes 3276824
  50.5 8.6 %home.1 = (f32[16,288,128]{2,1,0:T(8,128)}, f32[400,512]{1,0:T(8,128)S(1)}, f32[400,512]{1,0:T(8,128)S(1)}) custom-call(s32[2,8,128]{2,1,0:T(8,128)S(1)} %get-tuple-element.39.refs_0_, s32[2,8,128]{2,1,0:T(8,128)S(1)} %collective-permute-done.refs_1_, s32[2,8,128]{2,1,0:T(8,128)S(1)} %collective-permute-done.1.refs_2_, ...), custom_call_target="tpu_custom_call" | custom-call | flops 11000000512 | bytes 33000000 | tf_op jit(solution)/shard_map/home/pallas_call | solution.py:457
  59.0 1.7 %collective-permute-done.6.refs_3_ = s16[416,512]{1,0:T(8,128)(2,1)S(1)} collective-permute-done((s16[416,512]{1,0:T(8,128)(2,1)S(1)}, s16[416,512]{1,0:T(8,128)(2,1)S(1)}, u32[]{:S(2)}, u32[]{:S(2)}) %collective-permute-start.6) | collective-permute-done | bytes 426016 | tf_op jit(solution)/shard_map/ppermute | solution.py:184
  60.7 1.7 %copy-done.12 = f32[16,288,128]{2,1,0:T(8,128)S(1)} copy-done((f32[16,288,128]{2,1,0:T(8,128)S(1)}, f32[16,288,128]{2,1,0:T(8,128)}, u32[]{:S(2)}) %copy-start.12) | copy-done | bytes 2359320
  64.2 5.7 %collective-permute-start.7 = (s16[4,288,128]{2,1,0:T(8,128)(2,1)S(1)}, s16[4,288,128]{2,1,0:T(8,128)(2,1)S(1)}, u32[]{:S(2)}, u32[]{:S(2)}) collective-permute-start(s16[4,288,128]{2,1,0:T(8,128)(2,1)S(1)} %get-tuple-element.56), channel_id=1, source_target_pairs={{0,2},{1,3},{2,0},{3,1},{4,6},{5,7},{6,4},{7,5},{8,10},{9,11},{10,... | collective-permute-start | bytes 884744 | tf_op jit(solution)/shard_map/ppermute | solution.py:184
  71.4 4.9 %collective-permute-done.7.refs_1_ = s16[4,288,128]{2,1,0:T(8,128)(2,1)S(1)} collective-permute-done((s16[4,288,128]{2,1,0:T(8,128)(2,1)S(1)}, s16[4,288,128]{2,1,0:T(8,128)(2,1)S(1)}, u32[]{:S(2)}, u32[]{:S(2)}) %collective-permute-start.7) | collective-permute-done | bytes 294944 | tf_op jit(solution)/shard_map/ppermute | solution.py:184
  76.3 9.0 %collective-permute-done.8.refs_2_ = s16[4,288,128]{2,1,0:T(8,128)(2,1)S(1)} collective-permute-done((s16[4,288,128]{2,1,0:T(8,128)(2,1)S(1)}, s16[4,288,128]{2,1,0:T(8,128)(2,1)S(1)}, u32[]{:S(2)}, u32[]{:S(2)}) %collective-permute-start.8) | collective-permute-done | bytes 294944 | tf_op jit(solution)/shard_map/ppermute | solution.py:184
  88.0 2.8 %collective-permute-start.12 = (s16[1,288,128]{2,1,0:T(8,128)(2,1)S(1)}, s16[1,288,128]{2,1,0:T(8,128)(2,1)S(1)}, u32[]{:S(2)}, u32[]{:S(2)}) collective-permute-start(s16[1,288,128]{2,1,0:T(8,128)(2,1)S(1)} %get-tuple-element.63), channel_id=1, source_target_pairs={{0,16},{1,17},{2,18},{3,19},{4,20},{5,21},{6,22},{7,23},{8,24},{9,... | collective-permute-start | bytes 221192 | tf_op jit(solution)/shard_map/ppermute | solution.py:184
  90.8 1.9 %collective-permute-start.13 = (s16[1,288,128]{2,1,0:T(8,128)(2,1)S(1)}, s16[1,288,128]{2,1,0:T(8,128)(2,1)S(1)}, u32[]{:S(2)}, u32[]{:S(2)}) collective-permute-start(s16[1,288,128]{2,1,0:T(8,128)(2,1)S(1)} %get-tuple-element.64), channel_id=1, source_target_pairs={{0,24},{1,25},{2,26},{3,27},{4,28},{5,29},{6,30},{7,31},{8,16},{9,... | collective-permute-start | bytes 221192 | tf_op jit(solution)/shard_map/ppermute | solution.py:184
  92.7 4.5 %collective-permute-done.12.refs_2_ = s16[1,288,128]{2,1,0:T(8,128)(2,1)S(1)} collective-permute-done((s16[1,288,128]{2,1,0:T(8,128)(2,1)S(1)}, s16[1,288,128]{2,1,0:T(8,128)(2,1)S(1)}, u32[]{:S(2)}, u32[]{:S(2)}) %collective-permute-start.12) | collective-permute-done | bytes 73760 | tf_op jit(solution)/shard_map/ppermute | solution.py:184
  97.5 1.9 %collective-permute-start.20 = (s16[1,288,128]{2,1,0:T(8,128)(2,1)S(1)}, s16[1,288,128]{2,1,0:T(8,128)(2,1)S(1)}, u32[]{:S(2)}, u32[]{:S(2)}) collective-permute-start(s16[1,288,128]{2,1,0:T(8,128)(2,1)S(1)} %get-tuple-element.70), channel_id=1, source_target_pairs={{0,8},{1,9},{2,10},{3,11},{4,12},{5,13},{6,14},{7,15},{8,0},{9,1},... | collective-permute-start | bytes 221192 | tf_op jit(solution)/shard_map/ppermute | solution.py:184
  100.3 1.6 %collective-permute-start.22 = (s16[1,288,128]{2,1,0:T(8,128)(2,1)S(1)}, s16[1,288,128]{2,1,0:T(8,128)(2,1)S(1)}, u32[]{:S(2)}, u32[]{:S(2)}) collective-permute-start(s16[1,288,128]{2,1,0:T(8,128)(2,1)S(1)} %get-tuple-element.70), channel_id=1, source_target_pairs={{0,24},{1,25},{2,26},{3,27},{4,28},{5,29},{6,30},{7,31},{8,16},{9,... | collective-permute-start | bytes 221192 | tf_op jit(solution)/shard_map/ppermute | solution.py:184
  102.0 5.8 %collective-permute-done.21 = s16[1,288,128]{2,1,0:T(8,128)(2,1)S(1)} collective-permute-done((s16[1,288,128]{2,1,0:T(8,128)(2,1)S(1)}, s16[1,288,128]{2,1,0:T(8,128)(2,1)S(1)}, u32[]{:S(2)}, u32[]{:S(2)}) %collective-permute-start.21) | collective-permute-done | bytes 73760 | tf_op jit(solution)/shard_map/ppermute | solution.py:184
  109.4 1.9 %collective-permute-start.28 = (s16[4,288,128]{2,1,0:T(8,128)(2,1)S(1)}, s16[4,288,128]{2,1,0:T(8,128)(2,1)S(1)}, u32[]{:S(2)}, u32[]{:S(2)}) collective-permute-start(s16[4,288,128]{2,1,0:T(8,128)(2,1)S(1)} %constant_dynamic-update-slice_fusion.refs_0_), channel_id=1, source_target_pairs={{0,6},{1,7},{2,4},{3,5},{4,2},{5,3},{6,0},{7,1},{8,14},{9,15},{10,... | collective-permute-start | bytes 884744 | tf_op jit(solution)/shard_map/ppermute | solution.py:184
  113.5 10.9 %collective-permute-done.18.refs_2_ = s16[416,128]{1,0:T(8,128)(2,1)S(1)} collective-permute-done((s16[416,128]{1,0:T(8,128)(2,1)S(1)}, s16[416,128]{1,0:T(8,128)(2,1)S(1)}, u32[]{:S(2)}, u32[]{:S(2)}) %collective-permute-start.18) | collective-permute-done | bytes 106528 | tf_op jit(solution)/shard_map/ppermute | solution.py:184
  126.4 1.7 %spread.2 = (f32[400,2560]{1,0:T(8,128)}, f32[400,256]{1,0:T(8,128)}) custom-call(s32[1]{0:T(128)} %bitcast.6.core, s16[4,288,128]{2,1,0:T(8,128)(2,1)S(1)} %constant_dynamic-update-slice_fusion.refs_0_, s16[4,288,128]{2,1,0:T(8,128)(2,1)S(1)} %collective-permute-done.24.refs_1_, s16[4,288,128]{2,1,0:T(8,128)(2,1)S(1)} %collective-permute-done.26.refs_2_, ...), custom_call_target="tpu_custom_call" | custom-call | flops 2000000000 | bytes 6000000 | tf_op jit(solution)/shard_map/spread/pallas_call | solution.py:672
  128.1 1.7 %spread.3 = (f32[400,2560]{1,0:T(8,128)}, f32[400,256]{1,0:T(8,128)}) custom-call(s32[1]{0:T(128)} %bitcast.5.core, s16[4,288,128]{2,1,0:T(8,128)(2,1)S(1)} %collective-permute-done.23.refs_0_, s16[4,288,128]{2,1,0:T(8,128)(2,1)S(1)} %collective-permute-done.25.refs_1_, ...), custom_call_target="tpu_custom_call", output_to_operand_aliasing={{0}: (5, {}), {1}: (6, {})} | custom-call | flops 2000000000 | bytes 6000000 | tf_op jit(solution)/shard_map/spread/pallas_call | solution.py:672
  (85 shorter events, 27.9 us)
Async XLA Ops:
  6.7 3.8 %collective-permute-start = (s32[2,8,128]{2,1,0:T(8,128)S(1)}, s32[2,8,128]{2,1,0:T(8,128)S(1)}, u32[]{:S(2)}, u32[]{:S(2)}) collective-permute-start(s32[2,8,128]{2,1,0:T(8,128)S(1)} %get-tuple-element.40), channel_id=1, source_target_pairs={{0,1},{1,0},{2,3},{3,2},{4,5},{5,4},{6,7},{7,6},{8,9},{9,8},{10,11... | collective-permute-start | bytes 24584 | tf_op jit(solution)/shard_map/ppermute | solution.py:184
  7.2 4.2 %collective-permute-start.1 = (s32[2,8,128]{2,1,0:T(8,128)S(1)}, s32[2,8,128]{2,1,0:T(8,128)S(1)}, u32[]{:S(2)}, u32[]{:S(2)}) collective-permute-start(s32[2,8,128]{2,1,0:T(8,128)S(1)} %get-tuple-element.41), channel_id=1, source_target_pairs={{0,2},{1,3},{2,0},{3,1},{4,6},{5,7},{6,4},{7,5},{8,10},{9,11},{10,... | collective-permute-start | bytes 24584 | tf_op jit(solution)/shard_map/ppermute | solution.py:184
  9.9 11.8 %collective-permute-start.3 = (bf16[400,512]{1,0:T(8,128)(2,1)S(1)}, bf16[400,512]{1,0:T(8,128)(2,1)S(1)}, u32[]{:S(2)}, u32[]{:S(2)}) collective-permute-start(bf16[400,512]{1,0:T(8,128)(2,1)S(1)} %bitcast.9), channel_id=1, source_target_pairs={{0,0},{1,17},{2,10},{3,27},{4,4},{5,21},{6,14},{7,31},{8,8},{9,25}... | collective-permute-start | bytes 1228808 | tf_op jit(solution)/shard_map/ppermute | solution.py:184
  21.7 10.7 %collective-permute-start.4 = (bf16[400,512]{1,0:T(8,128)(2,1)S(1)}, bf16[400,512]{1,0:T(8,128)(2,1)S(1)}, u32[]{:S(2)}, u32[]{:S(2)}) collective-permute-start(bf16[400,512]{1,0:T(8,128)(2,1)S(1)} %relay.1.refs_4_), channel_id=1, source_target_pairs={{0,4},{1,5},{2,6},{3,7},{4,0},{5,1},{6,2},{7,3},{8,12},{9,13},{10,... | collective-permute-start | bytes 1228808 | tf_op jit(solution)/shard_map/ppermute | solution.py:184
  44.1 16.5 %collective-permute-start.5 = (s16[16,288,128]{2,1,0:T(8,128)(2,1)S(1)}, s16[16,288,128]{2,1,0:T(8,128)(2,1)S(1)}, u32[]{:S(2)}, u32[]{:S(2)}) collective-permute-start(s16[16,288,128]{2,1,0:T(8,128)(2,1)S(1)} %get-tuple-element.52.refs_8_), channel_id=1, source_target_pairs={{0,1},{1,0},{2,3},{3,2},{4,5},{5,4},{6,7},{7,6},{8,9},{9,8},{10,11... | collective-permute-start | bytes 3538952 | tf_op jit(solution)/shard_map/ppermute | solution.py:184
  48.9 11.8 %collective-permute-start.6 = (s16[416,512]{1,0:T(8,128)(2,1)S(1)}, s16[416,512]{1,0:T(8,128)(2,1)S(1)}, u32[]{:S(2)}, u32[]{:S(2)}) collective-permute-start(s16[416,512]{1,0:T(8,128)(2,1)S(1)} %near.1.refs_7_), channel_id=1, source_target_pairs={{0,4},{1,5},{2,6},{3,7},{4,0},{5,1},{6,2},{7,3},{8,12},{9,13},{10,... | collective-permute-start | bytes 1277960 | tf_op jit(solution)/shard_map/ppermute | solution.py:184
  63.2 22.1 %collective-permute-start.10 = (s16[416,512]{1,0:T(8,128)(2,1)S(1)}, s16[416,512]{1,0:T(8,128)(2,1)S(1)}, u32[]{:S(2)}, u32[]{:S(2)}) collective-permute-start(s16[416,512]{1,0:T(8,128)(2,1)S(1)} %get-tuple-element.60), channel_id=1, source_target_pairs={{0,0},{1,17},{2,10},{3,27},{4,4},{5,21},{6,14},{7,31},{8,8},{9,25}... | collective-permute-start | bytes 1277960 | tf_op jit(solution)/shard_map/ppermute | solution.py:184
  64.2 12.2 %collective-permute-start.7 = (s16[4,288,128]{2,1,0:T(8,128)(2,1)S(1)}, s16[4,288,128]{2,1,0:T(8,128)(2,1)S(1)}, u32[]{:S(2)}, u32[]{:S(2)}) collective-permute-start(s16[4,288,128]{2,1,0:T(8,128)(2,1)S(1)} %get-tuple-element.56), channel_id=1, source_target_pairs={{0,2},{1,3},{2,0},{3,1},{4,6},{5,7},{6,4},{7,5},{8,10},{9,11},{10,... | collective-permute-start | bytes 884744 | tf_op jit(solution)/shard_map/ppermute | solution.py:184
  69.9 15.4 %collective-permute-start.8 = (s16[4,288,128]{2,1,0:T(8,128)(2,1)S(1)}, s16[4,288,128]{2,1,0:T(8,128)(2,1)S(1)}, u32[]{:S(2)}, u32[]{:S(2)}) collective-permute-start(s16[4,288,128]{2,1,0:T(8,128)(2,1)S(1)} %get-tuple-element.57), channel_id=1, source_target_pairs={{0,4},{1,5},{2,6},{3,7},{4,0},{5,1},{6,2},{7,3},{8,12},{9,13},{10,... | collective-permute-start | bytes 884744 | tf_op jit(solution)/shard_map/ppermute | solution.py:184
  71.4 13.9 %collective-permute-start.9 = (s16[4,288,128]{2,1,0:T(8,128)(2,1)S(1)}, s16[4,288,128]{2,1,0:T(8,128)(2,1)S(1)}, u32[]{:S(2)}, u32[]{:S(2)}) collective-permute-start(s16[4,288,128]{2,1,0:T(8,128)(2,1)S(1)} %get-tuple-element.58), channel_id=1, source_target_pairs={{0,6},{1,7},{2,4},{3,5},{4,2},{5,3},{6,0},{7,1},{8,14},{9,15},{10,... | collective-permute-start | bytes 884744 | tf_op jit(solution)/shard_map/ppermute | solution.py:184
  85.9 4.9 %collective-permute-start.11 = (s16[1,288,128]{2,1,0:T(8,128)(2,1)S(1)}, s16[1,288,128]{2,1,0:T(8,128)(2,1)S(1)}, u32[]{:S(2)}, u32[]{:S(2)}) collective-permute-start(s16[1,288,128]{2,1,0:T(8,128)(2,1)S(1)} %get-tuple-element.62), channel_id=1, source_target_pairs={{0,8},{1,9},{2,10},{3,11},{4,12},{5,13},{6,14},{7,15},{8,0},{9,1},... | collective-permute-start | bytes 221192 | tf_op jit(solution)/shard_map/ppermute | solution.py:184
  85.9 11.3 %collective-permute-start.14 = (s16[416,128]{1,0:T(8,128)(2,1)S(1)}, s16[416,128]{1,0:T(8,128)(2,1)S(1)}, u32[]{:S(2)}, u32[]{:S(2)}) collective-permute-start(s16[416,128]{1,0:T(8,128)(2,1)S(1)} %get-tuple-element.66), channel_id=1, source_target_pairs={{0,1},{1,0},{2,3},{3,2},{4,5},{5,4},{6,7},{7,6},{8,9},{9,8},{10,11... | collective-permute-start | bytes 319496 | tf_op jit(solution)/shard_map/ppermute | solution.py:184
  86.6 10.6 %collective-permute-start.15 = (s16[416,128]{1,0:T(8,128)(2,1)S(1)}, s16[416,128]{1,0:T(8,128)(2,1)S(1)}, u32[]{:S(2)}, u32[]{:S(2)}) collective-permute-start(s16[416,128]{1,0:T(8,128)(2,1)S(1)} %get-tuple-element.67), channel_id=1, source_target_pairs={{0,2},{1,3},{2,0},{3,1},{4,6},{5,7},{6,4},{7,5},{8,10},{9,11},{10,... | collective-permute-start | bytes 319496 | tf_op jit(solution)/shard_map/ppermute | solution.py:184
  87.5 9.7 %collective-permute-start.16 = (s16[416,128]{1,0:T(8,128)(2,1)S(1)}, s16[416,128]{1,0:T(8,128)(2,1)S(1)}, u32[]{:S(2)}, u32[]{:S(2)}) collective-permute-start(s16[416,128]{1,0:T(8,128)(2,1)S(1)} %get-tuple-element.68), channel_id=1, source_target_pairs={{0,3},{1,2},{2,1},{3,0},{4,7},{5,6},{6,5},{7,4},{8,11},{9,10},{10,... | collective-permute-start | bytes 319496 | tf_op jit(solution)/shard_map/ppermute | solution.py:184
  88.0 9.2 %collective-permute-start.12 = (s16[1,288,128]{2,1,0:T(8,128)(2,1)S(1)}, s16[1,288,128]{2,1,0:T(8,128)(2,1)S(1)}, u32[]{:S(2)}, u32[]{:S(2)}) collective-permute-start(s16[1,288,128]{2,1,0:T(8,128)(2,1)S(1)} %get-tuple-element.63), channel_id=1, source_target_pairs={{0,16},{1,17},{2,18},{3,19},{4,20},{5,21},{6,22},{7,23},{8,24},{9,... | collective-permute-start | bytes 221192 | tf_op jit(solution)/shard_map/ppermute | solution.py:184
  90.8 6.4 %collective-permute-start.13 = (s16[1,288,128]{2,1,0:T(8,128)(2,1)S(1)}, s16[1,288,128]{2,1,0:T(8,128)(2,1)S(1)}, u32[]{:S(2)}, u32[]{:S(2)}) collective-permute-start(s16[1,288,128]{2,1,0:T(8,128)(2,1)S(1)} %get-tuple-element.64), channel_id=1, source_target_pairs={{0,24},{1,25},{2,26},{3,27},{4,28},{5,29},{6,30},{7,31},{8,16},{9,... | collective-permute-start | bytes 221192 | tf_op jit(solution)/shard_map/ppermute | solution.py:184
  97.5 4.5 %collective-permute-start.20 = (s16[1,288,128]{2,1,0:T(8,128)(2,1)S(1)}, s16[1,288,128]{2,1,0:T(8,128)(2,1)S(1)}, u32[]{:S(2)}, u32[]{:S(2)}) collective-permute-start(s16[1,288,128]{2,1,0:T(8,128)(2,1)S(1)} %get-tuple-element.70), channel_id=1, source_target_pairs={{0,8},{1,9},{2,10},{3,11},{4,12},{5,13},{6,14},{7,15},{8,0},{9,1},... | collective-permute-start | bytes 221192 | tf_op jit(solution)/shard_map/ppermute | solution.py:184
  99.4 8.3 %collective-permute-start.21 = (s16[1,288,128]{2,1,0:T(8,128)(2,1)S(1)}, s16[1,288,128]{2,1,0:T(8,128)(2,1)S(1)}, u32[]{:S(2)}, u32[]{:S(2)}) collective-permute-start(s16[1,288,128]{2,1,0:T(8,128)(2,1)S(1)} %get-tuple-element.70), channel_id=1, source_target_pairs={{0,16},{1,17},{2,18},{3,19},{4,20},{5,21},{6,22},{7,23},{8,24},{9,... | collective-permute-start | bytes 221192 | tf_op jit(solution)/shard_map/ppermute | solution.py:184
  100.3 7.4 %collective-permute-start.22 = (s16[1,288,128]{2,1,0:T(8,128)(2,1)S(1)}, s16[1,288,128]{2,1,0:T(8,128)(2,1)S(1)}, u32[]{:S(2)}, u32[]{:S(2)}) collective-permute-start(s16[1,288,128]{2,1,0:T(8,128)(2,1)S(1)} %get-tuple-element.70), channel_id=1, source_target_pairs={{0,24},{1,25},{2,26},{3,27},{4,28},{5,29},{6,30},{7,31},{8,16},{9,... | collective-permute-start | bytes 221192 | tf_op jit(solution)/shard_map/ppermute | solution.py:184
  107.8 16.6 %collective-permute-start.24 = (s16[4,288,128]{2,1,0:T(8,128)(2,1)S(1)}, s16[4,288,128]{2,1,0:T(8,128)(2,1)S(1)}, u32[]{:S(2)}, u32[]{:S(2)}) collective-permute-start(s16[4,288,128]{2,1,0:T(8,128)(2,1)S(1)} %constant_dynamic-update-slice_fusion.refs_0_), channel_id=1, source_target_pairs={{0,2},{1,3},{2,0},{3,1},{4,6},{5,7},{6,4},{7,5},{8,10},{9,11},{10,... | collective-permute-start | bytes 884744 | tf_op jit(solution)/shard_map/ppermute | solution.py:184
  108.9 16.0 %collective-permute-start.26 = (s16[4,288,128]{2,1,0:T(8,128)(2,1)S(1)}, s16[4,288,128]{2,1,0:T(8,128)(2,1)S(1)}, u32[]{:S(2)}, u32[]{:S(2)}) collective-permute-start(s16[4,288,128]{2,1,0:T(8,128)(2,1)S(1)} %constant_dynamic-update-slice_fusion.refs_0_), channel_id=1, source_target_pairs={{0,4},{1,5},{2,6},{3,7},{4,0},{5,1},{6,2},{7,3},{8,12},{9,13},{10,... | collective-permute-start | bytes 884744 | tf_op jit(solution)/shard_map/ppermute | solution.py:184
  109.4 15.5 %collective-permute-start.28 = (s16[4,288,128]{2,1,0:T(8,128)(2,1)S(1)}, s16[4,288,128]{2,1,0:T(8,128)(2,1)S(1)}, u32[]{:S(2)}, u32[]{:S(2)}) collective-permute-start(s16[4,288,128]{2,1,0:T(8,128)(2,1)S(1)} %constant_dynamic-update-slice_fusion.refs_0_), channel_id=1, source_target_pairs={{0,6},{1,7},{2,4},{3,5},{4,2},{5,3},{6,0},{7,1},{8,14},{9,15},{10,... | collective-permute-start | bytes 884744 | tf_op jit(solution)/shard_map/ppermute | solution.py:184
  111.3 13.1 %collective-permute-start.18 = (s16[416,128]{1,0:T(8,128)(2,1)S(1)}, s16[416,128]{1,0:T(8,128)(2,1)S(1)}, u32[]{:S(2)}, u32[]{:S(2)}) collective-permute-start(s16[416,128]{1,0:T(8,128)(2,1)S(1)} %get-tuple-element.69.refs_0_), channel_id=1, source_target_pairs={{0,2},{1,3},{2,0},{3,1},{4,6},{5,7},{6,4},{7,5},{8,10},{9,11},{10,... | collective-permute-start | bytes 319496 | tf_op jit(solution)/shard_map/ppermute | solution.py:184
  112.6 12.8 %collective-permute-start.19 = (s16[416,128]{1,0:T(8,128)(2,1)S(1)}, s16[416,128]{1,0:T(8,128)(2,1)S(1)}, u32[]{:S(2)}, u32[]{:S(2)}) collective-permute-start(s16[416,128]{1,0:T(8,128)(2,1)S(1)} %get-tuple-element.69.refs_0_), channel_id=1, source_target_pairs={{0,3},{1,2},{2,1},{3,0},{4,7},{5,6},{6,5},{7,4},{8,11},{9,10},{10,... | collective-permute-start | bytes 319496 | tf_op jit(solution)/shard_map/ppermute | solution.py:184
  (22 other events, 48.8 us)

commit v3 on v2

--- a/solution.py
+++ b/solution.py
@@ -10,6 +10,7 @@
 F32 = jnp.float32
 BF16 = jnp.bfloat16
 LANES = 128
+REACH = 32766.0
 NT = (((1,), (1,)), ((), ()))
 NN = (((1,), (0,)), ((), ()))
 TN = (((0,), (0,)), ((), ()))
@@ -66,8 +67,11 @@
 def quantized(value):
     top = jnp.max(jnp.abs(value), axis=0, keepdims=True)
     exponent = jnp.floor(jnp.log2(jnp.maximum(top, 1e-30))) + 1.0
-    scaled = jnp.round(value * jnp.exp2(15.0 - exponent))
-    return jnp.clip(scaled, -32767.0, 32767.0), exponent
+    return jnp.round(value * (REACH * jnp.exp2(-exponent))), exponent
+
+
+def scale_of(exponent):
+    return jnp.exp2(exponent) * (1.0 / REACH)
 
 
 def to_words(value):
@@ -78,31 +82,17 @@
     return words.astype(jnp.int32).astype(F32)
 
 
-def pack_table(value):
+def pack_table(value, rows=None):
     scaled, exponent = quantized(value)
-    tail = jnp.broadcast_to(exponent, (16, value.shape[1]))
+    spare = (rows or value.shape[0] + 16) - value.shape[0]
+    tail = jnp.broadcast_to(exponent, (spare, value.shape[1]))
     return to_words(jnp.concatenate([scaled, tail], axis=0))
 
 
-def unpack_table(words):
-    depth = words.shape[0] - 16
+def unpack_table(words, depth=None):
+    depth = depth or words.shape[0] - 16
     value = from_words(words)
-    return value[:depth] * jnp.exp2(value[depth : depth + 1] - 15.0)
-
-
-def pack_chunk(value):
-    scaled, exponent = quantized(value)
-    rows = value.shape[0]
-    place = lax.broadcasted_iota(jnp.int32, value.shape, 0)
-    return to_words(jnp.where(place >= rows - 8, exponent, scaled))
-
-
-def unpack_chunk(words):
-    value = from_words(words)
-    rows = value.shape[0]
-    place = lax.broadcasted_iota(jnp.int32, value.shape, 0)
-    scale = jnp.exp2(value[rows - 1 : rows] - 15.0)
-    return jnp.where(place >= rows - 8, 0.0, value * scale)
+    return value[:depth] * scale_of(value[depth : depth + 1])
 
 
 class Plan:
@@ -200,9 +190,9 @@
                 out[block, 7:8, :] = jnp.full((1, LANES), live, jnp.int32)
 
 
-def prep_kernel(plan, *refs):
+def relation_kernel(plan, *refs):
     labels = refs[: plan.rels]
-    own, rem, relations, lhs_out, rel_out, rem_out, rel_split = refs[plan.rels :]
+    relations, rel_out, rel_split = refs[plan.rels :]
     depth = plan.width
     high, low = split(relations[...])
     rel_split[0:depth, :] = high
@@ -210,16 +200,28 @@
     for bucket in range(plan.buckets):
         for pair in range(0, plan.slots, 2):
             count = min(2, plan.slots - pair)
-            row = lambda at: plan.row(labels, bucket, (at,), pair, count)
             start = bucket * plan.bucket_edges + pair * LANES
-            cols = slice(start, start + count * LANES)
-            lhs_out[:, cols] = dot(own[...], one_hot(row(0), plan.prows), NN) + dot(
+            ids = plan.row(labels, bucket, (2,), pair, count)
+            rel_out[:, start : start + count * LANES] = folded(
+                dot(rel_split[...], one_hot(ids, plan.nrels), NN)
+            )
+
+
+def source_rows_kernel(plan, *refs):
+    labels = refs[: plan.rels]
+    own, rem = refs[plan.rels : plan.rels + 2]
+    lhs_out, rem_out = refs[-2:]
+    for bucket in range(plan.buckets):
+        for pair in range(0, plan.slots, 2):
+            count = min(2, plan.slots - pair)
+            row = lambda *kinds: plan.row(labels, bucket, kinds, pair, count)
+            start = bucket * plan.bucket_edges + pair * LANES
+            end = start + count * LANES
+            lhs_out[:, start:end] = dot(own[...], one_hot(row(0), plan.prows), NN) + dot(
                 rem[...], one_hot(row(1), plan.rems), NN
             )
-            rel_out[:, cols] = folded(dot(rel_split[...], one_hot(row(2), plan.nrels), NN))
-            ids = plan.row(labels, bucket, (4, 6), pair, count)
-            rem_out[:, 2 * start : 2 * (start + count * LANES)] = dot(
-                rem[...], one_hot(ids, plan.rems), NN
+            rem_out[:, 2 * start : 2 * end] = dot(
+                rem[...], one_hot(row(4, 6), plan.rems), NN
             ).astype(BF16)
 
 
@@ -247,8 +249,9 @@
     column = lax.broadcasted_iota(jnp.int32, (LANES, total), 1)
     keep = jnp.where(edge == column, 0.0, 1.0 / total)
     for slot in range(plan.slots):
-        cols = slice(slot * LANES, (slot + 1) * LANES)
-        wide = slice(slot * total, (slot + 1) * total)
+        at = bucket * plan.slots + slot
+        cols = slice(at * LANES, (at + 1) * LANES)
+        wide = slice(at * total, (at + 1) * total)
         ids = plan.row(labels, bucket, (3, 5), slot, 1)
         cand = dot(target[...], one_hot(ids, plan.prows), NN) + rem_in[:, wide].astype(F32)
         rhs = cand[:, :LANES]
@@ -329,62 +332,50 @@
                 parts.append(table[8 * sub : 8 * sub + 8, lane * LANES : (lane + 1) * LANES])
             else:
                 parts.append(jnp.zeros((8, LANES), F32))
-        spare = plan.chunk_rows - 8 * plan.chunk_units
-        parts.append(jnp.zeros((spare, LANES), F32))
         value = jnp.concatenate(parts, axis=0)
-        out[plan.position(chunk, me)] = pack_chunk(value) if away else value
+        out[plan.position(chunk, me)] = pack_table(value, plan.chunk_rows) if away else value
 
 
 def part_sum(plan, labels, bucket, grads):
     ids = plan.row(labels, bucket, (3, 5), 0, plan.slots)
     shift = lax.axis_index("rel") * plan.part_lanes
-    return folded(dot(grads, one_hot(ids ^ shift, plan.prows), NT))
+    start, wide = 2 * bucket * plan.bucket_edges, 2 * plan.bucket_edges
+    return folded(dot(grads[:, start : start + wide], one_hot(ids ^ shift, plan.prows), NT))
 
 
 def near_kernel(plan, bucket, *refs):
     labels = refs[: plan.rels]
-    grads, out = refs[plan.rels :]
-    out[...] = pack_table(part_sum(plan, labels, bucket, grads[...]))
+    grads, out = refs[plan.rels], refs[-1]
+    out[...] = pack_table(part_sum(plan, labels, bucket, grads))
 
 
 def home_kernel(plan, after, *refs):
     labels = refs[: plan.rels]
     grads = refs[plan.rels : plan.rels + 3]
-    keep, part, source, table = refs[plan.rels + 3 + after :]
+    keep, table = refs[plan.rels + 3 + after :]
     reduce_half(plan, False, labels, grads, table, keep)
-    part[...] = part_sum(plan, labels, 0, grads[2][:, : 2 * plan.bucket_edges])
-    ids = plan.whole_row(labels, (0,)) ^ (lax.axis_index("rel") * plan.part_lanes)
-    source[...] = folded(dot(grads[0][...], one_hot(ids, plan.prows), NT))
-
-
-def combine(keep, arrived, outs, last=False):
-    count = keep.shape[0]
-    share = count // len(outs)
-    for at in range(count):
-        value = keep[at]
-        for ref in arrived:
-            value = value + unpack_chunk(ref[at])
-        which, place = divmod(at, share)
-        outs[which][place] = pack_chunk(value) if (which or last) else value
-
-
-def stage_one_kernel(plan, *refs):
-    keep, core, part = refs[:3]
-    near = refs[3 : 2 + plan.buckets]
-    outs, far = refs[2 + plan.buckets : -1], refs[-1]
-    combine(keep, [core], outs)
-    value = part[...]
+
+
+def far_kernel(plan, *refs):
+    labels = refs[: plan.rels]
+    grads, near = refs[plan.rels], refs[plan.rels + 1 : plan.rels + plan.buckets]
+    out = refs[-1]
+    value = part_sum(plan, labels, 0, grads)
     for ref in near:
         value = value + unpack_table(ref[...])
-    far[...] = pack_table(value)
-
-
-def stage_two_kernel(plan, *refs):
-    size, later = len(plan.masks[1]), len(plan.masks[2])
-    keep, arrived, (source, far) = refs[0], refs[1:size], refs[size : size + 2]
-    outs = refs[size + 2 : size + 2 + later]
-    mine, shares = refs[size + 2 + later], refs[size + 3 + later :]
-    combine(keep, arrived, outs)
+    out[...] = pack_table(value)
+
+
+def source_kernel(plan, *refs):
+    labels = refs[: plan.rels]
+    grads, out = refs[plan.rels], refs[-1]
+    ids = plan.whole_row(labels, (0,)) ^ (lax.axis_index("rel") * plan.part_lanes)
+    out[...] = folded(dot(grads[...], one_hot(ids, plan.prows), NT))
+
+
+def share_kernel(plan, *refs):
+    source, far = refs[:2]
+    mine, shares = refs[-plan.rels], refs[len(refs) - plan.rels + 1 :]
     lanes = plan.part_lanes
     value = source[...] + unpack_table(far[...])
     mine[...] = value[:, :lanes]
@@ -392,19 +383,27 @@
         out[...] = pack_table(value[:, (at + 1) * lanes : (at + 2) * lanes])
 
 
-def stage_three_kernel(plan, *refs):
-    size = len(plan.masks[2])
-    keep, arrived = refs[0], refs[1:size]
-    mine, shares = refs[size], refs[size + 1 : size + plan.rels]
-    total, part = refs[size + plan.rels :]
-    combine(keep, arrived, [total], True)
-    value = mine[...]
-    for ref in shares:
+def mine_kernel(plan, *refs):
+    value = refs[0][...]
+    for ref in refs[1 : plan.rels]:
         value = value + unpack_table(ref[...])
-    part[...] = pack_table(value)
-
-
-def spread_kernel(plan, other, count, core, *refs):
+    refs[-1][...] = pack_table(value)
+
+
+def combine_kernel(plan, group, last, *refs):
+    keep, arrived, outs = refs[0], refs[1:group], refs[group:]
+    count, depth = keep.shape[0], keep.shape[1]
+    share = count // len(outs)
+    for at in range(count):
+        value = keep[at]
+        for ref in arrived:
+            value = value + unpack_table(ref[at], depth)
+        which, place = divmod(at, share)
+        packed = which or last
+        outs[which][place] = pack_table(value, plan.chunk_rows) if packed else value
+
+
+def spread_kernel(plan, count, side, *refs):
     pieces, (rel_out, rem_out, held) = refs[:count], refs[-3:]
     at = 0
     for piece in pieces:
@@ -412,7 +411,7 @@
         at += piece.shape[0]
     me = plan.me()
     for chunk in range(plan.half_chunks):
-        value = unpack_chunk(held[plan.position(chunk, me)])
+        value = unpack_table(held[plan.position(chunk, me)], 8 * plan.chunk_units)
         for index in range(plan.chunk_units):
             unit = chunk * plan.chunk_units + index
             if unit >= plan.units:
@@ -436,7 +435,7 @@
     out = refs[-1]
     rel = lax.axis_index("rel")
     lanes = plan.part_lanes
-    for mask, ref in enumerate(refs[:-1]):
+    for mask, ref in enumerate(refs[: plan.rels]):
         if lanes % LANES:
             out[:, mask * lanes : (mask + 1) * lanes] = unpack_table(ref[...])
         else:
@@ -452,15 +451,16 @@
 ANY = pl.BlockSpec(memory_space=pl.ANY)
 
 
-def call(kernel, outs, args, name, cost, limit=48, scratch=(), in_specs=None, out_specs=None, **more):
+def call(kernel, outs, args, name, cost, limit, scratch=(), in_specs=None, out_specs=None, **more):
     work = pl.CostEstimate(flops=int(cost * 1e9), bytes_accessed=int(cost * 3e6), transcendentals=0)
+    if "grid_spec" not in more:
+        more["in_specs"] = in_specs or [VMEM] * len(args)
+        more["out_specs"] = out_specs or [VMEM] * len(outs)
+        more["scratch_shapes"] = list(scratch)
     return pl.pallas_call(
         kernel,
         out_shape=outs,
-        in_specs=in_specs or [VMEM] * len(args),
-        out_specs=out_specs or [VMEM] * len(outs),
-        scratch_shapes=list(scratch),
-        compiler_params=pltpu.CompilerParams(vmem_limit_bytes=limit * 2**20),
+        compiler_params=pltpu.CompilerParams(vmem_limit_bytes=int(limit * 2**20)),
         cost_estimate=work,
         name=name,
         **more,
@@ -493,6 +493,7 @@
     smem = pl.BlockSpec(memory_space=pltpu.SMEM)
     own, rem, rels = partitions.T, remainder.T, relations.T
     edges, wide = plan.edges, plan.bucket_edges
+    grow = max(1, edges // 1024)
     buckets = plan.buckets
     afar = lambda d: d ^ (plan.bucket_mask(d % plan.rels, 0) * plan.rels)
     i16 = jnp.int16
@@ -505,24 +506,25 @@
         tables + [counts.reshape(-1)],
         "lists",
         1.0,
-        8,
+        60,
         in_specs=[VMEM] * 7 + [smem],
     )
     labels = [labels[0]] + [
         send(labels[mask], plan, lambda d, m=mask: d ^ m) for mask in range(1, plan.rels)
     ]
-    lhs, vec, cand_rem = call(
-        functools.partial(prep_kernel, plan),
-        [shape((width, edges), F32), shape((width, edges), F32), shape((width, 2 * edges), BF16)],
-        labels + [own, rem, rels],
-        "prep",
-        10.0,
+    (vec,) = call(
+        functools.partial(relation_kernel, plan),
+        [shape((width, edges), F32)],
+        labels + [rels],
+        "relation",
+        6.0,
+        24 * grow,
         scratch=[pltpu.VMEM((2 * width, plan.nrels), BF16)],
     )
     (first,) = call(
         relay_kernel,
         [shape((width, prows), BF16)],
-        [first, cand_rem],
+        [first, vec],
         "relay",
         0.1,
         1,
@@ -533,43 +535,44 @@
     targets = [first] + [
         send(first, plan, lambda d, b=bucket: d ^ (b * plan.rels)) for bucket in range(1, buckets)
     ]
+    lhs, cand_rem = call(
+        functools.partial(source_rows_kernel, plan),
+        [shape((width, edges), F32), shape((width, 2 * edges), BF16)],
+        labels + [own, rem, first],
+        "source_rows",
+        1.5,
+        12 * grow,
+        in_specs=[VMEM] * (len(labels) + 2) + [ANY],
+    )
 
     grad_shapes = lambda count: [
         shape((2 * width, count), BF16),
         shape((2 * width, count), BF16),
         shape((2 * width, 2 * count), BF16),
     ]
-    one = lambda b: pl.BlockSpec((width, wide), lambda i: (0, b))
-    two = lambda b: pl.BlockSpec((width, 2 * wide), lambda i: (0, b))
-    whole = lambda extent: pl.BlockSpec(extent, lambda i: (0,) * len(extent))
-    label_specs = [whole(label.shape) for label in labels]
     grads = []
     for bucket in range(buckets - 1):
-        outs = grad_shapes(wide)
         grads += call(
             functools.partial(bucket_kernel, plan, bucket),
-            outs,
+            grad_shapes(wide),
             labels + [targets[bucket], lhs, vec, cand_rem],
             "bucket",
-            7.0,
-            grid=(1,),
-            in_specs=label_specs + [whole(own.shape), one(bucket), one(bucket), two(bucket)],
-            out_specs=[whole(out.shape) for out in outs],
+            5.0,
+            16 * grow,
         )
     last = buckets - 1
     chunk = (plan.half_chunks, plan.chunk_rows, LANES)
+    bare = (plan.half_chunks, 8 * plan.chunk_units, LANES)
     table = [pltpu.VMEM((width, plan.half_lanes), F32)]
     made = call(
         functools.partial(last_kernel, plan),
         [shape(chunk, i16)] + grad_shapes(edges),
         labels + grads + [targets[last], lhs, vec, cand_rem],
         "last",
-        14.0,
-        grid=(1,),
-        in_specs=label_specs
-        + [ANY] * len(grads)
-        + [whole(own.shape), one(last), one(last), two(last)],
-        out_specs=[whole(chunk)] + [ANY] * 3,
+        12.0,
+        24 * grow,
+        in_specs=[VMEM] * len(labels) + [ANY] * len(grads) + [VMEM] * 4,
+        out_specs=[VMEM] + [ANY] * 3,
         scratch=[pltpu.VMEM(held.shape, BF16) for held in grad_shapes(edges)]
         + table
         + [pltpu.SemaphoreType.DMA((len(grads) + 3,))],
@@ -582,79 +585,122 @@
         packed += call(
             functools.partial(near_kernel, plan, bucket),
             [shape((width + 16, prows), i16)],
-            labels + [grads[2]],
+            labels + [grads[2], away],
             "near",
-            2.5,
-            grid=(1,),
-            in_specs=label_specs
-            + [pl.BlockSpec((2 * width, 2 * wide), lambda i, b=bucket: (0, b))],
-            out_specs=[whole((width + 16, prows))],
+            1.5,
+            12 * grow,
+            in_specs=[VMEM] * (len(labels) + 1) + [ANY],
         )
         near.append(send(packed[-1], plan, lambda d, b=bucket: d ^ (b * plan.rels)))
-    keep, part, source = call(
+    (keep,) = call(
         functools.partial(home_kernel, plan, len(packed) + 1),
-        [shape(chunk, F32), shape((width, prows), F32), shape((width, prows), F32)],
+        [shape(bare, F32)],
         labels + grads + packed + [away],
         "home",
-        11.0,
+        6.0,
+        16 * grow,
         in_specs=[VMEM] * (len(labels) + 3) + [ANY] * (len(packed) + 1),
         scratch=table,
     )
 
     def shares(count, size):
-        extent = (count // size,) + chunk[1:]
-        return [shape(extent, F32)] + [shape(extent, i16)] * (size - 1)
+        return [shape((count // size,) + bare[1:], F32)] + [
+            shape((count // size,) + chunk[1:], i16)
+        ] * (size - 1)
 
     def exchanged(values, masks):
         return [
             send(value, plan, lambda d, m=mask: d ^ m) for value, mask in zip(values, masks[1:])
         ]
 
+    def after(kernel, outs, args, others, name, cost, limit=12):
+        return call(
+            kernel,
+            outs,
+            list(args) + list(others),
+            name,
+            cost,
+            limit,
+            in_specs=[VMEM] * len(args) + [ANY] * len(others),
+        )
+
     size, later = len(plan.masks[1]), len(plan.masks[2])
     made = call(
-        functools.partial(stage_one_kernel, plan),
-        shares(chunk[0], size) + [shape((width + 16, prows), i16)],
-        [keep, core, part] + near,
-        "stage_one",
-        4.0,
-        16,
-    )
-    keep, arrived = made[0], exchanged(made[1:-1], plan.masks[1])
-    far = send(made[-1], plan, afar)
-
+        functools.partial(combine_kernel, plan, 2, False),
+        shares(chunk[0], size),
+        [keep, core],
+        "combine_cores",
+        1.0,
+        12,
+    )
+    keep, arrived = made[0], exchanged(made[1:], plan.masks[1])
+    (far,) = after(
+        functools.partial(far_kernel, plan),
+        [shape((width + 16, prows), i16)],
+        labels + [grads[2]] + near,
+        [keep],
+        "far",
+        2.0,
+        12 * grow,
+    )
+    (source,) = after(
+        functools.partial(source_kernel, plan),
+        [shape((width, prows), F32)],
+        labels + [grads[0]],
+        [far],
+        "source",
+        1.5,
+        12 * grow,
+    )
+    far = send(far, plan, afar)
+
+    made = after(
+        functools.partial(combine_kernel, plan, size, False),
+        shares(chunk[0] // size, later),
+        [keep] + arrived,
+        [],
+        "combine_xy",
+        1.0,
+    )
+    keep, arrived = made[0], exchanged(made[1:], plan.masks[2])
     lanes = plan.part_lanes
-    made = call(
-        functools.partial(stage_two_kernel, plan),
-        shares(chunk[0] // size, later)
-        + [shape((width, lanes), F32)]
-        + [shape((width + 16, lanes), i16)] * (plan.rels - 1),
-        [keep] + arrived + [source, far],
-        "stage_two",
-        3.0,
-        16,
-    )
-    keep, arrived = made[0], exchanged(made[1:later], plan.masks[2])
-    mine = [made[later]] + exchanged(made[later + 1 :], range(plan.rels))
-
-    total, part = call(
-        functools.partial(stage_three_kernel, plan),
-        [shape((1,) + chunk[1:], i16), shape((width + 16, lanes), i16)],
-        [keep] + arrived + mine,
-        "stage_three",
-        2.0,
-        16,
+    made = after(
+        functools.partial(share_kernel, plan),
+        [shape((width, lanes), F32)] + [shape((width + 16, lanes), i16)] * (plan.rels - 1),
+        [source, far],
+        [keep],
+        "share",
+        1.0,
+    )
+    mine = [made[0]] + exchanged(made[1:], range(plan.rels))
+
+    (total,) = after(
+        functools.partial(combine_kernel, plan, later, True),
+        [shape((1,) + chunk[1:], i16)],
+        [keep] + arrived,
+        [],
+        "combine_z",
+        0.5,
     )
     pieces = [total] + exchanged([total] * (later - 1), plan.masks[2])
+    (part,) = after(
+        functools.partial(mine_kernel, plan),
+        [shape((width + 16, lanes), i16)],
+        mine,
+        [total],
+        "mine",
+        0.5,
+    )
     owners = [part] + exchanged([part] * (plan.rels - 1), range(plan.rels))
     block = jnp.concatenate(pieces, axis=0)
     pieces = [block] + exchanged([block] * (size - 1), plan.masks[1])
-    (grad_partitions,) = call(
+    (grad_partitions,) = after(
         functools.partial(part_out_kernel, plan),
         [shape((width, prows), F32)],
         owners,
+        [block],
         "part_out",
-        2.0,
-        16,
+        1.0,
     )
     if lanes % LANES:
         order = jnp.arange(plan.rels) ^ lax.axis_index("rel")
@@ -664,30 +710,27 @@
     others = [send(piece, plan, lambda d: d ^ 1) for piece in pieces]
     side = lax.axis_index("rel") & 1
     outs = [shape((width, plan.nrels), F32), shape((width, plan.rems), F32)]
-    held = pltpu.VMEM(chunk, i16)
+    spec = lambda lanes: pl.BlockSpec((width, lanes), lambda i, half: (0, half[0]))
+    made = []
     for turn, group in enumerate([pieces, others]):
-        base = [] if turn == 0 else list(outs_made)
-        spec = lambda lanes: pl.BlockSpec((width, lanes), lambda i, half: (0, half[0]))
-        work = pl.CostEstimate(flops=int(2e9), bytes_accessed=int(6e6), transcendentals=0)
-        outs_made = pl.pallas_call(
-            functools.partial(spread_kernel, plan, turn, len(group)),
-            out_shape=outs,
+        made = call(
+            functools.partial(spread_kernel, plan, len(group)),
+            outs,
+            [(side ^ turn).reshape(1), *group, *made],
+            "spread",
+            2.0,
+            16,
             grid_spec=pltpu.PrefetchScalarGridSpec(
                 num_scalar_prefetch=1,
                 grid=(1,),
-                in_specs=[
-                    pl.BlockSpec(piece.shape, lambda i, half: (0, 0, 0)) for piece in group
-                ]
-                + [ANY] * len(base),
+                in_specs=[pl.BlockSpec(piece.shape, lambda i, half: (0, 0, 0)) for piece in group]
+                + [ANY] * len(made),
                 out_specs=[spec(plan.half_rel), spec(plan.half_rem)],
-                scratch_shapes=[held],
+                scratch_shapes=[pltpu.VMEM(chunk, i16)],
             ),
-            input_output_aliases={1 + len(group) + at: at for at in range(len(base))},
-            compiler_params=pltpu.CompilerParams(vmem_limit_bytes=24 * 2**20),
-            cost_estimate=work,
-            name="spread",
-        )((side ^ turn).reshape(1), *group, *base)
-    grad_relations, grad_remainder = outs_made
+            input_output_aliases={1 + len(group) + at: at for at in range(len(made))},
+        )
+    grad_relations, grad_remainder = made
     return grad_partitions.T, grad_remainder.T, grad_relations.T
 
 

time: 131 us -> 111 us (0.85)
  local copies, waits for them, and re-layouts: 11.4 us -> 2.87 us
  waiting for transfers between devices: 41.7 us -> 33.9 us
  Pallas kernels: 41.2 us -> 33.5 us
  starting transfers between devices: 34.6 us -> 39.7 us
    unnamed x35 -> x10, local copies, waits for them, and re-layouts: 11.4 us -> 2.87 us
    ppermute x30, waiting for transfers between devices: 41.7 us -> 33.9 us  [send(): return lax.ppermute(value, ('dom', 'rel'), pairs)]
    pallas_call x13 -> x18, Pallas kernels: 41.2 us -> 33.5 us  [call(): pl.pallas_call(kernel, out_shape=outs, compiler_params=pltpu.CompilerPara...]
    ppermute x30, starting transfers between devices: 34.6 us -> 39.7 us  [send(): return lax.ppermute(value, ('dom', 'rel'), pairs)]
  transfers between devices with their start and end apart: 30 -> 30, of which waited for: 10 -> 10; matrix products, arithmetic and copies ran while one was open for 0% -> 0% of each run, Pallas kernels for 20% -> 19%
where the time goes in v3:
time: 111 us
  starting transfers between devices  39.7 us (36%)
  waiting for transfers between devices  33.9 us (31%)
  Pallas kernels  33.5 us (30%)
  local copies, waits for them, and re-layouts  2.87 us (3%)
    ppermute x30, starting transfers between devices, send(): return lax.ppermute(value, ('dom', 'rel'), pairs)  39.7 us
    ppermute x30, waiting for transfers between devices, send(): return lax.ppermute(value, ('dom', 'rel'), pairs)  33.9 us
    pallas_call x18, Pallas kernels, call(): pl.pallas_call(kernel, out_shape=outs, compiler_params=pltpu.CompilerPara...  33.5 us
    unnamed x10, local copies, waits for them, and re-layouts  2.87 us
  transfers between devices with their start and end apart: 30, of which 10 were waited for; matrix products, arithmetic and copies ran while one was open for 0% of the time, Pallas kernels for 19%

profile of v3, /device:TPU:0, one launch (start us, length us, event | category | flops | bytes accessed | tf_op | source)
XLA Modules:
  0.0 110.9 jit_solution(8205832516812444656)
XLA Ops:
  2.6 2.6 %collective-permute-start.1 = (s32[2,8,128]{2,1,0:T(8,128)}, s32[2,8,128]{2,1,0:T(8,128)S(1)}, u32[]{:S(2)}, u32[]{:S(2)}) collective-permute-start(s32[2,8,128]{2,1,0:T(8,128)} %get-tuple-element.34), channel_id=1, source_target_pairs={{0,2},{1,3},{2,0},{3,1},{4,6},{5,7},{6,4},{7,5},{8,10},{9,11},{10,... | collective-permute-start | bytes 24584 | tf_op jit(solution)/shard_map/ppermute | solution.py:174
  8.5 2.2 %copy-done = f32[2560,400]{0,1:T(8,128)S(1)} copy-done((f32[2560,400]{0,1:T(8,128)S(1)}, f32[2560,400]{0,1:T(8,128)}, u32[]{:S(2)}) %copy-start) | copy-done | bytes 4096024
  11.3 4.4 %relation.1.refs_1_.refs_6_.refs_9_ = f32[400,1024]{1,0:T(8,128)S(1)} custom-call(s32[2,8,128]{2,1,0:T(8,128)S(1)} %copy-done.3, s32[2,8,128]{2,1,0:T(8,128)S(1)} %collective-permute-done.refs_1_, s32[2,8,128]{2,1,0:T(8,128)S(1)} %collective-permute-done.1.refs_2_, s32[2,8,128]{2,1,0:T(8,128)S(1)} %collective-permute-done.2.refs_3_, f32[400,2560]{1,0:T(8,128)S(1)} %bitcast.9), custom_call_target="tpu_custom_call" | custom-call | flops 6000000000 | bytes 18000000 | tf_op jit(solution)/shard_map/relation/pallas_call | solution.py:460
  15.7 1.6 %collective-permute-start.4 = (bf16[400,512]{1,0:T(8,128)(2,1)S(1)}, bf16[400,512]{1,0:T(8,128)(2,1)S(1)}, u32[]{:S(2)}, u32[]{:S(2)}) collective-permute-start(bf16[400,512]{1,0:T(8,128)(2,1)S(1)} %relay.1.refs_6_.refs_4_), channel_id=1, source_target_pairs={{0,4},{1,5},{2,6},{3,7},{4,0},{5,1},{6,2},{7,3},{8,12},{9,13},{10,... | collective-permute-start | bytes 1228808 | tf_op jit(solution)/shard_map/ppermute | solution.py:174
  18.6 4.1 %bucket.1 = (bf16[800,512]{1,0:T(8,128)(2,1)S(1)}, bf16[800,512]{1,0:T(8,128)(2,1)S(1)}, bf16[800,1024]{1,0:T(8,128)(2,1)S(1)}) custom-call(s32[2,8,128]{2,1,0:T(8,128)S(1)} %copy-done.4, s32[2,8,128]{2,1,0:T(8,128)S(1)} %collective-permute-done.refs_1_, s32[2,8,128]{2,1,0:T(8,128)S(1)} %collective-permute-done.1.refs_2_, ...), custom_call_target="tpu_custom_call" | custom-call | flops 5000000000 | bytes 15000000 | tf_op jit(solution)/shard_map/bucket/pallas_call | solution.py:460
  22.7 2.4 %collective-permute-done.4.refs_7_ = bf16[400,512]{1,0:T(8,128)(2,1)S(1)} collective-permute-done((bf16[400,512]{1,0:T(8,128)(2,1)S(1)}, bf16[400,512]{1,0:T(8,128)(2,1)S(1)}, u32[]{:S(2)}, u32[]{:S(2)}) %collective-permute-start.4) | collective-permute-done | bytes 409632 | tf_op jit(solution)/shard_map/ppermute | solution.py:174
  25.1 9.5 %last.1 = (s16[16,288,128]{2,1,0:T(8,128)(2,1)S(1)}, bf16[800,1024]{1,0:T(8,128)(2,1)S(1)}, bf16[800,1024]{1,0:T(8,128)(2,1)S(1)}, bf16[800,2048]{1,0:T(8,128)(2,1)S(1)}) custom-call(s32[2,8,128]{2,1,0:T(8,128)S(1)} %copy-done.4, s32[2,8,128]{2,1,0:T(8,128)S(1)} %collective-permute-done.refs_1_, s32[2,8,128]{2,1,0:T(8,128)S(1)} %collective-permute-done.1.refs_2_, ...), custom_call_target="tpu_custom_call" | custom-call | flops 12000000000 | bytes 36000000 | tf_op jit(solution)/shard_map/last/pallas_call | solution.py:460
  34.6 2.9 %collective-permute-start.6 = (s16[16,288,128]{2,1,0:T(8,128)(2,1)S(1)}, s16[16,288,128]{2,1,0:T(8,128)(2,1)S(1)}, u32[]{:S(2)}, u32[]{:S(2)}) collective-permute-start(s16[16,288,128]{2,1,0:T(8,128)(2,1)S(1)} %get-tuple-element.43.refs_5_.refs_8_), channel_id=1, source_target_pairs={{0,1},{1,0},{2,3},{3,2},{4,5},{5,4},{6,7},{7,6},{8,9},{9,8},{10,11... | collective-permute-start | bytes 3538952 | tf_op jit(solution)/shard_map/ppermute | solution.py:174
  38.7 1.6 %collective-permute-start.5 = (s16[416,512]{1,0:T(8,128)(2,1)S(1)}, s16[416,512]{1,0:T(8,128)(2,1)S(1)}, u32[]{:S(2)}, u32[]{:S(2)}) collective-permute-start(s16[416,512]{1,0:T(8,128)(2,1)S(1)} %near.1.refs_7_), channel_id=1, source_target_pairs={{0,4},{1,5},{2,6},{3,7},{4,0},{5,1},{6,2},{7,3},{8,12},{9,13},{10,... | collective-permute-start | bytes 1277960 | tf_op jit(solution)/shard_map/ppermute | solution.py:174
  40.3 3.6 %home.1.refs_0_ = f32[16,280,128]{2,1,0:T(8,128)S(1)} custom-call(s32[2,8,128]{2,1,0:T(8,128)S(1)} %copy-done.4, s32[2,8,128]{2,1,0:T(8,128)S(1)} %collective-permute-done.refs_1_, s32[2,8,128]{2,1,0:T(8,128)S(1)} %collective-permute-done.1.refs_2_, s32[2,8,128]{2,1,0:T(8,128)S(1)} %collective-permute-done.2.refs_3_, ...), custom_call_target="tpu_custom_call" | custom-call | flops 6000000000 | bytes 18000000 | tf_op jit(solution)/shard_map/home/pallas_call | solution.py:460
  44.5 5.0 %collective-permute-start.8 = (s16[4,288,128]{2,1,0:T(8,128)(2,1)S(1)}, s16[4,288,128]{2,1,0:T(8,128)(2,1)S(1)}, u32[]{:S(2)}, u32[]{:S(2)}) collective-permute-start(s16[4,288,128]{2,1,0:T(8,128)(2,1)S(1)} %get-tuple-element.46), channel_id=1, source_target_pairs={{0,2},{1,3},{2,0},{3,1},{4,6},{5,7},{6,4},{7,5},{8,10},{9,11},{10,... | collective-permute-start | bytes 884744 | tf_op jit(solution)/shard_map/ppermute | solution.py:174
  53.2 4.1 %collective-permute-done.8.refs_1_ = s16[4,288,128]{2,1,0:T(8,128)(2,1)S(1)} collective-permute-done((s16[4,288,128]{2,1,0:T(8,128)(2,1)S(1)}, s16[4,288,128]{2,1,0:T(8,128)(2,1)S(1)}, u32[]{:S(2)}, u32[]{:S(2)}) %collective-permute-start.8) | collective-permute-done | bytes 294944 | tf_op jit(solution)/shard_map/ppermute | solution.py:174
  57.3 7.4 %collective-permute-done.9.refs_2_ = s16[4,288,128]{2,1,0:T(8,128)(2,1)S(1)} collective-permute-done((s16[4,288,128]{2,1,0:T(8,128)(2,1)S(1)}, s16[4,288,128]{2,1,0:T(8,128)(2,1)S(1)}, u32[]{:S(2)}, u32[]{:S(2)}) %collective-permute-start.9) | collective-permute-done | bytes 294944 | tf_op jit(solution)/shard_map/ppermute | solution.py:174
  65.4 3.2 %collective-permute-start.15 = (s16[1,288,128]{2,1,0:T(8,128)(2,1)S(1)}, s16[1,288,128]{2,1,0:T(8,128)(2,1)S(1)}, u32[]{:S(2)}, u32[]{:S(2)}) collective-permute-start(s16[1,288,128]{2,1,0:T(8,128)(2,1)S(1)} %get-tuple-element.55), channel_id=1, source_target_pairs={{0,16},{1,17},{2,18},{3,19},{4,20},{5,21},{6,22},{7,23},{8,24},{9,... | collective-permute-start | bytes 221192 | tf_op jit(solution)/shard_map/ppermute | solution.py:174
  70.6 2.5 %collective-permute-done.15.refs_2_ = s16[1,288,128]{2,1,0:T(8,128)(2,1)S(1)} collective-permute-done((s16[1,288,128]{2,1,0:T(8,128)(2,1)S(1)}, s16[1,288,128]{2,1,0:T(8,128)(2,1)S(1)}, u32[]{:S(2)}, u32[]{:S(2)}) %collective-permute-start.15) | collective-permute-done | bytes 73760 | tf_op jit(solution)/shard_map/ppermute | solution.py:174
  73.0 1.8 %collective-permute-done.16.refs_3_ = s16[1,288,128]{2,1,0:T(8,128)(2,1)S(1)} collective-permute-done((s16[1,288,128]{2,1,0:T(8,128)(2,1)S(1)}, s16[1,288,128]{2,1,0:T(8,128)(2,1)S(1)}, u32[]{:S(2)}, u32[]{:S(2)}) %collective-permute-start.16) | collective-permute-done | bytes 73760 | tf_op jit(solution)/shard_map/ppermute | solution.py:174
  74.9 1.7 %collective-permute-start.22 = (s16[1,288,128]{2,1,0:T(8,128)(2,1)S(1)}, s16[1,288,128]{2,1,0:T(8,128)(2,1)S(1)}, u32[]{:S(2)}, u32[]{:S(2)}) collective-permute-start(s16[1,288,128]{2,1,0:T(8,128)(2,1)S(1)} %combine_z.1.refs_4_), channel_id=1, source_target_pairs={{0,24},{1,25},{2,26},{3,27},{4,28},{5,29},{6,30},{7,31},{8,16},{9,... | collective-permute-start | bytes 221192 | tf_op jit(solution)/shard_map/ppermute | solution.py:174
  76.6 2.8 %collective-permute-start.20 = (s16[1,288,128]{2,1,0:T(8,128)(2,1)S(1)}, s16[1,288,128]{2,1,0:T(8,128)(2,1)S(1)}, u32[]{:S(2)}, u32[]{:S(2)}) collective-permute-start(s16[1,288,128]{2,1,0:T(8,128)(2,1)S(1)} %combine_z.1.refs_4_), channel_id=1, source_target_pairs={{0,8},{1,9},{2,10},{3,11},{4,12},{5,13},{6,14},{7,15},{8,0},{9,1},... | collective-permute-start | bytes 221192 | tf_op jit(solution)/shard_map/ppermute | solution.py:174
  79.7 4.0 %collective-permute-start.12 = (s16[416,128]{1,0:T(8,128)(2,1)S(1)}, s16[416,128]{1,0:T(8,128)(2,1)S(1)}, u32[]{:S(2)}, u32[]{:S(2)}) collective-permute-start(s16[416,128]{1,0:T(8,128)(2,1)S(1)} %get-tuple-element.52), channel_id=1, source_target_pairs={{0,2},{1,3},{2,0},{3,1},{4,6},{5,7},{6,4},{7,5},{8,10},{9,11},{10,... | collective-permute-start | bytes 319496 | tf_op jit(solution)/shard_map/ppermute | solution.py:174
  83.8 3.2 %collective-permute-start.24 = (s16[4,288,128]{2,1,0:T(8,128)(2,1)S(1)}, s16[4,288,128]{2,1,0:T(8,128)(2,1)S(1)}, u32[]{:S(2)}, u32[]{:S(2)}) collective-permute-start(s16[4,288,128]{2,1,0:T(8,128)(2,1)S(1)} %pad_add_fusion.refs_4_.refs_0_), channel_id=1, source_target_pairs={{0,2},{1,3},{2,0},{3,1},{4,6},{5,7},{6,4},{7,5},{8,10},{9,11},{10,... | collective-permute-start | bytes 884744 | tf_op jit(solution)/shard_map/ppermute | solution.py:174
  89.8 2.2 %collective-permute-start.18 = (s16[416,128]{1,0:T(8,128)(2,1)S(1)}, s16[416,128]{1,0:T(8,128)(2,1)S(1)}, u32[]{:S(2)}, u32[]{:S(2)}) collective-permute-start(s16[416,128]{1,0:T(8,128)(2,1)S(1)} %mine.1.refs_0_), channel_id=1, source_target_pairs={{0,2},{1,3},{2,0},{3,1},{4,6},{5,7},{6,4},{7,5},{8,10},{9,11},{10,... | collective-permute-start | bytes 319496 | tf_op jit(solution)/shard_map/ppermute | solution.py:174
  93.0 11.7 %collective-permute-done.18.refs_2_ = s16[416,128]{1,0:T(8,128)(2,1)S(1)} collective-permute-done((s16[416,128]{1,0:T(8,128)(2,1)S(1)}, s16[416,128]{1,0:T(8,128)(2,1)S(1)}, u32[]{:S(2)}, u32[]{:S(2)}) %collective-permute-start.18) | collective-permute-done | bytes 106528 | tf_op jit(solution)/shard_map/ppermute | solution.py:174
  107.5 1.7 %spread.2 = (f32[400,2560]{1,0:T(8,128)}, f32[400,256]{1,0:T(8,128)}) custom-call(s32[1]{0:T(128)} %bitcast.6.side, s16[4,288,128]{2,1,0:T(8,128)(2,1)S(1)} %pad_add_fusion.refs_4_.refs_0_, s16[4,288,128]{2,1,0:T(8,128)(2,1)S(1)} %collective-permute-done.24.refs_1_, s16[4,288,128]{2,1,0:T(8,128)(2,1)S(1)} %collective-permute-done.26.refs_2_, ...), custom_call_target="tpu_custom_call" | custom-call | flops 2000000000 | bytes 6000000 | tf_op jit(solution)/shard_map/spread/pallas_call | solution.py:460
  109.2 1.7 %spread.3 = (f32[400,2560]{1,0:T(8,128)}, f32[400,256]{1,0:T(8,128)}) custom-call(s32[1]{0:T(128)} %bitcast.5.side, s16[4,288,128]{2,1,0:T(8,128)(2,1)S(1)} %collective-permute-done.23.refs_0_, s16[4,288,128]{2,1,0:T(8,128)(2,1)S(1)} %collective-permute-done.25.refs_1_, ...), custom_call_target="tpu_custom_call", output_to_operand_aliasing={{0}: (5, {}), {1}: (6, {})} | custom-call | flops 2000000000 | bytes 6000000 | tf_op jit(solution)/shard_map/spread/pallas_call | solution.py:460
  (65 shorter events, 22.3 us)
Async XLA Ops:
  5.2 10.5 %collective-permute-start.3 = (bf16[400,512]{1,0:T(8,128)(2,1)S(1)}, bf16[400,512]{1,0:T(8,128)(2,1)S(1)}, u32[]{:S(2)}, u32[]{:S(2)}) collective-permute-start(bf16[400,512]{1,0:T(8,128)(2,1)S(1)} %bitcast.10), channel_id=1, source_target_pairs={{0,0},{1,17},{2,10},{3,27},{4,4},{5,21},{6,14},{7,31},{8,8},{9,25}... | collective-permute-start | bytes 1228808 | tf_op jit(solution)/shard_map/ppermute | solution.py:174
  15.7 9.4 %collective-permute-start.4 = (bf16[400,512]{1,0:T(8,128)(2,1)S(1)}, bf16[400,512]{1,0:T(8,128)(2,1)S(1)}, u32[]{:S(2)}, u32[]{:S(2)}) collective-permute-start(bf16[400,512]{1,0:T(8,128)(2,1)S(1)} %relay.1.refs_6_.refs_4_), channel_id=1, source_target_pairs={{0,4},{1,5},{2,6},{3,7},{4,0},{5,1},{6,2},{7,3},{8,12},{9,13},{10,... | collective-permute-start | bytes 1228808 | tf_op jit(solution)/shard_map/ppermute | solution.py:174
  34.6 9.3 %collective-permute-start.6 = (s16[16,288,128]{2,1,0:T(8,128)(2,1)S(1)}, s16[16,288,128]{2,1,0:T(8,128)(2,1)S(1)}, u32[]{:S(2)}, u32[]{:S(2)}) collective-permute-start(s16[16,288,128]{2,1,0:T(8,128)(2,1)S(1)} %get-tuple-element.43.refs_5_.refs_8_), channel_id=1, source_target_pairs={{0,1},{1,0},{2,3},{3,2},{4,5},{5,4},{6,7},{7,6},{8,9},{9,8},{10,11... | collective-permute-start | bytes 3538952 | tf_op jit(solution)/shard_map/ppermute | solution.py:174
  38.7 12.4 %collective-permute-start.5 = (s16[416,512]{1,0:T(8,128)(2,1)S(1)}, s16[416,512]{1,0:T(8,128)(2,1)S(1)}, u32[]{:S(2)}, u32[]{:S(2)}) collective-permute-start(s16[416,512]{1,0:T(8,128)(2,1)S(1)} %near.1.refs_7_), channel_id=1, source_target_pairs={{0,4},{1,5},{2,6},{3,7},{4,0},{5,1},{6,2},{7,3},{8,12},{9,13},{10,... | collective-permute-start | bytes 1277960 | tf_op jit(solution)/shard_map/ppermute | solution.py:174
  44.5 12.8 %collective-permute-start.8 = (s16[4,288,128]{2,1,0:T(8,128)(2,1)S(1)}, s16[4,288,128]{2,1,0:T(8,128)(2,1)S(1)}, u32[]{:S(2)}, u32[]{:S(2)}) collective-permute-start(s16[4,288,128]{2,1,0:T(8,128)(2,1)S(1)} %get-tuple-element.46), channel_id=1, source_target_pairs={{0,2},{1,3},{2,0},{3,1},{4,6},{5,7},{6,4},{7,5},{8,10},{9,11},{10,... | collective-permute-start | bytes 884744 | tf_op jit(solution)/shard_map/ppermute | solution.py:174
  49.5 15.2 %collective-permute-start.9 = (s16[4,288,128]{2,1,0:T(8,128)(2,1)S(1)}, s16[4,288,128]{2,1,0:T(8,128)(2,1)S(1)}, u32[]{:S(2)}, u32[]{:S(2)}) collective-permute-start(s16[4,288,128]{2,1,0:T(8,128)(2,1)S(1)} %get-tuple-element.47), channel_id=1, source_target_pairs={{0,4},{1,5},{2,6},{3,7},{4,0},{5,1},{6,2},{7,3},{8,12},{9,13},{10,... | collective-permute-start | bytes 884744 | tf_op jit(solution)/shard_map/ppermute | solution.py:174
  50.1 14.7 %collective-permute-start.10 = (s16[4,288,128]{2,1,0:T(8,128)(2,1)S(1)}, s16[4,288,128]{2,1,0:T(8,128)(2,1)S(1)}, u32[]{:S(2)}, u32[]{:S(2)}) collective-permute-start(s16[4,288,128]{2,1,0:T(8,128)(2,1)S(1)} %get-tuple-element.48), channel_id=1, source_target_pairs={{0,6},{1,7},{2,4},{3,5},{4,2},{5,3},{6,0},{7,1},{8,14},{9,15},{10,... | collective-permute-start | bytes 884744 | tf_op jit(solution)/shard_map/ppermute | solution.py:174
  52.3 27.1 %collective-permute-start.7 = (s16[416,512]{1,0:T(8,128)(2,1)S(1)}, s16[416,512]{1,0:T(8,128)(2,1)S(1)}, u32[]{:S(2)}, u32[]{:S(2)}) collective-permute-start(s16[416,512]{1,0:T(8,128)(2,1)S(1)} %far.1.refs_5_), channel_id=1, source_target_pairs={{0,0},{1,17},{2,10},{3,27},{4,4},{5,21},{6,14},{7,31},{8,8},{9,25}... | collective-permute-start | bytes 1277960 | tf_op jit(solution)/shard_map/ppermute | solution.py:174
  65.0 5.5 %collective-permute-start.14 = (s16[1,288,128]{2,1,0:T(8,128)(2,1)S(1)}, s16[1,288,128]{2,1,0:T(8,128)(2,1)S(1)}, u32[]{:S(2)}, u32[]{:S(2)}) collective-permute-start(s16[1,288,128]{2,1,0:T(8,128)(2,1)S(1)} %get-tuple-element.54), channel_id=1, source_target_pairs={{0,8},{1,9},{2,10},{3,11},{4,12},{5,13},{6,14},{7,15},{8,0},{9,1},... | collective-permute-start | bytes 221192 | tf_op jit(solution)/shard_map/ppermute | solution.py:174
  65.4 7.6 %collective-permute-start.15 = (s16[1,288,128]{2,1,0:T(8,128)(2,1)S(1)}, s16[1,288,128]{2,1,0:T(8,128)(2,1)S(1)}, u32[]{:S(2)}, u32[]{:S(2)}) collective-permute-start(s16[1,288,128]{2,1,0:T(8,128)(2,1)S(1)} %get-tuple-element.55), channel_id=1, source_target_pairs={{0,16},{1,17},{2,18},{3,19},{4,20},{5,21},{6,22},{7,23},{8,24},{9,... | collective-permute-start | bytes 221192 | tf_op jit(solution)/shard_map/ppermute | solution.py:174
  68.6 6.2 %collective-permute-start.16 = (s16[1,288,128]{2,1,0:T(8,128)(2,1)S(1)}, s16[1,288,128]{2,1,0:T(8,128)(2,1)S(1)}, u32[]{:S(2)}, u32[]{:S(2)}) collective-permute-start(s16[1,288,128]{2,1,0:T(8,128)(2,1)S(1)} %get-tuple-element.56), channel_id=1, source_target_pairs={{0,24},{1,25},{2,26},{3,27},{4,28},{5,29},{6,30},{7,31},{8,16},{9,... | collective-permute-start | bytes 221192 | tf_op jit(solution)/shard_map/ppermute | solution.py:174
  74.9 8.8 %collective-permute-start.22 = (s16[1,288,128]{2,1,0:T(8,128)(2,1)S(1)}, s16[1,288,128]{2,1,0:T(8,128)(2,1)S(1)}, u32[]{:S(2)}, u32[]{:S(2)}) collective-permute-start(s16[1,288,128]{2,1,0:T(8,128)(2,1)S(1)} %combine_z.1.refs_4_), channel_id=1, source_target_pairs={{0,24},{1,25},{2,26},{3,27},{4,28},{5,29},{6,30},{7,31},{8,16},{9,... | collective-permute-start | bytes 221192 | tf_op jit(solution)/shard_map/ppermute | solution.py:174
  76.6 7.2 %collective-permute-start.21 = (s16[1,288,128]{2,1,0:T(8,128)(2,1)S(1)}, s16[1,288,128]{2,1,0:T(8,128)(2,1)S(1)}, u32[]{:S(2)}, u32[]{:S(2)}) collective-permute-start(s16[1,288,128]{2,1,0:T(8,128)(2,1)S(1)} %combine_z.1.refs_4_), channel_id=1, source_target_pairs={{0,16},{1,17},{2,18},{3,19},{4,20},{5,21},{6,22},{7,23},{8,24},{9,... | collective-permute-start | bytes 221192 | tf_op jit(solution)/shard_map/ppermute | solution.py:174
  76.6 7.2 %collective-permute-start.20 = (s16[1,288,128]{2,1,0:T(8,128)(2,1)S(1)}, s16[1,288,128]{2,1,0:T(8,128)(2,1)S(1)}, u32[]{:S(2)}, u32[]{:S(2)}) collective-permute-start(s16[1,288,128]{2,1,0:T(8,128)(2,1)S(1)} %combine_z.1.refs_4_), channel_id=1, source_target_pairs={{0,8},{1,9},{2,10},{3,11},{4,12},{5,13},{6,14},{7,15},{8,0},{9,1},... | collective-permute-start | bytes 221192 | tf_op jit(solution)/shard_map/ppermute | solution.py:174
  79.6 8.9 %collective-permute-start.11 = (s16[416,128]{1,0:T(8,128)(2,1)S(1)}, s16[416,128]{1,0:T(8,128)(2,1)S(1)}, u32[]{:S(2)}, u32[]{:S(2)}) collective-permute-start(s16[416,128]{1,0:T(8,128)(2,1)S(1)} %get-tuple-element.51), channel_id=1, source_target_pairs={{0,1},{1,0},{2,3},{3,2},{4,5},{5,4},{6,7},{7,6},{8,9},{9,8},{10,11... | collective-permute-start | bytes 319496 | tf_op jit(solution)/shard_map/ppermute | solution.py:174
  79.7 8.8 %collective-permute-start.12 = (s16[416,128]{1,0:T(8,128)(2,1)S(1)}, s16[416,128]{1,0:T(8,128)(2,1)S(1)}, u32[]{:S(2)}, u32[]{:S(2)}) collective-permute-start(s16[416,128]{1,0:T(8,128)(2,1)S(1)} %get-tuple-element.52), channel_id=1, source_target_pairs={{0,2},{1,3},{2,0},{3,1},{4,6},{5,7},{6,4},{7,5},{8,10},{9,11},{10,... | collective-permute-start | bytes 319496 | tf_op jit(solution)/shard_map/ppermute | solution.py:174
  83.7 5.6 %collective-permute-start.13 = (s16[416,128]{1,0:T(8,128)(2,1)S(1)}, s16[416,128]{1,0:T(8,128)(2,1)S(1)}, u32[]{:S(2)}, u32[]{:S(2)}) collective-permute-start(s16[416,128]{1,0:T(8,128)(2,1)S(1)} %get-tuple-element.53), channel_id=1, source_target_pairs={{0,3},{1,2},{2,1},{3,0},{4,7},{5,6},{6,5},{7,4},{8,11},{9,10},{10,... | collective-permute-start | bytes 319496 | tf_op jit(solution)/shard_map/ppermute | solution.py:174
  83.8 20.9 %collective-permute-start.24 = (s16[4,288,128]{2,1,0:T(8,128)(2,1)S(1)}, s16[4,288,128]{2,1,0:T(8,128)(2,1)S(1)}, u32[]{:S(2)}, u32[]{:S(2)}) collective-permute-start(s16[4,288,128]{2,1,0:T(8,128)(2,1)S(1)} %pad_add_fusion.refs_4_.refs_0_), channel_id=1, source_target_pairs={{0,2},{1,3},{2,0},{3,1},{4,6},{5,7},{6,4},{7,5},{8,10},{9,11},{10,... | collective-permute-start | bytes 884744 | tf_op jit(solution)/shard_map/ppermute | solution.py:174
  87.0 18.3 %collective-permute-start.26 = (s16[4,288,128]{2,1,0:T(8,128)(2,1)S(1)}, s16[4,288,128]{2,1,0:T(8,128)(2,1)S(1)}, u32[]{:S(2)}, u32[]{:S(2)}) collective-permute-start(s16[4,288,128]{2,1,0:T(8,128)(2,1)S(1)} %pad_add_fusion.refs_4_.refs_0_), channel_id=1, source_target_pairs={{0,4},{1,5},{2,6},{3,7},{4,0},{5,1},{6,2},{7,3},{8,12},{9,13},{10,... | collective-permute-start | bytes 884744 | tf_op jit(solution)/shard_map/ppermute | solution.py:174
  88.5 16.8 %collective-permute-start.28 = (s16[4,288,128]{2,1,0:T(8,128)(2,1)S(1)}, s16[4,288,128]{2,1,0:T(8,128)(2,1)S(1)}, u32[]{:S(2)}, u32[]{:S(2)}) collective-permute-start(s16[4,288,128]{2,1,0:T(8,128)(2,1)S(1)} %pad_add_fusion.refs_4_.refs_0_), channel_id=1, source_target_pairs={{0,6},{1,7},{2,4},{3,5},{4,2},{5,3},{6,0},{7,1},{8,14},{9,15},{10,... | collective-permute-start | bytes 884744 | tf_op jit(solution)/shard_map/ppermute | solution.py:174
  89.8 14.9 %collective-permute-start.18 = (s16[416,128]{1,0:T(8,128)(2,1)S(1)}, s16[416,128]{1,0:T(8,128)(2,1)S(1)}, u32[]{:S(2)}, u32[]{:S(2)}) collective-permute-start(s16[416,128]{1,0:T(8,128)(2,1)S(1)} %mine.1.refs_0_), channel_id=1, source_target_pairs={{0,2},{1,3},{2,0},{3,1},{4,6},{5,7},{6,4},{7,5},{8,10},{9,11},{10,... | collective-permute-start | bytes 319496 | tf_op jit(solution)/shard_map/ppermute | solution.py:174
  92.1 14.4 %collective-permute-start.19 = (s16[416,128]{1,0:T(8,128)(2,1)S(1)}, s16[416,128]{1,0:T(8,128)(2,1)S(1)}, u32[]{:S(2)}, u32[]{:S(2)}) collective-permute-start(s16[416,128]{1,0:T(8,128)(2,1)S(1)} %mine.1.refs_0_), channel_id=1, source_target_pairs={{0,3},{1,2},{2,1},{3,0},{4,7},{5,6},{6,5},{7,4},{8,11},{9,10},{10,... | collective-permute-start | bytes 319496 | tf_op jit(solution)/shard_map/ppermute | solution.py:174
  104.7 4.5 %collective-permute-start.23 = (s16[4,288,128]{2,1,0:T(8,128)(2,1)S(1)}, s16[4,288,128]{2,1,0:T(8,128)(2,1)S(1)}, u32[]{:S(2)}, u32[]{:S(2)}) collective-permute-start(s16[4,288,128]{2,1,0:T(8,128)(2,1)S(1)} %pad_add_fusion.refs_4_.refs_0_), channel_id=1, source_target_pairs={{0,1},{1,0},{2,3},{3,2},{4,5},{5,4},{6,7},{7,6},{8,9},{9,8},{10,11... | collective-permute-start | bytes 884744 | tf_op jit(solution)/shard_map/ppermute | solution.py:174
  104.7 4.5 %collective-permute-start.25 = (s16[4,288,128]{2,1,0:T(8,128)(2,1)S(1)}, s16[4,288,128]{2,1,0:T(8,128)(2,1)S(1)}, u32[]{:S(2)}, u32[]{:S(2)}) collective-permute-start(s16[4,288,128]{2,1,0:T(8,128)(2,1)S(1)} %collective-permute-done.24.refs_1_), channel_id=1, source_target_pairs={{0,1},{1,0},{2,3},{3,2},{4,5},{5,4},{6,7},{7,6},{8,9},{9,8},{10,11... | collective-permute-start | bytes 884744 | tf_op jit(solution)/shard_map/ppermute | solution.py:174
  (11 other events, 32.3 us)

commit v4 on v3

--- a/solution.py
+++ b/solution.py
@@ -134,8 +134,8 @@
         rows = []
         for slot in range(first, first + count):
             mask, turn = divmod(slot, self.maxb)
-            block = bucket * self.maxb + turn
-            rows += [labels[mask][block, kind : kind + 1, :] for kind in kinds]
+            block = labels[bucket * self.rels + mask]
+            rows += [block[turn, kind : kind + 1, :] for kind in kinds]
         return jnp.concatenate(rows, axis=1) if len(rows) > 1 else rows[0]
 
     def whole_row(self, labels, kinds):
@@ -158,15 +158,15 @@
                 out = out + (((relative >> (bit - 1)) & 1) << at)
         return out
 
-    def bucket_mask(self, rel, bucket):
-        return reverse_bits(rel, self.rels) * self.buckets + bucket
-
-    def dynamic_mask(self, rel, bucket):
+    def target_mask(self, rel):
+        return reverse_bits(rel, self.rels) * self.buckets
+
+    def dynamic_mask(self, rel):
         out = 0
         width = bits_of(self.rels)
         for bit in range(width):
             out = out + (((rel >> bit) & 1) << (width - 1 - bit))
-        return out * self.buckets + bucket
+        return out * self.buckets
 
 
 def send(value, plan, target):
@@ -178,51 +178,51 @@
     tables, counts, outs = refs[:7], refs[7], refs[8:]
     source = lax.axis_index("dom")
     rel = lax.axis_index("rel")
-    for mask, out in enumerate(outs):
-        for bucket in range(plan.buckets):
-            target = source ^ plan.dynamic_mask(rel ^ mask, bucket)
-            stop = lax.rem(source - target + plan.doms, plan.doms)
-            for turn in range(plan.maxb):
-                block = bucket * plan.maxb + turn
-                for at, table in enumerate(tables):
-                    out[block, at : at + 1, :] = table[0, stop, turn : turn + 1, :]
-                live = jnp.where(turn < counts[stop], 1, 0)
-                out[block, 7:8, :] = jnp.full((1, LANES), live, jnp.int32)
+    for at, out in enumerate(outs):
+        bucket, mask = divmod(at, plan.rels)
+        target = source ^ bucket ^ plan.dynamic_mask(rel ^ mask)
+        stop = lax.rem(source - target + plan.doms, plan.doms)
+        for turn in range(plan.maxb):
+            for kind, table in enumerate(tables):
+                out[turn, kind : kind + 1, :] = table[0, stop, turn : turn + 1, :]
+            live = jnp.where(turn < counts[stop], 1, 0)
+            out[turn, 7:8, :] = jnp.full((1, LANES), live, jnp.int32)
+
+
+def split_kernel(relations, out):
+    depth = relations.shape[0]
+    high, low = split(relations[...])
+    out[0:depth, :] = high
+    out[depth : 2 * depth, :] = low
 
 
 def relation_kernel(plan, *refs):
     labels = refs[: plan.rels]
-    relations, rel_out, rel_split = refs[plan.rels :]
-    depth = plan.width
-    high, low = split(relations[...])
-    rel_split[0:depth, :] = high
-    rel_split[depth : 2 * depth, :] = low
-    for bucket in range(plan.buckets):
-        for pair in range(0, plan.slots, 2):
-            count = min(2, plan.slots - pair)
-            start = bucket * plan.bucket_edges + pair * LANES
-            ids = plan.row(labels, bucket, (2,), pair, count)
-            rel_out[:, start : start + count * LANES] = folded(
-                dot(rel_split[...], one_hot(ids, plan.nrels), NN)
-            )
-
-
-def source_rows_kernel(plan, *refs):
+    relations, out = refs[plan.rels], refs[-1]
+    for pair in range(0, plan.slots, 2):
+        count = min(2, plan.slots - pair)
+        start = pair * LANES
+        ids = plan.row(labels, 0, (2,), pair, count)
+        out[:, start : start + count * LANES] = folded(
+            dot(relations[...], one_hot(ids, plan.nrels), NN)
+        )
+
+
+def rows_kernel(plan, *refs):
     labels = refs[: plan.rels]
     own, rem = refs[plan.rels : plan.rels + 2]
     lhs_out, rem_out = refs[-2:]
-    for bucket in range(plan.buckets):
-        for pair in range(0, plan.slots, 2):
-            count = min(2, plan.slots - pair)
-            row = lambda *kinds: plan.row(labels, bucket, kinds, pair, count)
-            start = bucket * plan.bucket_edges + pair * LANES
-            end = start + count * LANES
-            lhs_out[:, start:end] = dot(own[...], one_hot(row(0), plan.prows), NN) + dot(
-                rem[...], one_hot(row(1), plan.rems), NN
-            )
-            rem_out[:, 2 * start : 2 * end] = dot(
-                rem[...], one_hot(row(4, 6), plan.rems), NN
-            ).astype(BF16)
+    for pair in range(0, plan.slots, 2):
+        count = min(2, plan.slots - pair)
+        row = lambda *kinds: plan.row(labels, 0, kinds, pair, count)
+        start = pair * LANES
+        end = start + count * LANES
+        lhs_out[:, start:end] = dot(own[...], one_hot(row(0), plan.prows), NN) + dot(
+            rem[...], one_hot(row(1), plan.rems), NN
+        )
+        rem_out[:, 2 * start : 2 * end] = dot(
+            rem[...], one_hot(row(4, 6), plan.rems), NN
+        ).astype(BF16)
 
 
 def conjugate_parts(grad, other):
@@ -243,21 +243,20 @@
     )
 
 
-def bucket_grads(plan, bucket, labels, target, lhs_in, rel_in, rem_in, lhs_out, rel_out, cand_out, base):
+def bucket_grads(plan, labels, target, lhs_in, rel_in, rem_in, lhs_out, rel_out, cand_out, base):
     total = 2 * LANES
     edge = lax.broadcasted_iota(jnp.int32, (LANES, total), 0)
     column = lax.broadcasted_iota(jnp.int32, (LANES, total), 1)
     keep = jnp.where(edge == column, 0.0, 1.0 / total)
     for slot in range(plan.slots):
-        at = bucket * plan.slots + slot
-        cols = slice(at * LANES, (at + 1) * LANES)
-        wide = slice(at * total, (at + 1) * total)
-        ids = plan.row(labels, bucket, (3, 5), slot, 1)
+        cols = slice(slot * LANES, (slot + 1) * LANES)
+        wide = slice(slot * total, (slot + 1) * total)
+        ids = plan.row(labels, 0, (3, 5), slot, 1)
         cand = dot(target[...], one_hot(ids, plan.prows), NN) + rem_in[:, wide].astype(F32)
         rhs = cand[:, :LANES]
         lhs, vec = lhs_in[:, cols], rel_in[:, cols]
         u_vec = complex_product(lhs, vec)
-        live = plan.row(labels, bucket, (7,), slot, 1).astype(F32)
+        live = plan.row(labels, 0, (7,), slot, 1).astype(F32)
         positive = jnp.sum(u_vec * rhs, axis=0, keepdims=True)
         negative = dot3(u_vec, cand, TN)
         grad_pos = -jax.nn.sigmoid(-positive) * live
@@ -275,14 +274,15 @@
         store_split(cand_out, wide, grad_cand)
 
 
-def bucket_kernel(plan, bucket, *refs):
-    bucket_grads(plan, bucket, refs[: plan.rels], *refs[plan.rels :], 0)
+def bucket_kernel(plan, *refs):
+    bucket_grads(plan, refs[: plan.rels], *refs[plan.rels :], 0)
 
 
 def last_kernel(plan, *refs):
-    labels = refs[: plan.rels]
-    before = refs[plan.rels : plan.rels + 3 * (plan.buckets - 1)]
-    refs = refs[plan.rels + 3 * (plan.buckets - 1) :]
+    count = plan.rels * plan.buckets
+    labels = refs[:count]
+    before = refs[count : count + 3 * (plan.buckets - 1)]
+    refs = refs[count + 3 * (plan.buckets - 1) :]
     target, lhs_in, rel_in, rem_in = refs[:4]
     away, outs, helds, table, sems = refs[4], refs[5:8], refs[8:11], refs[11], refs[12]
     edges = plan.bucket_edges
@@ -295,7 +295,8 @@
         )
         loads[-1].start()
     base = (plan.buckets - 1) * plan.slots
-    bucket_grads(plan, plan.buckets - 1, labels, target, lhs_in, rel_in, rem_in, *helds, base)
+    own_labels = labels[count - plan.rels :]
+    bucket_grads(plan, own_labels, target, lhs_in, rel_in, rem_in, *helds, base)
     for load in loads:
         load.wait()
     stores = [
@@ -336,62 +337,55 @@
         out[plan.position(chunk, me)] = pack_table(value, plan.chunk_rows) if away else value
 
 
-def part_sum(plan, labels, bucket, grads):
-    ids = plan.row(labels, bucket, (3, 5), 0, plan.slots)
+def rows_sum(plan, ids, grads):
     shift = lax.axis_index("rel") * plan.part_lanes
-    start, wide = 2 * bucket * plan.bucket_edges, 2 * plan.bucket_edges
-    return folded(dot(grads[:, start : start + wide], one_hot(ids ^ shift, plan.prows), NT))
-
-
-def near_kernel(plan, bucket, *refs):
-    labels = refs[: plan.rels]
-    grads, out = refs[plan.rels], refs[-1]
-    out[...] = pack_table(part_sum(plan, labels, bucket, grads))
-
-
-def home_kernel(plan, after, *refs):
-    labels = refs[: plan.rels]
-    grads = refs[plan.rels : plan.rels + 3]
-    keep, table = refs[plan.rels + 3 + after :]
-    reduce_half(plan, False, labels, grads, table, keep)
-
-
-def far_kernel(plan, *refs):
-    labels = refs[: plan.rels]
-    grads, near = refs[plan.rels], refs[plan.rels + 1 : plan.rels + plan.buckets]
-    out = refs[-1]
-    value = part_sum(plan, labels, 0, grads)
-    for ref in near:
-        value = value + unpack_table(ref[...])
-    out[...] = pack_table(value)
-
-
-def source_kernel(plan, *refs):
-    labels = refs[: plan.rels]
-    grads, out = refs[plan.rels], refs[-1]
-    ids = plan.whole_row(labels, (0,)) ^ (lax.axis_index("rel") * plan.part_lanes)
-    out[...] = folded(dot(grads[...], one_hot(ids, plan.prows), NT))
+    return folded(dot(grads, one_hot(ids ^ shift, plan.prows), NT))
+
+
+def target_kernel(plan, *refs):
+    count = plan.rels * plan.buckets
+    ids = plan.whole_row(refs[:count], (3, 5))
+    refs[-1][...] = pack_table(rows_sum(plan, ids, refs[count][...]))
+
+
+def home_kernel(plan, *refs):
+    count = plan.rels * plan.buckets
+    keep, table = refs[-2:]
+    reduce_half(plan, False, refs[:count], refs[count : count + 3], table, keep)
+
+
+def source_sum(plan, labels, grads, bucket):
+    start = bucket * plan.bucket_edges
+    ids = plan.row(labels, 0, (0,), 0, plan.slots)
+    return rows_sum(plan, ids, grads[:, start : start + plan.bucket_edges])
+
+
+def to_shares(plan, value, outs):
+    lanes = plan.part_lanes
+    outs[0][...] = value[:, :lanes]
+    for at, out in enumerate(outs[1:], 1):
+        out[...] = pack_table(value[:, at * lanes : (at + 1) * lanes])
+
+
+def source_kernel(plan, bucket, *refs):
+    value = source_sum(plan, refs[: plan.rels], refs[plan.rels], bucket)
+    to_shares(plan, value, refs[-plan.rels :])
 
 
 def share_kernel(plan, *refs):
-    source, far = refs[:2]
-    mine, shares = refs[-plan.rels], refs[len(refs) - plan.rels + 1 :]
-    lanes = plan.part_lanes
-    value = source[...] + unpack_table(far[...])
-    mine[...] = value[:, :lanes]
-    for at, out in enumerate(shares):
-        out[...] = pack_table(value[:, (at + 1) * lanes : (at + 2) * lanes])
-
-
-def mine_kernel(plan, *refs):
+    value = source_sum(plan, refs[: plan.rels], refs[plan.rels], 0)
+    to_shares(plan, value + unpack_table(refs[plan.rels + 1][...]), refs[-plan.rels :])
+
+
+def add_kernel(count, *refs):
     value = refs[0][...]
-    for ref in refs[1 : plan.rels]:
+    for ref in refs[1:count]:
         value = value + unpack_table(ref[...])
     refs[-1][...] = pack_table(value)
 
 
-def combine_kernel(plan, group, last, *refs):
-    keep, arrived, outs = refs[0], refs[1:group], refs[group:]
+def combine_kernel(plan, group, last, after, *refs):
+    keep, arrived, outs = refs[0], refs[1:group], refs[group + after :]
     count, depth = keep.shape[0], keep.shape[1]
     share = count // len(outs)
     for at in range(count):
@@ -401,6 +395,12 @@
         which, place = divmod(at, share)
         packed = which or last
         outs[which][place] = pack_table(value, plan.chunk_rows) if packed else value
+
+
+def stack_kernel(*refs):
+    out = refs[-1]
+    for at in range(out.shape[0]):
+        out[at] = refs[at][0]
 
 
 def spread_kernel(plan, count, side, *refs):
@@ -495,125 +495,10 @@
     edges, wide = plan.edges, plan.bucket_edges
     grow = max(1, edges // 1024)
     buckets = plan.buckets
-    afar = lambda d: d ^ (plan.bucket_mask(d % plan.rels, 0) * plan.rels)
+    afar = lambda d: d ^ (plan.target_mask(d % plan.rels) * plan.rels)
     i16 = jnp.int16
 
-    first = send(own, plan, afar)
-    tables = [lhs_rows, lhs_rems, rel_ids, rhs_rows, rhs_rems, neg_rows, neg_rems]
-    labels = call(
-        functools.partial(lists_kernel, plan),
-        [shape((buckets * plan.maxb, 8, LANES), jnp.int32)] * plan.rels,
-        tables + [counts.reshape(-1)],
-        "lists",
-        1.0,
-        60,
-        in_specs=[VMEM] * 7 + [smem],
-    )
-    labels = [labels[0]] + [
-        send(labels[mask], plan, lambda d, m=mask: d ^ m) for mask in range(1, plan.rels)
-    ]
-    (vec,) = call(
-        functools.partial(relation_kernel, plan),
-        [shape((width, edges), F32)],
-        labels + [rels],
-        "relation",
-        6.0,
-        24 * grow,
-        scratch=[pltpu.VMEM((2 * width, plan.nrels), BF16)],
-    )
-    (first,) = call(
-        relay_kernel,
-        [shape((width, prows), BF16)],
-        [first, vec],
-        "relay",
-        0.1,
-        1,
-        in_specs=[ANY, ANY],
-        out_specs=[ANY],
-        input_output_aliases={0: 0},
-    )
-    targets = [first] + [
-        send(first, plan, lambda d, b=bucket: d ^ (b * plan.rels)) for bucket in range(1, buckets)
-    ]
-    lhs, cand_rem = call(
-        functools.partial(source_rows_kernel, plan),
-        [shape((width, edges), F32), shape((width, 2 * edges), BF16)],
-        labels + [own, rem, first],
-        "source_rows",
-        1.5,
-        12 * grow,
-        in_specs=[VMEM] * (len(labels) + 2) + [ANY],
-    )
-
-    grad_shapes = lambda count: [
-        shape((2 * width, count), BF16),
-        shape((2 * width, count), BF16),
-        shape((2 * width, 2 * count), BF16),
-    ]
-    grads = []
-    for bucket in range(buckets - 1):
-        grads += call(
-            functools.partial(bucket_kernel, plan, bucket),
-            grad_shapes(wide),
-            labels + [targets[bucket], lhs, vec, cand_rem],
-            "bucket",
-            5.0,
-            16 * grow,
-        )
-    last = buckets - 1
-    chunk = (plan.half_chunks, plan.chunk_rows, LANES)
-    bare = (plan.half_chunks, 8 * plan.chunk_units, LANES)
-    table = [pltpu.VMEM((width, plan.half_lanes), F32)]
-    made = call(
-        functools.partial(last_kernel, plan),
-        [shape(chunk, i16)] + grad_shapes(edges),
-        labels + grads + [targets[last], lhs, vec, cand_rem],
-        "last",
-        12.0,
-        24 * grow,
-        in_specs=[VMEM] * len(labels) + [ANY] * len(grads) + [VMEM] * 4,
-        out_specs=[VMEM] + [ANY] * 3,
-        scratch=[pltpu.VMEM(held.shape, BF16) for held in grad_shapes(edges)]
-        + table
-        + [pltpu.SemaphoreType.DMA((len(grads) + 3,))],
-    )
-    away, grads = made[0], list(made[1:])
-    core = send(away, plan, lambda d: d ^ 1)
-
-    near, packed = [], []
-    for bucket in range(1, buckets):
-        packed += call(
-            functools.partial(near_kernel, plan, bucket),
-            [shape((width + 16, prows), i16)],
-            labels + [grads[2], away],
-            "near",
-            1.5,
-            12 * grow,
-            in_specs=[VMEM] * (len(labels) + 1) + [ANY],
-        )
-        near.append(send(packed[-1], plan, lambda d, b=bucket: d ^ (b * plan.rels)))
-    (keep,) = call(
-        functools.partial(home_kernel, plan, len(packed) + 1),
-        [shape(bare, F32)],
-        labels + grads + packed + [away],
-        "home",
-        6.0,
-        16 * grow,
-        in_specs=[VMEM] * (len(labels) + 3) + [ANY] * (len(packed) + 1),
-        scratch=table,
-    )
-
-    def shares(count, size):
-        return [shape((count // size,) + bare[1:], F32)] + [
-            shape((count // size,) + chunk[1:], i16)
-        ] * (size - 1)
-
-    def exchanged(values, masks):
-        return [
-            send(value, plan, lambda d, m=mask: d ^ m) for value, mask in zip(values, masks[1:])
-        ]
-
-    def after(kernel, outs, args, others, name, cost, limit=12):
+    def after(kernel, outs, args, others, name, cost, limit=12, **more):
         return call(
             kernel,
             outs,
@@ -622,11 +507,118 @@
             cost,
             limit,
             in_specs=[VMEM] * len(args) + [ANY] * len(others),
-        )
+            **more,
+        )
+
+    target = send(own, plan, afar)
+    sources = [own] + [
+        send(own, plan, lambda d, b=bucket: d ^ (b * plan.rels)) for bucket in range(1, buckets)
+    ]
+    tables = [lhs_rows, lhs_rems, rel_ids, rhs_rows, rhs_rems, neg_rows, neg_rems]
+    labels = call(
+        functools.partial(lists_kernel, plan),
+        [shape((plan.maxb, 8, LANES), jnp.int32)] * (plan.rels * buckets),
+        tables + [counts.reshape(-1)],
+        "lists",
+        0.5,
+        60,
+        in_specs=[VMEM] * 7 + [smem],
+    )
+    labels = [labels[0]] + [
+        send(labels[mask], plan, lambda d, m=mask: d ^ m) for mask in range(1, len(labels))
+    ]
+    labels_of = lambda bucket: labels[bucket * plan.rels : (bucket + 1) * plan.rels]
+    (rel_split,) = call(
+        split_kernel, [shape((2 * width, plan.nrels), BF16)], [rels], "rel_split", 2.0, 50
+    )
+
+    grad_shapes = lambda count: [
+        shape((2 * width, count), BF16),
+        shape((2 * width, count), BF16),
+        shape((2 * width, 2 * count), BF16),
+    ]
+    inputs = []
+    for bucket in range(buckets):
+        (vec,) = call(
+            functools.partial(relation_kernel, plan),
+            [shape((width, wide), F32)],
+            labels_of(bucket) + [rel_split],
+            "relation",
+            2.0,
+            16 * grow,
+        )
+        lhs, cand_rem = call(
+            functools.partial(rows_kernel, plan),
+            [shape((width, wide), F32), shape((width, 2 * wide), BF16)],
+            labels_of(bucket) + [sources[bucket], rem],
+            "rows",
+            0.7,
+            12 * grow,
+        )
+        inputs.append([lhs, vec, cand_rem])
+    grads = []
+    for bucket in range(buckets - 1):
+        grads += call(
+            functools.partial(bucket_kernel, plan),
+            grad_shapes(wide),
+            labels_of(bucket) + [target] + inputs[bucket],
+            "bucket",
+            4.0,
+            16 * grow,
+        )
+    chunk = (plan.half_chunks, plan.chunk_rows, LANES)
+    bare = (plan.half_chunks, 8 * plan.chunk_units, LANES)
+    table = [pltpu.VMEM((width, plan.half_lanes), F32)]
+    made = call(
+        functools.partial(last_kernel, plan),
+        [shape(chunk, i16)] + grad_shapes(edges),
+        labels + grads + [target] + inputs[-1],
+        "last",
+        9.0,
+        24 * grow,
+        in_specs=[VMEM] * len(labels) + [ANY] * len(grads) + [VMEM] * 4,
+        out_specs=[VMEM] + [ANY] * 3,
+        scratch=[pltpu.VMEM(held.shape, BF16) for held in grad_shapes(edges)]
+        + table
+        + [pltpu.SemaphoreType.DMA((len(grads) + 3,))],
+    )
+    away, grads = made[0], list(made[1:])
+    core = send(away, plan, lambda d: d ^ 1)
+
+    (far,) = after(
+        functools.partial(target_kernel, plan),
+        [shape((width + 16, prows), i16)],
+        labels + [grads[2]],
+        [away],
+        "target",
+        1.8,
+        16 * grow,
+    )
+    (keep,) = after(
+        functools.partial(home_kernel, plan),
+        [shape(bare, F32)],
+        labels + grads,
+        [far],
+        "home",
+        4.0,
+        16 * grow,
+        scratch=table,
+    )
+    far = send(far, plan, afar)
+
+    def shares(count, size):
+        return [shape((count // size,) + bare[1:], F32)] + [
+            shape((count // size,) + chunk[1:], i16)
+        ] * (size - 1)
+
+    def exchanged(values, masks):
+        return [
+            send(value, plan, lambda d, m=mask: d ^ m) for value, mask in zip(values, masks[1:])
+        ]
 
     size, later = len(plan.masks[1]), len(plan.masks[2])
     made = call(
-        functools.partial(combine_kernel, plan, 2, False),
+        functools.partial(combine_kernel, plan, 2, False, 0),
         shares(chunk[0], size),
         [keep, core],
         "combine_cores",
@@ -634,57 +626,62 @@
         12,
     )
     keep, arrived = made[0], exchanged(made[1:], plan.masks[1])
-    (far,) = after(
-        functools.partial(far_kernel, plan),
-        [shape((width + 16, prows), i16)],
-        labels + [grads[2]] + near,
-        [keep],
-        "far",
-        2.0,
-        12 * grow,
-    )
-    (source,) = after(
-        functools.partial(source_kernel, plan),
-        [shape((width, prows), F32)],
-        labels + [grads[0]],
-        [far],
-        "source",
-        1.5,
-        12 * grow,
-    )
-    far = send(far, plan, afar)
+    lanes = plan.part_lanes
+    share_shapes = [shape((width, lanes), F32)] + [shape((width + 16, lanes), i16)] * (
+        plan.rels - 1
+    )
+    others = []
+    for bucket in range(1, buckets):
+        made = after(
+            functools.partial(source_kernel, plan, bucket),
+            share_shapes,
+            labels_of(bucket) + [grads[0]],
+            [keep],
+            "source",
+            1.0,
+        )
+        others.append([made[0]] + exchanged(made[1:], range(plan.rels)))
 
     made = after(
-        functools.partial(combine_kernel, plan, size, False),
+        functools.partial(combine_kernel, plan, size, False, len(others)),
         shares(chunk[0] // size, later),
         [keep] + arrived,
-        [],
+        [other[0] for other in others],
         "combine_xy",
         1.0,
     )
     keep, arrived = made[0], exchanged(made[1:], plan.masks[2])
-    lanes = plan.part_lanes
     made = after(
         functools.partial(share_kernel, plan),
-        [shape((width, lanes), F32)] + [shape((width + 16, lanes), i16)] * (plan.rels - 1),
-        [source, far],
+        share_shapes,
+        labels_of(0) + [grads[0], far],
         [keep],
         "share",
         1.0,
     )
     mine = [made[0]] + exchanged(made[1:], range(plan.rels))
+    for bucket in range(1, buckets):
+        (other,) = after(
+            functools.partial(add_kernel, plan.rels),
+            [shape((width + 16, lanes), i16)],
+            others[bucket - 1],
+            [made[0]],
+            "other",
+            0.3,
+        )
+        mine.append(send(other, plan, lambda d, b=bucket: d ^ (b * plan.rels)))
 
     (total,) = after(
-        functools.partial(combine_kernel, plan, later, True),
+        functools.partial(combine_kernel, plan, later, True, 1),
         [shape((1,) + chunk[1:], i16)],
         [keep] + arrived,
-        [],
+        [mine[0]],
         "combine_z",
         0.5,
     )
     pieces = [total] + exchanged([total] * (later - 1), plan.masks[2])
     (part,) = after(
-        functools.partial(mine_kernel, plan),
+        functools.partial(add_kernel, len(mine)),
         [shape((width + 16, lanes), i16)],
         mine,
         [total],
@@ -692,7 +689,14 @@
         0.5,
     )
     owners = [part] + exchanged([part] * (plan.rels - 1), range(plan.rels))
-    block = jnp.concatenate(pieces, axis=0)
+    (block,) = after(
+        stack_kernel,
+        [shape((len(pieces),) + chunk[1:], i16)],
+        pieces,
+        [part],
+        "stack",
+        0.3,
+    )
     pieces = [block] + exchanged([block] * (size - 1), plan.masks[1])
     (grad_partitions,) = after(
         functools.partial(part_out_kernel, plan),

time: 111 us -> 111 us (level)
  Pallas kernels: 33.5 us -> 36.9 us
  local copies, waits for them, and re-layouts: 2.87 us -> 0.03 us
  waiting for transfers between devices: 33.9 us -> 31.3 us
  starting transfers between devices: 39.7 us -> 41.8 us
    pallas_call x18 -> x21, Pallas kernels: 33.5 us -> 36.9 us  [call(): pl.pallas_call(kernel, out_shape=outs, compiler_params=pltpu.CompilerPara...]
    unnamed x10 -> x14, local copies, waits for them, and re-layouts: 2.87 us -> 0.03 us
    ppermute x30 -> x37, waiting for transfers between devices: 33.9 us -> 31.3 us  [send(): return lax.ppermute(value, ('dom', 'rel'), pairs)]
    ppermute x30 -> x37, starting transfers between devices: 39.7 us -> 41.8 us  [send(): return lax.ppermute(value, ('dom', 'rel'), pairs)]
  transfers between devices with their start and end apart: 30 -> 37, of which waited for: 10 -> 8; matrix products, arithmetic and copies ran while one was open for 0% -> 0% of each run, Pallas kernels for 19% -> 19%
where the time goes in v4:
time: 111 us
  starting transfers between devices  41.8 us (38%)
  Pallas kernels  36.9 us (33%)
  waiting for transfers between devices  31.3 us (28%)
    ppermute x37, starting transfers between devices, send(): return lax.ppermute(value, ('dom', 'rel'), pairs)  41.8 us
    pallas_call x21, Pallas kernels, call(): pl.pallas_call(kernel, out_shape=outs, compiler_params=pltpu.CompilerPara...  36.9 us
    ppermute x37, waiting for transfers between devices, send(): return lax.ppermute(value, ('dom', 'rel'), pairs)  31.3 us
  transfers between devices with their start and end apart: 37, of which 8 were waited for; matrix products, arithmetic and copies ran while one was open for 0% of the time, Pallas kernels for 19%

profile of v4, /device:TPU:0, one launch (start us, length us, event | category | flops | bytes accessed | tf_op | source)
XLA Modules:
  0.0 111.0 jit_solution(2270578419574925950)
XLA Ops:
  2.3 3.0 %collective-permute-start.8 = (bf16[400,512]{1,0:T(8,128)(2,1)}, bf16[400,512]{1,0:T(8,128)(2,1)S(1)}, u32[]{:S(2)}, u32[]{:S(2)}) collective-permute-start(bf16[400,512]{1,0:T(8,128)(2,1)} %bitcast.10), channel_id=1, source_target_pairs={{0,4},{1,5},{2,6},{3,7},{4,0},{5,1},{6,2},{7,3},{8,12},{9,13},{10,... | collective-permute-start | bytes 1228808 | tf_op jit(solution)/shard_map/ppermute | solution.py:174
  6.7 2.2 %collective-permute-start = (s32[1,8,128]{2,1,0:T(8,128)}, s32[1,8,128]{2,1,0:T(8,128)S(1)}, u32[]{:S(2)}, u32[]{:S(2)}) collective-permute-start(s32[1,8,128]{2,1,0:T(8,128)} %get-tuple-element.43), channel_id=1, source_target_pairs={{0,1},{1,0},{2,3},{3,2},{4,5},{5,4},{6,7},{7,6},{8,9},{9,8},{10,11... | collective-permute-start | bytes 12296 | tf_op jit(solution)/shard_map/ppermute | solution.py:174
  9.0 2.5 %collective-permute-start.1 = (s32[1,8,128]{2,1,0:T(8,128)}, s32[1,8,128]{2,1,0:T(8,128)S(1)}, u32[]{:S(2)}, u32[]{:S(2)}) collective-permute-start(s32[1,8,128]{2,1,0:T(8,128)} %get-tuple-element.44), channel_id=1, source_target_pairs={{0,2},{1,3},{2,0},{3,1},{4,6},{5,7},{6,4},{7,5},{8,10},{9,11},{10,... | collective-permute-start | bytes 12296 | tf_op jit(solution)/shard_map/ppermute | solution.py:174
  11.5 2.9 %rel_split.1.refs_4_ = bf16[800,2560]{1,0:T(8,128)(2,1)S(1)} custom-call(f32[400,2560]{1,0:T(8,128)} %bitcast.14), custom_call_target="tpu_custom_call" | custom-call | flops 2000000000 | bytes 6000000 | tf_op jit(solution)/shard_map/rel_split/pallas_call | solution.py:460
  16.0 2.0 %collective-permute-start.5 = (s32[1,8,128]{2,1,0:T(8,128)S(1)}, s32[1,8,128]{2,1,0:T(8,128)S(1)}, u32[]{:S(2)}, u32[]{:S(2)}) collective-permute-start(s32[1,8,128]{2,1,0:T(8,128)S(1)} %copy-done.4), channel_id=1, source_target_pairs={{0,6},{1,7},{2,4},{3,5},{4,2},{5,3},{6,0},{7,1},{8,14},{9,15},{10,... | collective-permute-start | bytes 12296 | tf_op jit(solution)/shard_map/ppermute | solution.py:174
  17.9 2.3 %relation.2.refs_6_ = f32[400,512]{1,0:T(8,128)S(1)} custom-call(s32[1,8,128]{2,1,0:T(8,128)S(1)} %copy-done.2, s32[1,8,128]{2,1,0:T(8,128)S(1)} %collective-permute-done.refs_1_, s32[1,8,128]{2,1,0:T(8,128)S(1)} %collective-permute-done.1.refs_2_, s32[1,8,128]{2,1,0:T(8,128)S(1)} %collective-permute-done.2.refs_3_, bf16[800,2560]{1,0:T(8,128)(2,1)S(1)} %rel_split.1.refs_4_), custom_call_target="tpu_custom_call" | custom-call | flops 2000000000 | bytes 6000000 | tf_op jit(solution)/shard_map/relation/pallas_call | solution.py:460
  22.0 2.2 %collective-permute-done.6.refs_3_.refs_7_ = s32[1,8,128]{2,1,0:T(8,128)S(1)} collective-permute-done((s32[1,8,128]{2,1,0:T(8,128)S(1)}, s32[1,8,128]{2,1,0:T(8,128)S(1)}, u32[]{:S(2)}, u32[]{:S(2)}) %collective-permute-start.6) | collective-permute-done | bytes 4128 | tf_op jit(solution)/shard_map/ppermute | solution.py:174
  24.2 2.3 %relation.3.refs_13_ = f32[400,512]{1,0:T(8,128)S(1)} custom-call(s32[1,8,128]{2,1,0:T(8,128)S(1)} %collective-permute-done.3.refs_0_.refs_4_, s32[1,8,128]{2,1,0:T(8,128)S(1)} %collective-permute-done.4.refs_1_.refs_5_, s32[1,8,128]{2,1,0:T(8,128)S(1)} %collective-permute-done.5.refs_2_.refs_6_, s32[1,8,128]{2,1,0:T(8,128)S(1)} %collective-permute-done.6.refs_3_.refs_7_, ...), custom_call_target="tpu_custom_call" | custom-call | flops 2000000000 | bytes 6000000 | tf_op jit(solution)/shard_map/relation/pallas_call | solution.py:460
  27.3 4.1 %bucket.1 = (bf16[800,512]{1,0:T(8,128)(2,1)S(1)}, bf16[800,512]{1,0:T(8,128)(2,1)S(1)}, bf16[800,1024]{1,0:T(8,128)(2,1)S(1)}) custom-call(s32[1,8,128]{2,1,0:T(8,128)S(1)} %copy-done.2, s32[1,8,128]{2,1,0:T(8,128)S(1)} %collective-permute-done.refs_1_, s32[1,8,128]{2,1,0:T(8,128)S(1)} %collective-permute-done.1.refs_2_, ...), custom_call_target="tpu_custom_call" | custom-call | flops 4000000000 | bytes 12000000 | tf_op jit(solution)/shard_map/bucket/pallas_call | solution.py:460
  31.4 9.6 %last.1 = (s16[16,288,128]{2,1,0:T(8,128)(2,1)S(1)}, bf16[800,1024]{1,0:T(8,128)(2,1)S(1)}, bf16[800,1024]{1,0:T(8,128)(2,1)S(1)}, bf16[800,2048]{1,0:T(8,128)(2,1)S(1)}) custom-call(s32[1,8,128]{2,1,0:T(8,128)S(1)} %copy-done.2, s32[1,8,128]{2,1,0:T(8,128)S(1)} %collective-permute-done.refs_1_, s32[1,8,128]{2,1,0:T(8,128)S(1)} %collective-permute-done.1.refs_2_, ...), custom_call_target="tpu_custom_call" | custom-call | flops 8999999488 | bytes 27000000 | tf_op jit(solution)/shard_map/last/pallas_call | solution.py:460
  41.1 2.0 %target.1.refs_11_ = s16[416,512]{1,0:T(8,128)(2,1)S(1)} custom-call(s32[1,8,128]{2,1,0:T(8,128)S(1)} %copy-done.2, s32[1,8,128]{2,1,0:T(8,128)S(1)} %collective-permute-done.refs_1_, s32[1,8,128]{2,1,0:T(8,128)S(1)} %collective-permute-done.1.refs_2_, s32[1,8,128]{2,1,0:T(8,128)S(1)} %collective-permute-done.2.refs_3_, ...), custom_call_target="tpu_custom_call" | custom-call | flops 1800000000 | bytes 5400000 | tf_op jit(solution)/shard_map/target/pallas_call | solution.py:460
  44.1 3.7 %home.1.refs_0_ = f32[16,280,128]{2,1,0:T(8,128)S(1)} custom-call(s32[1,8,128]{2,1,0:T(8,128)S(1)} %copy-done.2, s32[1,8,128]{2,1,0:T(8,128)S(1)} %collective-permute-done.refs_1_, s32[1,8,128]{2,1,0:T(8,128)S(1)} %collective-permute-done.1.refs_2_, s32[1,8,128]{2,1,0:T(8,128)S(1)} %collective-permute-done.2.refs_3_, ...), custom_call_target="tpu_custom_call" | custom-call | flops 4000000000 | bytes 12000000 | tf_op jit(solution)/shard_map/home/pallas_call | solution.py:460
  48.4 2.3 %collective-permute-start.11 = (s16[4,288,128]{2,1,0:T(8,128)(2,1)S(1)}, s16[4,288,128]{2,1,0:T(8,128)(2,1)S(1)}, u32[]{:S(2)}, u32[]{:S(2)}) collective-permute-start(s16[4,288,128]{2,1,0:T(8,128)(2,1)S(1)} %get-tuple-element.62), channel_id=1, source_target_pairs={{0,2},{1,3},{2,0},{3,1},{4,6},{5,7},{6,4},{7,5},{8,10},{9,11},{10,... | collective-permute-start | bytes 884744 | tf_op jit(solution)/shard_map/ppermute | solution.py:174
  54.6 3.5 %collective-permute-done.11.refs_1_ = s16[4,288,128]{2,1,0:T(8,128)(2,1)S(1)} collective-permute-done((s16[4,288,128]{2,1,0:T(8,128)(2,1)S(1)}, s16[4,288,128]{2,1,0:T(8,128)(2,1)S(1)}, u32[]{:S(2)}, u32[]{:S(2)}) %collective-permute-start.11) | collective-permute-done | bytes 294944 | tf_op jit(solution)/shard_map/ppermute | solution.py:174
  58.1 2.5 %collective-permute-start.18 = (s16[416,128]{1,0:T(8,128)(2,1)S(1)}, s16[416,128]{1,0:T(8,128)(2,1)S(1)}, u32[]{:S(2)}, u32[]{:S(2)}) collective-permute-start(s16[416,128]{1,0:T(8,128)(2,1)S(1)} %get-tuple-element.72), channel_id=1, source_target_pairs={{0,2},{1,3},{2,0},{3,1},{4,6},{5,7},{6,4},{7,5},{8,10},{9,11},{10,... | collective-permute-start | bytes 319496 | tf_op jit(solution)/shard_map/ppermute | solution.py:174
  60.6 5.0 %collective-permute-done.12.refs_2_ = s16[4,288,128]{2,1,0:T(8,128)(2,1)S(1)} collective-permute-done((s16[4,288,128]{2,1,0:T(8,128)(2,1)S(1)}, s16[4,288,128]{2,1,0:T(8,128)(2,1)S(1)}, u32[]{:S(2)}, u32[]{:S(2)}) %collective-permute-start.12) | collective-permute-done | bytes 294944 | tf_op jit(solution)/shard_map/ppermute | solution.py:174
  67.6 2.1 %collective-permute-start.22 = (s16[1,288,128]{2,1,0:T(8,128)(2,1)S(1)}, s16[1,288,128]{2,1,0:T(8,128)(2,1)S(1)}, u32[]{:S(2)}, u32[]{:S(2)}) collective-permute-start(s16[1,288,128]{2,1,0:T(8,128)(2,1)S(1)} %get-tuple-element.75), channel_id=1, source_target_pairs={{0,16},{1,17},{2,18},{3,19},{4,20},{5,21},{6,22},{7,23},{8,24},{9,... | collective-permute-start | bytes 221192 | tf_op jit(solution)/shard_map/ppermute | solution.py:174
  71.4 2.6 %collective-permute-start.20 = (s16[416,128]{1,0:T(8,128)(2,1)S(1)}, s16[416,128]{1,0:T(8,128)(2,1)S(1)}, u32[]{:S(2)}, u32[]{:S(2)}) collective-permute-start(s16[416,128]{1,0:T(8,128)(2,1)S(1)} %other.1), channel_id=1, source_target_pairs={{0,4},{1,5},{2,6},{3,7},{4,0},{5,1},{6,2},{7,3},{8,12},{9,13},{10,... | collective-permute-start | bytes 319496 | tf_op jit(solution)/shard_map/ppermute | solution.py:174
  79.1 2.2 %collective-permute-start.29 = (s16[1,288,128]{2,1,0:T(8,128)(2,1)S(1)}, s16[1,288,128]{2,1,0:T(8,128)(2,1)S(1)}, u32[]{:S(2)}, u32[]{:S(2)}) collective-permute-start(s16[1,288,128]{2,1,0:T(8,128)(2,1)S(1)} %combine_z.1.refs_5_.refs_0_), channel_id=1, source_target_pairs={{0,24},{1,25},{2,26},{3,27},{4,28},{5,29},{6,30},{7,31},{8,16},{9,... | collective-permute-start | bytes 221192 | tf_op jit(solution)/shard_map/ppermute | solution.py:174
  81.5 5.9 %collective-permute-done.28.refs_2_ = s16[1,288,128]{2,1,0:T(8,128)(2,1)S(1)} collective-permute-done((s16[1,288,128]{2,1,0:T(8,128)(2,1)S(1)}, s16[1,288,128]{2,1,0:T(8,128)(2,1)S(1)}, u32[]{:S(2)}, u32[]{:S(2)}) %collective-permute-start.28) | collective-permute-done | bytes 73760 | tf_op jit(solution)/shard_map/ppermute | solution.py:174
  88.2 2.1 %collective-permute-start.33 = (s16[4,288,128]{2,1,0:T(8,128)(2,1)S(1)}, s16[4,288,128]{2,1,0:T(8,128)(2,1)S(1)}, u32[]{:S(2)}, u32[]{:S(2)}) collective-permute-start(s16[4,288,128]{2,1,0:T(8,128)(2,1)S(1)} %stack.1.refs_4_.refs_0_), channel_id=1, source_target_pairs={{0,4},{1,5},{2,6},{3,7},{4,0},{5,1},{6,2},{7,3},{8,12},{9,13},{10,... | collective-permute-start | bytes 884744 | tf_op jit(solution)/shard_map/ppermute | solution.py:174
  92.9 12.6 %collective-permute-done.25.refs_2_ = s16[416,128]{1,0:T(8,128)(2,1)S(1)} collective-permute-done((s16[416,128]{1,0:T(8,128)(2,1)S(1)}, s16[416,128]{1,0:T(8,128)(2,1)S(1)}, u32[]{:S(2)}, u32[]{:S(2)}) %collective-permute-start.25) | collective-permute-done | bytes 106528 | tf_op jit(solution)/shard_map/ppermute | solution.py:174
  107.6 1.7 %spread.2 = (f32[400,2560]{1,0:T(8,128)}, f32[400,256]{1,0:T(8,128)}) custom-call(s32[1]{0:T(128)} %bitcast.6.side, s16[4,288,128]{2,1,0:T(8,128)(2,1)S(1)} %stack.1.refs_4_.refs_0_, s16[4,288,128]{2,1,0:T(8,128)(2,1)S(1)} %collective-permute-done.31.refs_1_, s16[4,288,128]{2,1,0:T(8,128)(2,1)S(1)} %collective-permute-done.33.refs_2_, ...), custom_call_target="tpu_custom_call" | custom-call | flops 2000000000 | bytes 6000000 | tf_op jit(solution)/shard_map/spread/pallas_call | solution.py:460
  109.3 1.7 %spread.3 = (f32[400,2560]{1,0:T(8,128)}, f32[400,256]{1,0:T(8,128)}) custom-call(s32[1]{0:T(128)} %bitcast.5.side, s16[4,288,128]{2,1,0:T(8,128)(2,1)S(1)} %collective-permute-done.30.refs_0_, s16[4,288,128]{2,1,0:T(8,128)(2,1)S(1)} %collective-permute-done.32.refs_1_, ...), custom_call_target="tpu_custom_call", output_to_operand_aliasing={{0}: (5, {}), {1}: (6, {})} | custom-call | flops 2000000000 | bytes 6000000 | tf_op jit(solution)/shard_map/spread/pallas_call | solution.py:460
  (85 shorter events, 27.1 us)
Async XLA Ops:
  0.6 26.6 %collective-permute-start.7 = (bf16[400,512]{1,0:T(8,128)(2,1)}, bf16[400,512]{1,0:T(8,128)(2,1)S(1)}, u32[]{:S(2)}, u32[]{:S(2)}) collective-permute-start(bf16[400,512]{1,0:T(8,128)(2,1)} %bitcast.9), channel_id=1, source_target_pairs={{0,0},{1,17},{2,10},{3,27},{4,4},{5,21},{6,14},{7,31},{8,8},{9,25}... | collective-permute-start | bytes 1228808 | tf_op jit(solution)/shard_map/ppermute | solution.py:174
  2.3 24.2 %collective-permute-start.8 = (bf16[400,512]{1,0:T(8,128)(2,1)}, bf16[400,512]{1,0:T(8,128)(2,1)S(1)}, u32[]{:S(2)}, u32[]{:S(2)}) collective-permute-start(bf16[400,512]{1,0:T(8,128)(2,1)} %bitcast.10), channel_id=1, source_target_pairs={{0,4},{1,5},{2,6},{3,7},{4,0},{5,1},{6,2},{7,3},{8,12},{9,13},{10,... | collective-permute-start | bytes 1228808 | tf_op jit(solution)/shard_map/ppermute | solution.py:174
  6.7 7.6 %collective-permute-start = (s32[1,8,128]{2,1,0:T(8,128)}, s32[1,8,128]{2,1,0:T(8,128)S(1)}, u32[]{:S(2)}, u32[]{:S(2)}) collective-permute-start(s32[1,8,128]{2,1,0:T(8,128)} %get-tuple-element.43), channel_id=1, source_target_pairs={{0,1},{1,0},{2,3},{3,2},{4,5},{5,4},{6,7},{7,6},{8,9},{9,8},{10,11... | collective-permute-start | bytes 12296 | tf_op jit(solution)/shard_map/ppermute | solution.py:174
  15.0 7.0 %collective-permute-start.4 = (s32[1,8,128]{2,1,0:T(8,128)S(1)}, s32[1,8,128]{2,1,0:T(8,128)S(1)}, u32[]{:S(2)}, u32[]{:S(2)}) collective-permute-start(s32[1,8,128]{2,1,0:T(8,128)S(1)} %copy-done.5), channel_id=1, source_target_pairs={{0,5},{1,4},{2,7},{3,6},{4,1},{5,0},{6,3},{7,2},{8,13},{9,12},{10,... | collective-permute-start | bytes 12296 | tf_op jit(solution)/shard_map/ppermute | solution.py:174
  16.0 6.0 %collective-permute-start.5 = (s32[1,8,128]{2,1,0:T(8,128)S(1)}, s32[1,8,128]{2,1,0:T(8,128)S(1)}, u32[]{:S(2)}, u32[]{:S(2)}) collective-permute-start(s32[1,8,128]{2,1,0:T(8,128)S(1)} %copy-done.4), channel_id=1, source_target_pairs={{0,6},{1,7},{2,4},{3,5},{4,2},{5,3},{6,0},{7,1},{8,14},{9,15},{10,... | collective-permute-start | bytes 12296 | tf_op jit(solution)/shard_map/ppermute | solution.py:174
  41.0 6.7 %collective-permute-start.10 = (s16[16,288,128]{2,1,0:T(8,128)(2,1)S(1)}, s16[16,288,128]{2,1,0:T(8,128)(2,1)S(1)}, u32[]{:S(2)}, u32[]{:S(2)}) collective-permute-start(s16[16,288,128]{2,1,0:T(8,128)(2,1)S(1)} %get-tuple-element.59.refs_9_), channel_id=1, source_target_pairs={{0,1},{1,0},{2,3},{3,2},{4,5},{5,4},{6,7},{7,6},{8,9},{9,8},{10,11... | collective-permute-start | bytes 3538952 | tf_op jit(solution)/shard_map/ppermute | solution.py:174
  43.2 24.4 %collective-permute-start.9 = (s16[416,512]{1,0:T(8,128)(2,1)S(1)}, s16[416,512]{1,0:T(8,128)(2,1)S(1)}, u32[]{:S(2)}, u32[]{:S(2)}) collective-permute-start(s16[416,512]{1,0:T(8,128)(2,1)S(1)} %target.1.refs_11_), channel_id=1, source_target_pairs={{0,0},{1,17},{2,10},{3,27},{4,4},{5,21},{6,14},{7,31},{8,8},{9,25}... | collective-permute-start | bytes 1277960 | tf_op jit(solution)/shard_map/ppermute | solution.py:174
  48.4 9.7 %collective-permute-start.11 = (s16[4,288,128]{2,1,0:T(8,128)(2,1)S(1)}, s16[4,288,128]{2,1,0:T(8,128)(2,1)S(1)}, u32[]{:S(2)}, u32[]{:S(2)}) collective-permute-start(s16[4,288,128]{2,1,0:T(8,128)(2,1)S(1)} %get-tuple-element.62), channel_id=1, source_target_pairs={{0,2},{1,3},{2,0},{3,1},{4,6},{5,7},{6,4},{7,5},{8,10},{9,11},{10,... | collective-permute-start | bytes 884744 | tf_op jit(solution)/shard_map/ppermute | solution.py:174
  50.7 14.8 %collective-permute-start.12 = (s16[4,288,128]{2,1,0:T(8,128)(2,1)S(1)}, s16[4,288,128]{2,1,0:T(8,128)(2,1)S(1)}, u32[]{:S(2)}, u32[]{:S(2)}) collective-permute-start(s16[4,288,128]{2,1,0:T(8,128)(2,1)S(1)} %get-tuple-element.63), channel_id=1, source_target_pairs={{0,4},{1,5},{2,6},{3,7},{4,0},{5,1},{6,2},{7,3},{8,12},{9,13},{10,... | collective-permute-start | bytes 884744 | tf_op jit(solution)/shard_map/ppermute | solution.py:174
  52.2 13.5 %collective-permute-start.13 = (s16[4,288,128]{2,1,0:T(8,128)(2,1)S(1)}, s16[4,288,128]{2,1,0:T(8,128)(2,1)S(1)}, u32[]{:S(2)}, u32[]{:S(2)}) collective-permute-start(s16[4,288,128]{2,1,0:T(8,128)(2,1)S(1)} %get-tuple-element.64), channel_id=1, source_target_pairs={{0,6},{1,7},{2,4},{3,5},{4,2},{5,3},{6,0},{7,1},{8,14},{9,15},{10,... | collective-permute-start | bytes 884744 | tf_op jit(solution)/shard_map/ppermute | solution.py:174
  53.0 17.5 %collective-permute-start.17 = (s16[416,128]{1,0:T(8,128)(2,1)S(1)}, s16[416,128]{1,0:T(8,128)(2,1)S(1)}, u32[]{:S(2)}, u32[]{:S(2)}) collective-permute-start(s16[416,128]{1,0:T(8,128)(2,1)S(1)} %get-tuple-element.71), channel_id=1, source_target_pairs={{0,1},{1,0},{2,3},{3,2},{4,5},{5,4},{6,7},{7,6},{8,9},{9,8},{10,11... | collective-permute-start | bytes 319496 | tf_op jit(solution)/shard_map/ppermute | solution.py:174
  58.1 13.2 %collective-permute-start.18 = (s16[416,128]{1,0:T(8,128)(2,1)S(1)}, s16[416,128]{1,0:T(8,128)(2,1)S(1)}, u32[]{:S(2)}, u32[]{:S(2)}) collective-permute-start(s16[416,128]{1,0:T(8,128)(2,1)S(1)} %get-tuple-element.72), channel_id=1, source_target_pairs={{0,2},{1,3},{2,0},{3,1},{4,6},{5,7},{6,4},{7,5},{8,10},{9,11},{10,... | collective-permute-start | bytes 319496 | tf_op jit(solution)/shard_map/ppermute | solution.py:174
  66.0 8.0 %collective-permute-start.21 = (s16[1,288,128]{2,1,0:T(8,128)(2,1)S(1)}, s16[1,288,128]{2,1,0:T(8,128)(2,1)S(1)}, u32[]{:S(2)}, u32[]{:S(2)}) collective-permute-start(s16[1,288,128]{2,1,0:T(8,128)(2,1)S(1)} %get-tuple-element.74), channel_id=1, source_target_pairs={{0,8},{1,9},{2,10},{3,11},{4,12},{5,13},{6,14},{7,15},{8,0},{9,1},... | collective-permute-start | bytes 221192 | tf_op jit(solution)/shard_map/ppermute | solution.py:174
  67.6 8.2 %collective-permute-start.22 = (s16[1,288,128]{2,1,0:T(8,128)(2,1)S(1)}, s16[1,288,128]{2,1,0:T(8,128)(2,1)S(1)}, u32[]{:S(2)}, u32[]{:S(2)}) collective-permute-start(s16[1,288,128]{2,1,0:T(8,128)(2,1)S(1)} %get-tuple-element.75), channel_id=1, source_target_pairs={{0,16},{1,17},{2,18},{3,19},{4,20},{5,21},{6,22},{7,23},{8,24},{9,... | collective-permute-start | bytes 221192 | tf_op jit(solution)/shard_map/ppermute | solution.py:174
  70.4 6.3 %collective-permute-start.23 = (s16[1,288,128]{2,1,0:T(8,128)(2,1)S(1)}, s16[1,288,128]{2,1,0:T(8,128)(2,1)S(1)}, u32[]{:S(2)}, u32[]{:S(2)}) collective-permute-start(s16[1,288,128]{2,1,0:T(8,128)(2,1)S(1)} %get-tuple-element.76), channel_id=1, source_target_pairs={{0,24},{1,25},{2,26},{3,27},{4,28},{5,29},{6,30},{7,31},{8,16},{9,... | collective-permute-start | bytes 221192 | tf_op jit(solution)/shard_map/ppermute | solution.py:174
  71.4 6.8 %collective-permute-start.20 = (s16[416,128]{1,0:T(8,128)(2,1)S(1)}, s16[416,128]{1,0:T(8,128)(2,1)S(1)}, u32[]{:S(2)}, u32[]{:S(2)}) collective-permute-start(s16[416,128]{1,0:T(8,128)(2,1)S(1)} %other.1), channel_id=1, source_target_pairs={{0,4},{1,5},{2,6},{3,7},{4,0},{5,1},{6,2},{7,3},{8,12},{9,13},{10,... | collective-permute-start | bytes 319496 | tf_op jit(solution)/shard_map/ppermute | solution.py:174
  74.1 7.3 %collective-permute-start.15 = (s16[416,128]{1,0:T(8,128)(2,1)S(1)}, s16[416,128]{1,0:T(8,128)(2,1)S(1)}, u32[]{:S(2)}, u32[]{:S(2)}) collective-permute-start(s16[416,128]{1,0:T(8,128)(2,1)S(1)} %get-tuple-element.69), channel_id=1, source_target_pairs={{0,2},{1,3},{2,0},{3,1},{4,6},{5,7},{6,4},{7,5},{8,10},{9,11},{10,... | collective-permute-start | bytes 319496 | tf_op jit(solution)/shard_map/ppermute | solution.py:174
  78.3 9.1 %collective-permute-start.28 = (s16[1,288,128]{2,1,0:T(8,128)(2,1)S(1)}, s16[1,288,128]{2,1,0:T(8,128)(2,1)S(1)}, u32[]{:S(2)}, u32[]{:S(2)}) collective-permute-start(s16[1,288,128]{2,1,0:T(8,128)(2,1)S(1)} %combine_z.1.refs_5_.refs_0_), channel_id=1, source_target_pairs={{0,16},{1,17},{2,18},{3,19},{4,20},{5,21},{6,22},{7,23},{8,24},{9,... | collective-permute-start | bytes 221192 | tf_op jit(solution)/shard_map/ppermute | solution.py:174
  79.1 8.3 %collective-permute-start.29 = (s16[1,288,128]{2,1,0:T(8,128)(2,1)S(1)}, s16[1,288,128]{2,1,0:T(8,128)(2,1)S(1)}, u32[]{:S(2)}, u32[]{:S(2)}) collective-permute-start(s16[1,288,128]{2,1,0:T(8,128)(2,1)S(1)} %combine_z.1.refs_5_.refs_0_), channel_id=1, source_target_pairs={{0,24},{1,25},{2,26},{3,27},{4,28},{5,29},{6,30},{7,31},{8,16},{9,... | collective-permute-start | bytes 221192 | tf_op jit(solution)/shard_map/ppermute | solution.py:174
  87.4 18.1 %collective-permute-start.31 = (s16[4,288,128]{2,1,0:T(8,128)(2,1)S(1)}, s16[4,288,128]{2,1,0:T(8,128)(2,1)S(1)}, u32[]{:S(2)}, u32[]{:S(2)}) collective-permute-start(s16[4,288,128]{2,1,0:T(8,128)(2,1)S(1)} %stack.1.refs_4_.refs_0_), channel_id=1, source_target_pairs={{0,2},{1,3},{2,0},{3,1},{4,6},{5,7},{6,4},{7,5},{8,10},{9,11},{10,... | collective-permute-start | bytes 884744 | tf_op jit(solution)/shard_map/ppermute | solution.py:174
  88.2 17.8 %collective-permute-start.33 = (s16[4,288,128]{2,1,0:T(8,128)(2,1)S(1)}, s16[4,288,128]{2,1,0:T(8,128)(2,1)S(1)}, u32[]{:S(2)}, u32[]{:S(2)}) collective-permute-start(s16[4,288,128]{2,1,0:T(8,128)(2,1)S(1)} %stack.1.refs_4_.refs_0_), channel_id=1, source_target_pairs={{0,4},{1,5},{2,6},{3,7},{4,0},{5,1},{6,2},{7,3},{8,12},{9,13},{10,... | collective-permute-start | bytes 884744 | tf_op jit(solution)/shard_map/ppermute | solution.py:174
  90.3 15.8 %collective-permute-start.35 = (s16[4,288,128]{2,1,0:T(8,128)(2,1)S(1)}, s16[4,288,128]{2,1,0:T(8,128)(2,1)S(1)}, u32[]{:S(2)}, u32[]{:S(2)}) collective-permute-start(s16[4,288,128]{2,1,0:T(8,128)(2,1)S(1)} %stack.1.refs_4_.refs_0_), channel_id=1, source_target_pairs={{0,6},{1,7},{2,4},{3,5},{4,2},{5,3},{6,0},{7,1},{8,14},{9,15},{10,... | collective-permute-start | bytes 884744 | tf_op jit(solution)/shard_map/ppermute | solution.py:174
  91.0 14.5 %collective-permute-start.25 = (s16[416,128]{1,0:T(8,128)(2,1)S(1)}, s16[416,128]{1,0:T(8,128)(2,1)S(1)}, u32[]{:S(2)}, u32[]{:S(2)}) collective-permute-start(s16[416,128]{1,0:T(8,128)(2,1)S(1)} %mine.1.refs_4_.refs_0_), channel_id=1, source_target_pairs={{0,2},{1,3},{2,0},{3,1},{4,6},{5,7},{6,4},{7,5},{8,10},{9,11},{10,... | collective-permute-start | bytes 319496 | tf_op jit(solution)/shard_map/ppermute | solution.py:174
  92.3 14.2 %collective-permute-start.26 = (s16[416,128]{1,0:T(8,128)(2,1)S(1)}, s16[416,128]{1,0:T(8,128)(2,1)S(1)}, u32[]{:S(2)}, u32[]{:S(2)}) collective-permute-start(s16[416,128]{1,0:T(8,128)(2,1)S(1)} %mine.1.refs_4_.refs_0_), channel_id=1, source_target_pairs={{0,3},{1,2},{2,1},{3,0},{4,7},{5,6},{6,5},{7,4},{8,11},{9,10},{10,... | collective-permute-start | bytes 319496 | tf_op jit(solution)/shard_map/ppermute | solution.py:174
  (20 other events, 82.7 us)

commit v5 on v4

--- a/solution.py
+++ b/solution.py
@@ -93,6 +93,37 @@
     depth = depth or words.shape[0] - 16
     value = from_words(words)
     return value[:depth] * scale_of(value[depth : depth + 1])
+
+
+class Part:
+    def __init__(self, plan, units, groups):
+        self.units = units
+        self.rows = (units + 2) // 2 * 16
+        self.masks = [self.group_masks(bits) for bits in groups]
+        order = [bit for group in groups for bit in reversed(group)]
+        self.place = {bit: len(order) - 1 - at for at, bit in enumerate(order)}
+        self.packed = (plan.half_chunks, self.rows, LANES)
+        self.bare = (plan.half_chunks, 8 * units, LANES)
+
+    @staticmethod
+    def group_masks(bits):
+        masks = []
+        for index in range(2 ** len(bits)):
+            masks.append(sum(((index >> at) & 1) << bit for at, bit in enumerate(bits)))
+        return masks
+
+    def position(self, chunk, me):
+        relative = chunk ^ (me >> 1)
+        out = 0
+        for bit, at in self.place.items():
+            out = out + (((relative >> (bit - 1)) & 1) << at)
+        return out
+
+    def shares(self, count, size):
+        count = count // size
+        return [shape((count,) + self.bare[1:], F32)] + [
+            shape((count,) + self.packed[1:], jnp.int16)
+        ] * (size - 1)
 
 
 class Plan:
@@ -111,31 +142,24 @@
         self.units = (self.half_lanes // LANES) * self.subs
         self.half_chunks = self.devices // 2
         self.chunk_units = -(-self.units // self.half_chunks)
-        self.chunk_rows = (self.chunk_units + 2) // 2 * 16
         rel_bits = bits_of(rels)
         all_bits = rel_bits + bits_of(doms)
-        self.groups = [
-            [0],
-            list(range(1, rel_bits + 1)),
-            list(range(rel_bits + 1, all_bits)),
-        ]
-        self.masks = [self.group_masks(bits) for bits in self.groups]
-        order = [bit for group in self.groups for bit in reversed(group)]
-        self.place = {bit: all_bits - 1 - at for at, bit in enumerate(order)}
-
-    @staticmethod
-    def group_masks(bits):
-        masks = []
-        for index in range(2 ** len(bits)):
-            masks.append(sum(((index >> at) & 1) << bit for at, bit in enumerate(bits)))
-        return masks
+        near = list(range(1, rel_bits + 1))
+        far = list(range(rel_bits + 1, all_bits))
+        self.parts = [Part(self, self.chunk_units, [near, far])]
+
+    def chunk_blocks(self, chunk, part):
+        first = chunk * self.chunk_units + (self.parts[0].units if part else 0)
+        blocks = []
+        for unit in range(first, first + self.parts[part].units):
+            lane, sub = divmod(unit, self.subs)
+            blocks.append((lane * LANES, 8 * sub) if unit < self.units else None)
+        return blocks
 
     def row(self, labels, bucket, kinds, first, count):
         rows = []
         for slot in range(first, first + count):
-            mask, turn = divmod(slot, self.maxb)
-            block = labels[bucket * self.rels + mask]
-            rows += [block[turn, kind : kind + 1, :] for kind in kinds]
+            rows += [labels[bucket][slot, kind : kind + 1, :] for kind in kinds]
         return jnp.concatenate(rows, axis=1) if len(rows) > 1 else rows[0]
 
     def whole_row(self, labels, kinds):
@@ -146,17 +170,6 @@
 
     def me(self):
         return lax.axis_index("dom") * self.rels + lax.axis_index("rel")
-
-    def low_chunk(self, device):
-        return device >> 1
-
-    def position(self, chunk, me):
-        relative = chunk ^ (me >> 1)
-        out = 0
-        for bit, at in self.place.items():
-            if bit:
-                out = out + (((relative >> (bit - 1)) & 1) << at)
-        return out
 
     def target_mask(self, rel):
         return reverse_bits(rel, self.rels) * self.buckets
@@ -178,15 +191,24 @@
     tables, counts, outs = refs[:7], refs[7], refs[8:]
     source = lax.axis_index("dom")
     rel = lax.axis_index("rel")
-    for at, out in enumerate(outs):
-        bucket, mask = divmod(at, plan.rels)
-        target = source ^ bucket ^ plan.dynamic_mask(rel ^ mask)
-        stop = lax.rem(source - target + plan.doms, plan.doms)
-        for turn in range(plan.maxb):
-            for kind, table in enumerate(tables):
-                out[turn, kind : kind + 1, :] = table[0, stop, turn : turn + 1, :]
-            live = jnp.where(turn < counts[stop], 1, 0)
-            out[turn, 7:8, :] = jnp.full((1, LANES), live, jnp.int32)
+    for mask, out in enumerate(outs):
+        for bucket in range(plan.buckets):
+            target = source ^ bucket ^ plan.dynamic_mask(rel ^ mask)
+            stop = lax.rem(source - target + plan.doms, plan.doms)
+            for turn in range(plan.maxb):
+                at = bucket * plan.maxb + turn
+                for kind, table in enumerate(tables):
+                    out[at, kind : kind + 1, :] = table[0, stop, turn : turn + 1, :]
+                live = jnp.where(turn < counts[stop], 1, 0)
+                out[at, 7:8, :] = jnp.full((1, LANES), live, jnp.int32)
+
+
+def forward_kernel(plan, *refs):
+    lists, outs = refs[: plan.rels], refs[plan.rels :]
+    for bucket, out in enumerate(outs):
+        for mask, ref in enumerate(lists):
+            for turn in range(plan.maxb):
+                out[mask * plan.maxb + turn] = ref[bucket * plan.maxb + turn]
 
 
 def split_kernel(relations, out):
@@ -197,8 +219,7 @@
 
 
 def relation_kernel(plan, *refs):
-    labels = refs[: plan.rels]
-    relations, out = refs[plan.rels], refs[-1]
+    labels, relations, out = refs[:1], refs[1], refs[-1]
     for pair in range(0, plan.slots, 2):
         count = min(2, plan.slots - pair)
         start = pair * LANES
@@ -209,8 +230,7 @@
 
 
 def rows_kernel(plan, *refs):
-    labels = refs[: plan.rels]
-    own, rem = refs[plan.rels : plan.rels + 2]
+    labels, (own, rem) = refs[:1], refs[1:3]
     lhs_out, rem_out = refs[-2:]
     for pair in range(0, plan.slots, 2):
         count = min(2, plan.slots - pair)
@@ -275,16 +295,17 @@
 
 
 def bucket_kernel(plan, *refs):
-    bucket_grads(plan, refs[: plan.rels], *refs[plan.rels :], 0)
+    bucket_grads(plan, refs[:1], *refs[1:], 0)
 
 
 def last_kernel(plan, *refs):
-    count = plan.rels * plan.buckets
+    count = plan.buckets
     labels = refs[:count]
     before = refs[count : count + 3 * (plan.buckets - 1)]
     refs = refs[count + 3 * (plan.buckets - 1) :]
     target, lhs_in, rel_in, rem_in = refs[:4]
-    away, outs, helds, table, sems = refs[4], refs[5:8], refs[8:11], refs[11], refs[12]
+    away, refs = refs[4 : 4 + len(plan.parts)], refs[4 + len(plan.parts) :]
+    outs, helds, table, sems = refs[:3], refs[3:6], refs[6], refs[7]
     edges = plan.bucket_edges
     loads = []
     for at, ref in enumerate(before):
@@ -295,7 +316,7 @@
         )
         loads[-1].start()
     base = (plan.buckets - 1) * plan.slots
-    own_labels = labels[count - plan.rels :]
+    own_labels = labels[-1:]
     bucket_grads(plan, own_labels, target, lhs_in, rel_in, rem_in, *helds, base)
     for load in loads:
         load.wait()
@@ -310,7 +331,7 @@
         store.wait()
 
 
-def reduce_half(plan, away, labels, grads, table, out):
+def reduce_half(plan, away, labels, grads, table, outs):
     lhs_grads, rel_grads, cand_grads = grads
     me = plan.me()
     half = (me & 1) ^ (1 if away else 0)
@@ -326,15 +347,17 @@
         dot(lhs_grads[...], first, NT) + dot(cand_grads[...], second, NT)
     )
     for chunk in range(plan.half_chunks):
-        parts = []
-        for unit in range(chunk * plan.chunk_units, (chunk + 1) * plan.chunk_units):
-            if unit < plan.units:
-                lane, sub = divmod(unit, plan.subs)
-                parts.append(table[8 * sub : 8 * sub + 8, lane * LANES : (lane + 1) * LANES])
-            else:
-                parts.append(jnp.zeros((8, LANES), F32))
-        value = jnp.concatenate(parts, axis=0)
-        out[plan.position(chunk, me)] = pack_table(value, plan.chunk_rows) if away else value
+        for which, (part, out) in enumerate(zip(plan.parts, outs)):
+            value = jnp.concatenate(
+                [
+                    table[block[1] : block[1] + 8, block[0] : block[0] + LANES]
+                    if block
+                    else jnp.zeros((8, LANES), F32)
+                    for block in plan.chunk_blocks(chunk, which)
+                ],
+                axis=0,
+            )
+            out[part.position(chunk, me)] = pack_table(value, part.rows) if away else value
 
 
 def rows_sum(plan, ids, grads):
@@ -343,15 +366,14 @@
 
 
 def target_kernel(plan, *refs):
-    count = plan.rels * plan.buckets
+    count = plan.buckets
     ids = plan.whole_row(refs[:count], (3, 5))
     refs[-1][...] = pack_table(rows_sum(plan, ids, refs[count][...]))
 
 
 def home_kernel(plan, *refs):
-    count = plan.rels * plan.buckets
-    keep, table = refs[-2:]
-    reduce_half(plan, False, refs[:count], refs[count : count + 3], table, keep)
+    count = plan.buckets
+    reduce_half(plan, False, refs[:count], refs[count : count + 3], refs[-1], refs[-1 - len(plan.parts) : -1])
 
 
 def source_sum(plan, labels, grads, bucket):
@@ -368,13 +390,13 @@
 
 
 def source_kernel(plan, bucket, *refs):
-    value = source_sum(plan, refs[: plan.rels], refs[plan.rels], bucket)
+    value = source_sum(plan, refs[:1], refs[1], bucket)
     to_shares(plan, value, refs[-plan.rels :])
 
 
 def share_kernel(plan, *refs):
-    value = source_sum(plan, refs[: plan.rels], refs[plan.rels], 0)
-    to_shares(plan, value + unpack_table(refs[plan.rels + 1][...]), refs[-plan.rels :])
+    value = source_sum(plan, refs[:1], refs[1], 0)
+    to_shares(plan, value + unpack_table(refs[2][...]), refs[-plan.rels :])
 
 
 def add_kernel(count, *refs):
@@ -384,51 +406,60 @@
     refs[-1][...] = pack_table(value)
 
 
-def combine_kernel(plan, group, last, after, *refs):
-    keep, arrived, outs = refs[0], refs[1:group], refs[group + after :]
-    count, depth = keep.shape[0], keep.shape[1]
-    share = count // len(outs)
-    for at in range(count):
-        value = keep[at]
-        for ref in arrived:
-            value = value + unpack_table(ref[at], depth)
-        which, place = divmod(at, share)
-        packed = which or last
-        outs[which][place] = pack_table(value, plan.chunk_rows) if packed else value
-
-
-def stack_kernel(*refs):
-    out = refs[-1]
-    for at in range(out.shape[0]):
-        out[at] = refs[at][0]
-
-
-def spread_kernel(plan, count, side, *refs):
-    pieces, (rel_out, rem_out, held) = refs[:count], refs[-3:]
-    at = 0
-    for piece in pieces:
-        held[at : at + piece.shape[0]] = piece[...]
-        at += piece.shape[0]
+def combine_kernel(plan, arrivals, sizes, after, *refs):
+    at, out_at = 0, sum(arrivals) + len(arrivals) + after
+    for part, count, size in zip(plan.parts, arrivals, sizes):
+        keep, arrived = refs[at], refs[at + 1 : at + 1 + count]
+        outs = refs[out_at : out_at + size]
+        at, out_at = at + 1 + count, out_at + size
+        share = keep.shape[0] // size
+        for place in range(keep.shape[0]):
+            value = keep[place]
+            for ref in arrived:
+                value = value + unpack_table(ref[place], 8 * part.units)
+            which, inner = divmod(place, share)
+            packed = which or size == 1
+            outs[which][inner] = pack_table(value, part.rows) if packed else value
+
+
+def stack_kernel(plan, counts, *refs):
+    outs = refs[-len(counts) :]
+    first = 0
+    for count, out in zip(counts, outs):
+        for at in range(count):
+            out[at] = refs[first + at][0]
+        first += count
+
+
+def spread_kernel(plan, counts, side, *refs):
+    helds = refs[len(refs) - len(counts) :]
+    rel_out, rem_out = refs[-2 - len(counts) : len(refs) - len(counts)]
     me = plan.me()
+    first = 0
+    for count, held in zip(counts, helds):
+        at = 0
+        for piece in refs[first : first + count]:
+            held[at : at + piece.shape[0]] = piece[...]
+            at += piece.shape[0]
+        first += count
     for chunk in range(plan.half_chunks):
-        value = unpack_table(held[plan.position(chunk, me)], 8 * plan.chunk_units)
-        for index in range(plan.chunk_units):
-            unit = chunk * plan.chunk_units + index
-            if unit >= plan.units:
-                break
-            lane, sub = divmod(unit, plan.subs)
-            lane = lane * LANES
-            rows = slice(8 * sub, 8 * sub + 8)
-            block = value[8 * index : 8 * index + 8]
-            if lane < plan.half_rel:
-                rel_out[rows, lane : lane + LANES] = block
-            else:
-                lane -= plan.half_rel
-                rem_out[rows, lane : lane + LANES] = block
-
-
-def relay_kernel(*refs):
-    pass
+        for which, (part, held) in enumerate(zip(plan.parts, helds)):
+            value = unpack_table(held[part.position(chunk, me)], 8 * part.units)
+            for index, block in enumerate(plan.chunk_blocks(chunk, which)):
+                if block is None:
+                    break
+                lane, sub = block
+                rows = slice(sub, sub + 8)
+                piece = value[8 * index : 8 * index + 8]
+                if lane < plan.half_rel:
+                    rel_out[rows, lane : lane + LANES] = piece
+                else:
+                    lane -= plan.half_rel
+                    rem_out[rows, lane : lane + LANES] = piece
+
+
+def copy_kernel(*refs):
+    refs[-1][...] = refs[0][...]
 
 
 def part_out_kernel(plan, *refs):
@@ -498,6 +529,11 @@
     afar = lambda d: d ^ (plan.target_mask(d % plan.rels) * plan.rels)
     i16 = jnp.int16
 
+    def exchanged(values, masks):
+        return [
+            send(value, plan, lambda d, m=mask: d ^ m) for value, mask in zip(values, masks[1:])
+        ]
+
     def after(kernel, outs, args, others, name, cost, limit=12, **more):
         return call(
             kernel,
@@ -510,24 +546,37 @@
             **more,
         )
 
-    target = send(own, plan, afar)
-    sources = [own] + [
-        send(own, plan, lambda d, b=bucket: d ^ (b * plan.rels)) for bucket in range(1, buckets)
-    ]
     tables = [lhs_rows, lhs_rems, rel_ids, rhs_rows, rhs_rems, neg_rows, neg_rems]
-    labels = call(
+    lists = call(
         functools.partial(lists_kernel, plan),
-        [shape((plan.maxb, 8, LANES), jnp.int32)] * (plan.rels * buckets),
+        [shape((buckets * plan.maxb, 8, LANES), jnp.int32)] * plan.rels,
         tables + [counts.reshape(-1)],
         "lists",
         0.5,
         60,
         in_specs=[VMEM] * 7 + [smem],
     )
+    lists = [lists[0]] + exchanged(lists[1:], range(plan.rels))
+    (own,) = after(
+        copy_kernel, [shape(own.shape, own.dtype)], [own], lists[1:], "own", 0.3, 4
+    )
+    target = send(own, plan, afar)
+    sources = [own] + [
+        send(own, plan, lambda d, b=bucket: d ^ (b * plan.rels)) for bucket in range(1, buckets)
+    ]
+    labels = call(
+        functools.partial(forward_kernel, plan),
+        [shape((plan.slots, 8, LANES), jnp.int32)] * buckets,
+        lists,
+        "forward",
+        0.2,
+        8,
+    )
     labels = [labels[0]] + [
-        send(labels[mask], plan, lambda d, m=mask: d ^ m) for mask in range(1, len(labels))
+        send(labels[bucket], plan, lambda d, b=bucket: d ^ (b * plan.rels))
+        for bucket in range(1, buckets)
     ]
-    labels_of = lambda bucket: labels[bucket * plan.rels : (bucket + 1) * plan.rels]
+    labels_of = lambda bucket: [labels[bucket]]
     (rel_split,) = call(
         split_kernel, [shape((2 * width, plan.nrels), BF16)], [rels], "rel_split", 2.0, 50
     )
@@ -566,37 +615,51 @@
             4.0,
             16 * grow,
         )
-    chunk = (plan.half_chunks, plan.chunk_rows, LANES)
-    bare = (plan.half_chunks, 8 * plan.chunk_units, LANES)
     table = [pltpu.VMEM((width, plan.half_lanes), F32)]
     made = call(
         functools.partial(last_kernel, plan),
-        [shape(chunk, i16)] + grad_shapes(edges),
+        [shape(part.packed, i16) for part in plan.parts] + grad_shapes(edges),
         labels + grads + [target] + inputs[-1],
         "last",
         9.0,
         24 * grow,
         in_specs=[VMEM] * len(labels) + [ANY] * len(grads) + [VMEM] * 4,
-        out_specs=[VMEM] + [ANY] * 3,
+        out_specs=[VMEM] * len(plan.parts) + [ANY] * 3,
         scratch=[pltpu.VMEM(held.shape, BF16) for held in grad_shapes(edges)]
         + table
         + [pltpu.SemaphoreType.DMA((len(grads) + 3,))],
     )
-    away, grads = made[0], list(made[1:])
-    core = send(away, plan, lambda d: d ^ 1)
-
+    away, grads = made[: len(plan.parts)], list(made[len(plan.parts) :])
+    cores = [send(value, plan, lambda d: d ^ 1) for value in away]
+
+    lanes = plan.part_lanes
+    share_shapes = [shape((width, lanes), F32)] + [shape((width + 16, lanes), i16)] * (
+        plan.rels - 1
+    )
+    others, order = [], away[0]
+    for bucket in range(1, buckets):
+        made = after(
+            functools.partial(source_kernel, plan, bucket),
+            share_shapes,
+            labels_of(bucket) + [grads[0]],
+            [order],
+            "source",
+            0.8,
+        )
+        others.append([made[0]] + exchanged(made[1:], range(plan.rels)))
+        order = made[0]
     (far,) = after(
         functools.partial(target_kernel, plan),
         [shape((width + 16, prows), i16)],
         labels + [grads[2]],
-        [away],
+        [order],
         "target",
         1.8,
         16 * grow,
     )
-    (keep,) = after(
+    keeps = after(
         functools.partial(home_kernel, plan),
-        [shape(bare, F32)],
+        [shape(part.bare, F32) for part in plan.parts],
         labels + grads,
         [far],
         "home",
@@ -606,133 +669,122 @@
     )
     far = send(far, plan, afar)
 
-    def shares(count, size):
-        return [shape((count // size,) + bare[1:], F32)] + [
-            shape((count // size,) + chunk[1:], i16)
-        ] * (size - 1)
-
-    def exchanged(values, masks):
-        return [
-            send(value, plan, lambda d, m=mask: d ^ m) for value, mask in zip(values, masks[1:])
-        ]
-
-    size, later = len(plan.masks[1]), len(plan.masks[2])
-    made = call(
-        functools.partial(combine_kernel, plan, 2, False, 0),
-        shares(chunk[0], size),
-        [keep, core],
-        "combine_cores",
-        1.0,
-        12,
-    )
-    keep, arrived = made[0], exchanged(made[1:], plan.masks[1])
-    lanes = plan.part_lanes
-    share_shapes = [shape((width, lanes), F32)] + [shape((width + 16, lanes), i16)] * (
-        plan.rels - 1
-    )
-    others = []
+    def combine(keeps, arrived, order, level, name):
+        sizes = [len(part.masks[level]) if level < 2 else 1 for part in plan.parts]
+        outs, args = [], []
+        for part, keep, pieces, size in zip(plan.parts, keeps, arrived, sizes):
+            args += [keep] + pieces
+            if level < 2:
+                outs += part.shares(keep.shape[0], size)
+            else:
+                outs.append(shape((1,) + part.packed[1:], i16))
+        made = after(
+            functools.partial(
+                combine_kernel, plan, [len(pieces) for pieces in arrived], sizes, len(order)
+            ),
+            outs,
+            args,
+            order,
+            name,
+            0.5,
+        )
+        if level == 2:
+            return made, []
+        keeps, arrived = [], []
+        for part, size in zip(plan.parts, sizes):
+            group, made = made[:size], made[size:]
+            keeps.append(group[0])
+            arrived.append(exchanged(group[1:], part.masks[level]))
+        return keeps, arrived
+
+    order, crossing = keeps[0], []
     for bucket in range(1, buckets):
-        made = after(
-            functools.partial(source_kernel, plan, bucket),
-            share_shapes,
-            labels_of(bucket) + [grads[0]],
-            [keep],
-            "source",
-            1.0,
-        )
-        others.append([made[0]] + exchanged(made[1:], range(plan.rels)))
-
-    made = after(
-        functools.partial(combine_kernel, plan, size, False, len(others)),
-        shares(chunk[0] // size, later),
-        [keep] + arrived,
-        [other[0] for other in others],
-        "combine_xy",
-        1.0,
-    )
-    keep, arrived = made[0], exchanged(made[1:], plan.masks[2])
+        (order,) = after(
+            functools.partial(add_kernel, plan.rels),
+            [shape((width + 16, lanes), i16)],
+            others[bucket - 1],
+            [order],
+            "other",
+            0.3,
+        )
+        crossing.append(send(order, plan, lambda d, b=bucket: d ^ (b * plan.rels)))
+    keeps, arrived = combine(keeps, [[core] for core in cores], [order], 0, "combine_cores")
+    keeps, arrived = combine(keeps, arrived, [], 1, "combine_first")
     made = after(
         functools.partial(share_kernel, plan),
         share_shapes,
         labels_of(0) + [grads[0], far],
-        [keep],
+        [keeps[0]],
         "share",
-        1.0,
-    )
-    mine = [made[0]] + exchanged(made[1:], range(plan.rels))
-    for bucket in range(1, buckets):
-        (other,) = after(
-            functools.partial(add_kernel, plan.rels),
-            [shape((width + 16, lanes), i16)],
-            others[bucket - 1],
-            [made[0]],
-            "other",
-            0.3,
-        )
-        mine.append(send(other, plan, lambda d, b=bucket: d ^ (b * plan.rels)))
-
-    (total,) = after(
-        functools.partial(combine_kernel, plan, later, True, 1),
-        [shape((1,) + chunk[1:], i16)],
-        [keep] + arrived,
-        [mine[0]],
-        "combine_z",
-        0.5,
-    )
-    pieces = [total] + exchanged([total] * (later - 1), plan.masks[2])
-    (part,) = after(
+        0.8,
+    )
+    mine, order = [made[0]] + exchanged(made[1:], range(plan.rels)) + crossing, made[0]
+    totals, _ = combine(keeps, arrived, [order], 2, "combine_last")
+
+    pieces = [
+        [total] + exchanged([total] * (len(part.masks[1]) - 1), part.masks[1])
+        for part, total in zip(plan.parts, totals)
+    ]
+    (owner,) = after(
         functools.partial(add_kernel, len(mine)),
         [shape((width + 16, lanes), i16)],
         mine,
-        [total],
+        [totals[0]],
         "mine",
-        0.5,
-    )
-    owners = [part] + exchanged([part] * (plan.rels - 1), range(plan.rels))
-    (block,) = after(
-        stack_kernel,
-        [shape((len(pieces),) + chunk[1:], i16)],
-        pieces,
-        [part],
-        "stack",
         0.3,
     )
-    pieces = [block] + exchanged([block] * (size - 1), plan.masks[1])
+    owners = [owner] + exchanged([owner] * (plan.rels - 1), range(plan.rels))
     (grad_partitions,) = after(
         functools.partial(part_out_kernel, plan),
         [shape((width, prows), F32)],
         owners,
-        [block],
+        [],
         "part_out",
         1.0,
     )
+    blocks = after(
+        functools.partial(stack_kernel, plan, [len(group) for group in pieces]),
+        [
+            shape((len(group),) + part.packed[1:], i16)
+            for part, group in zip(plan.parts, pieces)
+        ],
+        sum(pieces, []),
+        [grad_partitions],
+        "stack",
+        0.3,
+    )
+    pieces = [
+        [block] + exchanged([block] * (len(part.masks[0]) - 1), part.masks[0])
+        for part, block in zip(plan.parts, blocks)
+    ]
     if lanes % LANES:
         order = jnp.arange(plan.rels) ^ lax.axis_index("rel")
         split_lanes = grad_partitions.reshape(width, plan.rels, lanes)
         grad_partitions = jnp.take(split_lanes, order, axis=1).reshape(width, prows)
 
-    others = [send(piece, plan, lambda d: d ^ 1) for piece in pieces]
+    crossed = [[send(piece, plan, lambda d: d ^ 1) for piece in group] for group in pieces]
     side = lax.axis_index("rel") & 1
     outs = [shape((width, plan.nrels), F32), shape((width, plan.rems), F32)]
     spec = lambda lanes: pl.BlockSpec((width, lanes), lambda i, half: (0, half[0]))
     made = []
-    for turn, group in enumerate([pieces, others]):
+    for turn, groups in enumerate([pieces, crossed]):
+        flat = sum(groups, [])
         made = call(
-            functools.partial(spread_kernel, plan, len(group)),
+            functools.partial(spread_kernel, plan, [len(group) for group in groups]),
             outs,
-            [(side ^ turn).reshape(1), *group, *made],
+            [(side ^ turn).reshape(1), *flat, *made],
             "spread",
             2.0,
             16,
             grid_spec=pltpu.PrefetchScalarGridSpec(
                 num_scalar_prefetch=1,
                 grid=(1,),
-                in_specs=[pl.BlockSpec(piece.shape, lambda i, half: (0, 0, 0)) for piece in group]
+                in_specs=[pl.BlockSpec(piece.shape, lambda i, half: (0, 0, 0)) for piece in flat]
                 + [ANY] * len(made),
                 out_specs=[spec(plan.half_rel), spec(plan.half_rem)],
-                scratch_shapes=[pltpu.VMEM(chunk, i16)],
+                scratch_shapes=[pltpu.VMEM(part.packed, i16) for part in plan.parts],
             ),
-            input_output_aliases={1 + len(group) + at: at for at in range(len(made))},
+            input_output_aliases={1 + len(flat) + at: at for at in range(len(made))},
         )
     grad_relations, grad_remainder = made
     return grad_partitions.T, grad_remainder.T, grad_relations.T

time: 111 us -> 116 us (1.045)
  waiting for transfers between devices: 31.3 us -> 40 us
  starting transfers between devices: 41.8 us -> 36.9 us
    ppermute x37 -> x34, waiting for transfers between devices: 31.3 us -> 40 us  [send(): return lax.ppermute(value, ('dom', 'rel'), pairs)]
    ppermute x37 -> x34, starting transfers between devices: 41.8 us -> 36.9 us  [send(): return lax.ppermute(value, ('dom', 'rel'), pairs)]
    pallas_call x21 -> x23, Pallas kernels: 36.9 us -> 37 us  [call(): pl.pallas_call(kernel, out_shape=outs, compiler_params=pltpu.CompilerPara...]
  transfers between devices with their start and end apart: 37 -> 34, of which waited for: 8 -> 11; matrix products, arithmetic and copies ran while one was open for 0% -> 0% of each run, Pallas kernels for 19% -> 17%
where the time goes in v5:
time: 116 us
  waiting for transfers between devices  40 us (34%)
  Pallas kernels  37 us (32%)
  starting transfers between devices  36.9 us (32%)
  local copies, waits for them, and re-layouts  1.16 us (1%)
    ppermute x34, waiting for transfers between devices, send(): return lax.ppermute(value, ('dom', 'rel'), pairs)  40 us
    pallas_call x23, Pallas kernels, call(): pl.pallas_call(kernel, out_shape=outs, compiler_params=pltpu.CompilerPara...  37 us
    ppermute x34, starting transfers between devices, send(): return lax.ppermute(value, ('dom', 'rel'), pairs)  36.9 us
  transfers between devices with their start and end apart: 34, of which 11 were waited for; matrix products, arithmetic and copies ran while one was open for 0% of the time, Pallas kernels for 17%

profile of v5, /device:TPU:0, one launch (start us, length us, event | category | flops | bytes accessed | tf_op | source)
XLA Modules:
  0.0 116.0 jit_solution(2533706155377428746)
XLA Ops:
  2.6 2.6 %collective-permute-start.1 = (s32[2,8,128]{2,1,0:T(8,128)}, s32[2,8,128]{2,1,0:T(8,128)S(1)}, u32[]{:S(2)}, u32[]{:S(2)}) collective-permute-start(s32[2,8,128]{2,1,0:T(8,128)} %get-tuple-element.42), channel_id=1, source_target_pairs={{0,2},{1,3},{2,0},{3,1},{4,6},{5,7},{6,4},{7,5},{8,10},{9,11},{10,... | collective-permute-start | bytes 24584 | tf_op jit(solution)/shard_map/ppermute | solution.py:187
  5.2 2.9 %rel_split.1.refs_1_ = bf16[800,2560]{1,0:T(8,128)(2,1)S(1)} custom-call(f32[400,2560]{1,0:T(8,128)} %bitcast.13), custom_call_target="tpu_custom_call" | custom-call | flops 2000000000 | bytes 6000000 | tf_op jit(solution)/shard_map/rel_split/pallas_call | solution.py:491
  11.2 2.3 %relation.2.refs_3_ = f32[400,512]{1,0:T(8,128)S(1)} custom-call(s32[4,8,128]{2,1,0:T(8,128)S(1)} %get-tuple-element.44.refs_0_, bf16[800,2560]{1,0:T(8,128)(2,1)S(1)} %rel_split.1.refs_1_), custom_call_target="tpu_custom_call" | custom-call | flops 2000000000 | bytes 6000000 | tf_op jit(solution)/shard_map/relation/pallas_call | solution.py:491
  14.2 4.7 %collective-permute-done.3.refs_0_.refs_1_ = s32[4,8,128]{2,1,0:T(8,128)S(1)} collective-permute-done((s32[4,8,128]{2,1,0:T(8,128)S(1)}, s32[4,8,128]{2,1,0:T(8,128)S(1)}, u32[]{:S(2)}, u32[]{:S(2)}) %collective-permute-start.3) | collective-permute-done | bytes 16416 | tf_op jit(solution)/shard_map/ppermute | solution.py:187
  18.9 2.3 %relation.3.refs_7_ = f32[400,512]{1,0:T(8,128)S(1)} custom-call(s32[4,8,128]{2,1,0:T(8,128)S(1)} %collective-permute-done.3.refs_0_.refs_1_, bf16[800,2560]{1,0:T(8,128)(2,1)S(1)} %rel_split.1.refs_1_), custom_call_target="tpu_custom_call" | custom-call | flops 2000000000 | bytes 6000000 | tf_op jit(solution)/shard_map/relation/pallas_call | solution.py:491
  22.0 4.1 %bucket.1 = (bf16[800,512]{1,0:T(8,128)(2,1)S(1)}, bf16[800,512]{1,0:T(8,128)(2,1)S(1)}, bf16[800,1024]{1,0:T(8,128)(2,1)S(1)}) custom-call(s32[4,8,128]{2,1,0:T(8,128)S(1)} %get-tuple-element.44.refs_0_, bf16[400,512]{1,0:T(8,128)(2,1)S(1)} %collective-permute-done.4.refs_1_.refs_5_, f32[400,512]{1,0:T(8,128)S(1)} %get-tuple-element.46.refs_2_, ...), custom_call_target="tpu_custom_call" | custom-call | flops 4000000000 | bytes 12000000 | tf_op jit(solution)/shard_map/bucket/pallas_call | solution.py:491
  26.1 9.6 %last.1 = (s16[16,288,128]{2,1,0:T(8,128)(2,1)S(1)}, bf16[800,1024]{1,0:T(8,128)(2,1)S(1)}, bf16[800,1024]{1,0:T(8,128)(2,1)S(1)}, bf16[800,2048]{1,0:T(8,128)(2,1)S(1)}) custom-call(s32[4,8,128]{2,1,0:T(8,128)S(1)} %get-tuple-element.44.refs_0_, s32[4,8,128]{2,1,0:T(8,128)S(1)} %collective-permute-done.3.refs_0_.refs_1_, ...), custom_call_target="tpu_custom_call" | custom-call | flops 8999999488 | bytes 27000000 | tf_op jit(solution)/shard_map/last/pallas_call | solution.py:491
  35.7 2.8 %collective-permute-start.7 = (s16[16,288,128]{2,1,0:T(8,128)(2,1)S(1)}, s16[16,288,128]{2,1,0:T(8,128)(2,1)S(1)}, u32[]{:S(2)}, u32[]{:S(2)}) collective-permute-start(s16[16,288,128]{2,1,0:T(8,128)(2,1)S(1)} %get-tuple-element.55.refs_2_), channel_id=1, source_target_pairs={{0,1},{1,0},{2,3},{3,2},{4,5},{5,4},{6,7},{7,6},{8,9},{9,8},{10,11... | collective-permute-start | bytes 3538952 | tf_op jit(solution)/shard_map/ppermute | solution.py:187
  39.3 3.9 %collective-permute-start.10 = (s16[416,128]{1,0:T(8,128)(2,1)S(1)}, s16[416,128]{1,0:T(8,128)(2,1)S(1)}, u32[]{:S(2)}, u32[]{:S(2)}) collective-permute-start(s16[416,128]{1,0:T(8,128)(2,1)S(1)} %get-tuple-element.60), channel_id=1, source_target_pairs={{0,3},{1,2},{2,1},{3,0},{4,7},{5,6},{6,5},{7,4},{8,11},{9,10},{10,... | collective-permute-start | bytes 319496 | tf_op jit(solution)/shard_map/ppermute | solution.py:187
  43.7 2.0 %target.1.refs_5_ = s16[416,512]{1,0:T(8,128)(2,1)S(1)} custom-call(s32[4,8,128]{2,1,0:T(8,128)S(1)} %get-tuple-element.44.refs_0_, s32[4,8,128]{2,1,0:T(8,128)S(1)} %collective-permute-done.3.refs_0_.refs_1_, bf16[800,2048]{1,0:T(8,128)(2,1)S(1)} %get-tuple-element.54.refs_2_.refs_4_, f32[400,128]{1,0:T(8,128)S(1)} %get-tuple-element.56.refs_3_.refs_0_), custom_call_target="tpu_custom_call" | custom-call | flops 1800000000 | bytes 5400000 | tf_op jit(solution)/shard_map/target/pallas_call | solution.py:491
  46.7 3.7 %home.1.refs_4_.refs_0_ = f32[16,280,128]{2,1,0:T(8,128)S(1)} custom-call(s32[4,8,128]{2,1,0:T(8,128)S(1)} %get-tuple-element.44.refs_0_, s32[4,8,128]{2,1,0:T(8,128)S(1)} %collective-permute-done.3.refs_0_.refs_1_, bf16[800,1024]{1,0:T(8,128)(2,1)S(1)} %get-tuple-element.53.refs_1_.refs_2_, bf16[800,1024]{1,0:T(8,128)(2,1)S(1)} %get-tuple-element.57.refs_3_, ...), custom_call_target="tpu_custom_call" | custom-call | flops 4000000000 | bytes 12000000 | tf_op jit(solution)/shard_map/home/pallas_call | solution.py:491
  51.1 3.8 %collective-permute-start.11 = (s16[4,288,128]{2,1,0:T(8,128)(2,1)S(1)}, s16[4,288,128]{2,1,0:T(8,128)(2,1)S(1)}, u32[]{:S(2)}, u32[]{:S(2)}) collective-permute-start(s16[4,288,128]{2,1,0:T(8,128)(2,1)S(1)} %get-tuple-element.62), channel_id=1, source_target_pairs={{0,2},{1,3},{2,0},{3,1},{4,6},{5,7},{6,4},{7,5},{8,10},{9,11},{10,... | collective-permute-start | bytes 884744 | tf_op jit(solution)/shard_map/ppermute | solution.py:187
  58.0 4.5 %collective-permute-done.11.refs_1_ = s16[4,288,128]{2,1,0:T(8,128)(2,1)S(1)} collective-permute-done((s16[4,288,128]{2,1,0:T(8,128)(2,1)S(1)}, s16[4,288,128]{2,1,0:T(8,128)(2,1)S(1)}, u32[]{:S(2)}, u32[]{:S(2)}) %collective-permute-start.11) | collective-permute-done | bytes 294944 | tf_op jit(solution)/shard_map/ppermute | solution.py:187
  62.4 8.7 %collective-permute-done.12.refs_2_ = s16[4,288,128]{2,1,0:T(8,128)(2,1)S(1)} collective-permute-done((s16[4,288,128]{2,1,0:T(8,128)(2,1)S(1)}, s16[4,288,128]{2,1,0:T(8,128)(2,1)S(1)}, u32[]{:S(2)}, u32[]{:S(2)}) %collective-permute-start.12) | collective-permute-done | bytes 294944 | tf_op jit(solution)/shard_map/ppermute | solution.py:187
  73.8 2.1 %collective-permute-start.20 = (s16[1,288,128]{2,1,0:T(8,128)(2,1)S(1)}, s16[1,288,128]{2,1,0:T(8,128)(2,1)S(1)}, u32[]{:S(2)}, u32[]{:S(2)}) collective-permute-start(s16[1,288,128]{2,1,0:T(8,128)(2,1)S(1)} %get-tuple-element.72), channel_id=1, source_target_pairs={{0,24},{1,25},{2,26},{3,27},{4,28},{5,29},{6,30},{7,31},{8,16},{9,... | collective-permute-start | bytes 221192 | tf_op jit(solution)/shard_map/ppermute | solution.py:187
  77.8 2.5 %collective-permute-done.19.refs_2_ = s16[1,288,128]{2,1,0:T(8,128)(2,1)S(1)} collective-permute-done((s16[1,288,128]{2,1,0:T(8,128)(2,1)S(1)}, s16[1,288,128]{2,1,0:T(8,128)(2,1)S(1)}, u32[]{:S(2)}, u32[]{:S(2)}) %collective-permute-start.19) | collective-permute-done | bytes 73760 | tf_op jit(solution)/shard_map/ppermute | solution.py:187
  80.4 1.7 %collective-permute-done.15.refs_2_ = s16[416,128]{1,0:T(8,128)(2,1)S(1)} collective-permute-done((s16[416,128]{1,0:T(8,128)(2,1)S(1)}, s16[416,128]{1,0:T(8,128)(2,1)S(1)}, u32[]{:S(2)}, u32[]{:S(2)}) %collective-permute-start.15) | collective-permute-done | bytes 106528 | tf_op jit(solution)/shard_map/ppermute | solution.py:187
  82.1 3.4 %collective-permute-done.16.refs_3_ = s16[416,128]{1,0:T(8,128)(2,1)S(1)} collective-permute-done((s16[416,128]{1,0:T(8,128)(2,1)S(1)}, s16[416,128]{1,0:T(8,128)(2,1)S(1)}, u32[]{:S(2)}, u32[]{:S(2)}) %collective-permute-start.16) | collective-permute-done | bytes 106528 | tf_op jit(solution)/shard_map/ppermute | solution.py:187
  88.7 3.3 %collective-permute-start.26 = (s16[1,288,128]{2,1,0:T(8,128)(2,1)S(1)}, s16[1,288,128]{2,1,0:T(8,128)(2,1)S(1)}, u32[]{:S(2)}, u32[]{:S(2)}) collective-permute-start(s16[1,288,128]{2,1,0:T(8,128)(2,1)S(1)} %combine_last.1.refs_5_.refs_0_), channel_id=1, source_target_pairs={{0,24},{1,25},{2,26},{3,27},{4,28},{5,29},{6,30},{7,31},{8,16},{9,... | collective-permute-start | bytes 221192 | tf_op jit(solution)/shard_map/ppermute | solution.py:187
  94.0 2.8 %collective-permute-done.25.refs_2_ = s16[1,288,128]{2,1,0:T(8,128)(2,1)S(1)} collective-permute-done((s16[1,288,128]{2,1,0:T(8,128)(2,1)S(1)}, s16[1,288,128]{2,1,0:T(8,128)(2,1)S(1)}, u32[]{:S(2)}, u32[]{:S(2)}) %collective-permute-start.25) | collective-permute-done | bytes 73760 | tf_op jit(solution)/shard_map/ppermute | solution.py:187
  101.5 6.5 %collective-permute-done.28.refs_1_ = s16[4,288,128]{2,1,0:T(8,128)(2,1)S(1)} collective-permute-done((s16[4,288,128]{2,1,0:T(8,128)(2,1)S(1)}, s16[4,288,128]{2,1,0:T(8,128)(2,1)S(1)}, u32[]{:S(2)}, u32[]{:S(2)}) %collective-permute-start.28) | collective-permute-done | bytes 294944 | tf_op jit(solution)/shard_map/ppermute | solution.py:187
  108.0 4.1 %collective-permute-done.30.refs_2_ = s16[4,288,128]{2,1,0:T(8,128)(2,1)S(1)} collective-permute-done((s16[4,288,128]{2,1,0:T(8,128)(2,1)S(1)}, s16[4,288,128]{2,1,0:T(8,128)(2,1)S(1)}, u32[]{:S(2)}, u32[]{:S(2)}) %collective-permute-start.30) | collective-permute-done | bytes 294944 | tf_op jit(solution)/shard_map/ppermute | solution.py:187
  112.6 1.7 %spread.2 = (f32[400,2560]{1,0:T(8,128)}, f32[400,256]{1,0:T(8,128)}) custom-call(s32[1]{0:T(128)} %bitcast.6.side, s16[4,288,128]{2,1,0:T(8,128)(2,1)S(1)} %stack.1.refs_0_, s16[4,288,128]{2,1,0:T(8,128)(2,1)S(1)} %collective-permute-done.28.refs_1_, s16[4,288,128]{2,1,0:T(8,128)(2,1)S(1)} %collective-permute-done.30.refs_2_, ...), custom_call_target="tpu_custom_call" | custom-call | flops 2000000000 | bytes 6000000 | tf_op jit(solution)/shard_map/spread/pallas_call | solution.py:491
  114.3 1.7 %spread.3 = (f32[400,2560]{1,0:T(8,128)}, f32[400,256]{1,0:T(8,128)}) custom-call(s32[1]{0:T(128)} %bitcast.5.side, s16[4,288,128]{2,1,0:T(8,128)(2,1)S(1)} %collective-permute-done.27.refs_0_, s16[4,288,128]{2,1,0:T(8,128)(2,1)S(1)} %collective-permute-done.29.refs_1_, ...), custom_call_target="tpu_custom_call", output_to_operand_aliasing={{0}: (5, {}), {1}: (6, {})} | custom-call | flops 2000000000 | bytes 6000000 | tf_op jit(solution)/shard_map/spread/pallas_call | solution.py:491
  (75 shorter events, 27.5 us)
Async XLA Ops:
  8.4 13.5 %collective-permute-start.4 = (bf16[400,512]{1,0:T(8,128)(2,1)S(1)}, bf16[400,512]{1,0:T(8,128)(2,1)S(1)}, u32[]{:S(2)}, u32[]{:S(2)}) collective-permute-start(bf16[400,512]{1,0:T(8,128)(2,1)S(1)} %own.1.refs_1_), channel_id=1, source_target_pairs={{0,0},{1,17},{2,10},{3,27},{4,4},{5,21},{6,14},{7,31},{8,8},{9,25}... | collective-permute-start | bytes 1228808 | tf_op jit(solution)/shard_map/ppermute | solution.py:187
  9.1 12.1 %collective-permute-start.5 = (bf16[400,512]{1,0:T(8,128)(2,1)S(1)}, bf16[400,512]{1,0:T(8,128)(2,1)S(1)}, u32[]{:S(2)}, u32[]{:S(2)}) collective-permute-start(bf16[400,512]{1,0:T(8,128)(2,1)S(1)} %own.1.refs_1_), channel_id=1, source_target_pairs={{0,4},{1,5},{2,6},{3,7},{4,0},{5,1},{6,2},{7,3},{8,12},{9,13},{10,... | collective-permute-start | bytes 1228808 | tf_op jit(solution)/shard_map/ppermute | solution.py:187
  10.7 8.2 %collective-permute-start.3 = (s32[4,8,128]{2,1,0:T(8,128)S(1)}, s32[4,8,128]{2,1,0:T(8,128)S(1)}, u32[]{:S(2)}, u32[]{:S(2)}) collective-permute-start(s32[4,8,128]{2,1,0:T(8,128)S(1)} %get-tuple-element.45), channel_id=1, source_target_pairs={{0,4},{1,5},{2,6},{3,7},{4,0},{5,1},{6,2},{7,3},{8,12},{9,13},{10,... | collective-permute-start | bytes 49160 | tf_op jit(solution)/shard_map/ppermute | solution.py:187
  35.7 14.8 %collective-permute-start.7 = (s16[16,288,128]{2,1,0:T(8,128)(2,1)S(1)}, s16[16,288,128]{2,1,0:T(8,128)(2,1)S(1)}, u32[]{:S(2)}, u32[]{:S(2)}) collective-permute-start(s16[16,288,128]{2,1,0:T(8,128)(2,1)S(1)} %get-tuple-element.55.refs_2_), channel_id=1, source_target_pairs={{0,1},{1,0},{2,3},{3,2},{4,5},{5,4},{6,7},{7,6},{8,9},{9,8},{10,11... | collective-permute-start | bytes 3538952 | tf_op jit(solution)/shard_map/ppermute | solution.py:187
  39.3 11.1 %collective-permute-start.10 = (s16[416,128]{1,0:T(8,128)(2,1)S(1)}, s16[416,128]{1,0:T(8,128)(2,1)S(1)}, u32[]{:S(2)}, u32[]{:S(2)}) collective-permute-start(s16[416,128]{1,0:T(8,128)(2,1)S(1)} %get-tuple-element.60), channel_id=1, source_target_pairs={{0,3},{1,2},{2,1},{3,0},{4,7},{5,6},{6,5},{7,4},{8,11},{9,10},{10,... | collective-permute-start | bytes 319496 | tf_op jit(solution)/shard_map/ppermute | solution.py:187
  43.2 7.1 %collective-permute-start.8 = (s16[416,128]{1,0:T(8,128)(2,1)S(1)}, s16[416,128]{1,0:T(8,128)(2,1)S(1)}, u32[]{:S(2)}, u32[]{:S(2)}) collective-permute-start(s16[416,128]{1,0:T(8,128)(2,1)S(1)} %get-tuple-element.58), channel_id=1, source_target_pairs={{0,1},{1,0},{2,3},{3,2},{4,5},{5,4},{6,7},{7,6},{8,9},{9,8},{10,11... | collective-permute-start | bytes 319496 | tf_op jit(solution)/shard_map/ppermute | solution.py:187
  43.7 6.7 %collective-permute-start.9 = (s16[416,128]{1,0:T(8,128)(2,1)S(1)}, s16[416,128]{1,0:T(8,128)(2,1)S(1)}, u32[]{:S(2)}, u32[]{:S(2)}) collective-permute-start(s16[416,128]{1,0:T(8,128)(2,1)S(1)} %get-tuple-element.59), channel_id=1, source_target_pairs={{0,2},{1,3},{2,0},{3,1},{4,6},{5,7},{6,4},{7,5},{8,10},{9,11},{10,... | collective-permute-start | bytes 319496 | tf_op jit(solution)/shard_map/ppermute | solution.py:187
  45.8 30.1 %collective-permute-start.6 = (s16[416,512]{1,0:T(8,128)(2,1)S(1)}, s16[416,512]{1,0:T(8,128)(2,1)S(1)}, u32[]{:S(2)}, u32[]{:S(2)}) collective-permute-start(s16[416,512]{1,0:T(8,128)(2,1)S(1)} %target.1.refs_5_), channel_id=1, source_target_pairs={{0,0},{1,17},{2,10},{3,27},{4,4},{5,21},{6,14},{7,31},{8,8},{9,25}... | collective-permute-start | bytes 1277960 | tf_op jit(solution)/shard_map/ppermute | solution.py:187
  51.1 11.3 %collective-permute-start.11 = (s16[4,288,128]{2,1,0:T(8,128)(2,1)S(1)}, s16[4,288,128]{2,1,0:T(8,128)(2,1)S(1)}, u32[]{:S(2)}, u32[]{:S(2)}) collective-permute-start(s16[4,288,128]{2,1,0:T(8,128)(2,1)S(1)} %get-tuple-element.62), channel_id=1, source_target_pairs={{0,2},{1,3},{2,0},{3,1},{4,6},{5,7},{6,4},{7,5},{8,10},{9,11},{10,... | collective-permute-start | bytes 884744 | tf_op jit(solution)/shard_map/ppermute | solution.py:187
  54.9 16.2 %collective-permute-start.12 = (s16[4,288,128]{2,1,0:T(8,128)(2,1)S(1)}, s16[4,288,128]{2,1,0:T(8,128)(2,1)S(1)}, u32[]{:S(2)}, u32[]{:S(2)}) collective-permute-start(s16[4,288,128]{2,1,0:T(8,128)(2,1)S(1)} %get-tuple-element.63), channel_id=1, source_target_pairs={{0,4},{1,5},{2,6},{3,7},{4,0},{5,1},{6,2},{7,3},{8,12},{9,13},{10,... | collective-permute-start | bytes 884744 | tf_op jit(solution)/shard_map/ppermute | solution.py:187
  56.4 14.7 %collective-permute-start.13 = (s16[4,288,128]{2,1,0:T(8,128)(2,1)S(1)}, s16[4,288,128]{2,1,0:T(8,128)(2,1)S(1)}, u32[]{:S(2)}, u32[]{:S(2)}) collective-permute-start(s16[4,288,128]{2,1,0:T(8,128)(2,1)S(1)} %get-tuple-element.64), channel_id=1, source_target_pairs={{0,6},{1,7},{2,4},{3,5},{4,2},{5,3},{6,0},{7,1},{8,14},{9,15},{10,... | collective-permute-start | bytes 884744 | tf_op jit(solution)/shard_map/ppermute | solution.py:187
  56.5 23.9 %collective-permute-start.17 = (s16[416,128]{1,0:T(8,128)(2,1)S(1)}, s16[416,128]{1,0:T(8,128)(2,1)S(1)}, u32[]{:S(2)}, u32[]{:S(2)}) collective-permute-start(s16[416,128]{1,0:T(8,128)(2,1)S(1)} %other.1.refs_2_), channel_id=1, source_target_pairs={{0,4},{1,5},{2,6},{3,7},{4,0},{5,1},{6,2},{7,3},{8,12},{9,13},{10,... | collective-permute-start | bytes 319496 | tf_op jit(solution)/shard_map/ppermute | solution.py:187
  72.1 8.1 %collective-permute-start.19 = (s16[1,288,128]{2,1,0:T(8,128)(2,1)S(1)}, s16[1,288,128]{2,1,0:T(8,128)(2,1)S(1)}, u32[]{:S(2)}, u32[]{:S(2)}) collective-permute-start(s16[1,288,128]{2,1,0:T(8,128)(2,1)S(1)} %get-tuple-element.71), channel_id=1, source_target_pairs={{0,16},{1,17},{2,18},{3,19},{4,20},{5,21},{6,22},{7,23},{8,24},{9,... | collective-permute-start | bytes 221192 | tf_op jit(solution)/shard_map/ppermute | solution.py:187
  73.8 6.5 %collective-permute-start.20 = (s16[1,288,128]{2,1,0:T(8,128)(2,1)S(1)}, s16[1,288,128]{2,1,0:T(8,128)(2,1)S(1)}, u32[]{:S(2)}, u32[]{:S(2)}) collective-permute-start(s16[1,288,128]{2,1,0:T(8,128)(2,1)S(1)} %get-tuple-element.72), channel_id=1, source_target_pairs={{0,24},{1,25},{2,26},{3,27},{4,28},{5,29},{6,30},{7,31},{8,16},{9,... | collective-permute-start | bytes 221192 | tf_op jit(solution)/shard_map/ppermute | solution.py:187
  85.8 6.2 %collective-permute-start.22 = (s16[416,128]{1,0:T(8,128)(2,1)S(1)}, s16[416,128]{1,0:T(8,128)(2,1)S(1)}, u32[]{:S(2)}, u32[]{:S(2)}) collective-permute-start(s16[416,128]{1,0:T(8,128)(2,1)S(1)} %mine.1.refs_0_), channel_id=1, source_target_pairs={{0,2},{1,3},{2,0},{3,1},{4,6},{5,7},{6,4},{7,5},{8,10},{9,11},{10,... | collective-permute-start | bytes 319496 | tf_op jit(solution)/shard_map/ppermute | solution.py:187
  86.4 6.5 %collective-permute-start.23 = (s16[416,128]{1,0:T(8,128)(2,1)S(1)}, s16[416,128]{1,0:T(8,128)(2,1)S(1)}, u32[]{:S(2)}, u32[]{:S(2)}) collective-permute-start(s16[416,128]{1,0:T(8,128)(2,1)S(1)} %mine.1.refs_0_), channel_id=1, source_target_pairs={{0,3},{1,2},{2,1},{3,0},{4,7},{5,6},{6,5},{7,4},{8,11},{9,10},{10,... | collective-permute-start | bytes 319496 | tf_op jit(solution)/shard_map/ppermute | solution.py:187
  87.6 6.4 %collective-permute-start.24 = (s16[1,288,128]{2,1,0:T(8,128)(2,1)S(1)}, s16[1,288,128]{2,1,0:T(8,128)(2,1)S(1)}, u32[]{:S(2)}, u32[]{:S(2)}) collective-permute-start(s16[1,288,128]{2,1,0:T(8,128)(2,1)S(1)} %combine_last.1.refs_5_.refs_0_), channel_id=1, source_target_pairs={{0,8},{1,9},{2,10},{3,11},{4,12},{5,13},{6,14},{7,15},{8,0},{9,1},... | collective-permute-start | bytes 221192 | tf_op jit(solution)/shard_map/ppermute | solution.py:187
  87.6 9.2 %collective-permute-start.25 = (s16[1,288,128]{2,1,0:T(8,128)(2,1)S(1)}, s16[1,288,128]{2,1,0:T(8,128)(2,1)S(1)}, u32[]{:S(2)}, u32[]{:S(2)}) collective-permute-start(s16[1,288,128]{2,1,0:T(8,128)(2,1)S(1)} %combine_last.1.refs_5_.refs_0_), channel_id=1, source_target_pairs={{0,16},{1,17},{2,18},{3,19},{4,20},{5,21},{6,22},{7,23},{8,24},{9,... | collective-permute-start | bytes 221192 | tf_op jit(solution)/shard_map/ppermute | solution.py:187
  88.7 8.1 %collective-permute-start.26 = (s16[1,288,128]{2,1,0:T(8,128)(2,1)S(1)}, s16[1,288,128]{2,1,0:T(8,128)(2,1)S(1)}, u32[]{:S(2)}, u32[]{:S(2)}) collective-permute-start(s16[1,288,128]{2,1,0:T(8,128)(2,1)S(1)} %combine_last.1.refs_5_.refs_0_), channel_id=1, source_target_pairs={{0,24},{1,25},{2,26},{3,27},{4,28},{5,29},{6,30},{7,31},{8,16},{9,... | collective-permute-start | bytes 221192 | tf_op jit(solution)/shard_map/ppermute | solution.py:187
  98.0 10.0 %collective-permute-start.28 = (s16[4,288,128]{2,1,0:T(8,128)(2,1)S(1)}, s16[4,288,128]{2,1,0:T(8,128)(2,1)S(1)}, u32[]{:S(2)}, u32[]{:S(2)}) collective-permute-start(s16[4,288,128]{2,1,0:T(8,128)(2,1)S(1)} %stack.1.refs_0_), channel_id=1, source_target_pairs={{0,2},{1,3},{2,0},{3,1},{4,6},{5,7},{6,4},{7,5},{8,10},{9,11},{10,... | collective-permute-start | bytes 884744 | tf_op jit(solution)/shard_map/ppermute | solution.py:187
  98.7 13.4 %collective-permute-start.30 = (s16[4,288,128]{2,1,0:T(8,128)(2,1)S(1)}, s16[4,288,128]{2,1,0:T(8,128)(2,1)S(1)}, u32[]{:S(2)}, u32[]{:S(2)}) collective-permute-start(s16[4,288,128]{2,1,0:T(8,128)(2,1)S(1)} %stack.1.refs_0_), channel_id=1, source_target_pairs={{0,4},{1,5},{2,6},{3,7},{4,0},{5,1},{6,2},{7,3},{8,12},{9,13},{10,... | collective-permute-start | bytes 884744 | tf_op jit(solution)/shard_map/ppermute | solution.py:187
  100.2 11.9 %collective-permute-start.32 = (s16[4,288,128]{2,1,0:T(8,128)(2,1)S(1)}, s16[4,288,128]{2,1,0:T(8,128)(2,1)S(1)}, u32[]{:S(2)}, u32[]{:S(2)}) collective-permute-start(s16[4,288,128]{2,1,0:T(8,128)(2,1)S(1)} %stack.1.refs_0_), channel_id=1, source_target_pairs={{0,6},{1,7},{2,4},{3,5},{4,2},{5,3},{6,0},{7,1},{8,14},{9,15},{10,... | collective-permute-start | bytes 884744 | tf_op jit(solution)/shard_map/ppermute | solution.py:187
  101.5 12.7 %collective-permute-start.27 = (s16[4,288,128]{2,1,0:T(8,128)(2,1)S(1)}, s16[4,288,128]{2,1,0:T(8,128)(2,1)S(1)}, u32[]{:S(2)}, u32[]{:S(2)}) collective-permute-start(s16[4,288,128]{2,1,0:T(8,128)(2,1)S(1)} %stack.1.refs_0_), channel_id=1, source_target_pairs={{0,1},{1,0},{2,3},{3,2},{4,5},{5,4},{6,7},{7,6},{8,9},{9,8},{10,11... | collective-permute-start | bytes 884744 | tf_op jit(solution)/shard_map/ppermute | solution.py:187
  108.0 6.3 %collective-permute-start.29 = (s16[4,288,128]{2,1,0:T(8,128)(2,1)S(1)}, s16[4,288,128]{2,1,0:T(8,128)(2,1)S(1)}, u32[]{:S(2)}, u32[]{:S(2)}) collective-permute-start(s16[4,288,128]{2,1,0:T(8,128)(2,1)S(1)} %collective-permute-done.28.refs_1_), channel_id=1, source_target_pairs={{0,1},{1,0},{2,3},{3,2},{4,5},{5,4},{6,7},{7,6},{8,9},{9,8},{10,11... | collective-permute-start | bytes 884744 | tf_op jit(solution)/shard_map/ppermute | solution.py:187
  (14 other events, 54.1 us)

commit v6 on v5

--- a/solution.py
+++ b/solution.py
@@ -368,7 +368,10 @@
 def target_kernel(plan, *refs):
     count = plan.buckets
     ids = plan.whole_row(refs[:count], (3, 5))
-    refs[-1][...] = pack_table(rows_sum(plan, ids, refs[count][...]))
+    value = pack_table(rows_sum(plan, ids, refs[count][...]))
+    for at, out in enumerate(refs[-2:]):
+        lanes = out.shape[1]
+        out[...] = value[:, at * lanes : (at + 1) * lanes]
 
 
 def home_kernel(plan, *refs):
@@ -378,36 +381,65 @@
 
 def source_sum(plan, labels, grads, bucket):
     start = bucket * plan.bucket_edges
-    ids = plan.row(labels, 0, (0,), 0, plan.slots)
+    ids = plan.row(labels, bucket, (0,), 0, plan.slots)
     return rows_sum(plan, ids, grads[:, start : start + plan.bucket_edges])
 
 
-def to_shares(plan, value, outs):
+def deal(plan, value, bucket, outs):
+    keep, away = outs
     lanes = plan.part_lanes
-    outs[0][...] = value[:, :lanes]
-    for at, out in enumerate(outs[1:], 1):
-        out[...] = pack_table(value[:, at * lanes : (at + 1) * lanes])
-
-
-def source_kernel(plan, bucket, *refs):
-    value = source_sum(plan, refs[:1], refs[1], bucket)
-    to_shares(plan, value, refs[-plan.rels :])
-
-
-def share_kernel(plan, *refs):
-    value = source_sum(plan, refs[:1], refs[1], 0)
-    to_shares(plan, value + unpack_table(refs[2][...]), refs[-plan.rels :])
-
-
-def add_kernel(count, *refs):
+    for at in range(value.shape[1] // lanes):
+        share = value[:, at * lanes : (at + 1) * lanes]
+        to = slice(at // 2 * lanes, (at // 2 + 1) * lanes)
+        if at % 2:
+            away[bucket, :, to] = pack_table(share)
+        else:
+            keep[bucket, :, to] = share
+
+
+def sources_kernel(plan, *refs):
+    out = refs[-1]
+    for bucket in range(plan.buckets):
+        out[bucket] = source_sum(plan, refs[: plan.buckets], refs[plan.buckets], bucket)
+
+
+def share(plan, sources, *refs):
+    far, outs = refs[:-2], refs[-2:]
+    for bucket in range(plan.buckets):
+        value = sources[bucket]
+        if bucket == 0:
+            value = value + jnp.concatenate([unpack_table(ref[...]) for ref in far], axis=1)
+        deal(plan, value, bucket, outs)
+
+
+def deal_again(plan, keep, came, *outs):
+    for bucket in range(plan.buckets):
+        deal(plan, keep[bucket] + unpack_table(came[bucket]), bucket, outs)
+
+
+def deal_kernel(plan, *refs):
+    deal_again(plan, *refs)
+
+
+def settle(plan, keep, came, *outs):
+    for bucket, out in enumerate(outs):
+        value = keep[bucket] + unpack_table(came[bucket])
+        out[...] = pack_table(value) if bucket else value
+
+
+def mine_kernel(plan, *refs):
     value = refs[0][...]
-    for ref in refs[1:count]:
+    for ref in refs[1 : plan.buckets]:
         value = value + unpack_table(ref[...])
     refs[-1][...] = pack_table(value)
 
 
-def combine_kernel(plan, arrivals, sizes, after, *refs):
-    at, out_at = 0, sum(arrivals) + len(arrivals) + after
+def combine_kernel(plan, arrivals, sizes, beside, *refs):
+    at, out_at = 0, sum(arrivals) + len(arrivals)
+    if beside:
+        step, ins, outs = beside
+        step(plan, *refs[out_at : out_at + ins], *refs[len(refs) - outs :])
+        out_at += ins
     for part, count, size in zip(plan.parts, arrivals, sizes):
         keep, arrived = refs[at], refs[at + 1 : at + 1 + count]
         outs = refs[out_at : out_at + size]
@@ -423,7 +455,9 @@
 
 
 def stack_kernel(plan, counts, *refs):
-    outs = refs[-len(counts) :]
+    total = sum(counts)
+    outs, refs = refs[total + 2 : total + 2 + len(counts)], refs[: total + 2] + refs[total + 2 + len(counts) :]
+    settle(plan, *refs[total:])
     first = 0
     for count, out in zip(counts, outs):
         for at in range(count):
@@ -458,10 +492,6 @@
                     rem_out[rows, lane : lane + LANES] = piece
 
 
-def copy_kernel(*refs):
-    refs[-1][...] = refs[0][...]
-
-
 def part_out_kernel(plan, *refs):
     out = refs[-1]
     rel = lax.axis_index("rel")
@@ -546,6 +576,10 @@
             **more,
         )
 
+    target = send(own, plan, afar)
+    sources = [own] + [
+        send(own, plan, lambda d, b=bucket: d ^ (b * plan.rels)) for bucket in range(1, buckets)
+    ]
     tables = [lhs_rows, lhs_rems, rel_ids, rhs_rows, rhs_rems, neg_rows, neg_rems]
     lists = call(
         functools.partial(lists_kernel, plan),
@@ -557,13 +591,6 @@
         in_specs=[VMEM] * 7 + [smem],
     )
     lists = [lists[0]] + exchanged(lists[1:], range(plan.rels))
-    (own,) = after(
-        copy_kernel, [shape(own.shape, own.dtype)], [own], lists[1:], "own", 0.3, 4
-    )
-    target = send(own, plan, afar)
-    sources = [own] + [
-        send(own, plan, lambda d, b=bucket: d ^ (b * plan.rels)) for bucket in range(1, buckets)
-    ]
     labels = call(
         functools.partial(forward_kernel, plan),
         [shape((plan.slots, 8, LANES), jnp.int32)] * buckets,
@@ -632,44 +659,18 @@
     away, grads = made[: len(plan.parts)], list(made[len(plan.parts) :])
     cores = [send(value, plan, lambda d: d ^ 1) for value in away]
 
-    lanes = plan.part_lanes
-    share_shapes = [shape((width, lanes), F32)] + [shape((width + 16, lanes), i16)] * (
-        plan.rels - 1
-    )
-    others, order = [], away[0]
-    for bucket in range(1, buckets):
-        made = after(
-            functools.partial(source_kernel, plan, bucket),
-            share_shapes,
-            labels_of(bucket) + [grads[0]],
-            [order],
-            "source",
-            0.8,
-        )
-        others.append([made[0]] + exchanged(made[1:], range(plan.rels)))
-        order = made[0]
-    (far,) = after(
-        functools.partial(target_kernel, plan),
-        [shape((width + 16, prows), i16)],
-        labels + [grads[2]],
-        [order],
-        "target",
-        1.8,
-        16 * grow,
-    )
     keeps = after(
         functools.partial(home_kernel, plan),
         [shape(part.bare, F32) for part in plan.parts],
         labels + grads,
-        [far],
+        away,
         "home",
         4.0,
         16 * grow,
         scratch=table,
     )
-    far = send(far, plan, afar)
-
-    def combine(keeps, arrived, order, level, name):
+
+    def combine(keeps, arrived, level, name, step=None, step_args=(), step_outs=()):
         sizes = [len(part.masks[level]) if level < 2 else 1 for part in plan.parts]
         outs, args = [], []
         for part, keep, pieces, size in zip(plan.parts, keeps, arrived, sizes):
@@ -678,85 +679,112 @@
                 outs += part.shares(keep.shape[0], size)
             else:
                 outs.append(shape((1,) + part.packed[1:], i16))
+        beside = (step, len(step_args), len(step_outs)) if step else None
+        count = [len(pieces) for pieces in arrived]
         made = after(
-            functools.partial(
-                combine_kernel, plan, [len(pieces) for pieces in arrived], sizes, len(order)
-            ),
-            outs,
-            args,
-            order,
+            functools.partial(combine_kernel, plan, count, sizes, beside),
+            outs + list(step_outs),
+            args + list(step_args),
+            [],
             name,
-            0.5,
-        )
+            0.6,
+        )
+        made, beside = made[: len(outs)], made[len(outs) :]
         if level == 2:
-            return made, []
+            return made, [], beside
         keeps, arrived = [], []
         for part, size in zip(plan.parts, sizes):
             group, made = made[:size], made[size:]
             keeps.append(group[0])
             arrived.append(exchanged(group[1:], part.masks[level]))
-        return keeps, arrived
-
-    order, crossing = keeps[0], []
-    for bucket in range(1, buckets):
-        (order,) = after(
-            functools.partial(add_kernel, plan.rels),
-            [shape((width + 16, lanes), i16)],
-            others[bucket - 1],
-            [order],
-            "other",
-            0.3,
-        )
-        crossing.append(send(order, plan, lambda d, b=bucket: d ^ (b * plan.rels)))
-    keeps, arrived = combine(keeps, [[core] for core in cores], [order], 0, "combine_cores")
-    keeps, arrived = combine(keeps, arrived, [], 1, "combine_first")
-    made = after(
-        functools.partial(share_kernel, plan),
-        share_shapes,
-        labels_of(0) + [grads[0], far],
+        return keeps, arrived, beside
+
+    keeps, arrived, _ = combine(keeps, [[core] for core in cores], 0, "combine_cores")
+    far = after(
+        functools.partial(target_kernel, plan),
+        [shape((width + 16, prows // 2), i16)] * 2,
+        labels + [grads[2]],
         [keeps[0]],
-        "share",
-        0.8,
-    )
-    mine, order = [made[0]] + exchanged(made[1:], range(plan.rels)) + crossing, made[0]
-    totals, _ = combine(keeps, arrived, [order], 2, "combine_last")
-
+        "target",
+        1.8,
+        16 * grow,
+    )
+    (sources,) = after(
+        functools.partial(sources_kernel, plan),
+        [shape((buckets, width, prows), F32)],
+        labels + [grads[0]],
+        [far[0]],
+        "sources",
+        1.5,
+        16 * grow,
+    )
+    far = [send(value, plan, afar) for value in far]
+    lanes = plan.part_lanes
+    count, bit = plan.rels // 2, 1
+    dealt = lambda count: [
+        shape((buckets, width, count * lanes), F32),
+        shape((buckets, width + 16, count * lanes), i16),
+    ]
+    keeps, arrived, (mine, away) = combine(
+        keeps, arrived, 1, "combine_first", share, [sources] + far, dealt(count)
+    )
+    came = send(away, plan, lambda d: d ^ 1)
+    while count > 2:
+        count, bit = count // 2, bit * 2
+        mine, away = after(
+            functools.partial(deal_kernel, plan), dealt(count), [mine, came], [], "deal", 0.3
+        )
+        came = send(away, plan, lambda d, m=bit: d ^ m)
+    count, bit = count // 2, bit * 2
+    totals, _, (mine, away) = combine(
+        keeps, arrived, 2, "combine_last", deal_again, [mine, came], dealt(count)
+    )
+    came = send(away, plan, lambda d: d ^ bit)
     pieces = [
         [total] + exchanged([total] * (len(part.masks[1]) - 1), part.masks[1])
         for part, total in zip(plan.parts, totals)
     ]
-    (owner,) = after(
-        functools.partial(add_kernel, len(mine)),
-        [shape((width + 16, lanes), i16)],
-        mine,
-        [totals[0]],
-        "mine",
-        0.3,
-    )
-    owners = [owner] + exchanged([owner] * (plan.rels - 1), range(plan.rels))
-    (grad_partitions,) = after(
-        functools.partial(part_out_kernel, plan),
-        [shape((width, prows), F32)],
-        owners,
-        [],
-        "part_out",
-        1.0,
-    )
-    blocks = after(
+    flat = sum(pieces, [])
+    made = after(
         functools.partial(stack_kernel, plan, [len(group) for group in pieces]),
         [
             shape((len(group),) + part.packed[1:], i16)
             for part, group in zip(plan.parts, pieces)
-        ],
-        sum(pieces, []),
-        [grad_partitions],
+        ]
+        + [shape((width, lanes), F32)]
+        + [shape((width + 16, lanes), i16)] * (buckets - 1),
+        flat + [mine, came],
+        [],
         "stack",
-        0.3,
-    )
+        0.5,
+    )
+    blocks, made = made[: len(plan.parts)], made[len(plan.parts) :]
     pieces = [
         [block] + exchanged([block] * (len(part.masks[0]) - 1), part.masks[0])
         for part, block in zip(plan.parts, blocks)
     ]
+    mine = [made[0]] + exchanged(made[1:], range(0, plan.rels * buckets, plan.rels))
+    (owner,) = call(
+        functools.partial(mine_kernel, plan),
+        [shape((width + 16, lanes), i16)],
+        mine,
+        "mine",
+        0.3,
+        12,
+    )
+    owners = {0: owner}
+    while bit:
+        for mask in sorted(owners):
+            owners[mask | bit] = send(owners[mask], plan, lambda d, m=bit: d ^ m)
+        bit //= 2
+    (grad_partitions,) = after(
+        functools.partial(part_out_kernel, plan),
+        [shape((width, prows), F32)],
+        [owners[mask] for mask in range(plan.rels)],
+        [],
+        "part_out",
+        1.0,
+    )
     if lanes % LANES:
         order = jnp.arange(plan.rels) ^ lax.axis_index("rel")
         split_lanes = grad_partitions.reshape(width, plan.rels, lanes)

time: 116 us -> 108 us (0.931)
  waiting for transfers between devices: 40 us -> 32.9 us
    ppermute x34 -> x31, waiting for transfers between devices: 40 us -> 32.9 us  [send(): return lax.ppermute(value, ('dom', 'rel'), pairs)]
    ppermute x34 -> x31, starting transfers between devices: 36.9 us -> 36.4 us  [send(): return lax.ppermute(value, ('dom', 'rel'), pairs)]
    pallas_call x23 -> x20, Pallas kernels: 37 us -> 36.8 us  [call(): pl.pallas_call(kernel, out_shape=outs, compiler_params=pltpu.CompilerPara...]
  transfers between devices with their start and end apart: 34 -> 31, of which waited for: 11 -> 11; matrix products, arithmetic and copies ran while one was open for 0% -> 0% of each run, Pallas kernels for 17% -> 19%
where the time goes in v6:
time: 108 us; the launch traced here: 107 us
  Pallas kernels  36.8 us (34%)
  starting transfers between devices  36.4 us (34%)
  waiting for transfers between devices  32.9 us (30%)
    pallas_call x20, Pallas kernels, call(): pl.pallas_call(kernel, out_shape=outs, compiler_params=pltpu.CompilerPara...  36.8 us
    ppermute x31, starting transfers between devices, send(): return lax.ppermute(value, ('dom', 'rel'), pairs)  36.4 us
    ppermute x31, waiting for transfers between devices, send(): return lax.ppermute(value, ('dom', 'rel'), pairs)  32.9 us
  transfers between devices with their start and end apart: 31, of which 11 were waited for; matrix products, arithmetic and copies ran while one was open for 0% of the time, Pallas kernels for 19%

profile of v6, /device:TPU:0, one launch (start us, length us, event | category | flops | bytes accessed | tf_op | source)
XLA Modules:
  0.0 107.0 jit_solution(4933410749290223252)
XLA Ops:
  0.6 1.7 %collective-permute-start.4 = (bf16[400,512]{1,0:T(8,128)(2,1)}, bf16[400,512]{1,0:T(8,128)(2,1)S(1)}, u32[]{:S(2)}, u32[]{:S(2)}) collective-permute-start(bf16[400,512]{1,0:T(8,128)(2,1)} %bitcast.9), channel_id=1, source_target_pairs={{0,0},{1,17},{2,10},{3,27},{4,4},{5,21},{6,14},{7,31},{8,8},{9,25}... | collective-permute-start | bytes 1228808 | tf_op jit(solution)/shard_map/ppermute | solution.py:187
  2.3 3.0 %collective-permute-start.5 = (bf16[400,512]{1,0:T(8,128)(2,1)}, bf16[400,512]{1,0:T(8,128)(2,1)S(1)}, u32[]{:S(2)}, u32[]{:S(2)}) collective-permute-start(bf16[400,512]{1,0:T(8,128)(2,1)} %bitcast.10), channel_id=1, source_target_pairs={{0,4},{1,5},{2,6},{3,7},{4,0},{5,1},{6,2},{7,3},{8,12},{9,13},{10,... | collective-permute-start | bytes 1228808 | tf_op jit(solution)/shard_map/ppermute | solution.py:187
  6.7 2.2 %collective-permute-start = (s32[2,8,128]{2,1,0:T(8,128)}, s32[2,8,128]{2,1,0:T(8,128)S(1)}, u32[]{:S(2)}, u32[]{:S(2)}) collective-permute-start(s32[2,8,128]{2,1,0:T(8,128)} %get-tuple-element.43), channel_id=1, source_target_pairs={{0,1},{1,0},{2,3},{3,2},{4,5},{5,4},{6,7},{7,6},{8,9},{9,8},{10,11... | collective-permute-start | bytes 24584 | tf_op jit(solution)/shard_map/ppermute | solution.py:187
  8.9 2.5 %collective-permute-start.1 = (s32[2,8,128]{2,1,0:T(8,128)}, s32[2,8,128]{2,1,0:T(8,128)S(1)}, u32[]{:S(2)}, u32[]{:S(2)}) collective-permute-start(s32[2,8,128]{2,1,0:T(8,128)} %get-tuple-element.44), channel_id=1, source_target_pairs={{0,2},{1,3},{2,0},{3,1},{4,6},{5,7},{6,4},{7,5},{8,10},{9,11},{10,... | collective-permute-start | bytes 24584 | tf_op jit(solution)/shard_map/ppermute | solution.py:187
  11.4 2.9 %rel_split.1.refs_1_ = bf16[800,2560]{1,0:T(8,128)(2,1)S(1)} custom-call(f32[400,2560]{1,0:T(8,128)} %bitcast.14), custom_call_target="tpu_custom_call" | custom-call | flops 2000000000 | bytes 6000000 | tf_op jit(solution)/shard_map/rel_split/pallas_call | solution.py:521
  15.3 2.3 %relation.2.refs_3_ = f32[400,512]{1,0:T(8,128)S(1)} custom-call(s32[4,8,128]{2,1,0:T(8,128)S(1)} %get-tuple-element.46.refs_0_, bf16[800,2560]{1,0:T(8,128)(2,1)S(1)} %rel_split.1.refs_1_), custom_call_target="tpu_custom_call" | custom-call | flops 2000000000 | bytes 6000000 | tf_op jit(solution)/shard_map/relation/pallas_call | solution.py:521
  18.5 2.3 %relation.3.refs_7_ = f32[400,512]{1,0:T(8,128)S(1)} custom-call(s32[4,8,128]{2,1,0:T(8,128)S(1)} %collective-permute-done.3.refs_0_.refs_1_, bf16[800,2560]{1,0:T(8,128)(2,1)S(1)} %rel_split.1.refs_1_), custom_call_target="tpu_custom_call" | custom-call | flops 2000000000 | bytes 6000000 | tf_op jit(solution)/shard_map/relation/pallas_call | solution.py:521
  21.5 4.1 %bucket.1 = (bf16[800,512]{1,0:T(8,128)(2,1)S(1)}, bf16[800,512]{1,0:T(8,128)(2,1)S(1)}, bf16[800,1024]{1,0:T(8,128)(2,1)S(1)}) custom-call(s32[4,8,128]{2,1,0:T(8,128)S(1)} %get-tuple-element.46.refs_0_, bf16[400,512]{1,0:T(8,128)(2,1)S(1)} %collective-permute-done.4.refs_1_.refs_5_, f32[400,512]{1,0:T(8,128)S(1)} %get-tuple-element.48.refs_2_, ...), custom_call_target="tpu_custom_call" | custom-call | flops 4000000000 | bytes 12000000 | tf_op jit(solution)/shard_map/bucket/pallas_call | solution.py:521
  25.6 9.6 %last.1 = (s16[16,288,128]{2,1,0:T(8,128)(2,1)S(1)}, bf16[800,1024]{1,0:T(8,128)(2,1)S(1)}, bf16[800,1024]{1,0:T(8,128)(2,1)S(1)}, bf16[800,2048]{1,0:T(8,128)(2,1)S(1)}) custom-call(s32[4,8,128]{2,1,0:T(8,128)S(1)} %get-tuple-element.46.refs_0_, s32[4,8,128]{2,1,0:T(8,128)S(1)} %collective-permute-done.3.refs_0_.refs_1_, ...), custom_call_target="tpu_custom_call" | custom-call | flops 8999999488 | bytes 27000000 | tf_op jit(solution)/shard_map/last/pallas_call | solution.py:521
  35.4 3.7 %home.1.refs_0_ = f32[16,280,128]{2,1,0:T(8,128)S(1)} custom-call(s32[4,8,128]{2,1,0:T(8,128)S(1)} %get-tuple-element.46.refs_0_, s32[4,8,128]{2,1,0:T(8,128)S(1)} %collective-permute-done.3.refs_0_.refs_1_, bf16[800,1024]{1,0:T(8,128)(2,1)S(1)} %get-tuple-element.55.refs_2_, bf16[800,1024]{1,0:T(8,128)(2,1)S(1)} %get-tuple-element.56.refs_3_, ...), custom_call_target="tpu_custom_call" | custom-call | flops 4000000000 | bytes 12000000 | tf_op jit(solution)/shard_map/home/pallas_call | solution.py:521
  43.2 2.0 %target.1 = (s16[416,256]{1,0:T(8,128)(2,1)S(1)}, s16[416,256]{1,0:T(8,128)(2,1)S(1)}) custom-call(s32[4,8,128]{2,1,0:T(8,128)S(1)} %get-tuple-element.46.refs_0_, s32[4,8,128]{2,1,0:T(8,128)S(1)} %collective-permute-done.3.refs_0_.refs_1_, bf16[800,2048]{1,0:T(8,128)(2,1)S(1)} %get-tuple-element.57.refs_4_.refs_2_, ...), custom_call_target="tpu_custom_call" | custom-call | flops 1800000000 | bytes 5400000 | tf_op jit(solution)/shard_map/target/pallas_call | solution.py:521
  49.5 6.9 %collective-permute-done.8.refs_2_ = s16[4,288,128]{2,1,0:T(8,128)(2,1)S(1)} collective-permute-done((s16[4,288,128]{2,1,0:T(8,128)(2,1)S(1)}, s16[4,288,128]{2,1,0:T(8,128)(2,1)S(1)}, u32[]{:S(2)}, u32[]{:S(2)}) %collective-permute-start.8) | collective-permute-done | bytes 294944 | tf_op jit(solution)/shard_map/ppermute | solution.py:187
  57.0 2.4 %collective-permute-start.15 = (s16[2,416,256]{2,1,0:T(8,128)(2,1)S(1)}, s16[2,416,256]{2,1,0:T(8,128)(2,1)S(1)}, u32[]{:S(2)}, u32[]{:S(2)}) collective-permute-start(s16[2,416,256]{2,1,0:T(8,128)(2,1)S(1)} %get-tuple-element.70), channel_id=1, source_target_pairs={{0,1},{1,0},{2,3},{3,2},{4,5},{5,4},{6,7},{7,6},{8,9},{9,8},{10,11... | collective-permute-start | bytes 1277960 | tf_op jit(solution)/shard_map/ppermute | solution.py:187
  59.4 2.2 %collective-permute-start.13 = (s16[1,288,128]{2,1,0:T(8,128)(2,1)S(1)}, s16[1,288,128]{2,1,0:T(8,128)(2,1)S(1)}, u32[]{:S(2)}, u32[]{:S(2)}) collective-permute-start(s16[1,288,128]{2,1,0:T(8,128)(2,1)S(1)} %get-tuple-element.67), channel_id=1, source_target_pairs={{0,16},{1,17},{2,18},{3,19},{4,20},{5,21},{6,22},{7,23},{8,24},{9,... | collective-permute-start | bytes 221192 | tf_op jit(solution)/shard_map/ppermute | solution.py:187
  61.6 2.2 %collective-permute-start.14 = (s16[1,288,128]{2,1,0:T(8,128)(2,1)S(1)}, s16[1,288,128]{2,1,0:T(8,128)(2,1)S(1)}, u32[]{:S(2)}, u32[]{:S(2)}) collective-permute-start(s16[1,288,128]{2,1,0:T(8,128)(2,1)S(1)} %get-tuple-element.68), channel_id=1, source_target_pairs={{0,24},{1,25},{2,26},{3,27},{4,28},{5,29},{6,30},{7,31},{8,16},{9,... | collective-permute-start | bytes 221192 | tf_op jit(solution)/shard_map/ppermute | solution.py:187
  64.8 3.8 %collective-permute-done.13.refs_2_ = s16[1,288,128]{2,1,0:T(8,128)(2,1)S(1)} collective-permute-done((s16[1,288,128]{2,1,0:T(8,128)(2,1)S(1)}, s16[1,288,128]{2,1,0:T(8,128)(2,1)S(1)}, u32[]{:S(2)}, u32[]{:S(2)}) %collective-permute-start.13) | collective-permute-done | bytes 73760 | tf_op jit(solution)/shard_map/ppermute | solution.py:187
  68.9 2.7 %collective-permute-start.19 = (s16[2,416,128]{2,1,0:T(8,128)(2,1)S(1)}, s16[2,416,128]{2,1,0:T(8,128)(2,1)S(1)}, u32[]{:S(2)}, u32[]{:S(2)}) collective-permute-start(s16[2,416,128]{2,1,0:T(8,128)(2,1)S(1)} %get-tuple-element.73), channel_id=1, source_target_pairs={{0,2},{1,3},{2,0},{3,1},{4,6},{5,7},{6,4},{7,5},{8,10},{9,11},{10,... | collective-permute-start | bytes 638984 | tf_op jit(solution)/shard_map/ppermute | solution.py:187
  74.2 1.7 %collective-permute-start.18 = (s16[1,288,128]{2,1,0:T(8,128)(2,1)S(1)}, s16[1,288,128]{2,1,0:T(8,128)(2,1)S(1)}, u32[]{:S(2)}, u32[]{:S(2)}) collective-permute-start(s16[1,288,128]{2,1,0:T(8,128)(2,1)S(1)} %get-tuple-element.71.refs_0_), channel_id=1, source_target_pairs={{0,24},{1,25},{2,26},{3,27},{4,28},{5,29},{6,30},{7,31},{8,16},{9,... | collective-permute-start | bytes 221192 | tf_op jit(solution)/shard_map/ppermute | solution.py:187
  76.2 5.0 %collective-permute-done.17.refs_2_ = s16[1,288,128]{2,1,0:T(8,128)(2,1)S(1)} collective-permute-done((s16[1,288,128]{2,1,0:T(8,128)(2,1)S(1)}, s16[1,288,128]{2,1,0:T(8,128)(2,1)S(1)}, u32[]{:S(2)}, u32[]{:S(2)}) %collective-permute-start.17) | collective-permute-done | bytes 73760 | tf_op jit(solution)/shard_map/ppermute | solution.py:187
  83.0 1.9 %collective-permute-start.29 = (s16[4,288,128]{2,1,0:T(8,128)(2,1)S(1)}, s16[4,288,128]{2,1,0:T(8,128)(2,1)S(1)}, u32[]{:S(2)}, u32[]{:S(2)}) collective-permute-start(s16[4,288,128]{2,1,0:T(8,128)(2,1)S(1)} %get-tuple-element.76.refs_0_), channel_id=1, source_target_pairs={{0,6},{1,7},{2,4},{3,5},{4,2},{5,3},{6,0},{7,1},{8,14},{9,15},{10,... | collective-permute-start | bytes 884744 | tf_op jit(solution)/shard_map/ppermute | solution.py:187
  86.2 10.2 %collective-permute-done.20.refs_1_ = s16[416,128]{1,0:T(8,128)(2,1)S(1)} collective-permute-done((s16[416,128]{1,0:T(8,128)(2,1)S(1)}, s16[416,128]{1,0:T(8,128)(2,1)S(1)}, u32[]{:S(2)}, u32[]{:S(2)}) %collective-permute-start.20) | collective-permute-done | bytes 106528 | tf_op jit(solution)/shard_map/ppermute | solution.py:187
  98.1 3.2 %collective-permute-done.22.refs_2_ = s16[416,128]{1,0:T(8,128)(2,1)S(1)} collective-permute-done((s16[416,128]{1,0:T(8,128)(2,1)S(1)}, s16[416,128]{1,0:T(8,128)(2,1)S(1)}, u32[]{:S(2)}, u32[]{:S(2)}) %collective-permute-start.22) | collective-permute-done | bytes 106528 | tf_op jit(solution)/shard_map/ppermute | solution.py:187
  102.3 1.7 %spread.2 = (f32[400,2560]{1,0:T(8,128)}, f32[400,256]{1,0:T(8,128)}) custom-call(s32[1]{0:T(128)} %bitcast.6.side, s16[4,288,128]{2,1,0:T(8,128)(2,1)S(1)} %get-tuple-element.76.refs_0_, s16[4,288,128]{2,1,0:T(8,128)(2,1)S(1)} %collective-permute-done.25.refs_1_, s16[4,288,128]{2,1,0:T(8,128)(2,1)S(1)} %collective-permute-done.27.refs_2_, ...), custom_call_target="tpu_custom_call" | custom-call | flops 2000000000 | bytes 6000000 | tf_op jit(solution)/shard_map/spread/pallas_call | solution.py:521
  105.3 1.7 %spread.3 = (f32[400,2560]{1,0:T(8,128)}, f32[400,256]{1,0:T(8,128)}) custom-call(s32[1]{0:T(128)} %bitcast.5.side, s16[4,288,128]{2,1,0:T(8,128)(2,1)S(1)} %collective-permute-done.24.refs_0_, s16[4,288,128]{2,1,0:T(8,128)(2,1)S(1)} %collective-permute-done.26.refs_1_, ...), custom_call_target="tpu_custom_call", output_to_operand_aliasing={{0}: (5, {}), {1}: (6, {})} | custom-call | flops 2000000000 | bytes 6000000 | tf_op jit(solution)/shard_map/spread/pallas_call | solution.py:521
  (64 shorter events, 24.4 us)
Async XLA Ops:
  0.6 20.9 %collective-permute-start.4 = (bf16[400,512]{1,0:T(8,128)(2,1)}, bf16[400,512]{1,0:T(8,128)(2,1)S(1)}, u32[]{:S(2)}, u32[]{:S(2)}) collective-permute-start(bf16[400,512]{1,0:T(8,128)(2,1)} %bitcast.9), channel_id=1, source_target_pairs={{0,0},{1,17},{2,10},{3,27},{4,4},{5,21},{6,14},{7,31},{8,8},{9,25}... | collective-permute-start | bytes 1228808 | tf_op jit(solution)/shard_map/ppermute | solution.py:187
  2.3 18.5 %collective-permute-start.5 = (bf16[400,512]{1,0:T(8,128)(2,1)}, bf16[400,512]{1,0:T(8,128)(2,1)S(1)}, u32[]{:S(2)}, u32[]{:S(2)}) collective-permute-start(bf16[400,512]{1,0:T(8,128)(2,1)} %bitcast.10), channel_id=1, source_target_pairs={{0,4},{1,5},{2,6},{3,7},{4,0},{5,1},{6,2},{7,3},{8,12},{9,13},{10,... | collective-permute-start | bytes 1228808 | tf_op jit(solution)/shard_map/ppermute | solution.py:187
  6.7 7.6 %collective-permute-start = (s32[2,8,128]{2,1,0:T(8,128)}, s32[2,8,128]{2,1,0:T(8,128)S(1)}, u32[]{:S(2)}, u32[]{:S(2)}) collective-permute-start(s32[2,8,128]{2,1,0:T(8,128)} %get-tuple-element.43), channel_id=1, source_target_pairs={{0,1},{1,0},{2,3},{3,2},{4,5},{5,4},{6,7},{7,6},{8,9},{9,8},{10,11... | collective-permute-start | bytes 24584 | tf_op jit(solution)/shard_map/ppermute | solution.py:187
  8.9 5.4 %collective-permute-start.1 = (s32[2,8,128]{2,1,0:T(8,128)}, s32[2,8,128]{2,1,0:T(8,128)S(1)}, u32[]{:S(2)}, u32[]{:S(2)}) collective-permute-start(s32[2,8,128]{2,1,0:T(8,128)} %get-tuple-element.44), channel_id=1, source_target_pairs={{0,2},{1,3},{2,0},{3,1},{4,6},{5,7},{6,4},{7,5},{8,10},{9,11},{10,... | collective-permute-start | bytes 24584 | tf_op jit(solution)/shard_map/ppermute | solution.py:187
  35.3 3.7 %collective-permute-start.6 = (s16[16,288,128]{2,1,0:T(8,128)(2,1)S(1)}, s16[16,288,128]{2,1,0:T(8,128)(2,1)S(1)}, u32[]{:S(2)}, u32[]{:S(2)}) collective-permute-start(s16[16,288,128]{2,1,0:T(8,128)(2,1)S(1)} %get-tuple-element.58.refs_5_), channel_id=1, source_target_pairs={{0,1},{1,0},{2,3},{3,2},{4,5},{5,4},{6,7},{7,6},{8,9},{9,8},{10,11... | collective-permute-start | bytes 3538952 | tf_op jit(solution)/shard_map/ppermute | solution.py:187
  39.6 9.9 %collective-permute-start.7 = (s16[4,288,128]{2,1,0:T(8,128)(2,1)S(1)}, s16[4,288,128]{2,1,0:T(8,128)(2,1)S(1)}, u32[]{:S(2)}, u32[]{:S(2)}) collective-permute-start(s16[4,288,128]{2,1,0:T(8,128)(2,1)S(1)} %get-tuple-element.60), channel_id=1, source_target_pairs={{0,2},{1,3},{2,0},{3,1},{4,6},{5,7},{6,4},{7,5},{8,10},{9,11},{10,... | collective-permute-start | bytes 884744 | tf_op jit(solution)/shard_map/ppermute | solution.py:187
  41.1 15.3 %collective-permute-start.8 = (s16[4,288,128]{2,1,0:T(8,128)(2,1)S(1)}, s16[4,288,128]{2,1,0:T(8,128)(2,1)S(1)}, u32[]{:S(2)}, u32[]{:S(2)}) collective-permute-start(s16[4,288,128]{2,1,0:T(8,128)(2,1)S(1)} %get-tuple-element.61), channel_id=1, source_target_pairs={{0,4},{1,5},{2,6},{3,7},{4,0},{5,1},{6,2},{7,3},{8,12},{9,13},{10,... | collective-permute-start | bytes 884744 | tf_op jit(solution)/shard_map/ppermute | solution.py:187
  42.5 13.9 %collective-permute-start.9 = (s16[4,288,128]{2,1,0:T(8,128)(2,1)S(1)}, s16[4,288,128]{2,1,0:T(8,128)(2,1)S(1)}, u32[]{:S(2)}, u32[]{:S(2)}) collective-permute-start(s16[4,288,128]{2,1,0:T(8,128)(2,1)S(1)} %get-tuple-element.62), channel_id=1, source_target_pairs={{0,6},{1,7},{2,4},{3,5},{4,2},{5,3},{6,0},{7,1},{8,14},{9,15},{10,... | collective-permute-start | bytes 884744 | tf_op jit(solution)/shard_map/ppermute | solution.py:187
  57.0 11.6 %collective-permute-start.15 = (s16[2,416,256]{2,1,0:T(8,128)(2,1)S(1)}, s16[2,416,256]{2,1,0:T(8,128)(2,1)S(1)}, u32[]{:S(2)}, u32[]{:S(2)}) collective-permute-start(s16[2,416,256]{2,1,0:T(8,128)(2,1)S(1)} %get-tuple-element.70), channel_id=1, source_target_pairs={{0,1},{1,0},{2,3},{3,2},{4,5},{5,4},{6,7},{7,6},{8,9},{9,8},{10,11... | collective-permute-start | bytes 1277960 | tf_op jit(solution)/shard_map/ppermute | solution.py:187
  59.4 5.4 %collective-permute-start.12 = (s16[1,288,128]{2,1,0:T(8,128)(2,1)S(1)}, s16[1,288,128]{2,1,0:T(8,128)(2,1)S(1)}, u32[]{:S(2)}, u32[]{:S(2)}) collective-permute-start(s16[1,288,128]{2,1,0:T(8,128)(2,1)S(1)} %get-tuple-element.66), channel_id=1, source_target_pairs={{0,8},{1,9},{2,10},{3,11},{4,12},{5,13},{6,14},{7,15},{8,0},{9,1},... | collective-permute-start | bytes 221192 | tf_op jit(solution)/shard_map/ppermute | solution.py:187
  59.4 9.2 %collective-permute-start.13 = (s16[1,288,128]{2,1,0:T(8,128)(2,1)S(1)}, s16[1,288,128]{2,1,0:T(8,128)(2,1)S(1)}, u32[]{:S(2)}, u32[]{:S(2)}) collective-permute-start(s16[1,288,128]{2,1,0:T(8,128)(2,1)S(1)} %get-tuple-element.67), channel_id=1, source_target_pairs={{0,16},{1,17},{2,18},{3,19},{4,20},{5,21},{6,22},{7,23},{8,24},{9,... | collective-permute-start | bytes 221192 | tf_op jit(solution)/shard_map/ppermute | solution.py:187
  61.6 7.0 %collective-permute-start.14 = (s16[1,288,128]{2,1,0:T(8,128)(2,1)S(1)}, s16[1,288,128]{2,1,0:T(8,128)(2,1)S(1)}, u32[]{:S(2)}, u32[]{:S(2)}) collective-permute-start(s16[1,288,128]{2,1,0:T(8,128)(2,1)S(1)} %get-tuple-element.68), channel_id=1, source_target_pairs={{0,24},{1,25},{2,26},{3,27},{4,28},{5,29},{6,30},{7,31},{8,16},{9,... | collective-permute-start | bytes 221192 | tf_op jit(solution)/shard_map/ppermute | solution.py:187
  68.9 12.3 %collective-permute-start.19 = (s16[2,416,128]{2,1,0:T(8,128)(2,1)S(1)}, s16[2,416,128]{2,1,0:T(8,128)(2,1)S(1)}, u32[]{:S(2)}, u32[]{:S(2)}) collective-permute-start(s16[2,416,128]{2,1,0:T(8,128)(2,1)S(1)} %get-tuple-element.73), channel_id=1, source_target_pairs={{0,2},{1,3},{2,0},{3,1},{4,6},{5,7},{6,4},{7,5},{8,10},{9,11},{10,... | collective-permute-start | bytes 638984 | tf_op jit(solution)/shard_map/ppermute | solution.py:187
  71.6 4.6 %collective-permute-start.16 = (s16[1,288,128]{2,1,0:T(8,128)(2,1)S(1)}, s16[1,288,128]{2,1,0:T(8,128)(2,1)S(1)}, u32[]{:S(2)}, u32[]{:S(2)}) collective-permute-start(s16[1,288,128]{2,1,0:T(8,128)(2,1)S(1)} %get-tuple-element.71.refs_0_), channel_id=1, source_target_pairs={{0,8},{1,9},{2,10},{3,11},{4,12},{5,13},{6,14},{7,15},{8,0},{9,1},... | collective-permute-start | bytes 221192 | tf_op jit(solution)/shard_map/ppermute | solution.py:187
  73.2 8.0 %collective-permute-start.17 = (s16[1,288,128]{2,1,0:T(8,128)(2,1)S(1)}, s16[1,288,128]{2,1,0:T(8,128)(2,1)S(1)}, u32[]{:S(2)}, u32[]{:S(2)}) collective-permute-start(s16[1,288,128]{2,1,0:T(8,128)(2,1)S(1)} %get-tuple-element.71.refs_0_), channel_id=1, source_target_pairs={{0,16},{1,17},{2,18},{3,19},{4,20},{5,21},{6,22},{7,23},{8,24},{9,... | collective-permute-start | bytes 221192 | tf_op jit(solution)/shard_map/ppermute | solution.py:187
  74.2 7.0 %collective-permute-start.18 = (s16[1,288,128]{2,1,0:T(8,128)(2,1)S(1)}, s16[1,288,128]{2,1,0:T(8,128)(2,1)S(1)}, u32[]{:S(2)}, u32[]{:S(2)}) collective-permute-start(s16[1,288,128]{2,1,0:T(8,128)(2,1)S(1)} %get-tuple-element.71.refs_0_), channel_id=1, source_target_pairs={{0,24},{1,25},{2,26},{3,27},{4,28},{5,29},{6,30},{7,31},{8,16},{9,... | collective-permute-start | bytes 221192 | tf_op jit(solution)/shard_map/ppermute | solution.py:187
  81.3 19.9 %collective-permute-start.25 = (s16[4,288,128]{2,1,0:T(8,128)(2,1)S(1)}, s16[4,288,128]{2,1,0:T(8,128)(2,1)S(1)}, u32[]{:S(2)}, u32[]{:S(2)}) collective-permute-start(s16[4,288,128]{2,1,0:T(8,128)(2,1)S(1)} %get-tuple-element.76.refs_0_), channel_id=1, source_target_pairs={{0,2},{1,3},{2,0},{3,1},{4,6},{5,7},{6,4},{7,5},{8,10},{9,11},{10,... | collective-permute-start | bytes 884744 | tf_op jit(solution)/shard_map/ppermute | solution.py:187
  81.7 20.0 %collective-permute-start.27 = (s16[4,288,128]{2,1,0:T(8,128)(2,1)S(1)}, s16[4,288,128]{2,1,0:T(8,128)(2,1)S(1)}, u32[]{:S(2)}, u32[]{:S(2)}) collective-permute-start(s16[4,288,128]{2,1,0:T(8,128)(2,1)S(1)} %get-tuple-element.76.refs_0_), channel_id=1, source_target_pairs={{0,4},{1,5},{2,6},{3,7},{4,0},{5,1},{6,2},{7,3},{8,12},{9,13},{10,... | collective-permute-start | bytes 884744 | tf_op jit(solution)/shard_map/ppermute | solution.py:187
  83.0 18.8 %collective-permute-start.29 = (s16[4,288,128]{2,1,0:T(8,128)(2,1)S(1)}, s16[4,288,128]{2,1,0:T(8,128)(2,1)S(1)}, u32[]{:S(2)}, u32[]{:S(2)}) collective-permute-start(s16[4,288,128]{2,1,0:T(8,128)(2,1)S(1)} %get-tuple-element.76.refs_0_), channel_id=1, source_target_pairs={{0,6},{1,7},{2,4},{3,5},{4,2},{5,3},{6,0},{7,1},{8,14},{9,15},{10,... | collective-permute-start | bytes 884744 | tf_op jit(solution)/shard_map/ppermute | solution.py:187
  84.9 11.5 %collective-permute-start.20 = (s16[416,128]{1,0:T(8,128)(2,1)S(1)}, s16[416,128]{1,0:T(8,128)(2,1)S(1)}, u32[]{:S(2)}, u32[]{:S(2)}) collective-permute-start(s16[416,128]{1,0:T(8,128)(2,1)S(1)} %get-tuple-element.75), channel_id=1, source_target_pairs={{0,4},{1,5},{2,6},{3,7},{4,0},{5,1},{6,2},{7,3},{8,12},{9,13},{10,... | collective-permute-start | bytes 319496 | tf_op jit(solution)/shard_map/ppermute | solution.py:187
  96.5 4.8 %collective-permute-start.22 = (s16[416,128]{1,0:T(8,128)(2,1)S(1)}, s16[416,128]{1,0:T(8,128)(2,1)S(1)}, u32[]{:S(2)}, u32[]{:S(2)}) collective-permute-start(s16[416,128]{1,0:T(8,128)(2,1)S(1)} %mine.1.refs_0_), channel_id=1, source_target_pairs={{0,2},{1,3},{2,0},{3,1},{4,6},{5,7},{6,4},{7,5},{8,10},{9,11},{10,... | collective-permute-start | bytes 319496 | tf_op jit(solution)/shard_map/ppermute | solution.py:187
  98.1 4.2 %collective-permute-start.21 = (s16[416,128]{1,0:T(8,128)(2,1)S(1)}, s16[416,128]{1,0:T(8,128)(2,1)S(1)}, u32[]{:S(2)}, u32[]{:S(2)}) collective-permute-start(s16[416,128]{1,0:T(8,128)(2,1)S(1)} %mine.1.refs_0_), channel_id=1, source_target_pairs={{0,1},{1,0},{2,3},{3,2},{4,5},{5,4},{6,7},{7,6},{8,9},{9,8},{10,11... | collective-permute-start | bytes 319496 | tf_op jit(solution)/shard_map/ppermute | solution.py:187
  101.2 4.0 %collective-permute-start.24 = (s16[4,288,128]{2,1,0:T(8,128)(2,1)S(1)}, s16[4,288,128]{2,1,0:T(8,128)(2,1)S(1)}, u32[]{:S(2)}, u32[]{:S(2)}) collective-permute-start(s16[4,288,128]{2,1,0:T(8,128)(2,1)S(1)} %get-tuple-element.76.refs_0_), channel_id=1, source_target_pairs={{0,1},{1,0},{2,3},{3,2},{4,5},{5,4},{6,7},{7,6},{8,9},{9,8},{10,11... | collective-permute-start | bytes 884744 | tf_op jit(solution)/shard_map/ppermute | solution.py:187
  101.2 4.0 %collective-permute-start.26 = (s16[4,288,128]{2,1,0:T(8,128)(2,1)S(1)}, s16[4,288,128]{2,1,0:T(8,128)(2,1)S(1)}, u32[]{:S(2)}, u32[]{:S(2)}) collective-permute-start(s16[4,288,128]{2,1,0:T(8,128)(2,1)S(1)} %collective-permute-done.25.refs_1_), channel_id=1, source_target_pairs={{0,1},{1,0},{2,3},{3,2},{4,5},{5,4},{6,7},{7,6},{8,9},{9,8},{10,11... | collective-permute-start | bytes 884744 | tf_op jit(solution)/shard_map/ppermute | solution.py:187
  (10 other events, 28.5 us)

commit v7 on v6

--- a/solution.py
+++ b/solution.py
@@ -298,37 +298,17 @@
     bucket_grads(plan, refs[:1], *refs[1:], 0)
 
 
-def last_kernel(plan, *refs):
-    count = plan.buckets
-    labels = refs[:count]
-    before = refs[count : count + 3 * (plan.buckets - 1)]
-    refs = refs[count + 3 * (plan.buckets - 1) :]
-    target, lhs_in, rel_in, rem_in = refs[:4]
-    away, refs = refs[4 : 4 + len(plan.parts)], refs[4 + len(plan.parts) :]
-    outs, helds, table, sems = refs[:3], refs[3:6], refs[6], refs[7]
-    edges = plan.bucket_edges
-    loads = []
+def last_kernel(plan, after, *refs):
+    labels, refs = refs[: plan.buckets], refs[plan.buckets :]
+    before, refs = refs[: 3 * (plan.buckets - 1)], refs[3 * (plan.buckets - 1) :]
+    inputs, refs = refs[:4], refs[4 + after :]
+    away, outs, table = refs[: len(plan.parts)], refs[-4:-1], refs[-1]
+    bucket_grads(plan, labels[:1], *inputs, *outs, 0)
     for at, ref in enumerate(before):
-        wide = edges * (2 if at % 3 == 2 else 1)
-        start = (at // 3) * wide
-        loads.append(
-            pltpu.make_async_copy(ref, helds[at % 3].at[:, start : start + wide], sems.at[at])
-        )
-        loads[-1].start()
-    base = (plan.buckets - 1) * plan.slots
-    own_labels = labels[-1:]
-    bucket_grads(plan, own_labels, target, lhs_in, rel_in, rem_in, *helds, base)
-    for load in loads:
-        load.wait()
-    stores = [
-        pltpu.make_async_copy(held, out, sems.at[len(loads) + at])
-        for at, (held, out) in enumerate(zip(helds, outs))
-    ]
-    for store in stores:
-        store.start()
-    reduce_half(plan, True, labels, helds, table, away)
-    for store in stores:
-        store.wait()
+        wide = ref.shape[1]
+        start = (at // 3 + 1) * wide
+        outs[at % 3][:, start : start + wide] = ref[...]
+    reduce_half(plan, True, labels, outs, table, away)
 
 
 def reduce_half(plan, away, labels, grads, table, outs):
@@ -379,63 +359,62 @@
     reduce_half(plan, False, refs[:count], refs[count : count + 3], refs[-1], refs[-1 - len(plan.parts) : -1])
 
 
-def source_sum(plan, labels, grads, bucket):
-    start = bucket * plan.bucket_edges
-    ids = plan.row(labels, bucket, (0,), 0, plan.slots)
-    return rows_sum(plan, ids, grads[:, start : start + plan.bucket_edges])
-
-
-def deal(plan, value, bucket, outs):
-    keep, away = outs
+def source_sum(plan, labels, grads):
+    return rows_sum(plan, plan.row([labels], 0, (0,), 0, plan.slots), grads)
+
+
+def deal(plan, value, keep, away):
     lanes = plan.part_lanes
     for at in range(value.shape[1] // lanes):
         share = value[:, at * lanes : (at + 1) * lanes]
         to = slice(at // 2 * lanes, (at // 2 + 1) * lanes)
         if at % 2:
-            away[bucket, :, to] = pack_table(share)
+            away[:, to] = pack_table(share)
         else:
-            keep[bucket, :, to] = share
-
-
-def sources_kernel(plan, *refs):
-    out = refs[-1]
-    for bucket in range(plan.buckets):
-        out[bucket] = source_sum(plan, refs[: plan.buckets], refs[plan.buckets], bucket)
-
-
-def share(plan, sources, *refs):
-    far, outs = refs[:-2], refs[-2:]
-    for bucket in range(plan.buckets):
-        value = sources[bucket]
-        if bucket == 0:
-            value = value + jnp.concatenate([unpack_table(ref[...]) for ref in far], axis=1)
-        deal(plan, value, bucket, outs)
+            keep[:, to] = share
+
+
+def source_kernel(plan, labels, grads, *outs):
+    deal(plan, source_sum(plan, labels, grads[...]), *outs)
+
+
+def own_source_kernel(plan, *refs):
+    refs[-1][...] = source_sum(plan, refs[0], refs[1][:, : plan.bucket_edges])
+
+
+def share(plan, count, *refs):
+    source, fars, others = refs[0], refs[1:3], refs[3 : 3 + 2 * count]
+    outs = refs[3 + 2 * count :]
+    far = jnp.concatenate([unpack_table(ref[...]) for ref in fars], axis=1)
+    deal(plan, source[...] + far, *outs[:2])
+    for at in range(0, 2 * count, 2):
+        deal_again(plan, *others[at : at + 2], *outs[at + 2 : at + 4])
 
 
 def deal_again(plan, keep, came, *outs):
-    for bucket in range(plan.buckets):
-        deal(plan, keep[bucket] + unpack_table(came[bucket]), bucket, outs)
+    deal(plan, keep[...] + unpack_table(came[...]), *outs)
+
+
+def deal_and_settle(plan, count, *refs):
+    ins, outs = refs[: 2 + 2 * count], refs[2 + 2 * count :]
+    deal_again(plan, *ins[:2], *outs[:2])
+    for at in range(count):
+        add_kernel(2, *ins[2 + 2 * at : 4 + 2 * at], outs[2 + at])
 
 
 def deal_kernel(plan, *refs):
     deal_again(plan, *refs)
 
 
-def settle(plan, keep, came, *outs):
-    for bucket, out in enumerate(outs):
-        value = keep[bucket] + unpack_table(came[bucket])
-        out[...] = pack_table(value) if bucket else value
-
-
-def mine_kernel(plan, *refs):
+def add_kernel(count, *refs):
     value = refs[0][...]
-    for ref in refs[1 : plan.buckets]:
+    for ref in refs[1:count]:
         value = value + unpack_table(ref[...])
     refs[-1][...] = pack_table(value)
 
 
-def combine_kernel(plan, arrivals, sizes, beside, *refs):
-    at, out_at = 0, sum(arrivals) + len(arrivals)
+def combine_kernel(plan, arrivals, sizes, beside, after, *refs):
+    at, out_at = 0, sum(arrivals) + len(arrivals) + after
     if beside:
         step, ins, outs = beside
         step(plan, *refs[out_at : out_at + ins], *refs[len(refs) - outs :])
@@ -455,9 +434,9 @@
 
 
 def stack_kernel(plan, counts, *refs):
-    total = sum(counts)
-    outs, refs = refs[total + 2 : total + 2 + len(counts)], refs[: total + 2] + refs[total + 2 + len(counts) :]
-    settle(plan, *refs[total:])
+    outs = refs[-1 - len(counts) : -1]
+    add = refs[sum(counts) : -1 - len(counts)]
+    add_kernel(len(add), *add, refs[-1])
     first = 0
     for count, out in zip(counts, outs):
         for at in range(count):
@@ -605,7 +584,15 @@
     ]
     labels_of = lambda bucket: [labels[bucket]]
     (rel_split,) = call(
-        split_kernel, [shape((2 * width, plan.nrels), BF16)], [rels], "rel_split", 2.0, 50
+        split_kernel,
+        [shape((2 * width, plan.nrels), BF16)],
+        [rels],
+        "rel_split",
+        2.0,
+        50,
+        in_specs=[pl.BlockSpec((width, 4 * LANES), lambda i: (0, i))],
+        out_specs=[pl.BlockSpec((2 * width, 4 * LANES), lambda i: (0, i))],
+        grid=(plan.nrels // (4 * LANES),),
     )
 
     grad_shapes = lambda count: [
@@ -632,9 +619,14 @@
             12 * grow,
         )
         inputs.append([lhs, vec, cand_rem])
-    grads = []
-    for bucket in range(buckets - 1):
-        grads += call(
+    lanes = plan.part_lanes
+    dealt = lambda count: [
+        shape((width, count * lanes), F32),
+        shape((width + 16, count * lanes), i16),
+    ]
+    grads, others = [], []
+    for bucket in range(1, buckets):
+        made = call(
             functools.partial(bucket_kernel, plan),
             grad_shapes(wide),
             labels_of(bucket) + [target] + inputs[bucket],
@@ -642,23 +634,32 @@
             4.0,
             16 * grow,
         )
+        grads += made
+        others.append(
+            call(
+                functools.partial(source_kernel, plan),
+                dealt(plan.rels // 2),
+                labels_of(bucket) + [made[0]],
+                "source",
+                0.8,
+                12 * grow,
+            )
+        )
     table = [pltpu.VMEM((width, plan.half_lanes), F32)]
-    made = call(
-        functools.partial(last_kernel, plan),
+    made = after(
+        functools.partial(last_kernel, plan, len(others)),
         [shape(part.packed, i16) for part in plan.parts] + grad_shapes(edges),
-        labels + grads + [target] + inputs[-1],
+        labels + grads + [target] + inputs[0],
+        [other[0] for other in others],
         "last",
         9.0,
-        24 * grow,
-        in_specs=[VMEM] * len(labels) + [ANY] * len(grads) + [VMEM] * 4,
-        out_specs=[VMEM] * len(plan.parts) + [ANY] * 3,
-        scratch=[pltpu.VMEM(held.shape, BF16) for held in grad_shapes(edges)]
-        + table
-        + [pltpu.SemaphoreType.DMA((len(grads) + 3,))],
-    )
-    away, grads = made[: len(plan.parts)], list(made[len(plan.parts) :])
+        20 * grow,
+        scratch=table,
+    )
+    away, grads = list(made[: len(plan.parts)]), list(made[len(plan.parts) :])
     cores = [send(value, plan, lambda d: d ^ 1) for value in away]
 
+    others = [[keep, send(value, plan, lambda d: d ^ 1)] for keep, value in others]
     keeps = after(
         functools.partial(home_kernel, plan),
         [shape(part.bare, F32) for part in plan.parts],
@@ -670,7 +671,7 @@
         scratch=table,
     )
 
-    def combine(keeps, arrived, level, name, step=None, step_args=(), step_outs=()):
+    def combine(keeps, arrived, level, name, step=None, step_args=(), step_outs=(), order=()):
         sizes = [len(part.masks[level]) if level < 2 else 1 for part in plan.parts]
         outs, args = [], []
         for part, keep, pieces, size in zip(plan.parts, keeps, arrived, sizes):
@@ -682,10 +683,10 @@
         beside = (step, len(step_args), len(step_outs)) if step else None
         count = [len(pieces) for pieces in arrived]
         made = after(
-            functools.partial(combine_kernel, plan, count, sizes, beside),
+            functools.partial(combine_kernel, plan, count, sizes, beside, len(order)),
             outs + list(step_outs),
             args + list(step_args),
-            [],
+            order,
             name,
             0.6,
         )
@@ -699,7 +700,9 @@
             arrived.append(exchanged(group[1:], part.masks[level]))
         return keeps, arrived, beside
 
-    keeps, arrived, _ = combine(keeps, [[core] for core in cores], 0, "combine_cores")
+    keeps, arrived, _ = combine(
+        keeps, [[core] for core in cores], 0, "combine_cores", order=[other[1] for other in others]
+    )
     far = after(
         functools.partial(target_kernel, plan),
         [shape((width + 16, prows // 2), i16)] * 2,
@@ -709,37 +712,52 @@
         1.8,
         16 * grow,
     )
-    (sources,) = after(
-        functools.partial(sources_kernel, plan),
-        [shape((buckets, width, prows), F32)],
-        labels + [grads[0]],
+    (source,) = after(
+        functools.partial(own_source_kernel, plan),
+        [shape((width, prows), F32)],
+        labels_of(0) + [grads[0]],
         [far[0]],
-        "sources",
-        1.5,
+        "own_source",
+        0.8,
         16 * grow,
     )
     far = [send(value, plan, afar) for value in far]
-    lanes = plan.part_lanes
-    count, bit = plan.rels // 2, 1
-    dealt = lambda count: [
-        shape((buckets, width, count * lanes), F32),
-        shape((buckets, width + 16, count * lanes), i16),
+    def deal_on(pairs, count, bit):
+        while count > 2:
+            count, bit = count // 2, bit * 2
+            made = [
+                after(functools.partial(deal_kernel, plan), dealt(count), pair, [], "deal", 0.3)
+                for pair in pairs
+            ]
+            pairs = [[keep, send(value, plan, lambda d, m=bit: d ^ m)] for keep, value in made]
+        return pairs, count // 2, bit * 2
+
+    others, count, bit = deal_on(others, plan.rels // 2, 1)
+    keeps, arrived, made = combine(
+        keeps,
+        arrived,
+        1,
+        "combine_first",
+        lambda plan, *refs: share(plan, len(others), *refs),
+        [source] + far + sum(others, []),
+        dealt(plan.rels // 2) + dealt(count) * len(others),
+    )
+    mine = [[made[0], send(made[1], plan, lambda d: d ^ 1)]]
+    others = [
+        [made[at], send(made[at + 1], plan, lambda d: d ^ bit)] for at in range(2, len(made), 2)
     ]
-    keeps, arrived, (mine, away) = combine(
-        keeps, arrived, 1, "combine_first", share, [sources] + far, dealt(count)
-    )
-    came = send(away, plan, lambda d: d ^ 1)
-    while count > 2:
-        count, bit = count // 2, bit * 2
-        mine, away = after(
-            functools.partial(deal_kernel, plan), dealt(count), [mine, came], [], "deal", 0.3
-        )
-        came = send(away, plan, lambda d, m=bit: d ^ m)
-    count, bit = count // 2, bit * 2
-    totals, _, (mine, away) = combine(
-        keeps, arrived, 2, "combine_last", deal_again, [mine, came], dealt(count)
-    )
-    came = send(away, plan, lambda d: d ^ bit)
+    (mine,), count, bit = deal_on(mine, plan.rels // 2, 1)
+    totals, _, made = combine(
+        keeps,
+        arrived,
+        2,
+        "combine_last",
+        lambda plan, *refs: deal_and_settle(plan, len(others), *refs),
+        mine + sum(others, []),
+        dealt(count) + [shape((width + 16, lanes), i16)] * len(others),
+    )
+    mine, came = made[0], send(made[1], plan, lambda d: d ^ bit)
+    crossing = exchanged(made[2:], range(0, plan.rels * buckets, plan.rels))
     pieces = [
         [total] + exchanged([total] * (len(part.masks[1]) - 1), part.masks[1])
         for part, total in zip(plan.parts, totals)
@@ -751,28 +769,17 @@
             shape((len(group),) + part.packed[1:], i16)
             for part, group in zip(plan.parts, pieces)
         ]
-        + [shape((width, lanes), F32)]
-        + [shape((width + 16, lanes), i16)] * (buckets - 1),
-        flat + [mine, came],
+        + [shape((width + 16, lanes), i16)],
+        flat + [mine, came] + crossing,
         [],
         "stack",
         0.5,
     )
-    blocks, made = made[: len(plan.parts)], made[len(plan.parts) :]
+    blocks, owners = made[:-1], {0: made[-1]}
     pieces = [
         [block] + exchanged([block] * (len(part.masks[0]) - 1), part.masks[0])
         for part, block in zip(plan.parts, blocks)
     ]
-    mine = [made[0]] + exchanged(made[1:], range(0, plan.rels * buckets, plan.rels))
-    (owner,) = call(
-        functools.partial(mine_kernel, plan),
-        [shape((width + 16, lanes), i16)],
-        mine,
-        "mine",
-        0.3,
-        12,
-    )
-    owners = {0: owner}
     while bit:
         for mask in sorted(owners):
             owners[mask | bit] = send(owners[mask], plan, lambda d, m=bit: d ^ m)

time: 108 us -> 104 us (0.963)
  waiting for transfers between devices: 32.9 us -> 28.5 us
  starting transfers between devices: 36.4 us -> 37.5 us
    ppermute x31 -> x33, waiting for transfers between devices: 32.9 us -> 28.5 us  [send(): return lax.ppermute(value, ('dom', 'rel'), pairs)]
    ppermute x31 -> x33, starting transfers between devices: 36.4 us -> 37.5 us  [send(): return lax.ppermute(value, ('dom', 'rel'), pairs)]
  transfers between devices with their start and end apart: 31 -> 33, of which waited for: 11 -> 10; matrix products, arithmetic and copies ran while one was open for 0% -> 0% of each run, Pallas kernels for 19% -> 20%
where the time goes in v7:
time: 104 us; the launch traced here: 103 us
  starting transfers between devices  37.5 us (36%)
  Pallas kernels  36.3 us (35%)
  waiting for transfers between devices  28.5 us (27%)
    ppermute x33, starting transfers between devices, send(): return lax.ppermute(value, ('dom', 'rel'), pairs)  37.5 us
    pallas_call x20, Pallas kernels, call(): pl.pallas_call(kernel, out_shape=outs, compiler_params=pltpu.CompilerPara...  36.3 us
    ppermute x33, waiting for transfers between devices, send(): return lax.ppermute(value, ('dom', 'rel'), pairs)  28.5 us
  transfers between devices with their start and end apart: 33, of which 10 were waited for; matrix products, arithmetic and copies ran while one was open for 0% of the time, Pallas kernels for 20%

profile of v7, /device:TPU:0, one launch (start us, length us, event | category | flops | bytes accessed | tf_op | source)
XLA Modules:
  0.0 103.2 jit_solution(1101911014278296050)
XLA Ops:
  0.6 3.0 %collective-permute-start.5 = (bf16[400,512]{1,0:T(8,128)(2,1)}, bf16[400,512]{1,0:T(8,128)(2,1)S(1)}, u32[]{:S(2)}, u32[]{:S(2)}) collective-permute-start(bf16[400,512]{1,0:T(8,128)(2,1)} %bitcast.9), channel_id=1, source_target_pairs={{0,4},{1,5},{2,6},{3,7},{4,0},{5,1},{6,2},{7,3},{8,12},{9,13},{10,... | collective-permute-start | bytes 1228808 | tf_op jit(solution)/shard_map/ppermute | solution.py:187
  6.8 2.1 %collective-permute-start = (s32[2,8,128]{2,1,0:T(8,128)}, s32[2,8,128]{2,1,0:T(8,128)S(1)}, u32[]{:S(2)}, u32[]{:S(2)}) collective-permute-start(s32[2,8,128]{2,1,0:T(8,128)} %get-tuple-element.47), channel_id=1, source_target_pairs={{0,1},{1,0},{2,3},{3,2},{4,5},{5,4},{6,7},{7,6},{8,9},{9,8},{10,11... | collective-permute-start | bytes 24584 | tf_op jit(solution)/shard_map/ppermute | solution.py:187
  8.9 2.5 %collective-permute-start.1 = (s32[2,8,128]{2,1,0:T(8,128)}, s32[2,8,128]{2,1,0:T(8,128)S(1)}, u32[]{:S(2)}, u32[]{:S(2)}) collective-permute-start(s32[2,8,128]{2,1,0:T(8,128)} %get-tuple-element.48), channel_id=1, source_target_pairs={{0,2},{1,3},{2,0},{3,1},{4,6},{5,7},{6,4},{7,5},{8,10},{9,11},{10,... | collective-permute-start | bytes 24584 | tf_op jit(solution)/shard_map/ppermute | solution.py:187
  11.4 4.0 %rel_split.1.refs_1_ = bf16[800,2560]{1,0:T(8,128)(2,1)S(1)} custom-call(f32[400,2560]{1,0:T(8,128)} %bitcast.14), custom_call_target="tpu_custom_call" | custom-call | flops 2000000000 | bytes 6000000 | tf_op jit(solution)/shard_map/rel_split/pallas_call | solution.py:500
  16.1 2.3 %relation.3.refs_7_ = f32[400,512]{1,0:T(8,128)S(1)} custom-call(s32[4,8,128]{2,1,0:T(8,128)S(1)} %get-tuple-element.50.refs_0_, bf16[800,2560]{1,0:T(8,128)(2,1)S(1)} %rel_split.1.refs_1_), custom_call_target="tpu_custom_call" | custom-call | flops 2000000000 | bytes 6000000 | tf_op jit(solution)/shard_map/relation/pallas_call | solution.py:500
  19.3 2.3 %relation.2.refs_3_ = f32[400,512]{1,0:T(8,128)S(1)} custom-call(s32[4,8,128]{2,1,0:T(8,128)S(1)} %collective-permute-done.3.refs_0_.labels.refs_1_, bf16[800,2560]{1,0:T(8,128)(2,1)S(1)} %rel_split.1.refs_1_), custom_call_target="tpu_custom_call" | custom-call | flops 2000000000 | bytes 6000000 | tf_op jit(solution)/shard_map/relation/pallas_call | solution.py:500
  22.3 4.1 %bucket.1 = (bf16[800,512]{1,0:T(8,128)(2,1)S(1)}, bf16[800,512]{1,0:T(8,128)(2,1)S(1)}, bf16[800,1024]{1,0:T(8,128)(2,1)S(1)}) custom-call(s32[4,8,128]{2,1,0:T(8,128)S(1)} %collective-permute-done.3.refs_0_.labels.refs_1_, bf16[400,512]{1,0:T(8,128)(2,1)S(1)} %collective-permute-done.4.refs_1_.refs_5_, f32[400,512]{1,0:T(8,128)S(1)} %get-tuple-element.52.refs_2_, ...), custom_call_target="tpu_custom_call" | custom-call | flops 4000000000 | bytes 12000000 | tf_op jit(solution)/shard_map/bucket/pallas_call | solution.py:500
  27.1 7.9 %last.1 = (s16[16,288,128]{2,1,0:T(8,128)(2,1)S(1)}, bf16[800,1024]{1,0:T(8,128)(2,1)S(1)}, bf16[800,1024]{1,0:T(8,128)(2,1)S(1)}, bf16[800,2048]{1,0:T(8,128)(2,1)S(1)}) custom-call(s32[4,8,128]{2,1,0:T(8,128)S(1)} %get-tuple-element.50.refs_0_, s32[4,8,128]{2,1,0:T(8,128)S(1)} %collective-permute-done.3.refs_0_.labels.refs_1_, ...), custom_call_target="tpu_custom_call" | custom-call | flops 8999999488 | bytes 27000000 | tf_op jit(solution)/shard_map/last/pallas_call | solution.py:500
  35.5 3.6 %home.1.refs_0_ = f32[16,280,128]{2,1,0:T(8,128)S(1)} custom-call(s32[4,8,128]{2,1,0:T(8,128)S(1)} %get-tuple-element.50.refs_0_, s32[4,8,128]{2,1,0:T(8,128)S(1)} %collective-permute-done.3.refs_0_.labels.refs_1_, bf16[800,1024]{1,0:T(8,128)(2,1)S(1)} %get-tuple-element.60.refs_2_.refs_1_, bf16[800,1024]{1,0:T(8,128)(2,1)S(1)} %get-tuple-element.61.refs_3_, ...), custom_call_target="tpu_custom_call" | custom-call | flops 4000000000 | bytes 12000000 | tf_op jit(solution)/shard_map/home/pallas_call | solution.py:500
  39.8 2.3 %collective-permute-start.10 = (s16[4,288,128]{2,1,0:T(8,128)(2,1)S(1)}, s16[4,288,128]{2,1,0:T(8,128)(2,1)S(1)}, u32[]{:S(2)}, u32[]{:S(2)}) collective-permute-start(s16[4,288,128]{2,1,0:T(8,128)(2,1)S(1)} %get-tuple-element.68), channel_id=1, source_target_pairs={{0,6},{1,7},{2,4},{3,5},{4,2},{5,3},{6,0},{7,1},{8,14},{9,15},{10,... | collective-permute-start | bytes 884744 | tf_op jit(solution)/shard_map/ppermute | solution.py:187
  43.4 2.0 %target.1 = (s16[416,256]{1,0:T(8,128)(2,1)S(1)}, s16[416,256]{1,0:T(8,128)(2,1)S(1)}) custom-call(s32[4,8,128]{2,1,0:T(8,128)S(1)} %get-tuple-element.50.refs_0_, s32[4,8,128]{2,1,0:T(8,128)S(1)} %collective-permute-done.3.refs_0_.labels.refs_1_, bf16[800,2048]{1,0:T(8,128)(2,1)S(1)} %get-tuple-element.62.refs_4_.refs_2_, ...), custom_call_target="tpu_custom_call" | custom-call | flops 1800000000 | bytes 5400000 | tf_op jit(solution)/shard_map/target/pallas_call | solution.py:500
  47.4 3.3 %collective-permute-done.10.refs_3_ = s16[4,288,128]{2,1,0:T(8,128)(2,1)S(1)} collective-permute-done((s16[4,288,128]{2,1,0:T(8,128)(2,1)S(1)}, s16[4,288,128]{2,1,0:T(8,128)(2,1)S(1)}, u32[]{:S(2)}, u32[]{:S(2)}) %collective-permute-start.10) | collective-permute-done | bytes 294944 | tf_op jit(solution)/shard_map/ppermute | solution.py:187
  50.7 5.3 %collective-permute-done.8.refs_1_ = s16[4,288,128]{2,1,0:T(8,128)(2,1)S(1)} collective-permute-done((s16[4,288,128]{2,1,0:T(8,128)(2,1)S(1)}, s16[4,288,128]{2,1,0:T(8,128)(2,1)S(1)}, u32[]{:S(2)}, u32[]{:S(2)}) %collective-permute-start.8) | collective-permute-done | bytes 294944 | tf_op jit(solution)/shard_map/ppermute | solution.py:187
  56.7 3.0 %collective-permute-start.16 = (s16[416,256]{1,0:T(8,128)(2,1)S(1)}, s16[416,256]{1,0:T(8,128)(2,1)S(1)}, u32[]{:S(2)}, u32[]{:S(2)}) collective-permute-start(s16[416,256]{1,0:T(8,128)(2,1)S(1)} %get-tuple-element.76), channel_id=1, source_target_pairs={{0,1},{1,0},{2,3},{3,2},{4,5},{5,4},{6,7},{7,6},{8,9},{9,8},{10,11... | collective-permute-start | bytes 638984 | tf_op jit(solution)/shard_map/ppermute | solution.py:187
  59.6 2.5 %collective-permute-start.17 = (s16[416,128]{1,0:T(8,128)(2,1)S(1)}, s16[416,128]{1,0:T(8,128)(2,1)S(1)}, u32[]{:S(2)}, u32[]{:S(2)}) collective-permute-start(s16[416,128]{1,0:T(8,128)(2,1)S(1)} %get-tuple-element.78), channel_id=1, source_target_pairs={{0,2},{1,3},{2,0},{3,1},{4,6},{5,7},{6,4},{7,5},{8,10},{9,11},{10,... | collective-permute-start | bytes 319496 | tf_op jit(solution)/shard_map/ppermute | solution.py:187
  62.1 2.2 %collective-permute-start.14 = (s16[1,288,128]{2,1,0:T(8,128)(2,1)S(1)}, s16[1,288,128]{2,1,0:T(8,128)(2,1)S(1)}, u32[]{:S(2)}, u32[]{:S(2)}) collective-permute-start(s16[1,288,128]{2,1,0:T(8,128)(2,1)S(1)} %get-tuple-element.73), channel_id=1, source_target_pairs={{0,16},{1,17},{2,18},{3,19},{4,20},{5,21},{6,22},{7,23},{8,24},{9,... | collective-permute-start | bytes 221192 | tf_op jit(solution)/shard_map/ppermute | solution.py:187
  64.3 2.2 %collective-permute-start.15 = (s16[1,288,128]{2,1,0:T(8,128)(2,1)S(1)}, s16[1,288,128]{2,1,0:T(8,128)(2,1)S(1)}, u32[]{:S(2)}, u32[]{:S(2)}) collective-permute-start(s16[1,288,128]{2,1,0:T(8,128)(2,1)S(1)} %get-tuple-element.74), channel_id=1, source_target_pairs={{0,24},{1,25},{2,26},{3,27},{4,28},{5,29},{6,30},{7,31},{8,16},{9,... | collective-permute-start | bytes 221192 | tf_op jit(solution)/shard_map/ppermute | solution.py:187
  67.5 3.8 %collective-permute-done.14.refs_2_ = s16[1,288,128]{2,1,0:T(8,128)(2,1)S(1)} collective-permute-done((s16[1,288,128]{2,1,0:T(8,128)(2,1)S(1)}, s16[1,288,128]{2,1,0:T(8,128)(2,1)S(1)}, u32[]{:S(2)}, u32[]{:S(2)}) %collective-permute-start.14) | collective-permute-done | bytes 73760 | tf_op jit(solution)/shard_map/ppermute | solution.py:187
  77.7 4.7 %collective-permute-done.19.refs_2_ = s16[1,288,128]{2,1,0:T(8,128)(2,1)S(1)} collective-permute-done((s16[1,288,128]{2,1,0:T(8,128)(2,1)S(1)}, s16[1,288,128]{2,1,0:T(8,128)(2,1)S(1)}, u32[]{:S(2)}, u32[]{:S(2)}) %collective-permute-start.19) | collective-permute-done | bytes 73760 | tf_op jit(solution)/shard_map/ppermute | solution.py:187
  82.5 1.7 %collective-permute-start.27 = (s16[4,288,128]{2,1,0:T(8,128)(2,1)S(1)}, s16[4,288,128]{2,1,0:T(8,128)(2,1)S(1)}, u32[]{:S(2)}, u32[]{:S(2)}) collective-permute-start(s16[4,288,128]{2,1,0:T(8,128)(2,1)S(1)} %get-tuple-element.84.refs_0_), channel_id=1, source_target_pairs={{0,2},{1,3},{2,0},{3,1},{4,6},{5,7},{6,4},{7,5},{8,10},{9,11},{10,... | collective-permute-start | bytes 884744 | tf_op jit(solution)/shard_map/ppermute | solution.py:187
  86.1 1.7 %collective-permute-start.24 = (s16[416,128]{1,0:T(8,128)(2,1)S(1)}, s16[416,128]{1,0:T(8,128)(2,1)S(1)}, u32[]{:S(2)}, u32[]{:S(2)}) collective-permute-start(s16[416,128]{1,0:T(8,128)(2,1)S(1)} %get-tuple-element.83.refs_0_), channel_id=1, source_target_pairs={{0,2},{1,3},{2,0},{3,1},{4,6},{5,7},{6,4},{7,5},{8,10},{9,11},{10,... | collective-permute-start | bytes 319496 | tf_op jit(solution)/shard_map/ppermute | solution.py:187
  87.8 9.7 %collective-permute-done.24.refs_2_ = s16[416,128]{1,0:T(8,128)(2,1)S(1)} collective-permute-done((s16[416,128]{1,0:T(8,128)(2,1)S(1)}, s16[416,128]{1,0:T(8,128)(2,1)S(1)}, u32[]{:S(2)}, u32[]{:S(2)}) %collective-permute-start.24) | collective-permute-done | bytes 106528 | tf_op jit(solution)/shard_map/ppermute | solution.py:187
  99.8 1.7 %spread.2 = (f32[400,2560]{1,0:T(8,128)}, f32[400,256]{1,0:T(8,128)}) custom-call(s32[1]{0:T(128)} %bitcast.6.side, s16[4,288,128]{2,1,0:T(8,128)(2,1)S(1)} %get-tuple-element.84.refs_0_, s16[4,288,128]{2,1,0:T(8,128)(2,1)S(1)} %collective-permute-done.27.refs_1_, s16[4,288,128]{2,1,0:T(8,128)(2,1)S(1)} %collective-permute-done.29.refs_2_, ...), custom_call_target="tpu_custom_call" | custom-call | flops 2000000000 | bytes 6000000 | tf_op jit(solution)/shard_map/spread/pallas_call | solution.py:500
  101.5 1.7 %spread.3 = (f32[400,2560]{1,0:T(8,128)}, f32[400,256]{1,0:T(8,128)}) custom-call(s32[1]{0:T(128)} %bitcast.5.side, s16[4,288,128]{2,1,0:T(8,128)(2,1)S(1)} %collective-permute-done.26.refs_0_, s16[4,288,128]{2,1,0:T(8,128)(2,1)S(1)} %collective-permute-done.28.refs_1_, ...), custom_call_target="tpu_custom_call", output_to_operand_aliasing={{0}: (5, {}), {1}: (6, {})} | custom-call | flops 2000000000 | bytes 6000000 | tf_op jit(solution)/shard_map/spread/pallas_call | solution.py:500
  (68 shorter events, 22.9 us)
Async XLA Ops:
  0.6 20.9 %collective-permute-start.5 = (bf16[400,512]{1,0:T(8,128)(2,1)}, bf16[400,512]{1,0:T(8,128)(2,1)S(1)}, u32[]{:S(2)}, u32[]{:S(2)}) collective-permute-start(bf16[400,512]{1,0:T(8,128)(2,1)} %bitcast.9), channel_id=1, source_target_pairs={{0,4},{1,5},{2,6},{3,7},{4,0},{5,1},{6,2},{7,3},{8,12},{9,13},{10,... | collective-permute-start | bytes 1228808 | tf_op jit(solution)/shard_map/ppermute | solution.py:187
  3.7 18.6 %collective-permute-start.4 = (bf16[400,512]{1,0:T(8,128)(2,1)}, bf16[400,512]{1,0:T(8,128)(2,1)S(1)}, u32[]{:S(2)}, u32[]{:S(2)}) collective-permute-start(bf16[400,512]{1,0:T(8,128)(2,1)} %bitcast.10), channel_id=1, source_target_pairs={{0,0},{1,17},{2,10},{3,27},{4,4},{5,21},{6,14},{7,31},{8,8},{9,25}... | collective-permute-start | bytes 1228808 | tf_op jit(solution)/shard_map/ppermute | solution.py:187
  6.8 8.6 %collective-permute-start = (s32[2,8,128]{2,1,0:T(8,128)}, s32[2,8,128]{2,1,0:T(8,128)S(1)}, u32[]{:S(2)}, u32[]{:S(2)}) collective-permute-start(s32[2,8,128]{2,1,0:T(8,128)} %get-tuple-element.47), channel_id=1, source_target_pairs={{0,1},{1,0},{2,3},{3,2},{4,5},{5,4},{6,7},{7,6},{8,9},{9,8},{10,11... | collective-permute-start | bytes 24584 | tf_op jit(solution)/shard_map/ppermute | solution.py:187
  8.9 6.5 %collective-permute-start.1 = (s32[2,8,128]{2,1,0:T(8,128)}, s32[2,8,128]{2,1,0:T(8,128)S(1)}, u32[]{:S(2)}, u32[]{:S(2)}) collective-permute-start(s32[2,8,128]{2,1,0:T(8,128)} %get-tuple-element.48), channel_id=1, source_target_pairs={{0,2},{1,3},{2,0},{3,1},{4,6},{5,7},{6,4},{7,5},{8,10},{9,11},{10,... | collective-permute-start | bytes 24584 | tf_op jit(solution)/shard_map/ppermute | solution.py:187
  35.0 4.2 %collective-permute-start.6 = (s16[16,288,128]{2,1,0:T(8,128)(2,1)S(1)}, s16[16,288,128]{2,1,0:T(8,128)(2,1)S(1)}, u32[]{:S(2)}, u32[]{:S(2)}) collective-permute-start(s16[16,288,128]{2,1,0:T(8,128)(2,1)S(1)} %get-tuple-element.63.refs_5_), channel_id=1, source_target_pairs={{0,1},{1,0},{2,3},{3,2},{4,5},{5,4},{6,7},{7,6},{8,9},{9,8},{10,11... | collective-permute-start | bytes 3538952 | tf_op jit(solution)/shard_map/ppermute | solution.py:187
  35.0 4.2 %collective-permute-start.7 = (s16[416,256]{1,0:T(8,128)(2,1)S(1)}, s16[416,256]{1,0:T(8,128)(2,1)S(1)}, u32[]{:S(2)}, u32[]{:S(2)}) collective-permute-start(s16[416,256]{1,0:T(8,128)(2,1)S(1)} %get-tuple-element.64), channel_id=1, source_target_pairs={{0,1},{1,0},{2,3},{3,2},{4,5},{5,4},{6,7},{7,6},{8,9},{9,8},{10,11... | collective-permute-start | bytes 638984 | tf_op jit(solution)/shard_map/ppermute | solution.py:187
  39.8 10.9 %collective-permute-start.10 = (s16[4,288,128]{2,1,0:T(8,128)(2,1)S(1)}, s16[4,288,128]{2,1,0:T(8,128)(2,1)S(1)}, u32[]{:S(2)}, u32[]{:S(2)}) collective-permute-start(s16[4,288,128]{2,1,0:T(8,128)(2,1)S(1)} %get-tuple-element.68), channel_id=1, source_target_pairs={{0,6},{1,7},{2,4},{3,5},{4,2},{5,3},{6,0},{7,1},{8,14},{9,15},{10,... | collective-permute-start | bytes 884744 | tf_op jit(solution)/shard_map/ppermute | solution.py:187
  42.1 13.9 %collective-permute-start.8 = (s16[4,288,128]{2,1,0:T(8,128)(2,1)S(1)}, s16[4,288,128]{2,1,0:T(8,128)(2,1)S(1)}, u32[]{:S(2)}, u32[]{:S(2)}) collective-permute-start(s16[4,288,128]{2,1,0:T(8,128)(2,1)S(1)} %get-tuple-element.66), channel_id=1, source_target_pairs={{0,2},{1,3},{2,0},{3,1},{4,6},{5,7},{6,4},{7,5},{8,10},{9,11},{10,... | collective-permute-start | bytes 884744 | tf_op jit(solution)/shard_map/ppermute | solution.py:187
  42.7 13.4 %collective-permute-start.9 = (s16[4,288,128]{2,1,0:T(8,128)(2,1)S(1)}, s16[4,288,128]{2,1,0:T(8,128)(2,1)S(1)}, u32[]{:S(2)}, u32[]{:S(2)}) collective-permute-start(s16[4,288,128]{2,1,0:T(8,128)(2,1)S(1)} %get-tuple-element.67), channel_id=1, source_target_pairs={{0,4},{1,5},{2,6},{3,7},{4,0},{5,1},{6,2},{7,3},{8,12},{9,13},{10,... | collective-permute-start | bytes 884744 | tf_op jit(solution)/shard_map/ppermute | solution.py:187
  56.7 14.7 %collective-permute-start.16 = (s16[416,256]{1,0:T(8,128)(2,1)S(1)}, s16[416,256]{1,0:T(8,128)(2,1)S(1)}, u32[]{:S(2)}, u32[]{:S(2)}) collective-permute-start(s16[416,256]{1,0:T(8,128)(2,1)S(1)} %get-tuple-element.76), channel_id=1, source_target_pairs={{0,1},{1,0},{2,3},{3,2},{4,5},{5,4},{6,7},{7,6},{8,9},{9,8},{10,11... | collective-permute-start | bytes 638984 | tf_op jit(solution)/shard_map/ppermute | solution.py:187
  59.6 11.7 %collective-permute-start.17 = (s16[416,128]{1,0:T(8,128)(2,1)S(1)}, s16[416,128]{1,0:T(8,128)(2,1)S(1)}, u32[]{:S(2)}, u32[]{:S(2)}) collective-permute-start(s16[416,128]{1,0:T(8,128)(2,1)S(1)} %get-tuple-element.78), channel_id=1, source_target_pairs={{0,2},{1,3},{2,0},{3,1},{4,6},{5,7},{6,4},{7,5},{8,10},{9,11},{10,... | collective-permute-start | bytes 319496 | tf_op jit(solution)/shard_map/ppermute | solution.py:187
  62.1 5.4 %collective-permute-start.13 = (s16[1,288,128]{2,1,0:T(8,128)(2,1)S(1)}, s16[1,288,128]{2,1,0:T(8,128)(2,1)S(1)}, u32[]{:S(2)}, u32[]{:S(2)}) collective-permute-start(s16[1,288,128]{2,1,0:T(8,128)(2,1)S(1)} %get-tuple-element.72), channel_id=1, source_target_pairs={{0,8},{1,9},{2,10},{3,11},{4,12},{5,13},{6,14},{7,15},{8,0},{9,1},... | collective-permute-start | bytes 221192 | tf_op jit(solution)/shard_map/ppermute | solution.py:187
  62.1 9.2 %collective-permute-start.14 = (s16[1,288,128]{2,1,0:T(8,128)(2,1)S(1)}, s16[1,288,128]{2,1,0:T(8,128)(2,1)S(1)}, u32[]{:S(2)}, u32[]{:S(2)}) collective-permute-start(s16[1,288,128]{2,1,0:T(8,128)(2,1)S(1)} %get-tuple-element.73), channel_id=1, source_target_pairs={{0,16},{1,17},{2,18},{3,19},{4,20},{5,21},{6,22},{7,23},{8,24},{9,... | collective-permute-start | bytes 221192 | tf_op jit(solution)/shard_map/ppermute | solution.py:187
  64.3 7.0 %collective-permute-start.15 = (s16[1,288,128]{2,1,0:T(8,128)(2,1)S(1)}, s16[1,288,128]{2,1,0:T(8,128)(2,1)S(1)}, u32[]{:S(2)}, u32[]{:S(2)}) collective-permute-start(s16[1,288,128]{2,1,0:T(8,128)(2,1)S(1)} %get-tuple-element.74), channel_id=1, source_target_pairs={{0,24},{1,25},{2,26},{3,27},{4,28},{5,29},{6,30},{7,31},{8,16},{9,... | collective-permute-start | bytes 221192 | tf_op jit(solution)/shard_map/ppermute | solution.py:187
  71.6 10.8 %collective-permute-start.21 = (s16[416,128]{1,0:T(8,128)(2,1)S(1)}, s16[416,128]{1,0:T(8,128)(2,1)S(1)}, u32[]{:S(2)}, u32[]{:S(2)}) collective-permute-start(s16[416,128]{1,0:T(8,128)(2,1)S(1)} %get-tuple-element.81), channel_id=1, source_target_pairs={{0,2},{1,3},{2,0},{3,1},{4,6},{5,7},{6,4},{7,5},{8,10},{9,11},{10,... | collective-permute-start | bytes 319496 | tf_op jit(solution)/shard_map/ppermute | solution.py:187
  71.8 10.6 %collective-permute-start.22 = (s16[416,128]{1,0:T(8,128)(2,1)S(1)}, s16[416,128]{1,0:T(8,128)(2,1)S(1)}, u32[]{:S(2)}, u32[]{:S(2)}) collective-permute-start(s16[416,128]{1,0:T(8,128)(2,1)S(1)} %get-tuple-element.82), channel_id=1, source_target_pairs={{0,4},{1,5},{2,6},{3,7},{4,0},{5,1},{6,2},{7,3},{8,12},{9,13},{10,... | collective-permute-start | bytes 319496 | tf_op jit(solution)/shard_map/ppermute | solution.py:187
  73.1 4.6 %collective-permute-start.18 = (s16[1,288,128]{2,1,0:T(8,128)(2,1)S(1)}, s16[1,288,128]{2,1,0:T(8,128)(2,1)S(1)}, u32[]{:S(2)}, u32[]{:S(2)}) collective-permute-start(s16[1,288,128]{2,1,0:T(8,128)(2,1)S(1)} %get-tuple-element.79.refs_0_), channel_id=1, source_target_pairs={{0,8},{1,9},{2,10},{3,11},{4,12},{5,13},{6,14},{7,15},{8,0},{9,1},... | collective-permute-start | bytes 221192 | tf_op jit(solution)/shard_map/ppermute | solution.py:187
  74.6 7.8 %collective-permute-start.19 = (s16[1,288,128]{2,1,0:T(8,128)(2,1)S(1)}, s16[1,288,128]{2,1,0:T(8,128)(2,1)S(1)}, u32[]{:S(2)}, u32[]{:S(2)}) collective-permute-start(s16[1,288,128]{2,1,0:T(8,128)(2,1)S(1)} %get-tuple-element.79.refs_0_), channel_id=1, source_target_pairs={{0,16},{1,17},{2,18},{3,19},{4,20},{5,21},{6,22},{7,23},{8,24},{9,... | collective-permute-start | bytes 221192 | tf_op jit(solution)/shard_map/ppermute | solution.py:187
  75.9 6.5 %collective-permute-start.20 = (s16[1,288,128]{2,1,0:T(8,128)(2,1)S(1)}, s16[1,288,128]{2,1,0:T(8,128)(2,1)S(1)}, u32[]{:S(2)}, u32[]{:S(2)}) collective-permute-start(s16[1,288,128]{2,1,0:T(8,128)(2,1)S(1)} %get-tuple-element.79.refs_0_), channel_id=1, source_target_pairs={{0,24},{1,25},{2,26},{3,27},{4,28},{5,29},{6,30},{7,31},{8,16},{9,... | collective-permute-start | bytes 221192 | tf_op jit(solution)/shard_map/ppermute | solution.py:187
  82.5 15.4 %collective-permute-start.27 = (s16[4,288,128]{2,1,0:T(8,128)(2,1)S(1)}, s16[4,288,128]{2,1,0:T(8,128)(2,1)S(1)}, u32[]{:S(2)}, u32[]{:S(2)}) collective-permute-start(s16[4,288,128]{2,1,0:T(8,128)(2,1)S(1)} %get-tuple-element.84.refs_0_), channel_id=1, source_target_pairs={{0,2},{1,3},{2,0},{3,1},{4,6},{5,7},{6,4},{7,5},{8,10},{9,11},{10,... | collective-permute-start | bytes 884744 | tf_op jit(solution)/shard_map/ppermute | solution.py:187
  84.3 13.8 %collective-permute-start.29 = (s16[4,288,128]{2,1,0:T(8,128)(2,1)S(1)}, s16[4,288,128]{2,1,0:T(8,128)(2,1)S(1)}, u32[]{:S(2)}, u32[]{:S(2)}) collective-permute-start(s16[4,288,128]{2,1,0:T(8,128)(2,1)S(1)} %get-tuple-element.84.refs_0_), channel_id=1, source_target_pairs={{0,4},{1,5},{2,6},{3,7},{4,0},{5,1},{6,2},{7,3},{8,12},{9,13},{10,... | collective-permute-start | bytes 884744 | tf_op jit(solution)/shard_map/ppermute | solution.py:187
  84.8 13.7 %collective-permute-start.31 = (s16[4,288,128]{2,1,0:T(8,128)(2,1)S(1)}, s16[4,288,128]{2,1,0:T(8,128)(2,1)S(1)}, u32[]{:S(2)}, u32[]{:S(2)}) collective-permute-start(s16[4,288,128]{2,1,0:T(8,128)(2,1)S(1)} %get-tuple-element.84.refs_0_), channel_id=1, source_target_pairs={{0,6},{1,7},{2,4},{3,5},{4,2},{5,3},{6,0},{7,1},{8,14},{9,15},{10,... | collective-permute-start | bytes 884744 | tf_op jit(solution)/shard_map/ppermute | solution.py:187
  86.1 11.4 %collective-permute-start.24 = (s16[416,128]{1,0:T(8,128)(2,1)S(1)}, s16[416,128]{1,0:T(8,128)(2,1)S(1)}, u32[]{:S(2)}, u32[]{:S(2)}) collective-permute-start(s16[416,128]{1,0:T(8,128)(2,1)S(1)} %get-tuple-element.83.refs_0_), channel_id=1, source_target_pairs={{0,2},{1,3},{2,0},{3,1},{4,6},{5,7},{6,4},{7,5},{8,10},{9,11},{10,... | collective-permute-start | bytes 319496 | tf_op jit(solution)/shard_map/ppermute | solution.py:187
  87.8 9.7 %collective-permute-start.23 = (s16[416,128]{1,0:T(8,128)(2,1)S(1)}, s16[416,128]{1,0:T(8,128)(2,1)S(1)}, u32[]{:S(2)}, u32[]{:S(2)}) collective-permute-start(s16[416,128]{1,0:T(8,128)(2,1)S(1)} %get-tuple-element.83.refs_0_), channel_id=1, source_target_pairs={{0,1},{1,0},{2,3},{3,2},{4,5},{5,4},{6,7},{7,6},{8,9},{9,8},{10,11... | collective-permute-start | bytes 319496 | tf_op jit(solution)/shard_map/ppermute | solution.py:187
  (12 other events, 35.1 us)

commit v8 on v7

--- a/solution.py
+++ b/solution.py
@@ -37,14 +37,8 @@
     return lax.dot_general(left, right, dims, preferred_element_type=F32)
 
 
-def dot3(left, right, dims):
-    left_high, left_low = split(left)
-    right_high, right_low = split(right)
-    return (
-        dot(left_high, right_high, dims)
-        + dot(left_high, right_low, dims)
-        + dot(left_low, right_high, dims)
-    )
+def stacked(parts, axis):
+    return jnp.concatenate(parts, axis=axis)
 
 
 def one_hot(ids, rows, base=0):
@@ -188,7 +182,8 @@
 
 
 def lists_kernel(plan, *refs):
-    tables, counts, outs = refs[:7], refs[7], refs[8:]
+    tables, counts, own, outs = refs[:7], refs[7], refs[8], refs[10:-1]
+    refs[-1][...] = own[...]
     source = lax.axis_index("dom")
     rel = lax.axis_index("rel")
     for mask, out in enumerate(outs):
@@ -278,11 +273,18 @@
         u_vec = complex_product(lhs, vec)
         live = plan.row(labels, 0, (7,), slot, 1).astype(F32)
         positive = jnp.sum(u_vec * rhs, axis=0, keepdims=True)
-        negative = dot3(u_vec, cand, TN)
+        u_high, u_low = split(u_vec)
+        cand_high, cand_low = split(cand)
+        u_both, cand_both = stacked([u_high, u_low], 1), stacked([cand_high, cand_low], 0)
+        negative = dot(u_both, cand_high, TN)
+        negative = negative[:LANES] + negative[LANES:] + dot(u_high, cand_low, TN)
         grad_pos = -jax.nn.sigmoid(-positive) * live
         grad_neg = jax.nn.sigmoid(negative) * keep * live[0:1, 0:1]
-        grad_u = grad_pos * rhs + dot3(cand, grad_neg, NT)
-        from_neg = dot3(u_vec, grad_neg, NN)
+        neg_high, neg_low = split(grad_neg)
+        grad_u = folded(dot(cand_both, neg_high, NT)) + dot(cand_high, neg_low, NT)
+        grad_u = grad_pos * rhs + grad_u
+        from_neg = folded(dot(stacked([u_high, u_low], 0), neg_high, NN))
+        from_neg = from_neg + dot(u_high, neg_low, NN)
         grad_cand = jnp.concatenate(
             [from_neg[:, :LANES] + grad_pos * u_vec, from_neg[:, LANES:]], axis=1
         )
@@ -298,21 +300,36 @@
     bucket_grads(plan, refs[:1], *refs[1:], 0)
 
 
-def last_kernel(plan, after, *refs):
+def last_kernel(plan, *refs):
     labels, refs = refs[: plan.buckets], refs[plan.buckets :]
     before, refs = refs[: 3 * (plan.buckets - 1)], refs[3 * (plan.buckets - 1) :]
-    inputs, refs = refs[:4], refs[4 + after :]
-    away, outs, table = refs[: len(plan.parts)], refs[-4:-1], refs[-1]
-    bucket_grads(plan, labels[:1], *inputs, *outs, 0)
+    inputs, refs = refs[:4], refs[4:]
+    away, rem_part, outs, table = refs[: len(plan.parts)], refs[-5], refs[-4:-1], refs[-1]
+    base = (plan.buckets - 1) * plan.slots
+    bucket_grads(plan, labels[-1:], *inputs, *outs, base)
     for at, ref in enumerate(before):
         wide = ref.shape[1]
-        start = (at // 3 + 1) * wide
+        start = at // 3 * wide
         outs[at % 3][:, start : start + wide] = ref[...]
-    reduce_half(plan, True, labels, outs, table, away)
-
-
-def reduce_half(plan, away, labels, grads, table, outs):
-    lhs_grads, rel_grads, cand_grads = grads
+    lhs_grads, rel_grads, cand_grads = outs
+    first = one_hot(plan.whole_row(labels, (1,)), plan.rems)
+    second = one_hot(plan.whole_row(labels, (4, 6)), plan.rems)
+    rem = folded(dot(lhs_grads[...], first, NT) + dot(cand_grads[...], second, NT))
+    low, high = rem[:, : plan.half_rem], rem[:, plan.half_rem :]
+    core = lax.axis_index("rel") & 1
+    rem_part[...] = jnp.where(core == 0, low, high)
+    table[:, plan.half_rel :] = jnp.where(core == 0, high, low)
+    reduce_half(plan, True, labels, rel_grads, table, away)
+
+
+def home_kernel(plan, *refs):
+    count = plan.buckets
+    outs, table = refs[-1 - len(plan.parts) : -1], refs[-1]
+    table[:, plan.half_rel :] = refs[count + 1][...]
+    reduce_half(plan, False, refs[:count], refs[count], table, outs)
+
+
+def reduce_half(plan, away, labels, rel_grads, table, outs):
     me = plan.me()
     half = (me & 1) ^ (1 if away else 0)
     step = 2 * LANES if plan.half_rel % (2 * LANES) == 0 else LANES
@@ -320,12 +337,6 @@
     for start in range(0, plan.half_rel, step):
         hot = one_hot(ids, step, start)
         table[:, start : start + step] = folded(dot(rel_grads[...], hot, NT))
-    base = half * plan.half_rem
-    first = one_hot(plan.whole_row(labels, (1,)), plan.half_rem, base)
-    second = one_hot(plan.whole_row(labels, (4, 6)), plan.half_rem, base)
-    table[:, plan.half_rel :] = folded(
-        dot(lhs_grads[...], first, NT) + dot(cand_grads[...], second, NT)
-    )
     for chunk in range(plan.half_chunks):
         for which, (part, out) in enumerate(zip(plan.parts, outs)):
             value = jnp.concatenate(
@@ -354,11 +365,6 @@
         out[...] = value[:, at * lanes : (at + 1) * lanes]
 
 
-def home_kernel(plan, *refs):
-    count = plan.buckets
-    reduce_half(plan, False, refs[:count], refs[count : count + 3], refs[-1], refs[-1 - len(plan.parts) : -1])
-
-
 def source_sum(plan, labels, grads):
     return rows_sum(plan, plan.row([labels], 0, (0,), 0, plan.slots), grads)
 
@@ -374,8 +380,10 @@
             keep[:, to] = share
 
 
-def source_kernel(plan, labels, grads, *outs):
-    deal(plan, source_sum(plan, labels, grads[...]), *outs)
+def source_kernel(plan, bucket, *refs):
+    start = bucket * plan.bucket_edges
+    grads = refs[1][:, start : start + plan.bucket_edges]
+    deal(plan, source_sum(plan, refs[0], grads), *refs[-2:])
 
 
 def own_source_kernel(plan, *refs):
@@ -555,21 +563,30 @@
             **more,
         )
 
+    (rel_split,) = call(
+        split_kernel,
+        [shape((2 * width, plan.nrels), BF16)],
+        [rels],
+        "rel_split",
+        2.0,
+        50,
+    )
+    tables = [lhs_rows, lhs_rems, rel_ids, rhs_rows, rhs_rems, neg_rows, neg_rems]
+    *lists, own = call(
+        functools.partial(lists_kernel, plan),
+        [shape((buckets * plan.maxb, 8, LANES), jnp.int32)] * plan.rels
+        + [shape(own.shape, own.dtype)],
+        tables + [counts.reshape(-1), own, rel_split],
+        "lists",
+        0.5,
+        8,
+        in_specs=[VMEM] * 7 + [smem, VMEM, ANY],
+    )
+    lists = [lists[0]] + exchanged(lists[1:], range(plan.rels))
     target = send(own, plan, afar)
     sources = [own] + [
         send(own, plan, lambda d, b=bucket: d ^ (b * plan.rels)) for bucket in range(1, buckets)
     ]
-    tables = [lhs_rows, lhs_rems, rel_ids, rhs_rows, rhs_rems, neg_rows, neg_rems]
-    lists = call(
-        functools.partial(lists_kernel, plan),
-        [shape((buckets * plan.maxb, 8, LANES), jnp.int32)] * plan.rels,
-        tables + [counts.reshape(-1)],
-        "lists",
-        0.5,
-        60,
-        in_specs=[VMEM] * 7 + [smem],
-    )
-    lists = [lists[0]] + exchanged(lists[1:], range(plan.rels))
     labels = call(
         functools.partial(forward_kernel, plan),
         [shape((plan.slots, 8, LANES), jnp.int32)] * buckets,
@@ -583,18 +600,6 @@
         for bucket in range(1, buckets)
     ]
     labels_of = lambda bucket: [labels[bucket]]
-    (rel_split,) = call(
-        split_kernel,
-        [shape((2 * width, plan.nrels), BF16)],
-        [rels],
-        "rel_split",
-        2.0,
-        50,
-        in_specs=[pl.BlockSpec((width, 4 * LANES), lambda i: (0, i))],
-        out_specs=[pl.BlockSpec((2 * width, 4 * LANES), lambda i: (0, i))],
-        grid=(plan.nrels // (4 * LANES),),
-    )
-
     grad_shapes = lambda count: [
         shape((2 * width, count), BF16),
         shape((2 * width, count), BF16),
@@ -624,9 +629,9 @@
         shape((width, count * lanes), F32),
         shape((width + 16, count * lanes), i16),
     ]
-    grads, others = [], []
-    for bucket in range(1, buckets):
-        made = call(
+    grads = []
+    for bucket in range(buckets - 1):
+        grads += call(
             functools.partial(bucket_kernel, plan),
             grad_shapes(wide),
             labels_of(bucket) + [target] + inputs[bucket],
@@ -634,39 +639,42 @@
             4.0,
             16 * grow,
         )
-        grads += made
-        others.append(
-            call(
-                functools.partial(source_kernel, plan),
-                dealt(plan.rels // 2),
-                labels_of(bucket) + [made[0]],
-                "source",
-                0.8,
-                12 * grow,
-            )
-        )
     table = [pltpu.VMEM((width, plan.half_lanes), F32)]
-    made = after(
-        functools.partial(last_kernel, plan, len(others)),
-        [shape(part.packed, i16) for part in plan.parts] + grad_shapes(edges),
-        labels + grads + [target] + inputs[0],
-        [other[0] for other in others],
+    made = call(
+        functools.partial(last_kernel, plan),
+        [shape(part.packed, i16) for part in plan.parts]
+        + [shape((width, plan.half_rem), F32)]
+        + grad_shapes(edges),
+        labels + grads + [target] + inputs[-1],
         "last",
         9.0,
         20 * grow,
         scratch=table,
     )
-    away, grads = list(made[: len(plan.parts)]), list(made[len(plan.parts) :])
+    made, grads = list(made[:-3]), list(made[-3:])
+    away, rem_part = made[:-1], made[-1]
     cores = [send(value, plan, lambda d: d ^ 1) for value in away]
 
-    others = [[keep, send(value, plan, lambda d: d ^ 1)] for keep, value in others]
+    others, order = [], list(away)
+    for bucket in range(1, buckets):
+        keep, value = after(
+            functools.partial(source_kernel, plan, bucket),
+            dealt(plan.rels // 2),
+            labels_of(bucket) + [grads[0]],
+            order,
+            "source",
+            0.8,
+            12 * grow,
+        )
+        others.append([keep, send(value, plan, lambda d: d ^ 1)])
+        order = [keep]
     keeps = after(
         functools.partial(home_kernel, plan),
         [shape(part.bare, F32) for part in plan.parts],
-        labels + grads,
-        away,
+        labels + [grads[1], rem_part],
+        order,
         "home",
-        4.0,
+        3.0,
         16 * grow,
         scratch=table,
     )

time: 104 us -> 106 us (1.019)
  starting transfers between devices: 37.5 us -> 40.2 us
  waiting for transfers between devices: 28.5 us -> 31.1 us
  Pallas kernels: 36.3 us -> 33.7 us
    ppermute x33, starting transfers between devices: 37.5 us -> 40.2 us  [send(): return lax.ppermute(value, ('dom', 'rel'), pairs)]
    ppermute x33, waiting for transfers between devices: 28.5 us -> 31.1 us  [send(): return lax.ppermute(value, ('dom', 'rel'), pairs)]
    pallas_call x20, Pallas kernels: 36.3 us -> 33.7 us  [call(): pl.pallas_call(kernel, out_shape=outs, compiler_params=pltpu.CompilerPara...]
  transfers between devices with their start and end apart: 33 -> 33, of which waited for: 10 -> 12; matrix products, arithmetic and copies ran while one was open for 0% -> 0% of each run, Pallas kernels for 20% -> 14%
where the time goes in v8:
time: 106 us
  starting transfers between devices  40.2 us (38%)
  Pallas kernels  33.7 us (32%)
  waiting for transfers between devices  31.1 us (29%)
    ppermute x33, starting transfers between devices, send(): return lax.ppermute(value, ('dom', 'rel'), pairs)  40.2 us
    pallas_call x20, Pallas kernels, call(): pl.pallas_call(kernel, out_shape=outs, compiler_params=pltpu.CompilerPara...  33.7 us
    ppermute x33, waiting for transfers between devices, send(): return lax.ppermute(value, ('dom', 'rel'), pairs)  31.1 us
  transfers between devices with their start and end apart: 33, of which 12 were waited for; matrix products, arithmetic and copies ran while one was open for 0% of the time, Pallas kernels for 14%

profile of v8, /device:TPU:0, one launch (start us, length us, event | category | flops | bytes accessed | tf_op | source)
XLA Modules:
  0.0 106.1 jit_solution(15089145552695224204)
XLA Ops:
  0.7 3.0 %rel_split.1.refs_9_.refs_1_ = bf16[800,2560]{1,0:T(8,128)(2,1)S(1)} custom-call(f32[400,2560]{1,0:T(8,128)} %bitcast.13), custom_call_target="tpu_custom_call" | custom-call | flops 2000000000 | bytes 6000000 | tf_op jit(solution)/shard_map/rel_split/pallas_call | solution.py:508
  5.0 2.6 %collective-permute-start.1 = (s32[2,8,128]{2,1,0:T(8,128)S(1)}, s32[2,8,128]{2,1,0:T(8,128)S(1)}, u32[]{:S(2)}, u32[]{:S(2)}) collective-permute-start(s32[2,8,128]{2,1,0:T(8,128)S(1)} %get-tuple-element.50), channel_id=1, source_target_pairs={{0,2},{1,3},{2,0},{3,1},{4,6},{5,7},{6,4},{7,5},{8,10},{9,11},{10,... | collective-permute-start | bytes 24584 | tf_op jit(solution)/shard_map/ppermute | solution.py:181
  8.3 1.8 %collective-permute-start.5 = (bf16[400,512]{1,0:T(8,128)(2,1)S(1)}, bf16[400,512]{1,0:T(8,128)(2,1)S(1)}, u32[]{:S(2)}, u32[]{:S(2)}) collective-permute-start(bf16[400,512]{1,0:T(8,128)(2,1)S(1)} %get-tuple-element.54.refs_1_), channel_id=1, source_target_pairs={{0,4},{1,5},{2,6},{3,7},{4,0},{5,1},{6,2},{7,3},{8,12},{9,13},{10,... | collective-permute-start | bytes 1228808 | tf_op jit(solution)/shard_map/ppermute | solution.py:181
  10.6 2.3 %relation.2.refs_3_ = f32[400,512]{1,0:T(8,128)S(1)} custom-call(s32[4,8,128]{2,1,0:T(8,128)S(1)} %get-tuple-element.52.refs_0_, bf16[800,2560]{1,0:T(8,128)(2,1)S(1)} %rel_split.1.refs_9_.refs_1_), custom_call_target="tpu_custom_call" | custom-call | flops 2000000000 | bytes 6000000 | tf_op jit(solution)/shard_map/relation/pallas_call | solution.py:508
  15.2 2.6 %collective-permute-done.3.refs_0_.refs_1_ = s32[4,8,128]{2,1,0:T(8,128)S(1)} collective-permute-done((s32[4,8,128]{2,1,0:T(8,128)S(1)}, s32[4,8,128]{2,1,0:T(8,128)S(1)}, u32[]{:S(2)}, u32[]{:S(2)}) %collective-permute-start.3) | collective-permute-done | bytes 16416 | tf_op jit(solution)/shard_map/ppermute | solution.py:181
  17.8 2.3 %relation.3.refs_7_ = f32[400,512]{1,0:T(8,128)S(1)} custom-call(s32[4,8,128]{2,1,0:T(8,128)S(1)} %collective-permute-done.3.refs_0_.refs_1_, bf16[800,2560]{1,0:T(8,128)(2,1)S(1)} %rel_split.1.refs_9_.refs_1_), custom_call_target="tpu_custom_call" | custom-call | flops 2000000000 | bytes 6000000 | tf_op jit(solution)/shard_map/relation/pallas_call | solution.py:508
  20.8 4.3 %bucket.1 = (bf16[800,512]{1,0:T(8,128)(2,1)S(1)}, bf16[800,512]{1,0:T(8,128)(2,1)S(1)}, bf16[800,1024]{1,0:T(8,128)(2,1)S(1)}) custom-call(s32[4,8,128]{2,1,0:T(8,128)S(1)} %get-tuple-element.52.refs_0_, bf16[400,512]{1,0:T(8,128)(2,1)S(1)} %collective-permute-done.4.refs_1_.refs_5_, f32[400,512]{1,0:T(8,128)S(1)} %get-tuple-element.55.refs_2_, ...), custom_call_target="tpu_custom_call" | custom-call | flops 4000000000 | bytes 12000000 | tf_op jit(solution)/shard_map/bucket/pallas_call | solution.py:508
  25.1 8.1 %last.1 = (s16[16,288,128]{2,1,0:T(8,128)(2,1)S(1)}, f32[400,128]{1,0:T(8,128)S(1)}, bf16[800,1024]{1,0:T(8,128)(2,1)S(1)}, bf16[800,1024]{1,0:T(8,128)(2,1)S(1)}, bf16[800,2048]{1,0:T(8,128)(2,1)S(1)}) custom-call(s32[4,8,128]{2,1,0:T(8,128)S(1)} %get-tuple-element.52.refs_0_, s32[4,8,128]{2,1,0:T(8,128)S(1)} %collective-permute-done.3.refs_0_.refs_1_, ...), custom_call_target="tpu_custom_call" | custom-call | flops 8999999488 | bytes 27000000 | tf_op jit(solution)/shard_map/last/pallas_call | solution.py:508
  33.3 3.1 %collective-permute-start.6 = (s16[16,288,128]{2,1,0:T(8,128)(2,1)S(1)}, s16[16,288,128]{2,1,0:T(8,128)(2,1)S(1)}, u32[]{:S(2)}, u32[]{:S(2)}) collective-permute-start(s16[16,288,128]{2,1,0:T(8,128)(2,1)S(1)} %get-tuple-element.65.refs_2_), channel_id=1, source_target_pairs={{0,1},{1,0},{2,3},{3,2},{4,5},{5,4},{6,7},{7,6},{8,9},{9,8},{10,11... | collective-permute-start | bytes 3538952 | tf_op jit(solution)/shard_map/ppermute | solution.py:181
  37.1 2.4 %home.1.refs_0_ = f32[16,280,128]{2,1,0:T(8,128)S(1)} custom-call(s32[4,8,128]{2,1,0:T(8,128)S(1)} %get-tuple-element.52.refs_0_, s32[4,8,128]{2,1,0:T(8,128)S(1)} %collective-permute-done.3.refs_0_.refs_1_, bf16[800,1024]{1,0:T(8,128)(2,1)S(1)} %get-tuple-element.62.refs_2_, f32[400,128]{1,0:T(8,128)S(1)} %get-tuple-element.63.refs_3_, ...), custom_call_target="tpu_custom_call" | custom-call | flops 3000000000 | bytes 9000000 | tf_op jit(solution)/shard_map/home/pallas_call | solution.py:508
  40.2 5.5 %collective-permute-start.10 = (s16[4,288,128]{2,1,0:T(8,128)(2,1)S(1)}, s16[4,288,128]{2,1,0:T(8,128)(2,1)S(1)}, u32[]{:S(2)}, u32[]{:S(2)}) collective-permute-start(s16[4,288,128]{2,1,0:T(8,128)(2,1)S(1)} %get-tuple-element.71), channel_id=1, source_target_pairs={{0,6},{1,7},{2,4},{3,5},{4,2},{5,3},{6,0},{7,1},{8,14},{9,15},{10,... | collective-permute-start | bytes 884744 | tf_op jit(solution)/shard_map/ppermute | solution.py:181
  46.4 2.0 %target.1 = (s16[416,256]{1,0:T(8,128)(2,1)S(1)}, s16[416,256]{1,0:T(8,128)(2,1)S(1)}) custom-call(s32[4,8,128]{2,1,0:T(8,128)S(1)} %get-tuple-element.52.refs_0_, s32[4,8,128]{2,1,0:T(8,128)S(1)} %collective-permute-done.3.refs_0_.refs_1_, bf16[800,2048]{1,0:T(8,128)(2,1)S(1)} %get-tuple-element.72.refs_2_, f32[4,280,128]{2,1,0:T(8,128)S(1)} %get-tuple-element.68.refs_3_.refs_0_), custom_call_target="tpu_custom_call" | custom-call | flops 1800000000 | bytes 5400000 | tf_op jit(solution)/shard_map/target/pallas_call | solution.py:508
  50.4 3.2 %collective-permute-done.10.refs_3_ = s16[4,288,128]{2,1,0:T(8,128)(2,1)S(1)} collective-permute-done((s16[4,288,128]{2,1,0:T(8,128)(2,1)S(1)}, s16[4,288,128]{2,1,0:T(8,128)(2,1)S(1)}, u32[]{:S(2)}, u32[]{:S(2)}) %collective-permute-start.10) | collective-permute-done | bytes 294944 | tf_op jit(solution)/shard_map/ppermute | solution.py:181
  53.7 5.4 %collective-permute-done.8.refs_1_ = s16[4,288,128]{2,1,0:T(8,128)(2,1)S(1)} collective-permute-done((s16[4,288,128]{2,1,0:T(8,128)(2,1)S(1)}, s16[4,288,128]{2,1,0:T(8,128)(2,1)S(1)}, u32[]{:S(2)}, u32[]{:S(2)}) %collective-permute-start.8) | collective-permute-done | bytes 294944 | tf_op jit(solution)/shard_map/ppermute | solution.py:181
  60.3 3.0 %collective-permute-start.16 = (s16[416,256]{1,0:T(8,128)(2,1)S(1)}, s16[416,256]{1,0:T(8,128)(2,1)S(1)}, u32[]{:S(2)}, u32[]{:S(2)}) collective-permute-start(s16[416,256]{1,0:T(8,128)(2,1)S(1)} %get-tuple-element.80), channel_id=1, source_target_pairs={{0,1},{1,0},{2,3},{3,2},{4,5},{5,4},{6,7},{7,6},{8,9},{9,8},{10,11... | collective-permute-start | bytes 638984 | tf_op jit(solution)/shard_map/ppermute | solution.py:181
  63.3 2.4 %collective-permute-start.17 = (s16[416,128]{1,0:T(8,128)(2,1)S(1)}, s16[416,128]{1,0:T(8,128)(2,1)S(1)}, u32[]{:S(2)}, u32[]{:S(2)}) collective-permute-start(s16[416,128]{1,0:T(8,128)(2,1)S(1)} %get-tuple-element.82), channel_id=1, source_target_pairs={{0,2},{1,3},{2,0},{3,1},{4,6},{5,7},{6,4},{7,5},{8,10},{9,11},{10,... | collective-permute-start | bytes 319496 | tf_op jit(solution)/shard_map/ppermute | solution.py:181
  65.9 2.4 %collective-permute-start.14 = (s16[1,288,128]{2,1,0:T(8,128)(2,1)S(1)}, s16[1,288,128]{2,1,0:T(8,128)(2,1)S(1)}, u32[]{:S(2)}, u32[]{:S(2)}) collective-permute-start(s16[1,288,128]{2,1,0:T(8,128)(2,1)S(1)} %get-tuple-element.77), channel_id=1, source_target_pairs={{0,16},{1,17},{2,18},{3,19},{4,20},{5,21},{6,22},{7,23},{8,24},{9,... | collective-permute-start | bytes 221192 | tf_op jit(solution)/shard_map/ppermute | solution.py:181
  68.3 1.8 %collective-permute-start.15 = (s16[1,288,128]{2,1,0:T(8,128)(2,1)S(1)}, s16[1,288,128]{2,1,0:T(8,128)(2,1)S(1)}, u32[]{:S(2)}, u32[]{:S(2)}) collective-permute-start(s16[1,288,128]{2,1,0:T(8,128)(2,1)S(1)} %get-tuple-element.78), channel_id=1, source_target_pairs={{0,24},{1,25},{2,26},{3,27},{4,28},{5,29},{6,30},{7,31},{8,16},{9,... | collective-permute-start | bytes 221192 | tf_op jit(solution)/shard_map/ppermute | solution.py:181
  71.0 4.0 %collective-permute-done.14.refs_2_ = s16[1,288,128]{2,1,0:T(8,128)(2,1)S(1)} collective-permute-done((s16[1,288,128]{2,1,0:T(8,128)(2,1)S(1)}, s16[1,288,128]{2,1,0:T(8,128)(2,1)S(1)}, u32[]{:S(2)}, u32[]{:S(2)}) %collective-permute-start.14) | collective-permute-done | bytes 73760 | tf_op jit(solution)/shard_map/ppermute | solution.py:181
  82.9 2.2 %collective-permute-done.19.refs_2_ = s16[1,288,128]{2,1,0:T(8,128)(2,1)S(1)} collective-permute-done((s16[1,288,128]{2,1,0:T(8,128)(2,1)S(1)}, s16[1,288,128]{2,1,0:T(8,128)(2,1)S(1)}, u32[]{:S(2)}, u32[]{:S(2)}) %collective-permute-start.19) | collective-permute-done | bytes 73760 | tf_op jit(solution)/shard_map/ppermute | solution.py:181
  86.1 1.8 %collective-permute-start.27 = (s16[4,288,128]{2,1,0:T(8,128)(2,1)S(1)}, s16[4,288,128]{2,1,0:T(8,128)(2,1)S(1)}, u32[]{:S(2)}, u32[]{:S(2)}) collective-permute-start(s16[4,288,128]{2,1,0:T(8,128)(2,1)S(1)} %get-tuple-element.88.refs_0_), channel_id=1, source_target_pairs={{0,2},{1,3},{2,0},{3,1},{4,6},{5,7},{6,4},{7,5},{8,10},{9,11},{10,... | collective-permute-start | bytes 884744 | tf_op jit(solution)/shard_map/ppermute | solution.py:181
  89.7 1.8 %collective-permute-start.24 = (s16[416,128]{1,0:T(8,128)(2,1)S(1)}, s16[416,128]{1,0:T(8,128)(2,1)S(1)}, u32[]{:S(2)}, u32[]{:S(2)}) collective-permute-start(s16[416,128]{1,0:T(8,128)(2,1)S(1)} %get-tuple-element.87.refs_0_), channel_id=1, source_target_pairs={{0,2},{1,3},{2,0},{3,1},{4,6},{5,7},{6,4},{7,5},{8,10},{9,11},{10,... | collective-permute-start | bytes 319496 | tf_op jit(solution)/shard_map/ppermute | solution.py:181
  91.5 8.9 %collective-permute-done.24.refs_2_ = s16[416,128]{1,0:T(8,128)(2,1)S(1)} collective-permute-done((s16[416,128]{1,0:T(8,128)(2,1)S(1)}, s16[416,128]{1,0:T(8,128)(2,1)S(1)}, u32[]{:S(2)}, u32[]{:S(2)}) %collective-permute-start.24) | collective-permute-done | bytes 106528 | tf_op jit(solution)/shard_map/ppermute | solution.py:181
  104.4 1.7 %spread.3 = (f32[400,2560]{1,0:T(8,128)}, f32[400,256]{1,0:T(8,128)}) custom-call(s32[1]{0:T(128)} %bitcast.5.side, s16[4,288,128]{2,1,0:T(8,128)(2,1)S(1)} %collective-permute-done.26.refs_0_, s16[4,288,128]{2,1,0:T(8,128)(2,1)S(1)} %collective-permute-done.28.refs_1_, ...), custom_call_target="tpu_custom_call", output_to_operand_aliasing={{0}: (5, {}), {1}: (6, {})} | custom-call | flops 2000000000 | bytes 6000000 | tf_op jit(solution)/shard_map/spread/pallas_call | solution.py:508
  (82 shorter events, 26.6 us)
Async XLA Ops:
  4.4 5.7 %collective-permute-start = (s32[2,8,128]{2,1,0:T(8,128)S(1)}, s32[2,8,128]{2,1,0:T(8,128)S(1)}, u32[]{:S(2)}, u32[]{:S(2)}) collective-permute-start(s32[2,8,128]{2,1,0:T(8,128)S(1)} %get-tuple-element.49), channel_id=1, source_target_pairs={{0,1},{1,0},{2,3},{3,2},{4,5},{5,4},{6,7},{7,6},{8,9},{9,8},{10,11... | collective-permute-start | bytes 24584 | tf_op jit(solution)/shard_map/ppermute | solution.py:181
  5.0 5.1 %collective-permute-start.1 = (s32[2,8,128]{2,1,0:T(8,128)S(1)}, s32[2,8,128]{2,1,0:T(8,128)S(1)}, u32[]{:S(2)}, u32[]{:S(2)}) collective-permute-start(s32[2,8,128]{2,1,0:T(8,128)S(1)} %get-tuple-element.50), channel_id=1, source_target_pairs={{0,2},{1,3},{2,0},{3,1},{4,6},{5,7},{6,4},{7,5},{8,10},{9,11},{10,... | collective-permute-start | bytes 24584 | tf_op jit(solution)/shard_map/ppermute | solution.py:181
  7.6 13.2 %collective-permute-start.4 = (bf16[400,512]{1,0:T(8,128)(2,1)S(1)}, bf16[400,512]{1,0:T(8,128)(2,1)S(1)}, u32[]{:S(2)}, u32[]{:S(2)}) collective-permute-start(bf16[400,512]{1,0:T(8,128)(2,1)S(1)} %get-tuple-element.54.refs_1_), channel_id=1, source_target_pairs={{0,0},{1,17},{2,10},{3,27},{4,4},{5,21},{6,14},{7,31},{8,8},{9,25}... | collective-permute-start | bytes 1228808 | tf_op jit(solution)/shard_map/ppermute | solution.py:181
  8.3 11.8 %collective-permute-start.5 = (bf16[400,512]{1,0:T(8,128)(2,1)S(1)}, bf16[400,512]{1,0:T(8,128)(2,1)S(1)}, u32[]{:S(2)}, u32[]{:S(2)}) collective-permute-start(bf16[400,512]{1,0:T(8,128)(2,1)S(1)} %get-tuple-element.54.refs_1_), channel_id=1, source_target_pairs={{0,4},{1,5},{2,6},{3,7},{4,0},{5,1},{6,2},{7,3},{8,12},{9,13},{10,... | collective-permute-start | bytes 1228808 | tf_op jit(solution)/shard_map/ppermute | solution.py:181
  12.9 4.9 %collective-permute-start.3 = (s32[4,8,128]{2,1,0:T(8,128)S(1)}, s32[4,8,128]{2,1,0:T(8,128)S(1)}, u32[]{:S(2)}, u32[]{:S(2)}) collective-permute-start(s32[4,8,128]{2,1,0:T(8,128)S(1)} %get-tuple-element.53), channel_id=1, source_target_pairs={{0,4},{1,5},{2,6},{3,7},{4,0},{5,1},{6,2},{7,3},{8,12},{9,13},{10,... | collective-permute-start | bytes 49160 | tf_op jit(solution)/shard_map/ppermute | solution.py:181
  33.3 6.3 %collective-permute-start.6 = (s16[16,288,128]{2,1,0:T(8,128)(2,1)S(1)}, s16[16,288,128]{2,1,0:T(8,128)(2,1)S(1)}, u32[]{:S(2)}, u32[]{:S(2)}) collective-permute-start(s16[16,288,128]{2,1,0:T(8,128)(2,1)S(1)} %get-tuple-element.65.refs_2_), channel_id=1, source_target_pairs={{0,1},{1,0},{2,3},{3,2},{4,5},{5,4},{6,7},{7,6},{8,9},{9,8},{10,11... | collective-permute-start | bytes 3538952 | tf_op jit(solution)/shard_map/ppermute | solution.py:181
  40.2 13.4 %collective-permute-start.10 = (s16[4,288,128]{2,1,0:T(8,128)(2,1)S(1)}, s16[4,288,128]{2,1,0:T(8,128)(2,1)S(1)}, u32[]{:S(2)}, u32[]{:S(2)}) collective-permute-start(s16[4,288,128]{2,1,0:T(8,128)(2,1)S(1)} %get-tuple-element.71), channel_id=1, source_target_pairs={{0,6},{1,7},{2,4},{3,5},{4,2},{5,3},{6,0},{7,1},{8,14},{9,15},{10,... | collective-permute-start | bytes 884744 | tf_op jit(solution)/shard_map/ppermute | solution.py:181
  45.8 13.3 %collective-permute-start.8 = (s16[4,288,128]{2,1,0:T(8,128)(2,1)S(1)}, s16[4,288,128]{2,1,0:T(8,128)(2,1)S(1)}, u32[]{:S(2)}, u32[]{:S(2)}) collective-permute-start(s16[4,288,128]{2,1,0:T(8,128)(2,1)S(1)} %get-tuple-element.69), channel_id=1, source_target_pairs={{0,2},{1,3},{2,0},{3,1},{4,6},{5,7},{6,4},{7,5},{8,10},{9,11},{10,... | collective-permute-start | bytes 884744 | tf_op jit(solution)/shard_map/ppermute | solution.py:181
  45.8 14.0 %collective-permute-start.9 = (s16[4,288,128]{2,1,0:T(8,128)(2,1)S(1)}, s16[4,288,128]{2,1,0:T(8,128)(2,1)S(1)}, u32[]{:S(2)}, u32[]{:S(2)}) collective-permute-start(s16[4,288,128]{2,1,0:T(8,128)(2,1)S(1)} %get-tuple-element.70), channel_id=1, source_target_pairs={{0,4},{1,5},{2,6},{3,7},{4,0},{5,1},{6,2},{7,3},{8,12},{9,13},{10,... | collective-permute-start | bytes 884744 | tf_op jit(solution)/shard_map/ppermute | solution.py:181
  60.3 14.6 %collective-permute-start.16 = (s16[416,256]{1,0:T(8,128)(2,1)S(1)}, s16[416,256]{1,0:T(8,128)(2,1)S(1)}, u32[]{:S(2)}, u32[]{:S(2)}) collective-permute-start(s16[416,256]{1,0:T(8,128)(2,1)S(1)} %get-tuple-element.80), channel_id=1, source_target_pairs={{0,1},{1,0},{2,3},{3,2},{4,5},{5,4},{6,7},{7,6},{8,9},{9,8},{10,11... | collective-permute-start | bytes 638984 | tf_op jit(solution)/shard_map/ppermute | solution.py:181
  63.3 11.6 %collective-permute-start.17 = (s16[416,128]{1,0:T(8,128)(2,1)S(1)}, s16[416,128]{1,0:T(8,128)(2,1)S(1)}, u32[]{:S(2)}, u32[]{:S(2)}) collective-permute-start(s16[416,128]{1,0:T(8,128)(2,1)S(1)} %get-tuple-element.82), channel_id=1, source_target_pairs={{0,2},{1,3},{2,0},{3,1},{4,6},{5,7},{6,4},{7,5},{8,10},{9,11},{10,... | collective-permute-start | bytes 319496 | tf_op jit(solution)/shard_map/ppermute | solution.py:181
  65.7 5.3 %collective-permute-start.13 = (s16[1,288,128]{2,1,0:T(8,128)(2,1)S(1)}, s16[1,288,128]{2,1,0:T(8,128)(2,1)S(1)}, u32[]{:S(2)}, u32[]{:S(2)}) collective-permute-start(s16[1,288,128]{2,1,0:T(8,128)(2,1)S(1)} %get-tuple-element.76), channel_id=1, source_target_pairs={{0,8},{1,9},{2,10},{3,11},{4,12},{5,13},{6,14},{7,15},{8,0},{9,1},... | collective-permute-start | bytes 221192 | tf_op jit(solution)/shard_map/ppermute | solution.py:181
  65.9 9.0 %collective-permute-start.14 = (s16[1,288,128]{2,1,0:T(8,128)(2,1)S(1)}, s16[1,288,128]{2,1,0:T(8,128)(2,1)S(1)}, u32[]{:S(2)}, u32[]{:S(2)}) collective-permute-start(s16[1,288,128]{2,1,0:T(8,128)(2,1)S(1)} %get-tuple-element.77), channel_id=1, source_target_pairs={{0,16},{1,17},{2,18},{3,19},{4,20},{5,21},{6,22},{7,23},{8,24},{9,... | collective-permute-start | bytes 221192 | tf_op jit(solution)/shard_map/ppermute | solution.py:181
  68.3 6.7 %collective-permute-start.15 = (s16[1,288,128]{2,1,0:T(8,128)(2,1)S(1)}, s16[1,288,128]{2,1,0:T(8,128)(2,1)S(1)}, u32[]{:S(2)}, u32[]{:S(2)}) collective-permute-start(s16[1,288,128]{2,1,0:T(8,128)(2,1)S(1)} %get-tuple-element.78), channel_id=1, source_target_pairs={{0,24},{1,25},{2,26},{3,27},{4,28},{5,29},{6,30},{7,31},{8,16},{9,... | collective-permute-start | bytes 221192 | tf_op jit(solution)/shard_map/ppermute | solution.py:181
  75.2 10.8 %collective-permute-start.21 = (s16[416,128]{1,0:T(8,128)(2,1)S(1)}, s16[416,128]{1,0:T(8,128)(2,1)S(1)}, u32[]{:S(2)}, u32[]{:S(2)}) collective-permute-start(s16[416,128]{1,0:T(8,128)(2,1)S(1)} %get-tuple-element.85), channel_id=1, source_target_pairs={{0,2},{1,3},{2,0},{3,1},{4,6},{5,7},{6,4},{7,5},{8,10},{9,11},{10,... | collective-permute-start | bytes 319496 | tf_op jit(solution)/shard_map/ppermute | solution.py:181
  75.4 10.6 %collective-permute-start.22 = (s16[416,128]{1,0:T(8,128)(2,1)S(1)}, s16[416,128]{1,0:T(8,128)(2,1)S(1)}, u32[]{:S(2)}, u32[]{:S(2)}) collective-permute-start(s16[416,128]{1,0:T(8,128)(2,1)S(1)} %get-tuple-element.86), channel_id=1, source_target_pairs={{0,4},{1,5},{2,6},{3,7},{4,0},{5,1},{6,2},{7,3},{8,12},{9,13},{10,... | collective-permute-start | bytes 319496 | tf_op jit(solution)/shard_map/ppermute | solution.py:181
  76.9 5.9 %collective-permute-start.18 = (s16[1,288,128]{2,1,0:T(8,128)(2,1)S(1)}, s16[1,288,128]{2,1,0:T(8,128)(2,1)S(1)}, u32[]{:S(2)}, u32[]{:S(2)}) collective-permute-start(s16[1,288,128]{2,1,0:T(8,128)(2,1)S(1)} %get-tuple-element.83.refs_0_), channel_id=1, source_target_pairs={{0,8},{1,9},{2,10},{3,11},{4,12},{5,13},{6,14},{7,15},{8,0},{9,1},... | collective-permute-start | bytes 221192 | tf_op jit(solution)/shard_map/ppermute | solution.py:181
  78.4 6.6 %collective-permute-start.19 = (s16[1,288,128]{2,1,0:T(8,128)(2,1)S(1)}, s16[1,288,128]{2,1,0:T(8,128)(2,1)S(1)}, u32[]{:S(2)}, u32[]{:S(2)}) collective-permute-start(s16[1,288,128]{2,1,0:T(8,128)(2,1)S(1)} %get-tuple-element.83.refs_0_), channel_id=1, source_target_pairs={{0,16},{1,17},{2,18},{3,19},{4,20},{5,21},{6,22},{7,23},{8,24},{9,... | collective-permute-start | bytes 221192 | tf_op jit(solution)/shard_map/ppermute | solution.py:181
  79.7 6.3 %collective-permute-start.20 = (s16[1,288,128]{2,1,0:T(8,128)(2,1)S(1)}, s16[1,288,128]{2,1,0:T(8,128)(2,1)S(1)}, u32[]{:S(2)}, u32[]{:S(2)}) collective-permute-start(s16[1,288,128]{2,1,0:T(8,128)(2,1)S(1)} %get-tuple-element.83.refs_0_), channel_id=1, source_target_pairs={{0,24},{1,25},{2,26},{3,27},{4,28},{5,29},{6,30},{7,31},{8,16},{9,... | collective-permute-start | bytes 221192 | tf_op jit(solution)/shard_map/ppermute | solution.py:181
  86.1 14.7 %collective-permute-start.27 = (s16[4,288,128]{2,1,0:T(8,128)(2,1)S(1)}, s16[4,288,128]{2,1,0:T(8,128)(2,1)S(1)}, u32[]{:S(2)}, u32[]{:S(2)}) collective-permute-start(s16[4,288,128]{2,1,0:T(8,128)(2,1)S(1)} %get-tuple-element.88.refs_0_), channel_id=1, source_target_pairs={{0,2},{1,3},{2,0},{3,1},{4,6},{5,7},{6,4},{7,5},{8,10},{9,11},{10,... | collective-permute-start | bytes 884744 | tf_op jit(solution)/shard_map/ppermute | solution.py:181
  88.0 13.0 %collective-permute-start.29 = (s16[4,288,128]{2,1,0:T(8,128)(2,1)S(1)}, s16[4,288,128]{2,1,0:T(8,128)(2,1)S(1)}, u32[]{:S(2)}, u32[]{:S(2)}) collective-permute-start(s16[4,288,128]{2,1,0:T(8,128)(2,1)S(1)} %get-tuple-element.88.refs_0_), channel_id=1, source_target_pairs={{0,4},{1,5},{2,6},{3,7},{4,0},{5,1},{6,2},{7,3},{8,12},{9,13},{10,... | collective-permute-start | bytes 884744 | tf_op jit(solution)/shard_map/ppermute | solution.py:181
  88.5 12.9 %collective-permute-start.31 = (s16[4,288,128]{2,1,0:T(8,128)(2,1)S(1)}, s16[4,288,128]{2,1,0:T(8,128)(2,1)S(1)}, u32[]{:S(2)}, u32[]{:S(2)}) collective-permute-start(s16[4,288,128]{2,1,0:T(8,128)(2,1)S(1)} %get-tuple-element.88.refs_0_), channel_id=1, source_target_pairs={{0,6},{1,7},{2,4},{3,5},{4,2},{5,3},{6,0},{7,1},{8,14},{9,15},{10,... | collective-permute-start | bytes 884744 | tf_op jit(solution)/shard_map/ppermute | solution.py:181
  89.7 10.6 %collective-permute-start.24 = (s16[416,128]{1,0:T(8,128)(2,1)S(1)}, s16[416,128]{1,0:T(8,128)(2,1)S(1)}, u32[]{:S(2)}, u32[]{:S(2)}) collective-permute-start(s16[416,128]{1,0:T(8,128)(2,1)S(1)} %get-tuple-element.87.refs_0_), channel_id=1, source_target_pairs={{0,2},{1,3},{2,0},{3,1},{4,6},{5,7},{6,4},{7,5},{8,10},{9,11},{10,... | collective-permute-start | bytes 319496 | tf_op jit(solution)/shard_map/ppermute | solution.py:181
  91.5 8.9 %collective-permute-start.23 = (s16[416,128]{1,0:T(8,128)(2,1)S(1)}, s16[416,128]{1,0:T(8,128)(2,1)S(1)}, u32[]{:S(2)}, u32[]{:S(2)}) collective-permute-start(s16[416,128]{1,0:T(8,128)(2,1)S(1)} %get-tuple-element.87.refs_0_), channel_id=1, source_target_pairs={{0,1},{1,0},{2,3},{3,2},{4,5},{5,4},{6,7},{7,6},{8,9},{9,8},{10,11... | collective-permute-start | bytes 319496 | tf_op jit(solution)/shard_map/ppermute | solution.py:181
  (19 other events, 55.9 us)

commit v9 on v8

--- a/solution.py
+++ b/solution.py
@@ -37,8 +37,14 @@
     return lax.dot_general(left, right, dims, preferred_element_type=F32)
 
 
-def stacked(parts, axis):
-    return jnp.concatenate(parts, axis=axis)
+def dot3(left, right, dims):
+    left_high, left_low = split(left)
+    right_high, right_low = split(right)
+    return (
+        dot(left_high, right_high, dims)
+        + dot(left_high, right_low, dims)
+        + dot(left_low, right_high, dims)
+    )
 
 
 def one_hot(ids, rows, base=0):
@@ -182,8 +188,7 @@
 
 
 def lists_kernel(plan, *refs):
-    tables, counts, own, outs = refs[:7], refs[7], refs[8], refs[10:-1]
-    refs[-1][...] = own[...]
+    tables, counts, outs = refs[:7], refs[7], refs[8:]
     source = lax.axis_index("dom")
     rel = lax.axis_index("rel")
     for mask, out in enumerate(outs):
@@ -273,18 +278,11 @@
         u_vec = complex_product(lhs, vec)
         live = plan.row(labels, 0, (7,), slot, 1).astype(F32)
         positive = jnp.sum(u_vec * rhs, axis=0, keepdims=True)
-        u_high, u_low = split(u_vec)
-        cand_high, cand_low = split(cand)
-        u_both, cand_both = stacked([u_high, u_low], 1), stacked([cand_high, cand_low], 0)
-        negative = dot(u_both, cand_high, TN)
-        negative = negative[:LANES] + negative[LANES:] + dot(u_high, cand_low, TN)
+        negative = dot3(u_vec, cand, TN)
         grad_pos = -jax.nn.sigmoid(-positive) * live
         grad_neg = jax.nn.sigmoid(negative) * keep * live[0:1, 0:1]
-        neg_high, neg_low = split(grad_neg)
-        grad_u = folded(dot(cand_both, neg_high, NT)) + dot(cand_high, neg_low, NT)
-        grad_u = grad_pos * rhs + grad_u
-        from_neg = folded(dot(stacked([u_high, u_low], 0), neg_high, NN))
-        from_neg = from_neg + dot(u_high, neg_low, NN)
+        grad_u = grad_pos * rhs + dot3(cand, grad_neg, NT)
+        from_neg = dot3(u_vec, grad_neg, NN)
         grad_cand = jnp.concatenate(
             [from_neg[:, :LANES] + grad_pos * u_vec, from_neg[:, LANES:]], axis=1
         )
@@ -563,6 +561,21 @@
             **more,
         )
 
+    tables = [lhs_rows, lhs_rems, rel_ids, rhs_rows, rhs_rems, neg_rows, neg_rems]
+    target = send(own, plan, afar)
+    sources = [own] + [
+        send(own, plan, lambda d, b=bucket: d ^ (b * plan.rels)) for bucket in range(1, buckets)
+    ]
+    lists = call(
+        functools.partial(lists_kernel, plan),
+        [shape((buckets * plan.maxb, 8, LANES), jnp.int32)] * plan.rels,
+        tables + [counts.reshape(-1)],
+        "lists",
+        0.5,
+        60,
+        in_specs=[VMEM] * 7 + [smem],
+    )
+    lists = [lists[0]] + exchanged(lists[1:], range(plan.rels))
     (rel_split,) = call(
         split_kernel,
         [shape((2 * width, plan.nrels), BF16)],
@@ -571,22 +584,6 @@
         2.0,
         50,
     )
-    tables = [lhs_rows, lhs_rems, rel_ids, rhs_rows, rhs_rems, neg_rows, neg_rems]
-    *lists, own = call(
-        functools.partial(lists_kernel, plan),
-        [shape((buckets * plan.maxb, 8, LANES), jnp.int32)] * plan.rels
-        + [shape(own.shape, own.dtype)],
-        tables + [counts.reshape(-1), own, rel_split],
-        "lists",
-        0.5,
-        8,
-        in_specs=[VMEM] * 7 + [smem, VMEM, ANY],
-    )
-    lists = [lists[0]] + exchanged(lists[1:], range(plan.rels))
-    target = send(own, plan, afar)
-    sources = [own] + [
-        send(own, plan, lambda d, b=bucket: d ^ (b * plan.rels)) for bucket in range(1, buckets)
-    ]
     labels = call(
         functools.partial(forward_kernel, plan),
         [shape((plan.slots, 8, LANES), jnp.int32)] * buckets,

time: 106 us -> 101 us (0.953)
  starting transfers between devices: 40.2 us -> 37.3 us
  waiting for transfers between devices: 31.1 us -> 28.9 us
    ppermute x33, starting transfers between devices: 40.2 us -> 37.3 us  [send(): return lax.ppermute(value, ('dom', 'rel'), pairs)]
    ppermute x33, waiting for transfers between devices: 31.1 us -> 28.9 us  [send(): return lax.ppermute(value, ('dom', 'rel'), pairs)]
  transfers between devices with their start and end apart: 33 -> 33, of which waited for: 12 -> 11; matrix products, arithmetic and copies ran while one was open for 0% -> 0% of each run, Pallas kernels for 14% -> 19%
where the time goes in v9:
time: 101 us
  starting transfers between devices  37.3 us (37%)
  Pallas kernels  34 us (34%)
  waiting for transfers between devices  28.9 us (29%)
    ppermute x33, starting transfers between devices, send(): return lax.ppermute(value, ('dom', 'rel'), pairs)  37.3 us
    pallas_call x20, Pallas kernels, call(): pl.pallas_call(kernel, out_shape=outs, compiler_params=pltpu.CompilerPara...  34 us
    ppermute x33, waiting for transfers between devices, send(): return lax.ppermute(value, ('dom', 'rel'), pairs)  28.9 us
  transfers between devices with their start and end apart: 33, of which 11 were waited for; matrix products, arithmetic and copies ran while one was open for 0% of the time, Pallas kernels for 19%

profile of v9, /device:TPU:0, one launch (start us, length us, event | category | flops | bytes accessed | tf_op | source)
XLA Modules:
  0.0 101.1 jit_solution(9607311951015577716)
XLA Ops:
  2.3 3.0 %collective-permute-start.5 = (bf16[400,512]{1,0:T(8,128)(2,1)}, bf16[400,512]{1,0:T(8,128)(2,1)S(1)}, u32[]{:S(2)}, u32[]{:S(2)}) collective-permute-start(bf16[400,512]{1,0:T(8,128)(2,1)} %bitcast.10), channel_id=1, source_target_pairs={{0,4},{1,5},{2,6},{3,7},{4,0},{5,1},{6,2},{7,3},{8,12},{9,13},{10,... | collective-permute-start | bytes 1228808 | tf_op jit(solution)/shard_map/ppermute | solution.py:187
  6.7 2.2 %collective-permute-start = (s32[2,8,128]{2,1,0:T(8,128)}, s32[2,8,128]{2,1,0:T(8,128)S(1)}, u32[]{:S(2)}, u32[]{:S(2)}) collective-permute-start(s32[2,8,128]{2,1,0:T(8,128)} %get-tuple-element.48), channel_id=1, source_target_pairs={{0,1},{1,0},{2,3},{3,2},{4,5},{5,4},{6,7},{7,6},{8,9},{9,8},{10,11... | collective-permute-start | bytes 24584 | tf_op jit(solution)/shard_map/ppermute | solution.py:187
  8.9 2.5 %collective-permute-start.1 = (s32[2,8,128]{2,1,0:T(8,128)}, s32[2,8,128]{2,1,0:T(8,128)S(1)}, u32[]{:S(2)}, u32[]{:S(2)}) collective-permute-start(s32[2,8,128]{2,1,0:T(8,128)} %get-tuple-element.49), channel_id=1, source_target_pairs={{0,2},{1,3},{2,0},{3,1},{4,6},{5,7},{6,4},{7,5},{8,10},{9,11},{10,... | collective-permute-start | bytes 24584 | tf_op jit(solution)/shard_map/ppermute | solution.py:187
  11.4 2.9 %rel_split.1.refs_1_ = bf16[800,2560]{1,0:T(8,128)(2,1)S(1)} custom-call(f32[400,2560]{1,0:T(8,128)} %bitcast.14), custom_call_target="tpu_custom_call" | custom-call | flops 2000000000 | bytes 6000000 | tf_op jit(solution)/shard_map/rel_split/pallas_call | solution.py:506
  15.3 2.3 %relation.2.refs_3_ = f32[400,512]{1,0:T(8,128)S(1)} custom-call(s32[4,8,128]{2,1,0:T(8,128)S(1)} %get-tuple-element.51.refs_0_, bf16[800,2560]{1,0:T(8,128)(2,1)S(1)} %rel_split.1.refs_1_), custom_call_target="tpu_custom_call" | custom-call | flops 2000000000 | bytes 6000000 | tf_op jit(solution)/shard_map/relation/pallas_call | solution.py:506
  18.5 2.3 %relation.3.refs_7_ = f32[400,512]{1,0:T(8,128)S(1)} custom-call(s32[4,8,128]{2,1,0:T(8,128)S(1)} %collective-permute-done.3.refs_0_.refs_1_, bf16[800,2560]{1,0:T(8,128)(2,1)S(1)} %rel_split.1.refs_1_), custom_call_target="tpu_custom_call" | custom-call | flops 2000000000 | bytes 6000000 | tf_op jit(solution)/shard_map/relation/pallas_call | solution.py:506
  21.5 4.1 %bucket.1 = (bf16[800,512]{1,0:T(8,128)(2,1)S(1)}, bf16[800,512]{1,0:T(8,128)(2,1)S(1)}, bf16[800,1024]{1,0:T(8,128)(2,1)S(1)}) custom-call(s32[4,8,128]{2,1,0:T(8,128)S(1)} %get-tuple-element.51.refs_0_, bf16[400,512]{1,0:T(8,128)(2,1)S(1)} %collective-permute-done.4.refs_1_.refs_5_, f32[400,512]{1,0:T(8,128)S(1)} %get-tuple-element.53.refs_2_, ...), custom_call_target="tpu_custom_call" | custom-call | flops 4000000000 | bytes 12000000 | tf_op jit(solution)/shard_map/bucket/pallas_call | solution.py:506
  25.6 7.9 %last.1 = (s16[16,288,128]{2,1,0:T(8,128)(2,1)S(1)}, f32[400,128]{1,0:T(8,128)S(1)}, bf16[800,1024]{1,0:T(8,128)(2,1)S(1)}, bf16[800,1024]{1,0:T(8,128)(2,1)S(1)}, bf16[800,2048]{1,0:T(8,128)(2,1)S(1)}) custom-call(s32[4,8,128]{2,1,0:T(8,128)S(1)} %get-tuple-element.51.refs_0_, s32[4,8,128]{2,1,0:T(8,128)S(1)} %collective-permute-done.3.refs_0_.refs_1_, ...), custom_call_target="tpu_custom_call" | custom-call | flops 8999999488 | bytes 27000000 | tf_op jit(solution)/shard_map/last/pallas_call | solution.py:506
  34.9 2.4 %home.1.refs_0_ = f32[16,280,128]{2,1,0:T(8,128)S(1)} custom-call(s32[4,8,128]{2,1,0:T(8,128)S(1)} %get-tuple-element.51.refs_0_, s32[4,8,128]{2,1,0:T(8,128)S(1)} %collective-permute-done.3.refs_0_.refs_1_, bf16[800,1024]{1,0:T(8,128)(2,1)S(1)} %get-tuple-element.60.refs_2_, f32[400,128]{1,0:T(8,128)S(1)} %get-tuple-element.61.refs_3_, ...), custom_call_target="tpu_custom_call" | custom-call | flops 3000000000 | bytes 9000000 | tf_op jit(solution)/shard_map/home/pallas_call | solution.py:506
  38.0 2.0 %collective-permute-start.10 = (s16[4,288,128]{2,1,0:T(8,128)(2,1)S(1)}, s16[4,288,128]{2,1,0:T(8,128)(2,1)S(1)}, u32[]{:S(2)}, u32[]{:S(2)}) collective-permute-start(s16[4,288,128]{2,1,0:T(8,128)(2,1)S(1)} %get-tuple-element.69), channel_id=1, source_target_pairs={{0,6},{1,7},{2,4},{3,5},{4,2},{5,3},{6,0},{7,1},{8,14},{9,15},{10,... | collective-permute-start | bytes 884744 | tf_op jit(solution)/shard_map/ppermute | solution.py:187
  41.5 2.0 %target.1 = (s16[416,256]{1,0:T(8,128)(2,1)S(1)}, s16[416,256]{1,0:T(8,128)(2,1)S(1)}) custom-call(s32[4,8,128]{2,1,0:T(8,128)S(1)} %get-tuple-element.51.refs_0_, s32[4,8,128]{2,1,0:T(8,128)S(1)} %collective-permute-done.3.refs_0_.refs_1_, bf16[800,2048]{1,0:T(8,128)(2,1)S(1)} %get-tuple-element.70.refs_2_, f32[4,280,128]{2,1,0:T(8,128)S(1)} %get-tuple-element.66.refs_3_.refs_0_), custom_call_target="tpu_custom_call" | custom-call | flops 1800000000 | bytes 5400000 | tf_op jit(solution)/shard_map/target/pallas_call | solution.py:506
  45.6 3.3 %collective-permute-done.10.refs_3_ = s16[4,288,128]{2,1,0:T(8,128)(2,1)S(1)} collective-permute-done((s16[4,288,128]{2,1,0:T(8,128)(2,1)S(1)}, s16[4,288,128]{2,1,0:T(8,128)(2,1)S(1)}, u32[]{:S(2)}, u32[]{:S(2)}) %collective-permute-start.10) | collective-permute-done | bytes 294944 | tf_op jit(solution)/shard_map/ppermute | solution.py:187
  48.9 5.2 %collective-permute-done.8.refs_1_ = s16[4,288,128]{2,1,0:T(8,128)(2,1)S(1)} collective-permute-done((s16[4,288,128]{2,1,0:T(8,128)(2,1)S(1)}, s16[4,288,128]{2,1,0:T(8,128)(2,1)S(1)}, u32[]{:S(2)}, u32[]{:S(2)}) %collective-permute-start.8) | collective-permute-done | bytes 294944 | tf_op jit(solution)/shard_map/ppermute | solution.py:187
  54.8 2.7 %collective-permute-start.16 = (s16[416,256]{1,0:T(8,128)(2,1)S(1)}, s16[416,256]{1,0:T(8,128)(2,1)S(1)}, u32[]{:S(2)}, u32[]{:S(2)}) collective-permute-start(s16[416,256]{1,0:T(8,128)(2,1)S(1)} %get-tuple-element.78), channel_id=1, source_target_pairs={{0,1},{1,0},{2,3},{3,2},{4,5},{5,4},{6,7},{7,6},{8,9},{9,8},{10,11... | collective-permute-start | bytes 638984 | tf_op jit(solution)/shard_map/ppermute | solution.py:187
  57.5 2.7 %collective-permute-start.17 = (s16[416,128]{1,0:T(8,128)(2,1)S(1)}, s16[416,128]{1,0:T(8,128)(2,1)S(1)}, u32[]{:S(2)}, u32[]{:S(2)}) collective-permute-start(s16[416,128]{1,0:T(8,128)(2,1)S(1)} %get-tuple-element.80), channel_id=1, source_target_pairs={{0,2},{1,3},{2,0},{3,1},{4,6},{5,7},{6,4},{7,5},{8,10},{9,11},{10,... | collective-permute-start | bytes 319496 | tf_op jit(solution)/shard_map/ppermute | solution.py:187
  60.2 2.0 %collective-permute-start.14 = (s16[1,288,128]{2,1,0:T(8,128)(2,1)S(1)}, s16[1,288,128]{2,1,0:T(8,128)(2,1)S(1)}, u32[]{:S(2)}, u32[]{:S(2)}) collective-permute-start(s16[1,288,128]{2,1,0:T(8,128)(2,1)S(1)} %get-tuple-element.75), channel_id=1, source_target_pairs={{0,16},{1,17},{2,18},{3,19},{4,20},{5,21},{6,22},{7,23},{8,24},{9,... | collective-permute-start | bytes 221192 | tf_op jit(solution)/shard_map/ppermute | solution.py:187
  62.1 2.4 %collective-permute-start.15 = (s16[1,288,128]{2,1,0:T(8,128)(2,1)S(1)}, s16[1,288,128]{2,1,0:T(8,128)(2,1)S(1)}, u32[]{:S(2)}, u32[]{:S(2)}) collective-permute-start(s16[1,288,128]{2,1,0:T(8,128)(2,1)S(1)} %get-tuple-element.76), channel_id=1, source_target_pairs={{0,24},{1,25},{2,26},{3,27},{4,28},{5,29},{6,30},{7,31},{8,16},{9,... | collective-permute-start | bytes 221192 | tf_op jit(solution)/shard_map/ppermute | solution.py:187
  65.6 3.8 %collective-permute-done.14.refs_2_ = s16[1,288,128]{2,1,0:T(8,128)(2,1)S(1)} collective-permute-done((s16[1,288,128]{2,1,0:T(8,128)(2,1)S(1)}, s16[1,288,128]{2,1,0:T(8,128)(2,1)S(1)}, u32[]{:S(2)}, u32[]{:S(2)}) %collective-permute-start.14) | collective-permute-done | bytes 73760 | tf_op jit(solution)/shard_map/ppermute | solution.py:187
  75.7 4.5 %collective-permute-done.19.refs_2_ = s16[1,288,128]{2,1,0:T(8,128)(2,1)S(1)} collective-permute-done((s16[1,288,128]{2,1,0:T(8,128)(2,1)S(1)}, s16[1,288,128]{2,1,0:T(8,128)(2,1)S(1)}, u32[]{:S(2)}, u32[]{:S(2)}) %collective-permute-start.19) | collective-permute-done | bytes 73760 | tf_op jit(solution)/shard_map/ppermute | solution.py:187
  80.4 1.7 %collective-permute-start.27 = (s16[4,288,128]{2,1,0:T(8,128)(2,1)S(1)}, s16[4,288,128]{2,1,0:T(8,128)(2,1)S(1)}, u32[]{:S(2)}, u32[]{:S(2)}) collective-permute-start(s16[4,288,128]{2,1,0:T(8,128)(2,1)S(1)} %get-tuple-element.86.refs_0_), channel_id=1, source_target_pairs={{0,2},{1,3},{2,0},{3,1},{4,6},{5,7},{6,4},{7,5},{8,10},{9,11},{10,... | collective-permute-start | bytes 884744 | tf_op jit(solution)/shard_map/ppermute | solution.py:187
  83.9 1.7 %collective-permute-start.24 = (s16[416,128]{1,0:T(8,128)(2,1)S(1)}, s16[416,128]{1,0:T(8,128)(2,1)S(1)}, u32[]{:S(2)}, u32[]{:S(2)}) collective-permute-start(s16[416,128]{1,0:T(8,128)(2,1)S(1)} %get-tuple-element.85.refs_0_), channel_id=1, source_target_pairs={{0,2},{1,3},{2,0},{3,1},{4,6},{5,7},{6,4},{7,5},{8,10},{9,11},{10,... | collective-permute-start | bytes 319496 | tf_op jit(solution)/shard_map/ppermute | solution.py:187
  85.6 9.7 %collective-permute-done.24.refs_2_ = s16[416,128]{1,0:T(8,128)(2,1)S(1)} collective-permute-done((s16[416,128]{1,0:T(8,128)(2,1)S(1)}, s16[416,128]{1,0:T(8,128)(2,1)S(1)}, u32[]{:S(2)}, u32[]{:S(2)}) %collective-permute-start.24) | collective-permute-done | bytes 106528 | tf_op jit(solution)/shard_map/ppermute | solution.py:187
  97.7 1.7 %spread.2 = (f32[400,2560]{1,0:T(8,128)}, f32[400,256]{1,0:T(8,128)}) custom-call(s32[1]{0:T(128)} %bitcast.6.side, s16[4,288,128]{2,1,0:T(8,128)(2,1)S(1)} %get-tuple-element.86.refs_0_, s16[4,288,128]{2,1,0:T(8,128)(2,1)S(1)} %collective-permute-done.27.refs_1_, s16[4,288,128]{2,1,0:T(8,128)(2,1)S(1)} %collective-permute-done.29.refs_2_, ...), custom_call_target="tpu_custom_call" | custom-call | flops 2000000000 | bytes 6000000 | tf_op jit(solution)/shard_map/spread/pallas_call | solution.py:506
  99.4 1.7 %spread.3 = (f32[400,2560]{1,0:T(8,128)}, f32[400,256]{1,0:T(8,128)}) custom-call(s32[1]{0:T(128)} %bitcast.5.side, s16[4,288,128]{2,1,0:T(8,128)(2,1)S(1)} %collective-permute-done.26.refs_0_, s16[4,288,128]{2,1,0:T(8,128)(2,1)S(1)} %collective-permute-done.28.refs_1_, ...), custom_call_target="tpu_custom_call", output_to_operand_aliasing={{0}: (5, {}), {1}: (6, {})} | custom-call | flops 2000000000 | bytes 6000000 | tf_op jit(solution)/shard_map/spread/pallas_call | solution.py:506
  (68 shorter events, 23.6 us)
Async XLA Ops:
  0.6 20.9 %collective-permute-start.4 = (bf16[400,512]{1,0:T(8,128)(2,1)}, bf16[400,512]{1,0:T(8,128)(2,1)S(1)}, u32[]{:S(2)}, u32[]{:S(2)}) collective-permute-start(bf16[400,512]{1,0:T(8,128)(2,1)} %bitcast.9), channel_id=1, source_target_pairs={{0,0},{1,17},{2,10},{3,27},{4,4},{5,21},{6,14},{7,31},{8,8},{9,25}... | collective-permute-start | bytes 1228808 | tf_op jit(solution)/shard_map/ppermute | solution.py:187
  2.3 18.5 %collective-permute-start.5 = (bf16[400,512]{1,0:T(8,128)(2,1)}, bf16[400,512]{1,0:T(8,128)(2,1)S(1)}, u32[]{:S(2)}, u32[]{:S(2)}) collective-permute-start(bf16[400,512]{1,0:T(8,128)(2,1)} %bitcast.10), channel_id=1, source_target_pairs={{0,4},{1,5},{2,6},{3,7},{4,0},{5,1},{6,2},{7,3},{8,12},{9,13},{10,... | collective-permute-start | bytes 1228808 | tf_op jit(solution)/shard_map/ppermute | solution.py:187
  6.7 7.6 %collective-permute-start = (s32[2,8,128]{2,1,0:T(8,128)}, s32[2,8,128]{2,1,0:T(8,128)S(1)}, u32[]{:S(2)}, u32[]{:S(2)}) collective-permute-start(s32[2,8,128]{2,1,0:T(8,128)} %get-tuple-element.48), channel_id=1, source_target_pairs={{0,1},{1,0},{2,3},{3,2},{4,5},{5,4},{6,7},{7,6},{8,9},{9,8},{10,11... | collective-permute-start | bytes 24584 | tf_op jit(solution)/shard_map/ppermute | solution.py:187
  8.9 5.4 %collective-permute-start.1 = (s32[2,8,128]{2,1,0:T(8,128)}, s32[2,8,128]{2,1,0:T(8,128)S(1)}, u32[]{:S(2)}, u32[]{:S(2)}) collective-permute-start(s32[2,8,128]{2,1,0:T(8,128)} %get-tuple-element.49), channel_id=1, source_target_pairs={{0,2},{1,3},{2,0},{3,1},{4,6},{5,7},{6,4},{7,5},{8,10},{9,11},{10,... | collective-permute-start | bytes 24584 | tf_op jit(solution)/shard_map/ppermute | solution.py:187
  33.6 3.8 %collective-permute-start.6 = (s16[16,288,128]{2,1,0:T(8,128)(2,1)S(1)}, s16[16,288,128]{2,1,0:T(8,128)(2,1)S(1)}, u32[]{:S(2)}, u32[]{:S(2)}) collective-permute-start(s16[16,288,128]{2,1,0:T(8,128)(2,1)S(1)} %get-tuple-element.63.refs_2_), channel_id=1, source_target_pairs={{0,1},{1,0},{2,3},{3,2},{4,5},{5,4},{6,7},{7,6},{8,9},{9,8},{10,11... | collective-permute-start | bytes 3538952 | tf_op jit(solution)/shard_map/ppermute | solution.py:187
  38.0 10.9 %collective-permute-start.10 = (s16[4,288,128]{2,1,0:T(8,128)(2,1)S(1)}, s16[4,288,128]{2,1,0:T(8,128)(2,1)S(1)}, u32[]{:S(2)}, u32[]{:S(2)}) collective-permute-start(s16[4,288,128]{2,1,0:T(8,128)(2,1)S(1)} %get-tuple-element.69), channel_id=1, source_target_pairs={{0,6},{1,7},{2,4},{3,5},{4,2},{5,3},{6,0},{7,1},{8,14},{9,15},{10,... | collective-permute-start | bytes 884744 | tf_op jit(solution)/shard_map/ppermute | solution.py:187
  40.0 14.1 %collective-permute-start.8 = (s16[4,288,128]{2,1,0:T(8,128)(2,1)S(1)}, s16[4,288,128]{2,1,0:T(8,128)(2,1)S(1)}, u32[]{:S(2)}, u32[]{:S(2)}) collective-permute-start(s16[4,288,128]{2,1,0:T(8,128)(2,1)S(1)} %get-tuple-element.67), channel_id=1, source_target_pairs={{0,2},{1,3},{2,0},{3,1},{4,6},{5,7},{6,4},{7,5},{8,10},{9,11},{10,... | collective-permute-start | bytes 884744 | tf_op jit(solution)/shard_map/ppermute | solution.py:187
  40.8 13.4 %collective-permute-start.9 = (s16[4,288,128]{2,1,0:T(8,128)(2,1)S(1)}, s16[4,288,128]{2,1,0:T(8,128)(2,1)S(1)}, u32[]{:S(2)}, u32[]{:S(2)}) collective-permute-start(s16[4,288,128]{2,1,0:T(8,128)(2,1)S(1)} %get-tuple-element.68), channel_id=1, source_target_pairs={{0,4},{1,5},{2,6},{3,7},{4,0},{5,1},{6,2},{7,3},{8,12},{9,13},{10,... | collective-permute-start | bytes 884744 | tf_op jit(solution)/shard_map/ppermute | solution.py:187
  54.8 14.6 %collective-permute-start.16 = (s16[416,256]{1,0:T(8,128)(2,1)S(1)}, s16[416,256]{1,0:T(8,128)(2,1)S(1)}, u32[]{:S(2)}, u32[]{:S(2)}) collective-permute-start(s16[416,256]{1,0:T(8,128)(2,1)S(1)} %get-tuple-element.78), channel_id=1, source_target_pairs={{0,1},{1,0},{2,3},{3,2},{4,5},{5,4},{6,7},{7,6},{8,9},{9,8},{10,11... | collective-permute-start | bytes 638984 | tf_op jit(solution)/shard_map/ppermute | solution.py:187
  57.5 11.8 %collective-permute-start.17 = (s16[416,128]{1,0:T(8,128)(2,1)S(1)}, s16[416,128]{1,0:T(8,128)(2,1)S(1)}, u32[]{:S(2)}, u32[]{:S(2)}) collective-permute-start(s16[416,128]{1,0:T(8,128)(2,1)S(1)} %get-tuple-element.80), channel_id=1, source_target_pairs={{0,2},{1,3},{2,0},{3,1},{4,6},{5,7},{6,4},{7,5},{8,10},{9,11},{10,... | collective-permute-start | bytes 319496 | tf_op jit(solution)/shard_map/ppermute | solution.py:187
  60.2 5.4 %collective-permute-start.13 = (s16[1,288,128]{2,1,0:T(8,128)(2,1)S(1)}, s16[1,288,128]{2,1,0:T(8,128)(2,1)S(1)}, u32[]{:S(2)}, u32[]{:S(2)}) collective-permute-start(s16[1,288,128]{2,1,0:T(8,128)(2,1)S(1)} %get-tuple-element.74), channel_id=1, source_target_pairs={{0,8},{1,9},{2,10},{3,11},{4,12},{5,13},{6,14},{7,15},{8,0},{9,1},... | collective-permute-start | bytes 221192 | tf_op jit(solution)/shard_map/ppermute | solution.py:187
  60.2 9.2 %collective-permute-start.14 = (s16[1,288,128]{2,1,0:T(8,128)(2,1)S(1)}, s16[1,288,128]{2,1,0:T(8,128)(2,1)S(1)}, u32[]{:S(2)}, u32[]{:S(2)}) collective-permute-start(s16[1,288,128]{2,1,0:T(8,128)(2,1)S(1)} %get-tuple-element.75), channel_id=1, source_target_pairs={{0,16},{1,17},{2,18},{3,19},{4,20},{5,21},{6,22},{7,23},{8,24},{9,... | collective-permute-start | bytes 221192 | tf_op jit(solution)/shard_map/ppermute | solution.py:187
  62.1 7.2 %collective-permute-start.15 = (s16[1,288,128]{2,1,0:T(8,128)(2,1)S(1)}, s16[1,288,128]{2,1,0:T(8,128)(2,1)S(1)}, u32[]{:S(2)}, u32[]{:S(2)}) collective-permute-start(s16[1,288,128]{2,1,0:T(8,128)(2,1)S(1)} %get-tuple-element.76), channel_id=1, source_target_pairs={{0,24},{1,25},{2,26},{3,27},{4,28},{5,29},{6,30},{7,31},{8,16},{9,... | collective-permute-start | bytes 221192 | tf_op jit(solution)/shard_map/ppermute | solution.py:187
  69.6 10.6 %collective-permute-start.21 = (s16[416,128]{1,0:T(8,128)(2,1)S(1)}, s16[416,128]{1,0:T(8,128)(2,1)S(1)}, u32[]{:S(2)}, u32[]{:S(2)}) collective-permute-start(s16[416,128]{1,0:T(8,128)(2,1)S(1)} %get-tuple-element.83), channel_id=1, source_target_pairs={{0,2},{1,3},{2,0},{3,1},{4,6},{5,7},{6,4},{7,5},{8,10},{9,11},{10,... | collective-permute-start | bytes 319496 | tf_op jit(solution)/shard_map/ppermute | solution.py:187
  69.8 10.4 %collective-permute-start.22 = (s16[416,128]{1,0:T(8,128)(2,1)S(1)}, s16[416,128]{1,0:T(8,128)(2,1)S(1)}, u32[]{:S(2)}, u32[]{:S(2)}) collective-permute-start(s16[416,128]{1,0:T(8,128)(2,1)S(1)} %get-tuple-element.84), channel_id=1, source_target_pairs={{0,4},{1,5},{2,6},{3,7},{4,0},{5,1},{6,2},{7,3},{8,12},{9,13},{10,... | collective-permute-start | bytes 319496 | tf_op jit(solution)/shard_map/ppermute | solution.py:187
  71.0 4.7 %collective-permute-start.18 = (s16[1,288,128]{2,1,0:T(8,128)(2,1)S(1)}, s16[1,288,128]{2,1,0:T(8,128)(2,1)S(1)}, u32[]{:S(2)}, u32[]{:S(2)}) collective-permute-start(s16[1,288,128]{2,1,0:T(8,128)(2,1)S(1)} %get-tuple-element.81.refs_0_), channel_id=1, source_target_pairs={{0,8},{1,9},{2,10},{3,11},{4,12},{5,13},{6,14},{7,15},{8,0},{9,1},... | collective-permute-start | bytes 221192 | tf_op jit(solution)/shard_map/ppermute | solution.py:187
  72.5 7.7 %collective-permute-start.19 = (s16[1,288,128]{2,1,0:T(8,128)(2,1)S(1)}, s16[1,288,128]{2,1,0:T(8,128)(2,1)S(1)}, u32[]{:S(2)}, u32[]{:S(2)}) collective-permute-start(s16[1,288,128]{2,1,0:T(8,128)(2,1)S(1)} %get-tuple-element.81.refs_0_), channel_id=1, source_target_pairs={{0,16},{1,17},{2,18},{3,19},{4,20},{5,21},{6,22},{7,23},{8,24},{9,... | collective-permute-start | bytes 221192 | tf_op jit(solution)/shard_map/ppermute | solution.py:187
  73.8 6.5 %collective-permute-start.20 = (s16[1,288,128]{2,1,0:T(8,128)(2,1)S(1)}, s16[1,288,128]{2,1,0:T(8,128)(2,1)S(1)}, u32[]{:S(2)}, u32[]{:S(2)}) collective-permute-start(s16[1,288,128]{2,1,0:T(8,128)(2,1)S(1)} %get-tuple-element.81.refs_0_), channel_id=1, source_target_pairs={{0,24},{1,25},{2,26},{3,27},{4,28},{5,29},{6,30},{7,31},{8,16},{9,... | collective-permute-start | bytes 221192 | tf_op jit(solution)/shard_map/ppermute | solution.py:187
  80.4 15.5 %collective-permute-start.27 = (s16[4,288,128]{2,1,0:T(8,128)(2,1)S(1)}, s16[4,288,128]{2,1,0:T(8,128)(2,1)S(1)}, u32[]{:S(2)}, u32[]{:S(2)}) collective-permute-start(s16[4,288,128]{2,1,0:T(8,128)(2,1)S(1)} %get-tuple-element.86.refs_0_), channel_id=1, source_target_pairs={{0,2},{1,3},{2,0},{3,1},{4,6},{5,7},{6,4},{7,5},{8,10},{9,11},{10,... | collective-permute-start | bytes 884744 | tf_op jit(solution)/shard_map/ppermute | solution.py:187
  82.1 13.8 %collective-permute-start.29 = (s16[4,288,128]{2,1,0:T(8,128)(2,1)S(1)}, s16[4,288,128]{2,1,0:T(8,128)(2,1)S(1)}, u32[]{:S(2)}, u32[]{:S(2)}) collective-permute-start(s16[4,288,128]{2,1,0:T(8,128)(2,1)S(1)} %get-tuple-element.86.refs_0_), channel_id=1, source_target_pairs={{0,4},{1,5},{2,6},{3,7},{4,0},{5,1},{6,2},{7,3},{8,12},{9,13},{10,... | collective-permute-start | bytes 884744 | tf_op jit(solution)/shard_map/ppermute | solution.py:187
  82.6 13.7 %collective-permute-start.31 = (s16[4,288,128]{2,1,0:T(8,128)(2,1)S(1)}, s16[4,288,128]{2,1,0:T(8,128)(2,1)S(1)}, u32[]{:S(2)}, u32[]{:S(2)}) collective-permute-start(s16[4,288,128]{2,1,0:T(8,128)(2,1)S(1)} %get-tuple-element.86.refs_0_), channel_id=1, source_target_pairs={{0,6},{1,7},{2,4},{3,5},{4,2},{5,3},{6,0},{7,1},{8,14},{9,15},{10,... | collective-permute-start | bytes 884744 | tf_op jit(solution)/shard_map/ppermute | solution.py:187
  83.9 11.4 %collective-permute-start.24 = (s16[416,128]{1,0:T(8,128)(2,1)S(1)}, s16[416,128]{1,0:T(8,128)(2,1)S(1)}, u32[]{:S(2)}, u32[]{:S(2)}) collective-permute-start(s16[416,128]{1,0:T(8,128)(2,1)S(1)} %get-tuple-element.85.refs_0_), channel_id=1, source_target_pairs={{0,2},{1,3},{2,0},{3,1},{4,6},{5,7},{6,4},{7,5},{8,10},{9,11},{10,... | collective-permute-start | bytes 319496 | tf_op jit(solution)/shard_map/ppermute | solution.py:187
  85.6 9.7 %collective-permute-start.23 = (s16[416,128]{1,0:T(8,128)(2,1)S(1)}, s16[416,128]{1,0:T(8,128)(2,1)S(1)}, u32[]{:S(2)}, u32[]{:S(2)}) collective-permute-start(s16[416,128]{1,0:T(8,128)(2,1)S(1)} %get-tuple-element.85.refs_0_), channel_id=1, source_target_pairs={{0,1},{1,0},{2,3},{3,2},{4,5},{5,4},{6,7},{7,6},{8,9},{9,8},{10,11... | collective-permute-start | bytes 319496 | tf_op jit(solution)/shard_map/ppermute | solution.py:187
  95.3 4.0 %collective-permute-start.26 = (s16[4,288,128]{2,1,0:T(8,128)(2,1)S(1)}, s16[4,288,128]{2,1,0:T(8,128)(2,1)S(1)}, u32[]{:S(2)}, u32[]{:S(2)}) collective-permute-start(s16[4,288,128]{2,1,0:T(8,128)(2,1)S(1)} %get-tuple-element.86.refs_0_), channel_id=1, source_target_pairs={{0,1},{1,0},{2,3},{3,2},{4,5},{5,4},{6,7},{7,6},{8,9},{9,8},{10,11... | collective-permute-start | bytes 884744 | tf_op jit(solution)/shard_map/ppermute | solution.py:187
  (12 other events, 32.6 us)

commit v10 on v9

--- a/solution.py
+++ b/solution.py
@@ -357,10 +357,7 @@
 def target_kernel(plan, *refs):
     count = plan.buckets
     ids = plan.whole_row(refs[:count], (3, 5))
-    value = pack_table(rows_sum(plan, ids, refs[count][...]))
-    for at, out in enumerate(refs[-2:]):
-        lanes = out.shape[1]
-        out[...] = value[:, at * lanes : (at + 1) * lanes]
+    refs[-1][...] = pack_table(rows_sum(plan, ids, refs[count][...]))
 
 
 def source_sum(plan, labels, grads):
@@ -389,10 +386,9 @@
 
 
 def share(plan, count, *refs):
-    source, fars, others = refs[0], refs[1:3], refs[3 : 3 + 2 * count]
-    outs = refs[3 + 2 * count :]
-    far = jnp.concatenate([unpack_table(ref[...]) for ref in fars], axis=1)
-    deal(plan, source[...] + far, *outs[:2])
+    source, far, others = refs[0], refs[1], refs[2 : 2 + 2 * count]
+    outs = refs[2 + 2 * count :]
+    deal(plan, source[...] + unpack_table(far[...]), *outs[:2])
     for at in range(0, 2 * count, 2):
         deal_again(plan, *others[at : at + 2], *outs[at + 2 : at + 4])
 
@@ -477,6 +473,10 @@
                     rem_out[rows, lane : lane + LANES] = piece
 
 
+def relay_kernel(*refs):
+    pass
+
+
 def part_out_kernel(plan, *refs):
     out = refs[-1]
     rel = lax.axis_index("rel")
@@ -652,24 +652,11 @@
     away, rem_part = made[:-1], made[-1]
     cores = [send(value, plan, lambda d: d ^ 1) for value in away]
 
-    others, order = [], list(away)
-    for bucket in range(1, buckets):
-        keep, value = after(
-            functools.partial(source_kernel, plan, bucket),
-            dealt(plan.rels // 2),
-            labels_of(bucket) + [grads[0]],
-            order,
-            "source",
-            0.8,
-            12 * grow,
-        )
-        others.append([keep, send(value, plan, lambda d: d ^ 1)])
-        order = [keep]
     keeps = after(
         functools.partial(home_kernel, plan),
         [shape(part.bare, F32) for part in plan.parts],
         labels + [grads[1], rem_part],
-        order,
+        list(away),
         "home",
         3.0,
         16 * grow,
@@ -706,22 +693,35 @@
         return keeps, arrived, beside
 
     keeps, arrived, _ = combine(
-        keeps, [[core] for core in cores], 0, "combine_cores", order=[other[1] for other in others]
+        keeps, [[core] for core in cores], 0, "combine_cores"
     )
     far = after(
         functools.partial(target_kernel, plan),
-        [shape((width + 16, prows // 2), i16)] * 2,
+        [shape((width + 16, prows), i16)],
         labels + [grads[2]],
         [keeps[0]],
         "target",
         1.8,
         16 * grow,
     )
+    others, order = [], [far[0]]
+    for bucket in range(1, buckets):
+        keep, value = after(
+            functools.partial(source_kernel, plan, bucket),
+            dealt(plan.rels // 2),
+            labels_of(bucket) + [grads[0]],
+            order,
+            "source",
+            0.8,
+            12 * grow,
+        )
+        others.append([keep, send(value, plan, lambda d: d ^ 1)])
+        order = [keep]
     (source,) = after(
         functools.partial(own_source_kernel, plan),
         [shape((width, prows), F32)],
         labels_of(0) + [grads[0]],
-        [far[0]],
+        order,
         "own_source",
         0.8,
         16 * grow,
@@ -786,7 +786,21 @@
         for part, block in zip(plan.parts, blocks)
     ]
     while bit:
-        for mask in sorted(owners):
+        masks = sorted(owners)
+        if bit == 1:
+            held = call(
+                relay_kernel,
+                [shape((width + 16, lanes), i16)] * len(masks),
+                [owners[mask] for mask in masks] + pieces[0][1:],
+                "relay",
+                0.1,
+                1,
+                in_specs=[ANY] * (len(masks) + len(pieces[0]) - 1),
+                out_specs=[ANY] * len(masks),
+                input_output_aliases={at: at for at in range(len(masks))},
+            )
+            owners = dict(zip(masks, held))
+        for mask in masks:
             owners[mask | bit] = send(owners[mask], plan, lambda d, m=bit: d ^ m)
         bit //= 2
     (grad_partitions,) = after(

time: 101 us -> 103 us (1.020)
  waiting for transfers between devices: 28.9 us -> 34.2 us
  starting transfers between devices: 37.3 us -> 33.4 us
    ppermute x33 -> x32, waiting for transfers between devices: 28.9 us -> 34.2 us  [send(): return lax.ppermute(value, ('dom', 'rel'), pairs)]
    ppermute x33 -> x32, starting transfers between devices: 37.3 us -> 33.4 us  [send(): return lax.ppermute(value, ('dom', 'rel'), pairs)]
    pallas_call x20 -> x21, Pallas kernels: 34 us -> 34.1 us  [call(): pl.pallas_call(kernel, out_shape=outs, compiler_params=pltpu.CompilerPara...]
  transfers between devices with their start and end apart: 33 -> 32, of which waited for: 11 -> 13; matrix products, arithmetic and copies ran while one was open for 0% -> 0% of each run, Pallas kernels for 19% -> 16%
where the time goes in v10:
time: 103 us
  waiting for transfers between devices  34.2 us (33%)
  Pallas kernels  34.1 us (33%)
  starting transfers between devices  33.4 us (32%)
    ppermute x32, waiting for transfers between devices, send(): return lax.ppermute(value, ('dom', 'rel'), pairs)  34.2 us
    pallas_call x21, Pallas kernels, call(): pl.pallas_call(kernel, out_shape=outs, compiler_params=pltpu.CompilerPara...  34.1 us
    ppermute x32, starting transfers between devices, send(): return lax.ppermute(value, ('dom', 'rel'), pairs)  33.4 us
  transfers between devices with their start and end apart: 32, of which 13 were waited for; matrix products, arithmetic and copies ran while one was open for 0% of the time, Pallas kernels for 16%

profile of v10, /device:TPU:0, one launch (start us, length us, event | category | flops | bytes accessed | tf_op | source)
XLA Modules:
  0.0 102.7 jit_solution(4294387861107192097)
XLA Ops:
  0.6 1.7 %collective-permute-start.4 = (bf16[400,512]{1,0:T(8,128)(2,1)}, bf16[400,512]{1,0:T(8,128)(2,1)S(1)}, u32[]{:S(2)}, u32[]{:S(2)}) collective-permute-start(bf16[400,512]{1,0:T(8,128)(2,1)} %bitcast.9), channel_id=1, source_target_pairs={{0,0},{1,17},{2,10},{3,27},{4,4},{5,21},{6,14},{7,31},{8,8},{9,25}... | collective-permute-start | bytes 1228808 | tf_op jit(solution)/shard_map/ppermute | solution.py:187
  2.3 3.0 %collective-permute-start.5 = (bf16[400,512]{1,0:T(8,128)(2,1)}, bf16[400,512]{1,0:T(8,128)(2,1)S(1)}, u32[]{:S(2)}, u32[]{:S(2)}) collective-permute-start(bf16[400,512]{1,0:T(8,128)(2,1)} %bitcast.10), channel_id=1, source_target_pairs={{0,4},{1,5},{2,6},{3,7},{4,0},{5,1},{6,2},{7,3},{8,12},{9,13},{10,... | collective-permute-start | bytes 1228808 | tf_op jit(solution)/shard_map/ppermute | solution.py:187
  5.3 1.5 %lists.1 = (s32[2,8,128]{2,1,0:T(8,128)}, s32[2,8,128]{2,1,0:T(8,128)}, s32[2,8,128]{2,1,0:T(8,128)}, s32[2,8,128]{2,1,0:T(8,128)}) custom-call(s32[1,8,1,128]{3,2,1,0:T(1,128)} %refs_0_.1, s32[1,8,1,128]{3,2,1,0:T(1,128)} %refs_1_.1, s32[1,8,1,128]{3,2,1,0:T(1,128)} %refs_2_.1, s32[1,8,1,128]{3,2,1,0:T(1,128)} %refs_3_.1, s32[1,8,1,128]{3,2,1,0:T(1,128)} %refs_4_.1, ...), custom_call_target="tpu_custom_call" | custom-call | flops 500000000 | bytes 1500000 | tf_op jit(solution)/shard_map/lists/pallas_call | solution.py:506
  6.7 2.2 %collective-permute-start = (s32[2,8,128]{2,1,0:T(8,128)}, s32[2,8,128]{2,1,0:T(8,128)S(1)}, u32[]{:S(2)}, u32[]{:S(2)}) collective-permute-start(s32[2,8,128]{2,1,0:T(8,128)} %get-tuple-element.48), channel_id=1, source_target_pairs={{0,1},{1,0},{2,3},{3,2},{4,5},{5,4},{6,7},{7,6},{8,9},{9,8},{10,11... | collective-permute-start | bytes 24584 | tf_op jit(solution)/shard_map/ppermute | solution.py:187
  8.9 2.5 %collective-permute-start.1 = (s32[2,8,128]{2,1,0:T(8,128)}, s32[2,8,128]{2,1,0:T(8,128)S(1)}, u32[]{:S(2)}, u32[]{:S(2)}) collective-permute-start(s32[2,8,128]{2,1,0:T(8,128)} %get-tuple-element.49), channel_id=1, source_target_pairs={{0,2},{1,3},{2,0},{3,1},{4,6},{5,7},{6,4},{7,5},{8,10},{9,11},{10,... | collective-permute-start | bytes 24584 | tf_op jit(solution)/shard_map/ppermute | solution.py:187
  11.4 2.9 %rel_split.1.refs_1_ = bf16[800,2560]{1,0:T(8,128)(2,1)S(1)} custom-call(f32[400,2560]{1,0:T(8,128)} %bitcast.14), custom_call_target="tpu_custom_call" | custom-call | flops 2000000000 | bytes 6000000 | tf_op jit(solution)/shard_map/rel_split/pallas_call | solution.py:506
  15.3 2.3 %relation.2.refs_3_ = f32[400,512]{1,0:T(8,128)S(1)} custom-call(s32[4,8,128]{2,1,0:T(8,128)S(1)} %get-tuple-element.51.refs_0_, bf16[800,2560]{1,0:T(8,128)(2,1)S(1)} %rel_split.1.refs_1_), custom_call_target="tpu_custom_call" | custom-call | flops 2000000000 | bytes 6000000 | tf_op jit(solution)/shard_map/relation/pallas_call | solution.py:506
  18.5 2.3 %relation.3.refs_7_ = f32[400,512]{1,0:T(8,128)S(1)} custom-call(s32[4,8,128]{2,1,0:T(8,128)S(1)} %collective-permute-done.3.refs_0_.refs_1_, bf16[800,2560]{1,0:T(8,128)(2,1)S(1)} %rel_split.1.refs_1_), custom_call_target="tpu_custom_call" | custom-call | flops 2000000000 | bytes 6000000 | tf_op jit(solution)/shard_map/relation/pallas_call | solution.py:506
  21.5 4.1 %bucket.1 = (bf16[800,512]{1,0:T(8,128)(2,1)S(1)}, bf16[800,512]{1,0:T(8,128)(2,1)S(1)}, bf16[800,1024]{1,0:T(8,128)(2,1)S(1)}) custom-call(s32[4,8,128]{2,1,0:T(8,128)S(1)} %get-tuple-element.51.refs_0_, bf16[400,512]{1,0:T(8,128)(2,1)S(1)} %collective-permute-done.4.refs_1_.refs_5_, f32[400,512]{1,0:T(8,128)S(1)} %get-tuple-element.53.refs_2_, ...), custom_call_target="tpu_custom_call" | custom-call | flops 4000000000 | bytes 12000000 | tf_op jit(solution)/shard_map/bucket/pallas_call | solution.py:506
  25.6 8.0 %last.1 = (s16[16,288,128]{2,1,0:T(8,128)(2,1)S(1)}, f32[400,128]{1,0:T(8,128)S(1)}, bf16[800,1024]{1,0:T(8,128)(2,1)S(1)}, bf16[800,1024]{1,0:T(8,128)(2,1)S(1)}, bf16[800,2048]{1,0:T(8,128)(2,1)S(1)}) custom-call(s32[4,8,128]{2,1,0:T(8,128)S(1)} %get-tuple-element.51.refs_0_, s32[4,8,128]{2,1,0:T(8,128)S(1)} %collective-permute-done.3.refs_0_.refs_1_, ...), custom_call_target="tpu_custom_call" | custom-call | flops 8999999488 | bytes 27000000 | tf_op jit(solution)/shard_map/last/pallas_call | solution.py:506
  33.7 2.4 %home.1.refs_0_ = f32[16,280,128]{2,1,0:T(8,128)S(1)} custom-call(s32[4,8,128]{2,1,0:T(8,128)S(1)} %get-tuple-element.51.refs_0_, s32[4,8,128]{2,1,0:T(8,128)S(1)} %collective-permute-done.3.refs_0_.refs_1_, bf16[800,1024]{1,0:T(8,128)(2,1)S(1)} %get-tuple-element.60.refs_2_, f32[400,128]{1,0:T(8,128)S(1)} %get-tuple-element.61.refs_3_, ...), custom_call_target="tpu_custom_call" | custom-call | flops 3000000000 | bytes 9000000 | tf_op jit(solution)/shard_map/home/pallas_call | solution.py:506
  37.2 2.0 %target.1.refs_2_ = s16[416,512]{1,0:T(8,128)(2,1)S(1)} custom-call(s32[4,8,128]{2,1,0:T(8,128)S(1)} %get-tuple-element.51.refs_0_, s32[4,8,128]{2,1,0:T(8,128)S(1)} %collective-permute-done.3.refs_0_.refs_1_, bf16[800,2048]{1,0:T(8,128)(2,1)S(1)} %get-tuple-element.68.refs_2_, f32[4,280,128]{2,1,0:T(8,128)S(1)} %get-tuple-element.63.refs_3_.refs_0_), custom_call_target="tpu_custom_call" | custom-call | flops 1800000000 | bytes 5400000 | tf_op jit(solution)/shard_map/target/pallas_call | solution.py:506
  39.9 3.0 %collective-permute-start.7 = (s16[4,288,128]{2,1,0:T(8,128)(2,1)S(1)}, s16[4,288,128]{2,1,0:T(8,128)(2,1)S(1)}, u32[]{:S(2)}, u32[]{:S(2)}) collective-permute-start(s16[4,288,128]{2,1,0:T(8,128)(2,1)S(1)} %get-tuple-element.64), channel_id=1, source_target_pairs={{0,2},{1,3},{2,0},{3,1},{4,6},{5,7},{6,4},{7,5},{8,10},{9,11},{10,... | collective-permute-start | bytes 884744 | tf_op jit(solution)/shard_map/ppermute | solution.py:187
  42.9 1.5 %collective-permute-start.8 = (s16[4,288,128]{2,1,0:T(8,128)(2,1)S(1)}, s16[4,288,128]{2,1,0:T(8,128)(2,1)S(1)}, u32[]{:S(2)}, u32[]{:S(2)}) collective-permute-start(s16[4,288,128]{2,1,0:T(8,128)(2,1)S(1)} %get-tuple-element.65), channel_id=1, source_target_pairs={{0,4},{1,5},{2,6},{3,7},{4,0},{5,1},{6,2},{7,3},{8,12},{9,13},{10,... | collective-permute-start | bytes 884744 | tf_op jit(solution)/shard_map/ppermute | solution.py:187
  46.8 3.4 %collective-permute-done.7.refs_1_ = s16[4,288,128]{2,1,0:T(8,128)(2,1)S(1)} collective-permute-done((s16[4,288,128]{2,1,0:T(8,128)(2,1)S(1)}, s16[4,288,128]{2,1,0:T(8,128)(2,1)S(1)}, u32[]{:S(2)}, u32[]{:S(2)}) %collective-permute-start.7) | collective-permute-done | bytes 294944 | tf_op jit(solution)/shard_map/ppermute | solution.py:187
  50.3 8.4 %collective-permute-done.8.refs_2_ = s16[4,288,128]{2,1,0:T(8,128)(2,1)S(1)} collective-permute-done((s16[4,288,128]{2,1,0:T(8,128)(2,1)S(1)}, s16[4,288,128]{2,1,0:T(8,128)(2,1)S(1)}, u32[]{:S(2)}, u32[]{:S(2)}) %collective-permute-start.8) | collective-permute-done | bytes 294944 | tf_op jit(solution)/shard_map/ppermute | solution.py:187
  61.1 2.4 %collective-permute-start.13 = (s16[1,288,128]{2,1,0:T(8,128)(2,1)S(1)}, s16[1,288,128]{2,1,0:T(8,128)(2,1)S(1)}, u32[]{:S(2)}, u32[]{:S(2)}) collective-permute-start(s16[1,288,128]{2,1,0:T(8,128)(2,1)S(1)} %get-tuple-element.73), channel_id=1, source_target_pairs={{0,16},{1,17},{2,18},{3,19},{4,20},{5,21},{6,22},{7,23},{8,24},{9,... | collective-permute-start | bytes 221192 | tf_op jit(solution)/shard_map/ppermute | solution.py:187
  65.6 4.5 %collective-permute-done.13.refs_2_ = s16[1,288,128]{2,1,0:T(8,128)(2,1)S(1)} collective-permute-done((s16[1,288,128]{2,1,0:T(8,128)(2,1)S(1)}, s16[1,288,128]{2,1,0:T(8,128)(2,1)S(1)}, u32[]{:S(2)}, u32[]{:S(2)}) %collective-permute-start.13) | collective-permute-done | bytes 73760 | tf_op jit(solution)/shard_map/ppermute | solution.py:187
  75.4 1.8 %collective-permute-start.19 = (s16[1,288,128]{2,1,0:T(8,128)(2,1)S(1)}, s16[1,288,128]{2,1,0:T(8,128)(2,1)S(1)}, u32[]{:S(2)}, u32[]{:S(2)}) collective-permute-start(s16[1,288,128]{2,1,0:T(8,128)(2,1)S(1)} %get-tuple-element.79.refs_0_), channel_id=1, source_target_pairs={{0,24},{1,25},{2,26},{3,27},{4,28},{5,29},{6,30},{7,31},{8,16},{9,... | collective-permute-start | bytes 221192 | tf_op jit(solution)/shard_map/ppermute | solution.py:187
  77.2 3.3 %collective-permute-done.18.refs_2_ = s16[1,288,128]{2,1,0:T(8,128)(2,1)S(1)} collective-permute-done((s16[1,288,128]{2,1,0:T(8,128)(2,1)S(1)}, s16[1,288,128]{2,1,0:T(8,128)(2,1)S(1)}, u32[]{:S(2)}, u32[]{:S(2)}) %collective-permute-start.18) | collective-permute-done | bytes 73760 | tf_op jit(solution)/shard_map/ppermute | solution.py:187
  83.6 1.8 %collective-permute-start.25 = (s16[4,288,128]{2,1,0:T(8,128)(2,1)S(1)}, s16[4,288,128]{2,1,0:T(8,128)(2,1)S(1)}, u32[]{:S(2)}, u32[]{:S(2)}) collective-permute-start(s16[4,288,128]{2,1,0:T(8,128)(2,1)S(1)} %get-tuple-element.84.refs_0_), channel_id=1, source_target_pairs={{0,6},{1,7},{2,4},{3,5},{4,2},{5,3},{6,0},{7,1},{8,14},{9,15},{10,... | collective-permute-start | bytes 884744 | tf_op jit(solution)/shard_map/ppermute | solution.py:187
  85.7 10.9 %collective-permute-done.22.refs_1_ = s16[416,128]{1,0:T(8,128)(2,1)S(1)} collective-permute-done((s16[416,128]{1,0:T(8,128)(2,1)S(1)}, s16[416,128]{1,0:T(8,128)(2,1)S(1)}, u32[]{:S(2)}, u32[]{:S(2)}) %collective-permute-start.22) | collective-permute-done | bytes 106528 | tf_op jit(solution)/shard_map/ppermute | solution.py:187
  98.2 1.7 %spread.2 = (f32[400,2560]{1,0:T(8,128)}, f32[400,256]{1,0:T(8,128)}) custom-call(s32[1]{0:T(128)} %bitcast.6.side, s16[4,288,128]{2,1,0:T(8,128)(2,1)S(1)} %get-tuple-element.84.refs_0_, s16[4,288,128]{2,1,0:T(8,128)(2,1)S(1)} %collective-permute-done.23.refs_2_.refs_1_, s16[4,288,128]{2,1,0:T(8,128)(2,1)S(1)} %collective-permute-done.24.refs_3_.refs_2_, ...), custom_call_target="tpu_custom_call" | custom-call | flops 2000000000 | bytes 6000000 | tf_op jit(solution)/shard_map/spread/pallas_call | solution.py:506
  101.0 1.7 %spread.3 = (f32[400,2560]{1,0:T(8,128)}, f32[400,256]{1,0:T(8,128)}) custom-call(s32[1]{0:T(128)} %bitcast.5.side, s16[4,288,128]{2,1,0:T(8,128)(2,1)S(1)} %collective-permute-done.28.refs_0_, s16[4,288,128]{2,1,0:T(8,128)(2,1)S(1)} %collective-permute-done.29.refs_1_, ...), custom_call_target="tpu_custom_call", output_to_operand_aliasing={{0}: (5, {}), {1}: (6, {})} | custom-call | flops 2000000000 | bytes 6000000 | tf_op jit(solution)/shard_map/spread/pallas_call | solution.py:506
  (67 shorter events, 22.7 us)
Async XLA Ops:
  0.6 20.9 %collective-permute-start.4 = (bf16[400,512]{1,0:T(8,128)(2,1)}, bf16[400,512]{1,0:T(8,128)(2,1)S(1)}, u32[]{:S(2)}, u32[]{:S(2)}) collective-permute-start(bf16[400,512]{1,0:T(8,128)(2,1)} %bitcast.9), channel_id=1, source_target_pairs={{0,0},{1,17},{2,10},{3,27},{4,4},{5,21},{6,14},{7,31},{8,8},{9,25}... | collective-permute-start | bytes 1228808 | tf_op jit(solution)/shard_map/ppermute | solution.py:187
  2.3 18.5 %collective-permute-start.5 = (bf16[400,512]{1,0:T(8,128)(2,1)}, bf16[400,512]{1,0:T(8,128)(2,1)S(1)}, u32[]{:S(2)}, u32[]{:S(2)}) collective-permute-start(bf16[400,512]{1,0:T(8,128)(2,1)} %bitcast.10), channel_id=1, source_target_pairs={{0,4},{1,5},{2,6},{3,7},{4,0},{5,1},{6,2},{7,3},{8,12},{9,13},{10,... | collective-permute-start | bytes 1228808 | tf_op jit(solution)/shard_map/ppermute | solution.py:187
  6.7 7.6 %collective-permute-start = (s32[2,8,128]{2,1,0:T(8,128)}, s32[2,8,128]{2,1,0:T(8,128)S(1)}, u32[]{:S(2)}, u32[]{:S(2)}) collective-permute-start(s32[2,8,128]{2,1,0:T(8,128)} %get-tuple-element.48), channel_id=1, source_target_pairs={{0,1},{1,0},{2,3},{3,2},{4,5},{5,4},{6,7},{7,6},{8,9},{9,8},{10,11... | collective-permute-start | bytes 24584 | tf_op jit(solution)/shard_map/ppermute | solution.py:187
  8.9 5.4 %collective-permute-start.1 = (s32[2,8,128]{2,1,0:T(8,128)}, s32[2,8,128]{2,1,0:T(8,128)S(1)}, u32[]{:S(2)}, u32[]{:S(2)}) collective-permute-start(s32[2,8,128]{2,1,0:T(8,128)} %get-tuple-element.49), channel_id=1, source_target_pairs={{0,2},{1,3},{2,0},{3,1},{4,6},{5,7},{6,4},{7,5},{8,10},{9,11},{10,... | collective-permute-start | bytes 24584 | tf_op jit(solution)/shard_map/ppermute | solution.py:187
  39.2 19.5 %collective-permute-start.10 = (s16[416,512]{1,0:T(8,128)(2,1)S(1)}, s16[416,512]{1,0:T(8,128)(2,1)S(1)}, u32[]{:S(2)}, u32[]{:S(2)}) collective-permute-start(s16[416,512]{1,0:T(8,128)(2,1)S(1)} %target.1.refs_2_), channel_id=1, source_target_pairs={{0,0},{1,17},{2,10},{3,27},{4,4},{5,21},{6,14},{7,31},{8,8},{9,25}... | collective-permute-start | bytes 1277960 | tf_op jit(solution)/shard_map/ppermute | solution.py:187
  39.9 10.4 %collective-permute-start.7 = (s16[4,288,128]{2,1,0:T(8,128)(2,1)S(1)}, s16[4,288,128]{2,1,0:T(8,128)(2,1)S(1)}, u32[]{:S(2)}, u32[]{:S(2)}) collective-permute-start(s16[4,288,128]{2,1,0:T(8,128)(2,1)S(1)} %get-tuple-element.64), channel_id=1, source_target_pairs={{0,2},{1,3},{2,0},{3,1},{4,6},{5,7},{6,4},{7,5},{8,10},{9,11},{10,... | collective-permute-start | bytes 884744 | tf_op jit(solution)/shard_map/ppermute | solution.py:187
  42.9 15.8 %collective-permute-start.8 = (s16[4,288,128]{2,1,0:T(8,128)(2,1)S(1)}, s16[4,288,128]{2,1,0:T(8,128)(2,1)S(1)}, u32[]{:S(2)}, u32[]{:S(2)}) collective-permute-start(s16[4,288,128]{2,1,0:T(8,128)(2,1)S(1)} %get-tuple-element.65), channel_id=1, source_target_pairs={{0,4},{1,5},{2,6},{3,7},{4,0},{5,1},{6,2},{7,3},{8,12},{9,13},{10,... | collective-permute-start | bytes 884744 | tf_op jit(solution)/shard_map/ppermute | solution.py:187
  44.4 14.3 %collective-permute-start.9 = (s16[4,288,128]{2,1,0:T(8,128)(2,1)S(1)}, s16[4,288,128]{2,1,0:T(8,128)(2,1)S(1)}, u32[]{:S(2)}, u32[]{:S(2)}) collective-permute-start(s16[4,288,128]{2,1,0:T(8,128)(2,1)S(1)} %get-tuple-element.66), channel_id=1, source_target_pairs={{0,6},{1,7},{2,4},{3,5},{4,2},{5,3},{6,0},{7,1},{8,14},{9,15},{10,... | collective-permute-start | bytes 884744 | tf_op jit(solution)/shard_map/ppermute | solution.py:187
  59.3 10.8 %collective-permute-start.15 = (s16[416,256]{1,0:T(8,128)(2,1)S(1)}, s16[416,256]{1,0:T(8,128)(2,1)S(1)}, u32[]{:S(2)}, u32[]{:S(2)}) collective-permute-start(s16[416,256]{1,0:T(8,128)(2,1)S(1)} %get-tuple-element.76), channel_id=1, source_target_pairs={{0,1},{1,0},{2,3},{3,2},{4,5},{5,4},{6,7},{7,6},{8,9},{9,8},{10,11... | collective-permute-start | bytes 638984 | tf_op jit(solution)/shard_map/ppermute | solution.py:187
  59.3 10.8 %collective-permute-start.16 = (s16[416,128]{1,0:T(8,128)(2,1)S(1)}, s16[416,128]{1,0:T(8,128)(2,1)S(1)}, u32[]{:S(2)}, u32[]{:S(2)}) collective-permute-start(s16[416,128]{1,0:T(8,128)(2,1)S(1)} %get-tuple-element.78), channel_id=1, source_target_pairs={{0,2},{1,3},{2,0},{3,1},{4,6},{5,7},{6,4},{7,5},{8,10},{9,11},{10,... | collective-permute-start | bytes 319496 | tf_op jit(solution)/shard_map/ppermute | solution.py:187
  60.4 5.1 %collective-permute-start.12 = (s16[1,288,128]{2,1,0:T(8,128)(2,1)S(1)}, s16[1,288,128]{2,1,0:T(8,128)(2,1)S(1)}, u32[]{:S(2)}, u32[]{:S(2)}) collective-permute-start(s16[1,288,128]{2,1,0:T(8,128)(2,1)S(1)} %get-tuple-element.72), channel_id=1, source_target_pairs={{0,8},{1,9},{2,10},{3,11},{4,12},{5,13},{6,14},{7,15},{8,0},{9,1},... | collective-permute-start | bytes 221192 | tf_op jit(solution)/shard_map/ppermute | solution.py:187
  61.1 9.0 %collective-permute-start.13 = (s16[1,288,128]{2,1,0:T(8,128)(2,1)S(1)}, s16[1,288,128]{2,1,0:T(8,128)(2,1)S(1)}, u32[]{:S(2)}, u32[]{:S(2)}) collective-permute-start(s16[1,288,128]{2,1,0:T(8,128)(2,1)S(1)} %get-tuple-element.73), channel_id=1, source_target_pairs={{0,16},{1,17},{2,18},{3,19},{4,20},{5,21},{6,22},{7,23},{8,24},{9,... | collective-permute-start | bytes 221192 | tf_op jit(solution)/shard_map/ppermute | solution.py:187
  63.6 6.5 %collective-permute-start.14 = (s16[1,288,128]{2,1,0:T(8,128)(2,1)S(1)}, s16[1,288,128]{2,1,0:T(8,128)(2,1)S(1)}, u32[]{:S(2)}, u32[]{:S(2)}) collective-permute-start(s16[1,288,128]{2,1,0:T(8,128)(2,1)S(1)} %get-tuple-element.74), channel_id=1, source_target_pairs={{0,24},{1,25},{2,26},{3,27},{4,28},{5,29},{6,30},{7,31},{8,16},{9,... | collective-permute-start | bytes 221192 | tf_op jit(solution)/shard_map/ppermute | solution.py:187
  70.4 11.3 %collective-permute-start.20 = (s16[416,128]{1,0:T(8,128)(2,1)S(1)}, s16[416,128]{1,0:T(8,128)(2,1)S(1)}, u32[]{:S(2)}, u32[]{:S(2)}) collective-permute-start(s16[416,128]{1,0:T(8,128)(2,1)S(1)} %get-tuple-element.81), channel_id=1, source_target_pairs={{0,2},{1,3},{2,0},{3,1},{4,6},{5,7},{6,4},{7,5},{8,10},{9,11},{10,... | collective-permute-start | bytes 319496 | tf_op jit(solution)/shard_map/ppermute | solution.py:187
  71.4 10.3 %collective-permute-start.21 = (s16[416,128]{1,0:T(8,128)(2,1)S(1)}, s16[416,128]{1,0:T(8,128)(2,1)S(1)}, u32[]{:S(2)}, u32[]{:S(2)}) collective-permute-start(s16[416,128]{1,0:T(8,128)(2,1)S(1)} %get-tuple-element.82), channel_id=1, source_target_pairs={{0,4},{1,5},{2,6},{3,7},{4,0},{5,1},{6,2},{7,3},{8,12},{9,13},{10,... | collective-permute-start | bytes 319496 | tf_op jit(solution)/shard_map/ppermute | solution.py:187
  72.7 4.5 %collective-permute-start.17 = (s16[1,288,128]{2,1,0:T(8,128)(2,1)S(1)}, s16[1,288,128]{2,1,0:T(8,128)(2,1)S(1)}, u32[]{:S(2)}, u32[]{:S(2)}) collective-permute-start(s16[1,288,128]{2,1,0:T(8,128)(2,1)S(1)} %get-tuple-element.79.refs_0_), channel_id=1, source_target_pairs={{0,8},{1,9},{2,10},{3,11},{4,12},{5,13},{6,14},{7,15},{8,0},{9,1},... | collective-permute-start | bytes 221192 | tf_op jit(solution)/shard_map/ppermute | solution.py:187
  74.1 6.4 %collective-permute-start.18 = (s16[1,288,128]{2,1,0:T(8,128)(2,1)S(1)}, s16[1,288,128]{2,1,0:T(8,128)(2,1)S(1)}, u32[]{:S(2)}, u32[]{:S(2)}) collective-permute-start(s16[1,288,128]{2,1,0:T(8,128)(2,1)S(1)} %get-tuple-element.79.refs_0_), channel_id=1, source_target_pairs={{0,16},{1,17},{2,18},{3,19},{4,20},{5,21},{6,22},{7,23},{8,24},{9,... | collective-permute-start | bytes 221192 | tf_op jit(solution)/shard_map/ppermute | solution.py:187
  75.4 6.3 %collective-permute-start.19 = (s16[1,288,128]{2,1,0:T(8,128)(2,1)S(1)}, s16[1,288,128]{2,1,0:T(8,128)(2,1)S(1)}, u32[]{:S(2)}, u32[]{:S(2)}) collective-permute-start(s16[1,288,128]{2,1,0:T(8,128)(2,1)S(1)} %get-tuple-element.79.refs_0_), channel_id=1, source_target_pairs={{0,24},{1,25},{2,26},{3,27},{4,28},{5,29},{6,30},{7,31},{8,16},{9,... | collective-permute-start | bytes 221192 | tf_op jit(solution)/shard_map/ppermute | solution.py:187
  81.8 14.8 %collective-permute-start.23 = (s16[4,288,128]{2,1,0:T(8,128)(2,1)S(1)}, s16[4,288,128]{2,1,0:T(8,128)(2,1)S(1)}, u32[]{:S(2)}, u32[]{:S(2)}) collective-permute-start(s16[4,288,128]{2,1,0:T(8,128)(2,1)S(1)} %get-tuple-element.84.refs_0_), channel_id=1, source_target_pairs={{0,2},{1,3},{2,0},{3,1},{4,6},{5,7},{6,4},{7,5},{8,10},{9,11},{10,... | collective-permute-start | bytes 884744 | tf_op jit(solution)/shard_map/ppermute | solution.py:187
  82.3 14.4 %collective-permute-start.24 = (s16[4,288,128]{2,1,0:T(8,128)(2,1)S(1)}, s16[4,288,128]{2,1,0:T(8,128)(2,1)S(1)}, u32[]{:S(2)}, u32[]{:S(2)}) collective-permute-start(s16[4,288,128]{2,1,0:T(8,128)(2,1)S(1)} %get-tuple-element.84.refs_0_), channel_id=1, source_target_pairs={{0,4},{1,5},{2,6},{3,7},{4,0},{5,1},{6,2},{7,3},{8,12},{9,13},{10,... | collective-permute-start | bytes 884744 | tf_op jit(solution)/shard_map/ppermute | solution.py:187
  83.6 13.1 %collective-permute-start.25 = (s16[4,288,128]{2,1,0:T(8,128)(2,1)S(1)}, s16[4,288,128]{2,1,0:T(8,128)(2,1)S(1)}, u32[]{:S(2)}, u32[]{:S(2)}) collective-permute-start(s16[4,288,128]{2,1,0:T(8,128)(2,1)S(1)} %get-tuple-element.84.refs_0_), channel_id=1, source_target_pairs={{0,6},{1,7},{2,4},{3,5},{4,2},{5,3},{6,0},{7,1},{8,14},{9,15},{10,... | collective-permute-start | bytes 884744 | tf_op jit(solution)/shard_map/ppermute | solution.py:187
  85.3 11.3 %collective-permute-start.22 = (s16[416,128]{1,0:T(8,128)(2,1)S(1)}, s16[416,128]{1,0:T(8,128)(2,1)S(1)}, u32[]{:S(2)}, u32[]{:S(2)}) collective-permute-start(s16[416,128]{1,0:T(8,128)(2,1)S(1)} %get-tuple-element.83.refs_0_), channel_id=1, source_target_pairs={{0,2},{1,3},{2,0},{3,1},{4,6},{5,7},{6,4},{7,5},{8,10},{9,11},{10,... | collective-permute-start | bytes 319496 | tf_op jit(solution)/shard_map/ppermute | solution.py:187
  96.7 4.2 %collective-permute-start.28 = (s16[4,288,128]{2,1,0:T(8,128)(2,1)S(1)}, s16[4,288,128]{2,1,0:T(8,128)(2,1)S(1)}, u32[]{:S(2)}, u32[]{:S(2)}) collective-permute-start(s16[4,288,128]{2,1,0:T(8,128)(2,1)S(1)} %get-tuple-element.84.refs_0_), channel_id=1, source_target_pairs={{0,1},{1,0},{2,3},{3,2},{4,5},{5,4},{6,7},{7,6},{8,9},{9,8},{10,11... | collective-permute-start | bytes 884744 | tf_op jit(solution)/shard_map/ppermute | solution.py:187
  97.2 3.8 %collective-permute-start.29 = (s16[4,288,128]{2,1,0:T(8,128)(2,1)S(1)}, s16[4,288,128]{2,1,0:T(8,128)(2,1)S(1)}, u32[]{:S(2)}, u32[]{:S(2)}) collective-permute-start(s16[4,288,128]{2,1,0:T(8,128)(2,1)S(1)} %collective-permute-done.23.refs_2_.refs_1_), channel_id=1, source_target_pairs={{0,1},{1,0},{2,3},{3,2},{4,5},{5,4},{6,7},{7,6},{8,9},{9,8},{10,11... | collective-permute-start | bytes 884744 | tf_op jit(solution)/shard_map/ppermute | solution.py:187
  (11 other events, 29.9 us)

commit v11 on v9

--- a/solution.py
+++ b/solution.py
@@ -781,10 +781,16 @@
         0.5,
     )
     blocks, owners = made[:-1], {0: made[-1]}
-    pieces = [
-        [block] + exchanged([block] * (len(part.masks[0]) - 1), part.masks[0])
-        for part, block in zip(plan.parts, blocks)
-    ]
+    def gathered(block, masks):
+        if len(masks) != 4:
+            return [block] + exchanged([block] * (len(masks) - 1), masks)
+        half = block.shape[0] // 2
+        first, second = exchanged([block] * 2, masks[:3])
+        over_first = send(first[:half], plan, lambda d: d ^ masks[2])
+        over_second = send(second[half:], plan, lambda d: d ^ masks[1])
+        return [block, first, second, over_first, over_second]
+
+    pieces = [gathered(block, part.masks[0]) for part, block in zip(plan.parts, blocks)]
     while bit:
         for mask in sorted(owners):
             owners[mask | bit] = send(owners[mask], plan, lambda d, m=bit: d ^ m)

time: 101 us -> 99.5 us (0.985)
  waiting for transfers between devices: 28.9 us -> 27.8 us
    ppermute x33 -> x35, waiting for transfers between devices: 28.9 us -> 27.8 us  [send(): return lax.ppermute(value, ('dom', 'rel'), pairs)]
    ppermute x33 -> x35, starting transfers between devices: 37.3 us -> 36.6 us  [send(): return lax.ppermute(value, ('dom', 'rel'), pairs)]
  transfers between devices with their start and end apart: 33 -> 35, of which waited for: 11 -> 12; matrix products, arithmetic and copies ran while one was open for 0% -> 0% of each run, Pallas kernels for 19% -> 19%
where the time goes in v11:
time: 99.5 us; the launch traced here: 99.3 us
  starting transfers between devices  36.6 us (37%)
  Pallas kernels  34 us (34%)
  waiting for transfers between devices  27.8 us (28%)
    ppermute x35, starting transfers between devices, send(): return lax.ppermute(value, ('dom', 'rel'), pairs)  36.6 us
    pallas_call x20, Pallas kernels, call(): pl.pallas_call(kernel, out_shape=outs, compiler_params=pltpu.CompilerPara...  34 us
    ppermute x35, waiting for transfers between devices, send(): return lax.ppermute(value, ('dom', 'rel'), pairs)  27.8 us
  transfers between devices with their start and end apart: 35, of which 12 were waited for; matrix products, arithmetic and copies ran while one was open for 0% of the time, Pallas kernels for 19%

profile of v11, /device:TPU:0, one launch (start us, length us, event | category | flops | bytes accessed | tf_op | source)
XLA Modules:
  0.0 99.3 jit_solution(1001920421531078179)
XLA Ops:
  2.3 3.0 %collective-permute-start.5 = (bf16[400,512]{1,0:T(8,128)(2,1)}, bf16[400,512]{1,0:T(8,128)(2,1)S(1)}, u32[]{:S(2)}, u32[]{:S(2)}) collective-permute-start(bf16[400,512]{1,0:T(8,128)(2,1)} %bitcast.10), channel_id=1, source_target_pairs={{0,4},{1,5},{2,6},{3,7},{4,0},{5,1},{6,2},{7,3},{8,12},{9,13},{10,... | collective-permute-start | bytes 1228808 | tf_op jit(solution)/shard_map/ppermute | solution.py:187
  6.7 2.2 %collective-permute-start = (s32[2,8,128]{2,1,0:T(8,128)}, s32[2,8,128]{2,1,0:T(8,128)S(1)}, u32[]{:S(2)}, u32[]{:S(2)}) collective-permute-start(s32[2,8,128]{2,1,0:T(8,128)} %get-tuple-element.48), channel_id=1, source_target_pairs={{0,1},{1,0},{2,3},{3,2},{4,5},{5,4},{6,7},{7,6},{8,9},{9,8},{10,11... | collective-permute-start | bytes 24584 | tf_op jit(solution)/shard_map/ppermute | solution.py:187
  8.9 2.5 %collective-permute-start.1 = (s32[2,8,128]{2,1,0:T(8,128)}, s32[2,8,128]{2,1,0:T(8,128)S(1)}, u32[]{:S(2)}, u32[]{:S(2)}) collective-permute-start(s32[2,8,128]{2,1,0:T(8,128)} %get-tuple-element.49), channel_id=1, source_target_pairs={{0,2},{1,3},{2,0},{3,1},{4,6},{5,7},{6,4},{7,5},{8,10},{9,11},{10,... | collective-permute-start | bytes 24584 | tf_op jit(solution)/shard_map/ppermute | solution.py:187
  11.4 2.9 %rel_split.1.refs_1_ = bf16[800,2560]{1,0:T(8,128)(2,1)S(1)} custom-call(f32[400,2560]{1,0:T(8,128)} %bitcast.14), custom_call_target="tpu_custom_call" | custom-call | flops 2000000000 | bytes 6000000 | tf_op jit(solution)/shard_map/rel_split/pallas_call | solution.py:506
  15.3 2.3 %relation.2.refs_3_ = f32[400,512]{1,0:T(8,128)S(1)} custom-call(s32[4,8,128]{2,1,0:T(8,128)S(1)} %get-tuple-element.51.refs_0_, bf16[800,2560]{1,0:T(8,128)(2,1)S(1)} %rel_split.1.refs_1_), custom_call_target="tpu_custom_call" | custom-call | flops 2000000000 | bytes 6000000 | tf_op jit(solution)/shard_map/relation/pallas_call | solution.py:506
  18.5 2.3 %relation.3.refs_7_ = f32[400,512]{1,0:T(8,128)S(1)} custom-call(s32[4,8,128]{2,1,0:T(8,128)S(1)} %collective-permute-done.3.refs_0_.refs_1_, bf16[800,2560]{1,0:T(8,128)(2,1)S(1)} %rel_split.1.refs_1_), custom_call_target="tpu_custom_call" | custom-call | flops 2000000000 | bytes 6000000 | tf_op jit(solution)/shard_map/relation/pallas_call | solution.py:506
  21.5 4.1 %bucket.1 = (bf16[800,512]{1,0:T(8,128)(2,1)S(1)}, bf16[800,512]{1,0:T(8,128)(2,1)S(1)}, bf16[800,1024]{1,0:T(8,128)(2,1)S(1)}) custom-call(s32[4,8,128]{2,1,0:T(8,128)S(1)} %get-tuple-element.51.refs_0_, bf16[400,512]{1,0:T(8,128)(2,1)S(1)} %collective-permute-done.4.refs_1_.refs_5_, f32[400,512]{1,0:T(8,128)S(1)} %get-tuple-element.53.refs_2_, ...), custom_call_target="tpu_custom_call" | custom-call | flops 4000000000 | bytes 12000000 | tf_op jit(solution)/shard_map/bucket/pallas_call | solution.py:506
  25.6 7.9 %last.1 = (s16[16,288,128]{2,1,0:T(8,128)(2,1)S(1)}, f32[400,128]{1,0:T(8,128)S(1)}, bf16[800,1024]{1,0:T(8,128)(2,1)S(1)}, bf16[800,1024]{1,0:T(8,128)(2,1)S(1)}, bf16[800,2048]{1,0:T(8,128)(2,1)S(1)}) custom-call(s32[4,8,128]{2,1,0:T(8,128)S(1)} %get-tuple-element.51.refs_0_, s32[4,8,128]{2,1,0:T(8,128)S(1)} %collective-permute-done.3.refs_0_.refs_1_, ...), custom_call_target="tpu_custom_call" | custom-call | flops 8999999488 | bytes 27000000 | tf_op jit(solution)/shard_map/last/pallas_call | solution.py:506
  34.9 2.4 %home.1.refs_0_ = f32[16,280,128]{2,1,0:T(8,128)S(1)} custom-call(s32[4,8,128]{2,1,0:T(8,128)S(1)} %get-tuple-element.51.refs_0_, s32[4,8,128]{2,1,0:T(8,128)S(1)} %collective-permute-done.3.refs_0_.refs_1_, bf16[800,1024]{1,0:T(8,128)(2,1)S(1)} %get-tuple-element.60.refs_2_, f32[400,128]{1,0:T(8,128)S(1)} %get-tuple-element.61.refs_3_, ...), custom_call_target="tpu_custom_call" | custom-call | flops 3000000000 | bytes 9000000 | tf_op jit(solution)/shard_map/home/pallas_call | solution.py:506
  38.0 2.0 %collective-permute-start.10 = (s16[4,288,128]{2,1,0:T(8,128)(2,1)S(1)}, s16[4,288,128]{2,1,0:T(8,128)(2,1)S(1)}, u32[]{:S(2)}, u32[]{:S(2)}) collective-permute-start(s16[4,288,128]{2,1,0:T(8,128)(2,1)S(1)} %get-tuple-element.69), channel_id=1, source_target_pairs={{0,6},{1,7},{2,4},{3,5},{4,2},{5,3},{6,0},{7,1},{8,14},{9,15},{10,... | collective-permute-start | bytes 884744 | tf_op jit(solution)/shard_map/ppermute | solution.py:187
  41.5 2.0 %target.1 = (s16[416,256]{1,0:T(8,128)(2,1)S(1)}, s16[416,256]{1,0:T(8,128)(2,1)S(1)}) custom-call(s32[4,8,128]{2,1,0:T(8,128)S(1)} %get-tuple-element.51.refs_0_, s32[4,8,128]{2,1,0:T(8,128)S(1)} %collective-permute-done.3.refs_0_.refs_1_, bf16[800,2048]{1,0:T(8,128)(2,1)S(1)} %get-tuple-element.70.refs_2_, f32[4,280,128]{2,1,0:T(8,128)S(1)} %get-tuple-element.66.refs_3_.refs_0_), custom_call_target="tpu_custom_call" | custom-call | flops 1800000000 | bytes 5400000 | tf_op jit(solution)/shard_map/target/pallas_call | solution.py:506
  45.6 3.3 %collective-permute-done.10.refs_3_ = s16[4,288,128]{2,1,0:T(8,128)(2,1)S(1)} collective-permute-done((s16[4,288,128]{2,1,0:T(8,128)(2,1)S(1)}, s16[4,288,128]{2,1,0:T(8,128)(2,1)S(1)}, u32[]{:S(2)}, u32[]{:S(2)}) %collective-permute-start.10) | collective-permute-done | bytes 294944 | tf_op jit(solution)/shard_map/ppermute | solution.py:187
  48.9 5.2 %collective-permute-done.8.refs_1_ = s16[4,288,128]{2,1,0:T(8,128)(2,1)S(1)} collective-permute-done((s16[4,288,128]{2,1,0:T(8,128)(2,1)S(1)}, s16[4,288,128]{2,1,0:T(8,128)(2,1)S(1)}, u32[]{:S(2)}, u32[]{:S(2)}) %collective-permute-start.8) | collective-permute-done | bytes 294944 | tf_op jit(solution)/shard_map/ppermute | solution.py:187
  54.8 2.7 %collective-permute-start.16 = (s16[416,256]{1,0:T(8,128)(2,1)S(1)}, s16[416,256]{1,0:T(8,128)(2,1)S(1)}, u32[]{:S(2)}, u32[]{:S(2)}) collective-permute-start(s16[416,256]{1,0:T(8,128)(2,1)S(1)} %get-tuple-element.78), channel_id=1, source_target_pairs={{0,1},{1,0},{2,3},{3,2},{4,5},{5,4},{6,7},{7,6},{8,9},{9,8},{10,11... | collective-permute-start | bytes 638984 | tf_op jit(solution)/shard_map/ppermute | solution.py:187
  57.5 2.7 %collective-permute-start.17 = (s16[416,128]{1,0:T(8,128)(2,1)S(1)}, s16[416,128]{1,0:T(8,128)(2,1)S(1)}, u32[]{:S(2)}, u32[]{:S(2)}) collective-permute-start(s16[416,128]{1,0:T(8,128)(2,1)S(1)} %get-tuple-element.80), channel_id=1, source_target_pairs={{0,2},{1,3},{2,0},{3,1},{4,6},{5,7},{6,4},{7,5},{8,10},{9,11},{10,... | collective-permute-start | bytes 319496 | tf_op jit(solution)/shard_map/ppermute | solution.py:187
  60.2 2.0 %collective-permute-start.14 = (s16[1,288,128]{2,1,0:T(8,128)(2,1)S(1)}, s16[1,288,128]{2,1,0:T(8,128)(2,1)S(1)}, u32[]{:S(2)}, u32[]{:S(2)}) collective-permute-start(s16[1,288,128]{2,1,0:T(8,128)(2,1)S(1)} %get-tuple-element.75), channel_id=1, source_target_pairs={{0,16},{1,17},{2,18},{3,19},{4,20},{5,21},{6,22},{7,23},{8,24},{9,... | collective-permute-start | bytes 221192 | tf_op jit(solution)/shard_map/ppermute | solution.py:187
  62.1 2.4 %collective-permute-start.15 = (s16[1,288,128]{2,1,0:T(8,128)(2,1)S(1)}, s16[1,288,128]{2,1,0:T(8,128)(2,1)S(1)}, u32[]{:S(2)}, u32[]{:S(2)}) collective-permute-start(s16[1,288,128]{2,1,0:T(8,128)(2,1)S(1)} %get-tuple-element.76), channel_id=1, source_target_pairs={{0,24},{1,25},{2,26},{3,27},{4,28},{5,29},{6,30},{7,31},{8,16},{9,... | collective-permute-start | bytes 221192 | tf_op jit(solution)/shard_map/ppermute | solution.py:187
  65.6 3.8 %collective-permute-done.14.refs_2_ = s16[1,288,128]{2,1,0:T(8,128)(2,1)S(1)} collective-permute-done((s16[1,288,128]{2,1,0:T(8,128)(2,1)S(1)}, s16[1,288,128]{2,1,0:T(8,128)(2,1)S(1)}, u32[]{:S(2)}, u32[]{:S(2)}) %collective-permute-start.14) | collective-permute-done | bytes 73760 | tf_op jit(solution)/shard_map/ppermute | solution.py:187
  75.7 4.5 %collective-permute-done.19.refs_2_ = s16[1,288,128]{2,1,0:T(8,128)(2,1)S(1)} collective-permute-done((s16[1,288,128]{2,1,0:T(8,128)(2,1)S(1)}, s16[1,288,128]{2,1,0:T(8,128)(2,1)S(1)}, u32[]{:S(2)}, u32[]{:S(2)}) %collective-permute-start.19) | collective-permute-done | bytes 73760 | tf_op jit(solution)/shard_map/ppermute | solution.py:187
  80.4 1.7 %collective-permute-start.27 = (s16[4,288,128]{2,1,0:T(8,128)(2,1)S(1)}, s16[4,288,128]{2,1,0:T(8,128)(2,1)S(1)}, u32[]{:S(2)}, u32[]{:S(2)}) collective-permute-start(s16[4,288,128]{2,1,0:T(8,128)(2,1)S(1)} %get-tuple-element.86.refs_0_), channel_id=1, source_target_pairs={{0,2},{1,3},{2,0},{3,1},{4,6},{5,7},{6,4},{7,5},{8,10},{9,11},{10,... | collective-permute-start | bytes 884744 | tf_op jit(solution)/shard_map/ppermute | solution.py:187
  83.1 5.9 %collective-permute-done.24.refs_2_ = s16[416,128]{1,0:T(8,128)(2,1)S(1)} collective-permute-done((s16[416,128]{1,0:T(8,128)(2,1)S(1)}, s16[416,128]{1,0:T(8,128)(2,1)S(1)}, u32[]{:S(2)}, u32[]{:S(2)}) %collective-permute-start.24) | collective-permute-done | bytes 106528 | tf_op jit(solution)/shard_map/ppermute | solution.py:187
  92.6 2.7 %collective-permute-done.31.refs_3_ = s16[2,288,128]{2,1,0:T(8,128)(2,1)S(1)} collective-permute-done((s16[2,288,128]{2,1,0:T(8,128)(2,1)S(1)}, s16[2,288,128]{2,1,0:T(8,128)(2,1)S(1)}, u32[]{:S(2)}, u32[]{:S(2)}) %collective-permute-start.31) | collective-permute-done | bytes 147488 | tf_op jit(solution)/shard_map/ppermute | solution.py:187
  95.9 1.7 %spread.2 = (f32[400,2560]{1,0:T(8,128)}, f32[400,256]{1,0:T(8,128)}) custom-call(s32[1]{0:T(128)} %bitcast.6.side, s16[4,288,128]{2,1,0:T(8,128)(2,1)S(1)} %get-tuple-element.86.refs_0_, s16[4,288,128]{2,1,0:T(8,128)(2,1)S(1)} %collective-permute-done.27.refs_1_, s16[4,288,128]{2,1,0:T(8,128)(2,1)S(1)} %collective-permute-done.29.refs_2_, ...), custom_call_target="tpu_custom_call" | custom-call | flops 2000000000 | bytes 6000000 | tf_op jit(solution)/shard_map/spread/pallas_call | solution.py:506
  97.6 1.7 %spread.3 = (f32[400,2560]{1,0:T(8,128)}, f32[400,256]{1,0:T(8,128)}) custom-call(s32[1]{0:T(128)} %bitcast.5.side, s16[4,288,128]{2,1,0:T(8,128)(2,1)S(1)} %collective-permute-done.26.refs_0_, s16[4,288,128]{2,1,0:T(8,128)(2,1)S(1)} %collective-permute-done.28.refs_1_, ...), custom_call_target="tpu_custom_call", output_to_operand_aliasing={{0}: (6, {}), {1}: (7, {})} | custom-call | flops 2000000000 | bytes 6000000 | tf_op jit(solution)/shard_map/spread/pallas_call | solution.py:506
  (74 shorter events, 24.5 us)
Async XLA Ops:
  0.6 20.9 %collective-permute-start.4 = (bf16[400,512]{1,0:T(8,128)(2,1)}, bf16[400,512]{1,0:T(8,128)(2,1)S(1)}, u32[]{:S(2)}, u32[]{:S(2)}) collective-permute-start(bf16[400,512]{1,0:T(8,128)(2,1)} %bitcast.9), channel_id=1, source_target_pairs={{0,0},{1,17},{2,10},{3,27},{4,4},{5,21},{6,14},{7,31},{8,8},{9,25}... | collective-permute-start | bytes 1228808 | tf_op jit(solution)/shard_map/ppermute | solution.py:187
  2.3 18.5 %collective-permute-start.5 = (bf16[400,512]{1,0:T(8,128)(2,1)}, bf16[400,512]{1,0:T(8,128)(2,1)S(1)}, u32[]{:S(2)}, u32[]{:S(2)}) collective-permute-start(bf16[400,512]{1,0:T(8,128)(2,1)} %bitcast.10), channel_id=1, source_target_pairs={{0,4},{1,5},{2,6},{3,7},{4,0},{5,1},{6,2},{7,3},{8,12},{9,13},{10,... | collective-permute-start | bytes 1228808 | tf_op jit(solution)/shard_map/ppermute | solution.py:187
  6.7 7.6 %collective-permute-start = (s32[2,8,128]{2,1,0:T(8,128)}, s32[2,8,128]{2,1,0:T(8,128)S(1)}, u32[]{:S(2)}, u32[]{:S(2)}) collective-permute-start(s32[2,8,128]{2,1,0:T(8,128)} %get-tuple-element.48), channel_id=1, source_target_pairs={{0,1},{1,0},{2,3},{3,2},{4,5},{5,4},{6,7},{7,6},{8,9},{9,8},{10,11... | collective-permute-start | bytes 24584 | tf_op jit(solution)/shard_map/ppermute | solution.py:187
  38.0 10.9 %collective-permute-start.10 = (s16[4,288,128]{2,1,0:T(8,128)(2,1)S(1)}, s16[4,288,128]{2,1,0:T(8,128)(2,1)S(1)}, u32[]{:S(2)}, u32[]{:S(2)}) collective-permute-start(s16[4,288,128]{2,1,0:T(8,128)(2,1)S(1)} %get-tuple-element.69), channel_id=1, source_target_pairs={{0,6},{1,7},{2,4},{3,5},{4,2},{5,3},{6,0},{7,1},{8,14},{9,15},{10,... | collective-permute-start | bytes 884744 | tf_op jit(solution)/shard_map/ppermute | solution.py:187
  40.0 14.1 %collective-permute-start.8 = (s16[4,288,128]{2,1,0:T(8,128)(2,1)S(1)}, s16[4,288,128]{2,1,0:T(8,128)(2,1)S(1)}, u32[]{:S(2)}, u32[]{:S(2)}) collective-permute-start(s16[4,288,128]{2,1,0:T(8,128)(2,1)S(1)} %get-tuple-element.67), channel_id=1, source_target_pairs={{0,2},{1,3},{2,0},{3,1},{4,6},{5,7},{6,4},{7,5},{8,10},{9,11},{10,... | collective-permute-start | bytes 884744 | tf_op jit(solution)/shard_map/ppermute | solution.py:187
  40.8 13.4 %collective-permute-start.9 = (s16[4,288,128]{2,1,0:T(8,128)(2,1)S(1)}, s16[4,288,128]{2,1,0:T(8,128)(2,1)S(1)}, u32[]{:S(2)}, u32[]{:S(2)}) collective-permute-start(s16[4,288,128]{2,1,0:T(8,128)(2,1)S(1)} %get-tuple-element.68), channel_id=1, source_target_pairs={{0,4},{1,5},{2,6},{3,7},{4,0},{5,1},{6,2},{7,3},{8,12},{9,13},{10,... | collective-permute-start | bytes 884744 | tf_op jit(solution)/shard_map/ppermute | solution.py:187
  54.8 14.6 %collective-permute-start.16 = (s16[416,256]{1,0:T(8,128)(2,1)S(1)}, s16[416,256]{1,0:T(8,128)(2,1)S(1)}, u32[]{:S(2)}, u32[]{:S(2)}) collective-permute-start(s16[416,256]{1,0:T(8,128)(2,1)S(1)} %get-tuple-element.78), channel_id=1, source_target_pairs={{0,1},{1,0},{2,3},{3,2},{4,5},{5,4},{6,7},{7,6},{8,9},{9,8},{10,11... | collective-permute-start | bytes 638984 | tf_op jit(solution)/shard_map/ppermute | solution.py:187
  57.5 11.8 %collective-permute-start.17 = (s16[416,128]{1,0:T(8,128)(2,1)S(1)}, s16[416,128]{1,0:T(8,128)(2,1)S(1)}, u32[]{:S(2)}, u32[]{:S(2)}) collective-permute-start(s16[416,128]{1,0:T(8,128)(2,1)S(1)} %get-tuple-element.80), channel_id=1, source_target_pairs={{0,2},{1,3},{2,0},{3,1},{4,6},{5,7},{6,4},{7,5},{8,10},{9,11},{10,... | collective-permute-start | bytes 319496 | tf_op jit(solution)/shard_map/ppermute | solution.py:187
  60.2 5.4 %collective-permute-start.13 = (s16[1,288,128]{2,1,0:T(8,128)(2,1)S(1)}, s16[1,288,128]{2,1,0:T(8,128)(2,1)S(1)}, u32[]{:S(2)}, u32[]{:S(2)}) collective-permute-start(s16[1,288,128]{2,1,0:T(8,128)(2,1)S(1)} %get-tuple-element.74), channel_id=1, source_target_pairs={{0,8},{1,9},{2,10},{3,11},{4,12},{5,13},{6,14},{7,15},{8,0},{9,1},... | collective-permute-start | bytes 221192 | tf_op jit(solution)/shard_map/ppermute | solution.py:187
  60.2 9.2 %collective-permute-start.14 = (s16[1,288,128]{2,1,0:T(8,128)(2,1)S(1)}, s16[1,288,128]{2,1,0:T(8,128)(2,1)S(1)}, u32[]{:S(2)}, u32[]{:S(2)}) collective-permute-start(s16[1,288,128]{2,1,0:T(8,128)(2,1)S(1)} %get-tuple-element.75), channel_id=1, source_target_pairs={{0,16},{1,17},{2,18},{3,19},{4,20},{5,21},{6,22},{7,23},{8,24},{9,... | collective-permute-start | bytes 221192 | tf_op jit(solution)/shard_map/ppermute | solution.py:187
  62.1 7.2 %collective-permute-start.15 = (s16[1,288,128]{2,1,0:T(8,128)(2,1)S(1)}, s16[1,288,128]{2,1,0:T(8,128)(2,1)S(1)}, u32[]{:S(2)}, u32[]{:S(2)}) collective-permute-start(s16[1,288,128]{2,1,0:T(8,128)(2,1)S(1)} %get-tuple-element.76), channel_id=1, source_target_pairs={{0,24},{1,25},{2,26},{3,27},{4,28},{5,29},{6,30},{7,31},{8,16},{9,... | collective-permute-start | bytes 221192 | tf_op jit(solution)/shard_map/ppermute | solution.py:187
  69.6 10.6 %collective-permute-start.21 = (s16[416,128]{1,0:T(8,128)(2,1)S(1)}, s16[416,128]{1,0:T(8,128)(2,1)S(1)}, u32[]{:S(2)}, u32[]{:S(2)}) collective-permute-start(s16[416,128]{1,0:T(8,128)(2,1)S(1)} %get-tuple-element.83), channel_id=1, source_target_pairs={{0,2},{1,3},{2,0},{3,1},{4,6},{5,7},{6,4},{7,5},{8,10},{9,11},{10,... | collective-permute-start | bytes 319496 | tf_op jit(solution)/shard_map/ppermute | solution.py:187
  69.8 10.4 %collective-permute-start.22 = (s16[416,128]{1,0:T(8,128)(2,1)S(1)}, s16[416,128]{1,0:T(8,128)(2,1)S(1)}, u32[]{:S(2)}, u32[]{:S(2)}) collective-permute-start(s16[416,128]{1,0:T(8,128)(2,1)S(1)} %get-tuple-element.84), channel_id=1, source_target_pairs={{0,4},{1,5},{2,6},{3,7},{4,0},{5,1},{6,2},{7,3},{8,12},{9,13},{10,... | collective-permute-start | bytes 319496 | tf_op jit(solution)/shard_map/ppermute | solution.py:187
  72.5 7.7 %collective-permute-start.19 = (s16[1,288,128]{2,1,0:T(8,128)(2,1)S(1)}, s16[1,288,128]{2,1,0:T(8,128)(2,1)S(1)}, u32[]{:S(2)}, u32[]{:S(2)}) collective-permute-start(s16[1,288,128]{2,1,0:T(8,128)(2,1)S(1)} %get-tuple-element.81.refs_0_), channel_id=1, source_target_pairs={{0,16},{1,17},{2,18},{3,19},{4,20},{5,21},{6,22},{7,23},{8,24},{9,... | collective-permute-start | bytes 221192 | tf_op jit(solution)/shard_map/ppermute | solution.py:187
  73.8 6.5 %collective-permute-start.20 = (s16[1,288,128]{2,1,0:T(8,128)(2,1)S(1)}, s16[1,288,128]{2,1,0:T(8,128)(2,1)S(1)}, u32[]{:S(2)}, u32[]{:S(2)}) collective-permute-start(s16[1,288,128]{2,1,0:T(8,128)(2,1)S(1)} %get-tuple-element.81.refs_0_), channel_id=1, source_target_pairs={{0,24},{1,25},{2,26},{3,27},{4,28},{5,29},{6,30},{7,31},{8,16},{9,... | collective-permute-start | bytes 221192 | tf_op jit(solution)/shard_map/ppermute | solution.py:187
  80.4 8.6 %collective-permute-start.27 = (s16[4,288,128]{2,1,0:T(8,128)(2,1)S(1)}, s16[4,288,128]{2,1,0:T(8,128)(2,1)S(1)}, u32[]{:S(2)}, u32[]{:S(2)}) collective-permute-start(s16[4,288,128]{2,1,0:T(8,128)(2,1)S(1)} %get-tuple-element.86.refs_0_), channel_id=1, source_target_pairs={{0,2},{1,3},{2,0},{3,1},{4,6},{5,7},{6,4},{7,5},{8,10},{9,11},{10,... | collective-permute-start | bytes 884744 | tf_op jit(solution)/shard_map/ppermute | solution.py:187
  82.1 7.4 %collective-permute-start.29 = (s16[4,288,128]{2,1,0:T(8,128)(2,1)S(1)}, s16[4,288,128]{2,1,0:T(8,128)(2,1)S(1)}, u32[]{:S(2)}, u32[]{:S(2)}) collective-permute-start(s16[4,288,128]{2,1,0:T(8,128)(2,1)S(1)} %get-tuple-element.86.refs_0_), channel_id=1, source_target_pairs={{0,4},{1,5},{2,6},{3,7},{4,0},{5,1},{6,2},{7,3},{8,12},{9,13},{10,... | collective-permute-start | bytes 884744 | tf_op jit(solution)/shard_map/ppermute | solution.py:187
  82.6 6.4 %collective-permute-start.24 = (s16[416,128]{1,0:T(8,128)(2,1)S(1)}, s16[416,128]{1,0:T(8,128)(2,1)S(1)}, u32[]{:S(2)}, u32[]{:S(2)}) collective-permute-start(s16[416,128]{1,0:T(8,128)(2,1)S(1)} %get-tuple-element.85.refs_0_), channel_id=1, source_target_pairs={{0,2},{1,3},{2,0},{3,1},{4,6},{5,7},{6,4},{7,5},{8,10},{9,11},{10,... | collective-permute-start | bytes 319496 | tf_op jit(solution)/shard_map/ppermute | solution.py:187
  83.1 8.0 %collective-permute-start.23 = (s16[416,128]{1,0:T(8,128)(2,1)S(1)}, s16[416,128]{1,0:T(8,128)(2,1)S(1)}, u32[]{:S(2)}, u32[]{:S(2)}) collective-permute-start(s16[416,128]{1,0:T(8,128)(2,1)S(1)} %get-tuple-element.85.refs_0_), channel_id=1, source_target_pairs={{0,1},{1,0},{2,3},{3,2},{4,5},{5,4},{6,7},{7,6},{8,9},{9,8},{10,11... | collective-permute-start | bytes 319496 | tf_op jit(solution)/shard_map/ppermute | solution.py:187
  89.0 6.3 %collective-permute-start.31 = (s16[2,288,128]{2,1,0:T(8,128)(2,1)S(1)}, s16[2,288,128]{2,1,0:T(8,128)(2,1)S(1)}, u32[]{:S(2)}, u32[]{:S(2)}) collective-permute-start(s16[2,288,128]{2,1,0:T(8,128)(2,1)S(1)} %slice.8), channel_id=1, source_target_pairs={{0,4},{1,5},{2,6},{3,7},{4,0},{5,1},{6,2},{7,3},{8,12},{9,13},{10,... | collective-permute-start | bytes 442376 | tf_op jit(solution)/shard_map/ppermute | solution.py:187
  89.5 6.0 %collective-permute-start.33 = (s16[2,288,128]{2,1,0:T(8,128)(2,1)S(1)}, s16[2,288,128]{2,1,0:T(8,128)(2,1)S(1)}, u32[]{:S(2)}, u32[]{:S(2)}) collective-permute-start(s16[2,288,128]{2,1,0:T(8,128)(2,1)S(1)} %slice.9), channel_id=1, source_target_pairs={{0,2},{1,3},{2,0},{3,1},{4,6},{5,7},{6,4},{7,5},{8,10},{9,11},{10,... | collective-permute-start | bytes 442376 | tf_op jit(solution)/shard_map/ppermute | solution.py:187
  90.9 6.7 %collective-permute-start.26 = (s16[4,288,128]{2,1,0:T(8,128)(2,1)S(1)}, s16[4,288,128]{2,1,0:T(8,128)(2,1)S(1)}, u32[]{:S(2)}, u32[]{:S(2)}) collective-permute-start(s16[4,288,128]{2,1,0:T(8,128)(2,1)S(1)} %get-tuple-element.86.refs_0_), channel_id=1, source_target_pairs={{0,1},{1,0},{2,3},{3,2},{4,5},{5,4},{6,7},{7,6},{8,9},{9,8},{10,11... | collective-permute-start | bytes 884744 | tf_op jit(solution)/shard_map/ppermute | solution.py:187
  91.1 6.5 %collective-permute-start.28 = (s16[4,288,128]{2,1,0:T(8,128)(2,1)S(1)}, s16[4,288,128]{2,1,0:T(8,128)(2,1)S(1)}, u32[]{:S(2)}, u32[]{:S(2)}) collective-permute-start(s16[4,288,128]{2,1,0:T(8,128)(2,1)S(1)} %collective-permute-done.27.refs_1_), channel_id=1, source_target_pairs={{0,1},{1,0},{2,3},{3,2},{4,5},{5,4},{6,7},{7,6},{8,9},{9,8},{10,11... | collective-permute-start | bytes 884744 | tf_op jit(solution)/shard_map/ppermute | solution.py:187
  91.4 6.2 %collective-permute-start.30 = (s16[4,288,128]{2,1,0:T(8,128)(2,1)S(1)}, s16[4,288,128]{2,1,0:T(8,128)(2,1)S(1)}, u32[]{:S(2)}, u32[]{:S(2)}) collective-permute-start(s16[4,288,128]{2,1,0:T(8,128)(2,1)S(1)} %collective-permute-done.29.refs_2_), channel_id=1, source_target_pairs={{0,1},{1,0},{2,3},{3,2},{4,5},{5,4},{6,7},{7,6},{8,9},{9,8},{10,11... | collective-permute-start | bytes 884744 | tf_op jit(solution)/shard_map/ppermute | solution.py:187
  (14 other events, 41.8 us)

commit v12 on v11

--- a/solution.py
+++ b/solution.py
@@ -211,11 +211,23 @@
                 out[mask * plan.maxb + turn] = ref[bucket * plan.maxb + turn]
 
 
-def split_kernel(relations, out):
-    depth = relations.shape[0]
-    high, low = split(relations[...])
-    out[0:depth, :] = high
-    out[depth : 2 * depth, :] = low
+def split_kernel(relations, out, held, sems):
+    depth, total = relations.shape
+    step = 4 * LANES
+    loads = [
+        pltpu.make_async_copy(
+            relations.at[:, start : start + step], held.at[:, start : start + step], sems.at[at]
+        )
+        for at, start in enumerate(range(0, total, step))
+    ]
+    for load in loads:
+        load.start()
+    for at, load in enumerate(loads):
+        load.wait()
+        cols = slice(at * step, (at + 1) * step)
+        high, low = split(held[:, cols])
+        out[0:depth, cols] = high
+        out[depth : 2 * depth, cols] = low
 
 
 def relation_kernel(plan, *refs):
@@ -583,6 +595,11 @@
         "rel_split",
         2.0,
         50,
+        in_specs=[ANY],
+        scratch=[
+            pltpu.VMEM((width, plan.nrels), F32),
+            pltpu.SemaphoreType.DMA((plan.nrels // (4 * LANES),)),
+        ],
     )
     labels = call(
         functools.partial(forward_kernel, plan),
@@ -825,8 +842,7 @@
             grid_spec=pltpu.PrefetchScalarGridSpec(
                 num_scalar_prefetch=1,
                 grid=(1,),
-                in_specs=[pl.BlockSpec(piece.shape, lambda i, half: (0, 0, 0)) for piece in flat]
-                + [ANY] * len(made),
+                in_specs=[VMEM] * len(flat) + [ANY] * len(made),
                 out_specs=[spec(plan.half_rel), spec(plan.half_rem)],
                 scratch_shapes=[pltpu.VMEM(part.packed, i16) for part in plan.parts],
             ),

time: 99.5 us -> 99.7 us (level)
  transfers between devices with their start and end apart: 35 -> 35, of which waited for: 12 -> 12; matrix products, arithmetic and copies ran while one was open for 0% -> 0% of each run, Pallas kernels for 19% -> 18%
where the time goes in v12:
time: 99.7 us; the launch traced here: 99.4 us
  starting transfers between devices  36.7 us (37%)
  Pallas kernels  33.5 us (34%)
  waiting for transfers between devices  28.3 us (28%)
    ppermute x35, starting transfers between devices, send(): return lax.ppermute(value, ('dom', 'rel'), pairs)  36.7 us
    pallas_call x20, Pallas kernels, call(): pl.pallas_call(kernel, out_shape=outs, compiler_params=pltpu.CompilerPara...  33.5 us
    ppermute x35, waiting for transfers between devices, send(): return lax.ppermute(value, ('dom', 'rel'), pairs)  28.3 us
  transfers between devices with their start and end apart: 35, of which 12 were waited for; matrix products, arithmetic and copies ran while one was open for 0% of the time, Pallas kernels for 18%

profile of v12, /device:TPU:0, one launch (start us, length us, event | category | flops | bytes accessed | tf_op | source)
XLA Modules:
  0.0 99.4 jit_solution(17392038854773893263)
XLA Ops:
  2.3 3.0 %collective-permute-start.5 = (bf16[400,512]{1,0:T(8,128)(2,1)}, bf16[400,512]{1,0:T(8,128)(2,1)S(1)}, u32[]{:S(2)}, u32[]{:S(2)}) collective-permute-start(bf16[400,512]{1,0:T(8,128)(2,1)} %bitcast.10), channel_id=1, source_target_pairs={{0,4},{1,5},{2,6},{3,7},{4,0},{5,1},{6,2},{7,3},{8,12},{9,13},{10,... | collective-permute-start | bytes 1228808 | tf_op jit(solution)/shard_map/ppermute | solution.py:187
  6.7 2.2 %collective-permute-start = (s32[2,8,128]{2,1,0:T(8,128)}, s32[2,8,128]{2,1,0:T(8,128)S(1)}, u32[]{:S(2)}, u32[]{:S(2)}) collective-permute-start(s32[2,8,128]{2,1,0:T(8,128)} %get-tuple-element.48), channel_id=1, source_target_pairs={{0,1},{1,0},{2,3},{3,2},{4,5},{5,4},{6,7},{7,6},{8,9},{9,8},{10,11... | collective-permute-start | bytes 24584 | tf_op jit(solution)/shard_map/ppermute | solution.py:187
  8.9 2.5 %collective-permute-start.1 = (s32[2,8,128]{2,1,0:T(8,128)}, s32[2,8,128]{2,1,0:T(8,128)S(1)}, u32[]{:S(2)}, u32[]{:S(2)}) collective-permute-start(s32[2,8,128]{2,1,0:T(8,128)} %get-tuple-element.49), channel_id=1, source_target_pairs={{0,2},{1,3},{2,0},{3,1},{4,6},{5,7},{6,4},{7,5},{8,10},{9,11},{10,... | collective-permute-start | bytes 24584 | tf_op jit(solution)/shard_map/ppermute | solution.py:187
  11.4 2.3 %rel_split.1.refs_1_ = bf16[800,2560]{1,0:T(8,128)(2,1)S(1)} custom-call(f32[400,2560]{1,0:T(8,128)} %bitcast.14), custom_call_target="tpu_custom_call" | custom-call | flops 2000000000 | bytes 6000000 | tf_op jit(solution)/shard_map/rel_split/pallas_call | solution.py:518
  15.3 2.3 %relation.2.refs_3_ = f32[400,512]{1,0:T(8,128)S(1)} custom-call(s32[4,8,128]{2,1,0:T(8,128)S(1)} %get-tuple-element.51.refs_0_, bf16[800,2560]{1,0:T(8,128)(2,1)S(1)} %rel_split.1.refs_1_), custom_call_target="tpu_custom_call" | custom-call | flops 2000000000 | bytes 6000000 | tf_op jit(solution)/shard_map/relation/pallas_call | solution.py:518
  18.5 2.3 %relation.3.refs_7_ = f32[400,512]{1,0:T(8,128)S(1)} custom-call(s32[4,8,128]{2,1,0:T(8,128)S(1)} %collective-permute-done.3.refs_0_.refs_1_, bf16[800,2560]{1,0:T(8,128)(2,1)S(1)} %rel_split.1.refs_1_), custom_call_target="tpu_custom_call" | custom-call | flops 2000000000 | bytes 6000000 | tf_op jit(solution)/shard_map/relation/pallas_call | solution.py:518
  21.5 4.1 %bucket.1 = (bf16[800,512]{1,0:T(8,128)(2,1)S(1)}, bf16[800,512]{1,0:T(8,128)(2,1)S(1)}, bf16[800,1024]{1,0:T(8,128)(2,1)S(1)}) custom-call(s32[4,8,128]{2,1,0:T(8,128)S(1)} %get-tuple-element.51.refs_0_, bf16[400,512]{1,0:T(8,128)(2,1)S(1)} %collective-permute-done.4.refs_1_.refs_5_, f32[400,512]{1,0:T(8,128)S(1)} %get-tuple-element.53.refs_2_, ...), custom_call_target="tpu_custom_call" | custom-call | flops 4000000000 | bytes 12000000 | tf_op jit(solution)/shard_map/bucket/pallas_call | solution.py:518
  25.6 7.9 %last.1 = (s16[16,288,128]{2,1,0:T(8,128)(2,1)S(1)}, f32[400,128]{1,0:T(8,128)S(1)}, bf16[800,1024]{1,0:T(8,128)(2,1)S(1)}, bf16[800,1024]{1,0:T(8,128)(2,1)S(1)}, bf16[800,2048]{1,0:T(8,128)(2,1)S(1)}) custom-call(s32[4,8,128]{2,1,0:T(8,128)S(1)} %get-tuple-element.51.refs_0_, s32[4,8,128]{2,1,0:T(8,128)S(1)} %collective-permute-done.3.refs_0_.refs_1_, ...), custom_call_target="tpu_custom_call" | custom-call | flops 8999999488 | bytes 27000000 | tf_op jit(solution)/shard_map/last/pallas_call | solution.py:518
  34.9 2.4 %home.1.refs_0_ = f32[16,280,128]{2,1,0:T(8,128)S(1)} custom-call(s32[4,8,128]{2,1,0:T(8,128)S(1)} %get-tuple-element.51.refs_0_, s32[4,8,128]{2,1,0:T(8,128)S(1)} %collective-permute-done.3.refs_0_.refs_1_, bf16[800,1024]{1,0:T(8,128)(2,1)S(1)} %get-tuple-element.60.refs_2_, f32[400,128]{1,0:T(8,128)S(1)} %get-tuple-element.61.refs_3_, ...), custom_call_target="tpu_custom_call" | custom-call | flops 3000000000 | bytes 9000000 | tf_op jit(solution)/shard_map/home/pallas_call | solution.py:518
  38.0 2.0 %collective-permute-start.10 = (s16[4,288,128]{2,1,0:T(8,128)(2,1)S(1)}, s16[4,288,128]{2,1,0:T(8,128)(2,1)S(1)}, u32[]{:S(2)}, u32[]{:S(2)}) collective-permute-start(s16[4,288,128]{2,1,0:T(8,128)(2,1)S(1)} %get-tuple-element.69), channel_id=1, source_target_pairs={{0,6},{1,7},{2,4},{3,5},{4,2},{5,3},{6,0},{7,1},{8,14},{9,15},{10,... | collective-permute-start | bytes 884744 | tf_op jit(solution)/shard_map/ppermute | solution.py:187
  41.5 2.0 %target.1 = (s16[416,256]{1,0:T(8,128)(2,1)S(1)}, s16[416,256]{1,0:T(8,128)(2,1)S(1)}) custom-call(s32[4,8,128]{2,1,0:T(8,128)S(1)} %get-tuple-element.51.refs_0_, s32[4,8,128]{2,1,0:T(8,128)S(1)} %collective-permute-done.3.refs_0_.refs_1_, bf16[800,2048]{1,0:T(8,128)(2,1)S(1)} %get-tuple-element.70.refs_2_, f32[4,280,128]{2,1,0:T(8,128)S(1)} %get-tuple-element.66.refs_3_.refs_0_), custom_call_target="tpu_custom_call" | custom-call | flops 1800000000 | bytes 5400000 | tf_op jit(solution)/shard_map/target/pallas_call | solution.py:518
  45.6 3.3 %collective-permute-done.10.refs_3_ = s16[4,288,128]{2,1,0:T(8,128)(2,1)S(1)} collective-permute-done((s16[4,288,128]{2,1,0:T(8,128)(2,1)S(1)}, s16[4,288,128]{2,1,0:T(8,128)(2,1)S(1)}, u32[]{:S(2)}, u32[]{:S(2)}) %collective-permute-start.10) | collective-permute-done | bytes 294944 | tf_op jit(solution)/shard_map/ppermute | solution.py:187
  48.9 5.2 %collective-permute-done.8.refs_1_ = s16[4,288,128]{2,1,0:T(8,128)(2,1)S(1)} collective-permute-done((s16[4,288,128]{2,1,0:T(8,128)(2,1)S(1)}, s16[4,288,128]{2,1,0:T(8,128)(2,1)S(1)}, u32[]{:S(2)}, u32[]{:S(2)}) %collective-permute-start.8) | collective-permute-done | bytes 294944 | tf_op jit(solution)/shard_map/ppermute | solution.py:187
  54.8 2.5 %collective-permute-start.16 = (s16[416,256]{1,0:T(8,128)(2,1)S(1)}, s16[416,256]{1,0:T(8,128)(2,1)S(1)}, u32[]{:S(2)}, u32[]{:S(2)}) collective-permute-start(s16[416,256]{1,0:T(8,128)(2,1)S(1)} %get-tuple-element.78), channel_id=1, source_target_pairs={{0,1},{1,0},{2,3},{3,2},{4,5},{5,4},{6,7},{7,6},{8,9},{9,8},{10,11... | collective-permute-start | bytes 638984 | tf_op jit(solution)/shard_map/ppermute | solution.py:187
  57.3 2.5 %collective-permute-start.17 = (s16[416,128]{1,0:T(8,128)(2,1)S(1)}, s16[416,128]{1,0:T(8,128)(2,1)S(1)}, u32[]{:S(2)}, u32[]{:S(2)}) collective-permute-start(s16[416,128]{1,0:T(8,128)(2,1)S(1)} %get-tuple-element.80), channel_id=1, source_target_pairs={{0,2},{1,3},{2,0},{3,1},{4,6},{5,7},{6,4},{7,5},{8,10},{9,11},{10,... | collective-permute-start | bytes 319496 | tf_op jit(solution)/shard_map/ppermute | solution.py:187
  59.7 2.2 %collective-permute-start.14 = (s16[1,288,128]{2,1,0:T(8,128)(2,1)S(1)}, s16[1,288,128]{2,1,0:T(8,128)(2,1)S(1)}, u32[]{:S(2)}, u32[]{:S(2)}) collective-permute-start(s16[1,288,128]{2,1,0:T(8,128)(2,1)S(1)} %get-tuple-element.75), channel_id=1, source_target_pairs={{0,16},{1,17},{2,18},{3,19},{4,20},{5,21},{6,22},{7,23},{8,24},{9,... | collective-permute-start | bytes 221192 | tf_op jit(solution)/shard_map/ppermute | solution.py:187
  61.9 2.2 %collective-permute-start.15 = (s16[1,288,128]{2,1,0:T(8,128)(2,1)S(1)}, s16[1,288,128]{2,1,0:T(8,128)(2,1)S(1)}, u32[]{:S(2)}, u32[]{:S(2)}) collective-permute-start(s16[1,288,128]{2,1,0:T(8,128)(2,1)S(1)} %get-tuple-element.76), channel_id=1, source_target_pairs={{0,24},{1,25},{2,26},{3,27},{4,28},{5,29},{6,30},{7,31},{8,16},{9,... | collective-permute-start | bytes 221192 | tf_op jit(solution)/shard_map/ppermute | solution.py:187
  65.2 3.5 %collective-permute-done.14.refs_2_ = s16[1,288,128]{2,1,0:T(8,128)(2,1)S(1)} collective-permute-done((s16[1,288,128]{2,1,0:T(8,128)(2,1)S(1)}, s16[1,288,128]{2,1,0:T(8,128)(2,1)S(1)}, u32[]{:S(2)}, u32[]{:S(2)}) %collective-permute-start.14) | collective-permute-done | bytes 73760 | tf_op jit(solution)/shard_map/ppermute | solution.py:187
  75.5 4.7 %collective-permute-done.19.refs_2_ = s16[1,288,128]{2,1,0:T(8,128)(2,1)S(1)} collective-permute-done((s16[1,288,128]{2,1,0:T(8,128)(2,1)S(1)}, s16[1,288,128]{2,1,0:T(8,128)(2,1)S(1)}, u32[]{:S(2)}, u32[]{:S(2)}) %collective-permute-start.19) | collective-permute-done | bytes 73760 | tf_op jit(solution)/shard_map/ppermute | solution.py:187
  80.4 1.7 %collective-permute-start.27 = (s16[4,288,128]{2,1,0:T(8,128)(2,1)S(1)}, s16[4,288,128]{2,1,0:T(8,128)(2,1)S(1)}, u32[]{:S(2)}, u32[]{:S(2)}) collective-permute-start(s16[4,288,128]{2,1,0:T(8,128)(2,1)S(1)} %get-tuple-element.86.refs_0_), channel_id=1, source_target_pairs={{0,2},{1,3},{2,0},{3,1},{4,6},{5,7},{6,4},{7,5},{8,10},{9,11},{10,... | collective-permute-start | bytes 884744 | tf_op jit(solution)/shard_map/ppermute | solution.py:187
  83.0 6.1 %collective-permute-done.24.refs_2_ = s16[416,128]{1,0:T(8,128)(2,1)S(1)} collective-permute-done((s16[416,128]{1,0:T(8,128)(2,1)S(1)}, s16[416,128]{1,0:T(8,128)(2,1)S(1)}, u32[]{:S(2)}, u32[]{:S(2)}) %collective-permute-start.24) | collective-permute-done | bytes 106528 | tf_op jit(solution)/shard_map/ppermute | solution.py:187
  89.8 1.7 %collective-permute-start.33 = (s16[2,288,128]{2,1,0:T(8,128)(2,1)S(1)}, s16[2,288,128]{2,1,0:T(8,128)(2,1)S(1)}, u32[]{:S(2)}, u32[]{:S(2)}) collective-permute-start(s16[2,288,128]{2,1,0:T(8,128)(2,1)S(1)} %slice.9), channel_id=1, source_target_pairs={{0,2},{1,3},{2,0},{3,1},{4,6},{5,7},{6,4},{7,5},{8,10},{9,11},{10,... | collective-permute-start | bytes 442376 | tf_op jit(solution)/shard_map/ppermute | solution.py:187
  93.1 2.3 %collective-permute-done.31.refs_3_ = s16[2,288,128]{2,1,0:T(8,128)(2,1)S(1)} collective-permute-done((s16[2,288,128]{2,1,0:T(8,128)(2,1)S(1)}, s16[2,288,128]{2,1,0:T(8,128)(2,1)S(1)}, u32[]{:S(2)}, u32[]{:S(2)}) %collective-permute-start.31) | collective-permute-done | bytes 147488 | tf_op jit(solution)/shard_map/ppermute | solution.py:187
  97.7 1.7 %spread.3 = (f32[400,2560]{1,0:T(8,128)}, f32[400,256]{1,0:T(8,128)}) custom-call(s32[1]{0:T(128)} %bitcast.5.side, s16[4,288,128]{2,1,0:T(8,128)(2,1)S(1)} %collective-permute-done.26.refs_0_, s16[4,288,128]{2,1,0:T(8,128)(2,1)S(1)} %collective-permute-done.28.refs_1_, ...), custom_call_target="tpu_custom_call", output_to_operand_aliasing={{0}: (6, {}), {1}: (7, {})} | custom-call | flops 2000000000 | bytes 6000000 | tf_op jit(solution)/shard_map/spread/pallas_call | solution.py:518
  (74 shorter events, 25.9 us)
Async XLA Ops:
  0.6 20.9 %collective-permute-start.4 = (bf16[400,512]{1,0:T(8,128)(2,1)}, bf16[400,512]{1,0:T(8,128)(2,1)S(1)}, u32[]{:S(2)}, u32[]{:S(2)}) collective-permute-start(bf16[400,512]{1,0:T(8,128)(2,1)} %bitcast.9), channel_id=1, source_target_pairs={{0,0},{1,17},{2,10},{3,27},{4,4},{5,21},{6,14},{7,31},{8,8},{9,25}... | collective-permute-start | bytes 1228808 | tf_op jit(solution)/shard_map/ppermute | solution.py:187
  2.3 18.5 %collective-permute-start.5 = (bf16[400,512]{1,0:T(8,128)(2,1)}, bf16[400,512]{1,0:T(8,128)(2,1)S(1)}, u32[]{:S(2)}, u32[]{:S(2)}) collective-permute-start(bf16[400,512]{1,0:T(8,128)(2,1)} %bitcast.10), channel_id=1, source_target_pairs={{0,4},{1,5},{2,6},{3,7},{4,0},{5,1},{6,2},{7,3},{8,12},{9,13},{10,... | collective-permute-start | bytes 1228808 | tf_op jit(solution)/shard_map/ppermute | solution.py:187
  6.7 7.0 %collective-permute-start = (s32[2,8,128]{2,1,0:T(8,128)}, s32[2,8,128]{2,1,0:T(8,128)S(1)}, u32[]{:S(2)}, u32[]{:S(2)}) collective-permute-start(s32[2,8,128]{2,1,0:T(8,128)} %get-tuple-element.48), channel_id=1, source_target_pairs={{0,1},{1,0},{2,3},{3,2},{4,5},{5,4},{6,7},{7,6},{8,9},{9,8},{10,11... | collective-permute-start | bytes 24584 | tf_op jit(solution)/shard_map/ppermute | solution.py:187
  38.0 10.9 %collective-permute-start.10 = (s16[4,288,128]{2,1,0:T(8,128)(2,1)S(1)}, s16[4,288,128]{2,1,0:T(8,128)(2,1)S(1)}, u32[]{:S(2)}, u32[]{:S(2)}) collective-permute-start(s16[4,288,128]{2,1,0:T(8,128)(2,1)S(1)} %get-tuple-element.69), channel_id=1, source_target_pairs={{0,6},{1,7},{2,4},{3,5},{4,2},{5,3},{6,0},{7,1},{8,14},{9,15},{10,... | collective-permute-start | bytes 884744 | tf_op jit(solution)/shard_map/ppermute | solution.py:187
  40.0 14.1 %collective-permute-start.8 = (s16[4,288,128]{2,1,0:T(8,128)(2,1)S(1)}, s16[4,288,128]{2,1,0:T(8,128)(2,1)S(1)}, u32[]{:S(2)}, u32[]{:S(2)}) collective-permute-start(s16[4,288,128]{2,1,0:T(8,128)(2,1)S(1)} %get-tuple-element.67), channel_id=1, source_target_pairs={{0,2},{1,3},{2,0},{3,1},{4,6},{5,7},{6,4},{7,5},{8,10},{9,11},{10,... | collective-permute-start | bytes 884744 | tf_op jit(solution)/shard_map/ppermute | solution.py:187
  40.8 13.4 %collective-permute-start.9 = (s16[4,288,128]{2,1,0:T(8,128)(2,1)S(1)}, s16[4,288,128]{2,1,0:T(8,128)(2,1)S(1)}, u32[]{:S(2)}, u32[]{:S(2)}) collective-permute-start(s16[4,288,128]{2,1,0:T(8,128)(2,1)S(1)} %get-tuple-element.68), channel_id=1, source_target_pairs={{0,4},{1,5},{2,6},{3,7},{4,0},{5,1},{6,2},{7,3},{8,12},{9,13},{10,... | collective-permute-start | bytes 884744 | tf_op jit(solution)/shard_map/ppermute | solution.py:187
  54.8 13.9 %collective-permute-start.16 = (s16[416,256]{1,0:T(8,128)(2,1)S(1)}, s16[416,256]{1,0:T(8,128)(2,1)S(1)}, u32[]{:S(2)}, u32[]{:S(2)}) collective-permute-start(s16[416,256]{1,0:T(8,128)(2,1)S(1)} %get-tuple-element.78), channel_id=1, source_target_pairs={{0,1},{1,0},{2,3},{3,2},{4,5},{5,4},{6,7},{7,6},{8,9},{9,8},{10,11... | collective-permute-start | bytes 638984 | tf_op jit(solution)/shard_map/ppermute | solution.py:187
  57.3 11.4 %collective-permute-start.17 = (s16[416,128]{1,0:T(8,128)(2,1)S(1)}, s16[416,128]{1,0:T(8,128)(2,1)S(1)}, u32[]{:S(2)}, u32[]{:S(2)}) collective-permute-start(s16[416,128]{1,0:T(8,128)(2,1)S(1)} %get-tuple-element.80), channel_id=1, source_target_pairs={{0,2},{1,3},{2,0},{3,1},{4,6},{5,7},{6,4},{7,5},{8,10},{9,11},{10,... | collective-permute-start | bytes 319496 | tf_op jit(solution)/shard_map/ppermute | solution.py:187
  59.7 5.5 %collective-permute-start.13 = (s16[1,288,128]{2,1,0:T(8,128)(2,1)S(1)}, s16[1,288,128]{2,1,0:T(8,128)(2,1)S(1)}, u32[]{:S(2)}, u32[]{:S(2)}) collective-permute-start(s16[1,288,128]{2,1,0:T(8,128)(2,1)S(1)} %get-tuple-element.74), channel_id=1, source_target_pairs={{0,8},{1,9},{2,10},{3,11},{4,12},{5,13},{6,14},{7,15},{8,0},{9,1},... | collective-permute-start | bytes 221192 | tf_op jit(solution)/shard_map/ppermute | solution.py:187
  59.7 9.0 %collective-permute-start.14 = (s16[1,288,128]{2,1,0:T(8,128)(2,1)S(1)}, s16[1,288,128]{2,1,0:T(8,128)(2,1)S(1)}, u32[]{:S(2)}, u32[]{:S(2)}) collective-permute-start(s16[1,288,128]{2,1,0:T(8,128)(2,1)S(1)} %get-tuple-element.75), channel_id=1, source_target_pairs={{0,16},{1,17},{2,18},{3,19},{4,20},{5,21},{6,22},{7,23},{8,24},{9,... | collective-permute-start | bytes 221192 | tf_op jit(solution)/shard_map/ppermute | solution.py:187
  61.9 6.8 %collective-permute-start.15 = (s16[1,288,128]{2,1,0:T(8,128)(2,1)S(1)}, s16[1,288,128]{2,1,0:T(8,128)(2,1)S(1)}, u32[]{:S(2)}, u32[]{:S(2)}) collective-permute-start(s16[1,288,128]{2,1,0:T(8,128)(2,1)S(1)} %get-tuple-element.76), channel_id=1, source_target_pairs={{0,24},{1,25},{2,26},{3,27},{4,28},{5,29},{6,30},{7,31},{8,16},{9,... | collective-permute-start | bytes 221192 | tf_op jit(solution)/shard_map/ppermute | solution.py:187
  68.9 11.3 %collective-permute-start.21 = (s16[416,128]{1,0:T(8,128)(2,1)S(1)}, s16[416,128]{1,0:T(8,128)(2,1)S(1)}, u32[]{:S(2)}, u32[]{:S(2)}) collective-permute-start(s16[416,128]{1,0:T(8,128)(2,1)S(1)} %get-tuple-element.83), channel_id=1, source_target_pairs={{0,2},{1,3},{2,0},{3,1},{4,6},{5,7},{6,4},{7,5},{8,10},{9,11},{10,... | collective-permute-start | bytes 319496 | tf_op jit(solution)/shard_map/ppermute | solution.py:187
  69.3 11.0 %collective-permute-start.22 = (s16[416,128]{1,0:T(8,128)(2,1)S(1)}, s16[416,128]{1,0:T(8,128)(2,1)S(1)}, u32[]{:S(2)}, u32[]{:S(2)}) collective-permute-start(s16[416,128]{1,0:T(8,128)(2,1)S(1)} %get-tuple-element.84), channel_id=1, source_target_pairs={{0,4},{1,5},{2,6},{3,7},{4,0},{5,1},{6,2},{7,3},{8,12},{9,13},{10,... | collective-permute-start | bytes 319496 | tf_op jit(solution)/shard_map/ppermute | solution.py:187
  72.4 7.9 %collective-permute-start.19 = (s16[1,288,128]{2,1,0:T(8,128)(2,1)S(1)}, s16[1,288,128]{2,1,0:T(8,128)(2,1)S(1)}, u32[]{:S(2)}, u32[]{:S(2)}) collective-permute-start(s16[1,288,128]{2,1,0:T(8,128)(2,1)S(1)} %get-tuple-element.81.refs_0_), channel_id=1, source_target_pairs={{0,16},{1,17},{2,18},{3,19},{4,20},{5,21},{6,22},{7,23},{8,24},{9,... | collective-permute-start | bytes 221192 | tf_op jit(solution)/shard_map/ppermute | solution.py:187
  73.7 6.6 %collective-permute-start.20 = (s16[1,288,128]{2,1,0:T(8,128)(2,1)S(1)}, s16[1,288,128]{2,1,0:T(8,128)(2,1)S(1)}, u32[]{:S(2)}, u32[]{:S(2)}) collective-permute-start(s16[1,288,128]{2,1,0:T(8,128)(2,1)S(1)} %get-tuple-element.81.refs_0_), channel_id=1, source_target_pairs={{0,24},{1,25},{2,26},{3,27},{4,28},{5,29},{6,30},{7,31},{8,16},{9,... | collective-permute-start | bytes 221192 | tf_op jit(solution)/shard_map/ppermute | solution.py:187
  80.4 8.7 %collective-permute-start.27 = (s16[4,288,128]{2,1,0:T(8,128)(2,1)S(1)}, s16[4,288,128]{2,1,0:T(8,128)(2,1)S(1)}, u32[]{:S(2)}, u32[]{:S(2)}) collective-permute-start(s16[4,288,128]{2,1,0:T(8,128)(2,1)S(1)} %get-tuple-element.86.refs_0_), channel_id=1, source_target_pairs={{0,2},{1,3},{2,0},{3,1},{4,6},{5,7},{6,4},{7,5},{8,10},{9,11},{10,... | collective-permute-start | bytes 884744 | tf_op jit(solution)/shard_map/ppermute | solution.py:187
  82.1 7.6 %collective-permute-start.29 = (s16[4,288,128]{2,1,0:T(8,128)(2,1)S(1)}, s16[4,288,128]{2,1,0:T(8,128)(2,1)S(1)}, u32[]{:S(2)}, u32[]{:S(2)}) collective-permute-start(s16[4,288,128]{2,1,0:T(8,128)(2,1)S(1)} %get-tuple-element.86.refs_0_), channel_id=1, source_target_pairs={{0,4},{1,5},{2,6},{3,7},{4,0},{5,1},{6,2},{7,3},{8,12},{9,13},{10,... | collective-permute-start | bytes 884744 | tf_op jit(solution)/shard_map/ppermute | solution.py:187
  82.7 6.4 %collective-permute-start.24 = (s16[416,128]{1,0:T(8,128)(2,1)S(1)}, s16[416,128]{1,0:T(8,128)(2,1)S(1)}, u32[]{:S(2)}, u32[]{:S(2)}) collective-permute-start(s16[416,128]{1,0:T(8,128)(2,1)S(1)} %get-tuple-element.85.refs_0_), channel_id=1, source_target_pairs={{0,2},{1,3},{2,0},{3,1},{4,6},{5,7},{6,4},{7,5},{8,10},{9,11},{10,... | collective-permute-start | bytes 319496 | tf_op jit(solution)/shard_map/ppermute | solution.py:187
  83.0 8.5 %collective-permute-start.23 = (s16[416,128]{1,0:T(8,128)(2,1)S(1)}, s16[416,128]{1,0:T(8,128)(2,1)S(1)}, u32[]{:S(2)}, u32[]{:S(2)}) collective-permute-start(s16[416,128]{1,0:T(8,128)(2,1)S(1)} %get-tuple-element.85.refs_0_), channel_id=1, source_target_pairs={{0,1},{1,0},{2,3},{3,2},{4,5},{5,4},{6,7},{7,6},{8,9},{9,8},{10,11... | collective-permute-start | bytes 319496 | tf_op jit(solution)/shard_map/ppermute | solution.py:187
  89.1 6.3 %collective-permute-start.31 = (s16[2,288,128]{2,1,0:T(8,128)(2,1)S(1)}, s16[2,288,128]{2,1,0:T(8,128)(2,1)S(1)}, u32[]{:S(2)}, u32[]{:S(2)}) collective-permute-start(s16[2,288,128]{2,1,0:T(8,128)(2,1)S(1)} %slice.8), channel_id=1, source_target_pairs={{0,4},{1,5},{2,6},{3,7},{4,0},{5,1},{6,2},{7,3},{8,12},{9,13},{10,... | collective-permute-start | bytes 442376 | tf_op jit(solution)/shard_map/ppermute | solution.py:187
  89.8 6.0 %collective-permute-start.33 = (s16[2,288,128]{2,1,0:T(8,128)(2,1)S(1)}, s16[2,288,128]{2,1,0:T(8,128)(2,1)S(1)}, u32[]{:S(2)}, u32[]{:S(2)}) collective-permute-start(s16[2,288,128]{2,1,0:T(8,128)(2,1)S(1)} %slice.9), channel_id=1, source_target_pairs={{0,2},{1,3},{2,0},{3,1},{4,6},{5,7},{6,4},{7,5},{8,10},{9,11},{10,... | collective-permute-start | bytes 442376 | tf_op jit(solution)/shard_map/ppermute | solution.py:187
  91.5 6.1 %collective-permute-start.26 = (s16[4,288,128]{2,1,0:T(8,128)(2,1)S(1)}, s16[4,288,128]{2,1,0:T(8,128)(2,1)S(1)}, u32[]{:S(2)}, u32[]{:S(2)}) collective-permute-start(s16[4,288,128]{2,1,0:T(8,128)(2,1)S(1)} %get-tuple-element.86.refs_0_), channel_id=1, source_target_pairs={{0,1},{1,0},{2,3},{3,2},{4,5},{5,4},{6,7},{7,6},{8,9},{9,8},{10,11... | collective-permute-start | bytes 884744 | tf_op jit(solution)/shard_map/ppermute | solution.py:187
  91.5 6.1 %collective-permute-start.28 = (s16[4,288,128]{2,1,0:T(8,128)(2,1)S(1)}, s16[4,288,128]{2,1,0:T(8,128)(2,1)S(1)}, u32[]{:S(2)}, u32[]{:S(2)}) collective-permute-start(s16[4,288,128]{2,1,0:T(8,128)(2,1)S(1)} %collective-permute-done.27.refs_1_), channel_id=1, source_target_pairs={{0,1},{1,0},{2,3},{3,2},{4,5},{5,4},{6,7},{7,6},{8,9},{9,8},{10,11... | collective-permute-start | bytes 884744 | tf_op jit(solution)/shard_map/ppermute | solution.py:187
  92.0 5.6 %collective-permute-start.30 = (s16[4,288,128]{2,1,0:T(8,128)(2,1)S(1)}, s16[4,288,128]{2,1,0:T(8,128)(2,1)S(1)}, u32[]{:S(2)}, u32[]{:S(2)}) collective-permute-start(s16[4,288,128]{2,1,0:T(8,128)(2,1)S(1)} %collective-permute-done.29.refs_2_), channel_id=1, source_target_pairs={{0,1},{1,0},{2,3},{3,2},{4,5},{5,4},{6,7},{7,6},{8,9},{9,8},{10,11... | collective-permute-start | bytes 884744 | tf_op jit(solution)/shard_map/ppermute | solution.py:187
  (14 other events, 41.7 us)

commit v13 on v12

--- a/solution.py
+++ b/solution.py
@@ -462,10 +462,12 @@
         first += count
 
 
-def spread_kernel(plan, counts, side, *refs):
-    helds = refs[len(refs) - len(counts) :]
-    rel_out, rem_out = refs[-2 - len(counts) : len(refs) - len(counts)]
+def spread_kernel(plan, counts, other, *refs):
+    scratch = len(counts) + 2
+    helds, table, sems = refs[len(refs) - scratch : -2], refs[-2], refs[-1]
+    rel_out, rem_out = refs[-2 - scratch : len(refs) - scratch]
     me = plan.me()
+    half = (me & 1) ^ other
     first = 0
     for count, held in zip(counts, helds):
         at = 0
@@ -473,6 +475,7 @@
             held[at : at + piece.shape[0]] = piece[...]
             at += piece.shape[0]
         first += count
+    stores = []
     for chunk in range(plan.half_chunks):
         for which, (part, held) in enumerate(zip(plan.parts, helds)):
             value = unpack_table(held[part.position(chunk, me)], 8 * part.units)
@@ -480,13 +483,24 @@
                 if block is None:
                     break
                 lane, sub = block
-                rows = slice(sub, sub + 8)
-                piece = value[8 * index : 8 * index + 8]
-                if lane < plan.half_rel:
-                    rel_out[rows, lane : lane + LANES] = piece
-                else:
-                    lane -= plan.half_rel
-                    rem_out[rows, lane : lane + LANES] = piece
+                table[sub : sub + 8, lane : lane + LANES] = value[8 * index : 8 * index + 8]
+        whole = min((chunk + 1) * plan.chunk_units, plan.units) // plan.subs
+        for block in range(len(stores), whole):
+            lane = block * LANES
+            if lane < plan.half_rel:
+                out, start = rel_out, half * plan.half_rel + lane
+            else:
+                out, start = rem_out, half * plan.half_rem + lane - plan.half_rel
+            stores.append(
+                pltpu.make_async_copy(
+                    table.at[:, lane : lane + LANES],
+                    out.at[:, pl.ds(pl.multiple_of(start, LANES), LANES)],
+                    sems.at[block],
+                )
+            )
+            stores[-1].start()
+    for store in stores:
+        store.wait()
 
 
 def part_out_kernel(plan, *refs):
@@ -511,13 +525,12 @@
 
 def call(kernel, outs, args, name, cost, limit, scratch=(), in_specs=None, out_specs=None, **more):
     work = pl.CostEstimate(flops=int(cost * 1e9), bytes_accessed=int(cost * 3e6), transcendentals=0)
-    if "grid_spec" not in more:
-        more["in_specs"] = in_specs or [VMEM] * len(args)
-        more["out_specs"] = out_specs or [VMEM] * len(outs)
-        more["scratch_shapes"] = list(scratch)
     return pl.pallas_call(
         kernel,
         out_shape=outs,
+        in_specs=in_specs or [VMEM] * len(args),
+        out_specs=out_specs or [VMEM] * len(outs),
+        scratch_shapes=list(scratch),
         compiler_params=pltpu.CompilerParams(vmem_limit_bytes=int(limit * 2**20)),
         cost_estimate=work,
         name=name,
@@ -826,27 +839,25 @@
         grad_partitions = jnp.take(split_lanes, order, axis=1).reshape(width, prows)
 
     crossed = [[send(piece, plan, lambda d: d ^ 1) for piece in group] for group in pieces]
-    side = lax.axis_index("rel") & 1
     outs = [shape((width, plan.nrels), F32), shape((width, plan.rems), F32)]
-    spec = lambda lanes: pl.BlockSpec((width, lanes), lambda i, half: (0, half[0]))
     made = []
     for turn, groups in enumerate([pieces, crossed]):
         flat = sum(groups, [])
-        made = call(
-            functools.partial(spread_kernel, plan, [len(group) for group in groups]),
+        made = after(
+            functools.partial(spread_kernel, plan, [len(group) for group in groups], turn),
             outs,
-            [(side ^ turn).reshape(1), *flat, *made],
+            flat,
+            made,
             "spread",
             2.0,
             16,
-            grid_spec=pltpu.PrefetchScalarGridSpec(
-                num_scalar_prefetch=1,
-                grid=(1,),
-                in_specs=[VMEM] * len(flat) + [ANY] * len(made),
-                out_specs=[spec(plan.half_rel), spec(plan.half_rem)],
-                scratch_shapes=[pltpu.VMEM(part.packed, i16) for part in plan.parts],
-            ),
-            input_output_aliases={1 + len(flat) + at: at for at in range(len(made))},
+            out_specs=[ANY] * 2,
+            scratch=[pltpu.VMEM(part.packed, i16) for part in plan.parts]
+            + [
+                pltpu.VMEM((width, plan.half_lanes), F32),
+                pltpu.SemaphoreType.DMA((plan.half_lanes // LANES,)),
+            ],
+            input_output_aliases={len(flat) + at: at for at in range(len(made))},
         )
     grad_relations, grad_remainder = made
     return grad_partitions.T, grad_remainder.T, grad_relations.T

time: 99.7 us -> 101 us (1.013)
  waiting for transfers between devices: 28.3 us -> 29.5 us
    ppermute x35, waiting for transfers between devices: 28.3 us -> 29.5 us  [send(): return lax.ppermute(value, ('dom', 'rel'), pairs)]
where the time goes in v13:
time: 101 us
  starting transfers between devices  36.9 us (37%)
  Pallas kernels  33.3 us (33%)
  waiting for transfers between devices  29.5 us (29%)
  between operations  1.1 us (1%)
    ppermute x35, starting transfers between devices, send(): return lax.ppermute(value, ('dom', 'rel'), pairs)  36.9 us
    pallas_call x20, Pallas kernels, call(): pl.pallas_call(kernel, out_shape=outs, in_specs=in_specs or [VMEM] * len(...  33.3 us
    ppermute x35, waiting for transfers between devices, send(): return lax.ppermute(value, ('dom', 'rel'), pairs)  29.5 us
  transfers between devices with their start and end apart: 35, of which 12 were waited for; matrix products, arithmetic and copies ran while one was open for 0% of the time, Pallas kernels for 18%

profile of v13, /device:TPU:0, one launch (start us, length us, event | category | flops | bytes accessed | tf_op | source)
XLA Modules:
  0.0 100.8 jit_solution(14510556091977060177)
XLA Ops:
  0.6 3.0 %collective-permute-start.5 = (bf16[400,512]{1,0:T(8,128)(2,1)}, bf16[400,512]{1,0:T(8,128)(2,1)S(1)}, u32[]{:S(2)}, u32[]{:S(2)}) collective-permute-start(bf16[400,512]{1,0:T(8,128)(2,1)} %bitcast.7), channel_id=1, source_target_pairs={{0,4},{1,5},{2,6},{3,7},{4,0},{5,1},{6,2},{7,3},{8,12},{9,13},{10,... | collective-permute-start | bytes 1228808 | tf_op jit(solution)/shard_map/ppermute | solution.py:187
  3.7 1.6 %collective-permute-start.4 = (bf16[400,512]{1,0:T(8,128)(2,1)}, bf16[400,512]{1,0:T(8,128)(2,1)S(1)}, u32[]{:S(2)}, u32[]{:S(2)}) collective-permute-start(bf16[400,512]{1,0:T(8,128)(2,1)} %bitcast.8), channel_id=1, source_target_pairs={{0,0},{1,17},{2,10},{3,27},{4,4},{5,21},{6,14},{7,31},{8,8},{9,25}... | collective-permute-start | bytes 1228808 | tf_op jit(solution)/shard_map/ppermute | solution.py:187
  6.8 2.1 %collective-permute-start = (s32[2,8,128]{2,1,0:T(8,128)}, s32[2,8,128]{2,1,0:T(8,128)S(1)}, u32[]{:S(2)}, u32[]{:S(2)}) collective-permute-start(s32[2,8,128]{2,1,0:T(8,128)} %get-tuple-element.48), channel_id=1, source_target_pairs={{0,1},{1,0},{2,3},{3,2},{4,5},{5,4},{6,7},{7,6},{8,9},{9,8},{10,11... | collective-permute-start | bytes 24584 | tf_op jit(solution)/shard_map/ppermute | solution.py:187
  8.9 2.5 %collective-permute-start.1 = (s32[2,8,128]{2,1,0:T(8,128)}, s32[2,8,128]{2,1,0:T(8,128)S(1)}, u32[]{:S(2)}, u32[]{:S(2)}) collective-permute-start(s32[2,8,128]{2,1,0:T(8,128)} %get-tuple-element.49), channel_id=1, source_target_pairs={{0,2},{1,3},{2,0},{3,1},{4,6},{5,7},{6,4},{7,5},{8,10},{9,11},{10,... | collective-permute-start | bytes 24584 | tf_op jit(solution)/shard_map/ppermute | solution.py:187
  11.4 2.3 %rel_split.1.refs_1_ = bf16[800,2560]{1,0:T(8,128)(2,1)S(1)} custom-call(f32[400,2560]{1,0:T(8,128)} %bitcast.12), custom_call_target="tpu_custom_call" | custom-call | flops 2000000000 | bytes 6000000 | tf_op jit(solution)/shard_map/rel_split/pallas_call | solution.py:528
  15.3 2.3 %relation.2.refs_3_ = f32[400,512]{1,0:T(8,128)S(1)} custom-call(s32[4,8,128]{2,1,0:T(8,128)S(1)} %get-tuple-element.51.refs_0_, bf16[800,2560]{1,0:T(8,128)(2,1)S(1)} %rel_split.1.refs_1_), custom_call_target="tpu_custom_call" | custom-call | flops 2000000000 | bytes 6000000 | tf_op jit(solution)/shard_map/relation/pallas_call | solution.py:528
  18.5 2.3 %relation.3.refs_7_ = f32[400,512]{1,0:T(8,128)S(1)} custom-call(s32[4,8,128]{2,1,0:T(8,128)S(1)} %collective-permute-done.3.refs_0_.refs_1_, bf16[800,2560]{1,0:T(8,128)(2,1)S(1)} %rel_split.1.refs_1_), custom_call_target="tpu_custom_call" | custom-call | flops 2000000000 | bytes 6000000 | tf_op jit(solution)/shard_map/relation/pallas_call | solution.py:528
  21.5 4.1 %bucket.1 = (bf16[800,512]{1,0:T(8,128)(2,1)S(1)}, bf16[800,512]{1,0:T(8,128)(2,1)S(1)}, bf16[800,1024]{1,0:T(8,128)(2,1)S(1)}) custom-call(s32[4,8,128]{2,1,0:T(8,128)S(1)} %get-tuple-element.51.refs_0_, bf16[400,512]{1,0:T(8,128)(2,1)S(1)} %collective-permute-done.4.refs_1_.refs_5_, f32[400,512]{1,0:T(8,128)S(1)} %get-tuple-element.53.refs_2_, ...), custom_call_target="tpu_custom_call" | custom-call | flops 4000000000 | bytes 12000000 | tf_op jit(solution)/shard_map/bucket/pallas_call | solution.py:528
  25.6 7.9 %last.1 = (s16[16,288,128]{2,1,0:T(8,128)(2,1)S(1)}, f32[400,128]{1,0:T(8,128)S(1)}, bf16[800,1024]{1,0:T(8,128)(2,1)S(1)}, bf16[800,1024]{1,0:T(8,128)(2,1)S(1)}, bf16[800,2048]{1,0:T(8,128)(2,1)S(1)}) custom-call(s32[4,8,128]{2,1,0:T(8,128)S(1)} %get-tuple-element.51.refs_0_, s32[4,8,128]{2,1,0:T(8,128)S(1)} %collective-permute-done.3.refs_0_.refs_1_, ...), custom_call_target="tpu_custom_call" | custom-call | flops 8999999488 | bytes 27000000 | tf_op jit(solution)/shard_map/last/pallas_call | solution.py:528
  34.9 2.4 %home.1.refs_0_ = f32[16,280,128]{2,1,0:T(8,128)S(1)} custom-call(s32[4,8,128]{2,1,0:T(8,128)S(1)} %get-tuple-element.51.refs_0_, s32[4,8,128]{2,1,0:T(8,128)S(1)} %collective-permute-done.3.refs_0_.refs_1_, bf16[800,1024]{1,0:T(8,128)(2,1)S(1)} %get-tuple-element.60.refs_2_, f32[400,128]{1,0:T(8,128)S(1)} %get-tuple-element.61.refs_3_, ...), custom_call_target="tpu_custom_call" | custom-call | flops 3000000000 | bytes 9000000 | tf_op jit(solution)/shard_map/home/pallas_call | solution.py:528
  41.5 2.0 %target.1 = (s16[416,256]{1,0:T(8,128)(2,1)S(1)}, s16[416,256]{1,0:T(8,128)(2,1)S(1)}) custom-call(s32[4,8,128]{2,1,0:T(8,128)S(1)} %get-tuple-element.51.refs_0_, s32[4,8,128]{2,1,0:T(8,128)S(1)} %collective-permute-done.3.refs_0_.refs_1_, bf16[800,2048]{1,0:T(8,128)(2,1)S(1)} %get-tuple-element.70.refs_2_, f32[4,280,128]{2,1,0:T(8,128)S(1)} %get-tuple-element.66.refs_3_.refs_0_), custom_call_target="tpu_custom_call" | custom-call | flops 1800000000 | bytes 5400000 | tf_op jit(solution)/shard_map/target/pallas_call | solution.py:528
  45.6 2.3 %collective-permute-done.8.refs_1_ = s16[4,288,128]{2,1,0:T(8,128)(2,1)S(1)} collective-permute-done((s16[4,288,128]{2,1,0:T(8,128)(2,1)S(1)}, s16[4,288,128]{2,1,0:T(8,128)(2,1)S(1)}, u32[]{:S(2)}, u32[]{:S(2)}) %collective-permute-start.8) | collective-permute-done | bytes 294944 | tf_op jit(solution)/shard_map/ppermute | solution.py:187
  47.9 4.9 %collective-permute-done.9.refs_2_ = s16[4,288,128]{2,1,0:T(8,128)(2,1)S(1)} collective-permute-done((s16[4,288,128]{2,1,0:T(8,128)(2,1)S(1)}, s16[4,288,128]{2,1,0:T(8,128)(2,1)S(1)}, u32[]{:S(2)}, u32[]{:S(2)}) %collective-permute-start.9) | collective-permute-done | bytes 294944 | tf_op jit(solution)/shard_map/ppermute | solution.py:187
  54.6 2.3 %collective-permute-start.16 = (s16[416,256]{1,0:T(8,128)(2,1)S(1)}, s16[416,256]{1,0:T(8,128)(2,1)S(1)}, u32[]{:S(2)}, u32[]{:S(2)}) collective-permute-start(s16[416,256]{1,0:T(8,128)(2,1)S(1)} %get-tuple-element.78), channel_id=1, source_target_pairs={{0,1},{1,0},{2,3},{3,2},{4,5},{5,4},{6,7},{7,6},{8,9},{9,8},{10,11... | collective-permute-start | bytes 638984 | tf_op jit(solution)/shard_map/ppermute | solution.py:187
  57.0 2.5 %collective-permute-start.17 = (s16[416,128]{1,0:T(8,128)(2,1)S(1)}, s16[416,128]{1,0:T(8,128)(2,1)S(1)}, u32[]{:S(2)}, u32[]{:S(2)}) collective-permute-start(s16[416,128]{1,0:T(8,128)(2,1)S(1)} %get-tuple-element.80), channel_id=1, source_target_pairs={{0,2},{1,3},{2,0},{3,1},{4,6},{5,7},{6,4},{7,5},{8,10},{9,11},{10,... | collective-permute-start | bytes 319496 | tf_op jit(solution)/shard_map/ppermute | solution.py:187
  59.5 2.1 %collective-permute-start.14 = (s16[1,288,128]{2,1,0:T(8,128)(2,1)S(1)}, s16[1,288,128]{2,1,0:T(8,128)(2,1)S(1)}, u32[]{:S(2)}, u32[]{:S(2)}) collective-permute-start(s16[1,288,128]{2,1,0:T(8,128)(2,1)S(1)} %get-tuple-element.75), channel_id=1, source_target_pairs={{0,16},{1,17},{2,18},{3,19},{4,20},{5,21},{6,22},{7,23},{8,24},{9,... | collective-permute-start | bytes 221192 | tf_op jit(solution)/shard_map/ppermute | solution.py:187
  61.6 2.3 %collective-permute-start.15 = (s16[1,288,128]{2,1,0:T(8,128)(2,1)S(1)}, s16[1,288,128]{2,1,0:T(8,128)(2,1)S(1)}, u32[]{:S(2)}, u32[]{:S(2)}) collective-permute-start(s16[1,288,128]{2,1,0:T(8,128)(2,1)S(1)} %get-tuple-element.76), channel_id=1, source_target_pairs={{0,24},{1,25},{2,26},{3,27},{4,28},{5,29},{6,30},{7,31},{8,16},{9,... | collective-permute-start | bytes 221192 | tf_op jit(solution)/shard_map/ppermute | solution.py:187
  64.9 3.8 %collective-permute-done.14.refs_2_ = s16[1,288,128]{2,1,0:T(8,128)(2,1)S(1)} collective-permute-done((s16[1,288,128]{2,1,0:T(8,128)(2,1)S(1)}, s16[1,288,128]{2,1,0:T(8,128)(2,1)S(1)}, u32[]{:S(2)}, u32[]{:S(2)}) %collective-permute-start.14) | collective-permute-done | bytes 73760 | tf_op jit(solution)/shard_map/ppermute | solution.py:187
  70.5 2.2 %collective-permute-start.20 = (s16[1,288,128]{2,1,0:T(8,128)(2,1)S(1)}, s16[1,288,128]{2,1,0:T(8,128)(2,1)S(1)}, u32[]{:S(2)}, u32[]{:S(2)}) collective-permute-start(s16[1,288,128]{2,1,0:T(8,128)(2,1)S(1)} %get-tuple-element.81.refs_0_), channel_id=1, source_target_pairs={{0,24},{1,25},{2,26},{3,27},{4,28},{5,29},{6,30},{7,31},{8,16},{9,... | collective-permute-start | bytes 221192 | tf_op jit(solution)/shard_map/ppermute | solution.py:187
  74.9 2.2 %collective-permute-done.20.refs_3_ = s16[1,288,128]{2,1,0:T(8,128)(2,1)S(1)} collective-permute-done((s16[1,288,128]{2,1,0:T(8,128)(2,1)S(1)}, s16[1,288,128]{2,1,0:T(8,128)(2,1)S(1)}, u32[]{:S(2)}, u32[]{:S(2)}) %collective-permute-start.20) | collective-permute-done | bytes 73760 | tf_op jit(solution)/shard_map/ppermute | solution.py:187
  77.0 2.2 %collective-permute-done.19.refs_2_ = s16[1,288,128]{2,1,0:T(8,128)(2,1)S(1)} collective-permute-done((s16[1,288,128]{2,1,0:T(8,128)(2,1)S(1)}, s16[1,288,128]{2,1,0:T(8,128)(2,1)S(1)}, u32[]{:S(2)}, u32[]{:S(2)}) %collective-permute-start.19) | collective-permute-done | bytes 73760 | tf_op jit(solution)/shard_map/ppermute | solution.py:187
  79.9 1.6 %collective-permute-start.27 = (s16[4,288,128]{2,1,0:T(8,128)(2,1)S(1)}, s16[4,288,128]{2,1,0:T(8,128)(2,1)S(1)}, u32[]{:S(2)}, u32[]{:S(2)}) collective-permute-start(s16[4,288,128]{2,1,0:T(8,128)(2,1)S(1)} %get-tuple-element.86.refs_0_), channel_id=1, source_target_pairs={{0,2},{1,3},{2,0},{3,1},{4,6},{5,7},{6,4},{7,5},{8,10},{9,11},{10,... | collective-permute-start | bytes 884744 | tf_op jit(solution)/shard_map/ppermute | solution.py:187
  81.9 7.7 %collective-permute-done.24.refs_2_ = s16[416,128]{1,0:T(8,128)(2,1)S(1)} collective-permute-done((s16[416,128]{1,0:T(8,128)(2,1)S(1)}, s16[416,128]{1,0:T(8,128)(2,1)S(1)}, u32[]{:S(2)}, u32[]{:S(2)}) %collective-permute-start.24) | collective-permute-done | bytes 106528 | tf_op jit(solution)/shard_map/ppermute | solution.py:187
  89.6 1.7 %collective-permute-start.33 = (s16[2,288,128]{2,1,0:T(8,128)(2,1)S(1)}, s16[2,288,128]{2,1,0:T(8,128)(2,1)S(1)}, u32[]{:S(2)}, u32[]{:S(2)}) collective-permute-start(s16[2,288,128]{2,1,0:T(8,128)(2,1)S(1)} %slice.9), channel_id=1, source_target_pairs={{0,2},{1,3},{2,0},{3,1},{4,6},{5,7},{6,4},{7,5},{8,10},{9,11},{10,... | collective-permute-start | bytes 442376 | tf_op jit(solution)/shard_map/ppermute | solution.py:187
  (74 shorter events, 29.2 us)
Async XLA Ops:
  0.6 20.2 %collective-permute-start.5 = (bf16[400,512]{1,0:T(8,128)(2,1)}, bf16[400,512]{1,0:T(8,128)(2,1)S(1)}, u32[]{:S(2)}, u32[]{:S(2)}) collective-permute-start(bf16[400,512]{1,0:T(8,128)(2,1)} %bitcast.7), channel_id=1, source_target_pairs={{0,4},{1,5},{2,6},{3,7},{4,0},{5,1},{6,2},{7,3},{8,12},{9,13},{10,... | collective-permute-start | bytes 1228808 | tf_op jit(solution)/shard_map/ppermute | solution.py:187
  3.7 17.8 %collective-permute-start.4 = (bf16[400,512]{1,0:T(8,128)(2,1)}, bf16[400,512]{1,0:T(8,128)(2,1)S(1)}, u32[]{:S(2)}, u32[]{:S(2)}) collective-permute-start(bf16[400,512]{1,0:T(8,128)(2,1)} %bitcast.8), channel_id=1, source_target_pairs={{0,0},{1,17},{2,10},{3,27},{4,4},{5,21},{6,14},{7,31},{8,8},{9,25}... | collective-permute-start | bytes 1228808 | tf_op jit(solution)/shard_map/ppermute | solution.py:187
  6.8 7.0 %collective-permute-start = (s32[2,8,128]{2,1,0:T(8,128)}, s32[2,8,128]{2,1,0:T(8,128)S(1)}, u32[]{:S(2)}, u32[]{:S(2)}) collective-permute-start(s32[2,8,128]{2,1,0:T(8,128)} %get-tuple-element.48), channel_id=1, source_target_pairs={{0,1},{1,0},{2,3},{3,2},{4,5},{5,4},{6,7},{7,6},{8,9},{9,8},{10,11... | collective-permute-start | bytes 24584 | tf_op jit(solution)/shard_map/ppermute | solution.py:187
  38.0 9.9 %collective-permute-start.8 = (s16[4,288,128]{2,1,0:T(8,128)(2,1)S(1)}, s16[4,288,128]{2,1,0:T(8,128)(2,1)S(1)}, u32[]{:S(2)}, u32[]{:S(2)}) collective-permute-start(s16[4,288,128]{2,1,0:T(8,128)(2,1)S(1)} %get-tuple-element.67), channel_id=1, source_target_pairs={{0,2},{1,3},{2,0},{3,1},{4,6},{5,7},{6,4},{7,5},{8,10},{9,11},{10,... | collective-permute-start | bytes 884744 | tf_op jit(solution)/shard_map/ppermute | solution.py:187
  38.6 14.2 %collective-permute-start.9 = (s16[4,288,128]{2,1,0:T(8,128)(2,1)S(1)}, s16[4,288,128]{2,1,0:T(8,128)(2,1)S(1)}, u32[]{:S(2)}, u32[]{:S(2)}) collective-permute-start(s16[4,288,128]{2,1,0:T(8,128)(2,1)S(1)} %get-tuple-element.68), channel_id=1, source_target_pairs={{0,4},{1,5},{2,6},{3,7},{4,0},{5,1},{6,2},{7,3},{8,12},{9,13},{10,... | collective-permute-start | bytes 884744 | tf_op jit(solution)/shard_map/ppermute | solution.py:187
  40.0 14.1 %collective-permute-start.10 = (s16[4,288,128]{2,1,0:T(8,128)(2,1)S(1)}, s16[4,288,128]{2,1,0:T(8,128)(2,1)S(1)}, u32[]{:S(2)}, u32[]{:S(2)}) collective-permute-start(s16[4,288,128]{2,1,0:T(8,128)(2,1)S(1)} %get-tuple-element.69), channel_id=1, source_target_pairs={{0,6},{1,7},{2,4},{3,5},{4,2},{5,3},{6,0},{7,1},{8,14},{9,15},{10,... | collective-permute-start | bytes 884744 | tf_op jit(solution)/shard_map/ppermute | solution.py:187
  54.6 14.0 %collective-permute-start.16 = (s16[416,256]{1,0:T(8,128)(2,1)S(1)}, s16[416,256]{1,0:T(8,128)(2,1)S(1)}, u32[]{:S(2)}, u32[]{:S(2)}) collective-permute-start(s16[416,256]{1,0:T(8,128)(2,1)S(1)} %get-tuple-element.78), channel_id=1, source_target_pairs={{0,1},{1,0},{2,3},{3,2},{4,5},{5,4},{6,7},{7,6},{8,9},{9,8},{10,11... | collective-permute-start | bytes 638984 | tf_op jit(solution)/shard_map/ppermute | solution.py:187
  57.0 11.7 %collective-permute-start.17 = (s16[416,128]{1,0:T(8,128)(2,1)S(1)}, s16[416,128]{1,0:T(8,128)(2,1)S(1)}, u32[]{:S(2)}, u32[]{:S(2)}) collective-permute-start(s16[416,128]{1,0:T(8,128)(2,1)S(1)} %get-tuple-element.80), channel_id=1, source_target_pairs={{0,2},{1,3},{2,0},{3,1},{4,6},{5,7},{6,4},{7,5},{8,10},{9,11},{10,... | collective-permute-start | bytes 319496 | tf_op jit(solution)/shard_map/ppermute | solution.py:187
  59.5 9.2 %collective-permute-start.14 = (s16[1,288,128]{2,1,0:T(8,128)(2,1)S(1)}, s16[1,288,128]{2,1,0:T(8,128)(2,1)S(1)}, u32[]{:S(2)}, u32[]{:S(2)}) collective-permute-start(s16[1,288,128]{2,1,0:T(8,128)(2,1)S(1)} %get-tuple-element.75), channel_id=1, source_target_pairs={{0,16},{1,17},{2,18},{3,19},{4,20},{5,21},{6,22},{7,23},{8,24},{9,... | collective-permute-start | bytes 221192 | tf_op jit(solution)/shard_map/ppermute | solution.py:187
  61.6 7.1 %collective-permute-start.15 = (s16[1,288,128]{2,1,0:T(8,128)(2,1)S(1)}, s16[1,288,128]{2,1,0:T(8,128)(2,1)S(1)}, u32[]{:S(2)}, u32[]{:S(2)}) collective-permute-start(s16[1,288,128]{2,1,0:T(8,128)(2,1)S(1)} %get-tuple-element.76), channel_id=1, source_target_pairs={{0,24},{1,25},{2,26},{3,27},{4,28},{5,29},{6,30},{7,31},{8,16},{9,... | collective-permute-start | bytes 221192 | tf_op jit(solution)/shard_map/ppermute | solution.py:187
  68.9 10.3 %collective-permute-start.21 = (s16[416,128]{1,0:T(8,128)(2,1)S(1)}, s16[416,128]{1,0:T(8,128)(2,1)S(1)}, u32[]{:S(2)}, u32[]{:S(2)}) collective-permute-start(s16[416,128]{1,0:T(8,128)(2,1)S(1)} %get-tuple-element.83), channel_id=1, source_target_pairs={{0,2},{1,3},{2,0},{3,1},{4,6},{5,7},{6,4},{7,5},{8,10},{9,11},{10,... | collective-permute-start | bytes 319496 | tf_op jit(solution)/shard_map/ppermute | solution.py:187
  69.1 10.1 %collective-permute-start.22 = (s16[416,128]{1,0:T(8,128)(2,1)S(1)}, s16[416,128]{1,0:T(8,128)(2,1)S(1)}, u32[]{:S(2)}, u32[]{:S(2)}) collective-permute-start(s16[416,128]{1,0:T(8,128)(2,1)S(1)} %get-tuple-element.84), channel_id=1, source_target_pairs={{0,4},{1,5},{2,6},{3,7},{4,0},{5,1},{6,2},{7,3},{8,12},{9,13},{10,... | collective-permute-start | bytes 319496 | tf_op jit(solution)/shard_map/ppermute | solution.py:187
  70.5 6.6 %collective-permute-start.20 = (s16[1,288,128]{2,1,0:T(8,128)(2,1)S(1)}, s16[1,288,128]{2,1,0:T(8,128)(2,1)S(1)}, u32[]{:S(2)}, u32[]{:S(2)}) collective-permute-start(s16[1,288,128]{2,1,0:T(8,128)(2,1)S(1)} %get-tuple-element.81.refs_0_), channel_id=1, source_target_pairs={{0,24},{1,25},{2,26},{3,27},{4,28},{5,29},{6,30},{7,31},{8,16},{9,... | collective-permute-start | bytes 221192 | tf_op jit(solution)/shard_map/ppermute | solution.py:187
  72.6 6.6 %collective-permute-start.19 = (s16[1,288,128]{2,1,0:T(8,128)(2,1)S(1)}, s16[1,288,128]{2,1,0:T(8,128)(2,1)S(1)}, u32[]{:S(2)}, u32[]{:S(2)}) collective-permute-start(s16[1,288,128]{2,1,0:T(8,128)(2,1)S(1)} %get-tuple-element.81.refs_0_), channel_id=1, source_target_pairs={{0,16},{1,17},{2,18},{3,19},{4,20},{5,21},{6,22},{7,23},{8,24},{9,... | collective-permute-start | bytes 221192 | tf_op jit(solution)/shard_map/ppermute | solution.py:187
  73.4 5.8 %collective-permute-start.18 = (s16[1,288,128]{2,1,0:T(8,128)(2,1)S(1)}, s16[1,288,128]{2,1,0:T(8,128)(2,1)S(1)}, u32[]{:S(2)}, u32[]{:S(2)}) collective-permute-start(s16[1,288,128]{2,1,0:T(8,128)(2,1)S(1)} %get-tuple-element.81.refs_0_), channel_id=1, source_target_pairs={{0,8},{1,9},{2,10},{3,11},{4,12},{5,13},{6,14},{7,15},{8,0},{9,1},... | collective-permute-start | bytes 221192 | tf_op jit(solution)/shard_map/ppermute | solution.py:187
  79.4 10.2 %collective-permute-start.29 = (s16[4,288,128]{2,1,0:T(8,128)(2,1)S(1)}, s16[4,288,128]{2,1,0:T(8,128)(2,1)S(1)}, u32[]{:S(2)}, u32[]{:S(2)}) collective-permute-start(s16[4,288,128]{2,1,0:T(8,128)(2,1)S(1)} %get-tuple-element.86.refs_0_), channel_id=1, source_target_pairs={{0,4},{1,5},{2,6},{3,7},{4,0},{5,1},{6,2},{7,3},{8,12},{9,13},{10,... | collective-permute-start | bytes 884744 | tf_op jit(solution)/shard_map/ppermute | solution.py:187
  79.9 11.5 %collective-permute-start.27 = (s16[4,288,128]{2,1,0:T(8,128)(2,1)S(1)}, s16[4,288,128]{2,1,0:T(8,128)(2,1)S(1)}, u32[]{:S(2)}, u32[]{:S(2)}) collective-permute-start(s16[4,288,128]{2,1,0:T(8,128)(2,1)S(1)} %get-tuple-element.86.refs_0_), channel_id=1, source_target_pairs={{0,2},{1,3},{2,0},{3,1},{4,6},{5,7},{6,4},{7,5},{8,10},{9,11},{10,... | collective-permute-start | bytes 884744 | tf_op jit(solution)/shard_map/ppermute | solution.py:187
  81.5 8.1 %collective-permute-start.24 = (s16[416,128]{1,0:T(8,128)(2,1)S(1)}, s16[416,128]{1,0:T(8,128)(2,1)S(1)}, u32[]{:S(2)}, u32[]{:S(2)}) collective-permute-start(s16[416,128]{1,0:T(8,128)(2,1)S(1)} %get-tuple-element.85.refs_0_), channel_id=1, source_target_pairs={{0,2},{1,3},{2,0},{3,1},{4,6},{5,7},{6,4},{7,5},{8,10},{9,11},{10,... | collective-permute-start | bytes 319496 | tf_op jit(solution)/shard_map/ppermute | solution.py:187
  81.9 11.0 %collective-permute-start.23 = (s16[416,128]{1,0:T(8,128)(2,1)S(1)}, s16[416,128]{1,0:T(8,128)(2,1)S(1)}, u32[]{:S(2)}, u32[]{:S(2)}) collective-permute-start(s16[416,128]{1,0:T(8,128)(2,1)S(1)} %get-tuple-element.85.refs_0_), channel_id=1, source_target_pairs={{0,1},{1,0},{2,3},{3,2},{4,5},{5,4},{6,7},{7,6},{8,9},{9,8},{10,11... | collective-permute-start | bytes 319496 | tf_op jit(solution)/shard_map/ppermute | solution.py:187
  89.6 6.3 %collective-permute-start.33 = (s16[2,288,128]{2,1,0:T(8,128)(2,1)S(1)}, s16[2,288,128]{2,1,0:T(8,128)(2,1)S(1)}, u32[]{:S(2)}, u32[]{:S(2)}) collective-permute-start(s16[2,288,128]{2,1,0:T(8,128)(2,1)S(1)} %slice.9), channel_id=1, source_target_pairs={{0,2},{1,3},{2,0},{3,1},{4,6},{5,7},{6,4},{7,5},{8,10},{9,11},{10,... | collective-permute-start | bytes 442376 | tf_op jit(solution)/shard_map/ppermute | solution.py:187
  91.4 6.0 %collective-permute-start.31 = (s16[2,288,128]{2,1,0:T(8,128)(2,1)S(1)}, s16[2,288,128]{2,1,0:T(8,128)(2,1)S(1)}, u32[]{:S(2)}, u32[]{:S(2)}) collective-permute-start(s16[2,288,128]{2,1,0:T(8,128)(2,1)S(1)} %slice.8), channel_id=1, source_target_pairs={{0,4},{1,5},{2,6},{3,7},{4,0},{5,1},{6,2},{7,3},{8,12},{9,13},{10,... | collective-permute-start | bytes 442376 | tf_op jit(solution)/shard_map/ppermute | solution.py:187
  92.9 6.1 %collective-permute-start.26 = (s16[4,288,128]{2,1,0:T(8,128)(2,1)S(1)}, s16[4,288,128]{2,1,0:T(8,128)(2,1)S(1)}, u32[]{:S(2)}, u32[]{:S(2)}) collective-permute-start(s16[4,288,128]{2,1,0:T(8,128)(2,1)S(1)} %get-tuple-element.86.refs_0_), channel_id=1, source_target_pairs={{0,1},{1,0},{2,3},{3,2},{4,5},{5,4},{6,7},{7,6},{8,9},{9,8},{10,11... | collective-permute-start | bytes 884744 | tf_op jit(solution)/shard_map/ppermute | solution.py:187
  93.0 6.1 %collective-permute-start.30 = (s16[4,288,128]{2,1,0:T(8,128)(2,1)S(1)}, s16[4,288,128]{2,1,0:T(8,128)(2,1)S(1)}, u32[]{:S(2)}, u32[]{:S(2)}) collective-permute-start(s16[4,288,128]{2,1,0:T(8,128)(2,1)S(1)} %collective-permute-done.29.refs_2_), channel_id=1, source_target_pairs={{0,1},{1,0},{2,3},{3,2},{4,5},{5,4},{6,7},{7,6},{8,9},{9,8},{10,11... | collective-permute-start | bytes 884744 | tf_op jit(solution)/shard_map/ppermute | solution.py:187
  93.5 5.6 %collective-permute-start.28 = (s16[4,288,128]{2,1,0:T(8,128)(2,1)S(1)}, s16[4,288,128]{2,1,0:T(8,128)(2,1)S(1)}, u32[]{:S(2)}, u32[]{:S(2)}) collective-permute-start(s16[4,288,128]{2,1,0:T(8,128)(2,1)S(1)} %collective-permute-done.27.refs_1_), channel_id=1, source_target_pairs={{0,1},{1,0},{2,3},{3,2},{4,5},{5,4},{6,7},{7,6},{8,9},{9,8},{10,11... | collective-permute-start | bytes 884744 | tf_op jit(solution)/shard_map/ppermute | solution.py:187
  (14 other events, 43.9 us)

commit v14 on v13

--- a/solution.py
+++ b/solution.py
@@ -815,7 +815,8 @@
         if len(masks) != 4:
             return [block] + exchanged([block] * (len(masks) - 1), masks)
         half = block.shape[0] // 2
-        first, second = exchanged([block] * 2, masks[:3])
+        second = send(block, plan, lambda d: d ^ masks[2])
+        first = send(block, plan, lambda d: d ^ masks[1])
         over_first = send(first[:half], plan, lambda d: d ^ masks[2])
         over_second = send(second[half:], plan, lambda d: d ^ masks[1])
         return [block, first, second, over_first, over_second]

time: 101 us -> 101 us (level)
  no operation moved by 1% of the time
where the time goes in v14:
time: 101 us
  starting transfers between devices  36.9 us (37%)
  Pallas kernels  33.3 us (33%)
  waiting for transfers between devices  29.5 us (29%)
  between operations  1.1 us (1%)
    ppermute x35, starting transfers between devices, send(): return lax.ppermute(value, ('dom', 'rel'), pairs)  36.9 us
    pallas_call x20, Pallas kernels, call(): pl.pallas_call(kernel, out_shape=outs, in_specs=in_specs or [VMEM] * len(...  33.3 us
    ppermute x35, waiting for transfers between devices, send(): return lax.ppermute(value, ('dom', 'rel'), pairs)  29.5 us
  transfers between devices with their start and end apart: 35, of which 12 were waited for; matrix products, arithmetic and copies ran while one was open for 0% of the time, Pallas kernels for 18%

profile of v14, /device:TPU:0, one launch (start us, length us, event | category | flops | bytes accessed | tf_op | source)
XLA Modules:
  0.0 100.8 jit_solution(14510556091977060177)
XLA Ops:
  0.6 3.0 %collective-permute-start.5 = (bf16[400,512]{1,0:T(8,128)(2,1)}, bf16[400,512]{1,0:T(8,128)(2,1)S(1)}, u32[]{:S(2)}, u32[]{:S(2)}) collective-permute-start(bf16[400,512]{1,0:T(8,128)(2,1)} %bitcast.7), channel_id=1, source_target_pairs={{0,4},{1,5},{2,6},{3,7},{4,0},{5,1},{6,2},{7,3},{8,12},{9,13},{10,... | collective-permute-start | bytes 1228808 | tf_op jit(solution)/shard_map/ppermute | solution.py:187
  3.7 1.6 %collective-permute-start.4 = (bf16[400,512]{1,0:T(8,128)(2,1)}, bf16[400,512]{1,0:T(8,128)(2,1)S(1)}, u32[]{:S(2)}, u32[]{:S(2)}) collective-permute-start(bf16[400,512]{1,0:T(8,128)(2,1)} %bitcast.8), channel_id=1, source_target_pairs={{0,0},{1,17},{2,10},{3,27},{4,4},{5,21},{6,14},{7,31},{8,8},{9,25}... | collective-permute-start | bytes 1228808 | tf_op jit(solution)/shard_map/ppermute | solution.py:187
  6.8 2.1 %collective-permute-start = (s32[2,8,128]{2,1,0:T(8,128)}, s32[2,8,128]{2,1,0:T(8,128)S(1)}, u32[]{:S(2)}, u32[]{:S(2)}) collective-permute-start(s32[2,8,128]{2,1,0:T(8,128)} %get-tuple-element.48), channel_id=1, source_target_pairs={{0,1},{1,0},{2,3},{3,2},{4,5},{5,4},{6,7},{7,6},{8,9},{9,8},{10,11... | collective-permute-start | bytes 24584 | tf_op jit(solution)/shard_map/ppermute | solution.py:187
  8.9 2.5 %collective-permute-start.1 = (s32[2,8,128]{2,1,0:T(8,128)}, s32[2,8,128]{2,1,0:T(8,128)S(1)}, u32[]{:S(2)}, u32[]{:S(2)}) collective-permute-start(s32[2,8,128]{2,1,0:T(8,128)} %get-tuple-element.49), channel_id=1, source_target_pairs={{0,2},{1,3},{2,0},{3,1},{4,6},{5,7},{6,4},{7,5},{8,10},{9,11},{10,... | collective-permute-start | bytes 24584 | tf_op jit(solution)/shard_map/ppermute | solution.py:187
  11.4 2.3 %rel_split.1.refs_1_ = bf16[800,2560]{1,0:T(8,128)(2,1)S(1)} custom-call(f32[400,2560]{1,0:T(8,128)} %bitcast.12), custom_call_target="tpu_custom_call" | custom-call | flops 2000000000 | bytes 6000000 | tf_op jit(solution)/shard_map/rel_split/pallas_call | solution.py:528
  15.3 2.3 %relation.2.refs_3_ = f32[400,512]{1,0:T(8,128)S(1)} custom-call(s32[4,8,128]{2,1,0:T(8,128)S(1)} %get-tuple-element.51.refs_0_, bf16[800,2560]{1,0:T(8,128)(2,1)S(1)} %rel_split.1.refs_1_), custom_call_target="tpu_custom_call" | custom-call | flops 2000000000 | bytes 6000000 | tf_op jit(solution)/shard_map/relation/pallas_call | solution.py:528
  18.5 2.3 %relation.3.refs_7_ = f32[400,512]{1,0:T(8,128)S(1)} custom-call(s32[4,8,128]{2,1,0:T(8,128)S(1)} %collective-permute-done.3.refs_0_.refs_1_, bf16[800,2560]{1,0:T(8,128)(2,1)S(1)} %rel_split.1.refs_1_), custom_call_target="tpu_custom_call" | custom-call | flops 2000000000 | bytes 6000000 | tf_op jit(solution)/shard_map/relation/pallas_call | solution.py:528
  21.5 4.1 %bucket.1 = (bf16[800,512]{1,0:T(8,128)(2,1)S(1)}, bf16[800,512]{1,0:T(8,128)(2,1)S(1)}, bf16[800,1024]{1,0:T(8,128)(2,1)S(1)}) custom-call(s32[4,8,128]{2,1,0:T(8,128)S(1)} %get-tuple-element.51.refs_0_, bf16[400,512]{1,0:T(8,128)(2,1)S(1)} %collective-permute-done.4.refs_1_.refs_5_, f32[400,512]{1,0:T(8,128)S(1)} %get-tuple-element.53.refs_2_, ...), custom_call_target="tpu_custom_call" | custom-call | flops 4000000000 | bytes 12000000 | tf_op jit(solution)/shard_map/bucket/pallas_call | solution.py:528
  25.6 7.9 %last.1 = (s16[16,288,128]{2,1,0:T(8,128)(2,1)S(1)}, f32[400,128]{1,0:T(8,128)S(1)}, bf16[800,1024]{1,0:T(8,128)(2,1)S(1)}, bf16[800,1024]{1,0:T(8,128)(2,1)S(1)}, bf16[800,2048]{1,0:T(8,128)(2,1)S(1)}) custom-call(s32[4,8,128]{2,1,0:T(8,128)S(1)} %get-tuple-element.51.refs_0_, s32[4,8,128]{2,1,0:T(8,128)S(1)} %collective-permute-done.3.refs_0_.refs_1_, ...), custom_call_target="tpu_custom_call" | custom-call | flops 8999999488 | bytes 27000000 | tf_op jit(solution)/shard_map/last/pallas_call | solution.py:528
  34.9 2.4 %home.1.refs_0_ = f32[16,280,128]{2,1,0:T(8,128)S(1)} custom-call(s32[4,8,128]{2,1,0:T(8,128)S(1)} %get-tuple-element.51.refs_0_, s32[4,8,128]{2,1,0:T(8,128)S(1)} %collective-permute-done.3.refs_0_.refs_1_, bf16[800,1024]{1,0:T(8,128)(2,1)S(1)} %get-tuple-element.60.refs_2_, f32[400,128]{1,0:T(8,128)S(1)} %get-tuple-element.61.refs_3_, ...), custom_call_target="tpu_custom_call" | custom-call | flops 3000000000 | bytes 9000000 | tf_op jit(solution)/shard_map/home/pallas_call | solution.py:528
  41.5 2.0 %target.1 = (s16[416,256]{1,0:T(8,128)(2,1)S(1)}, s16[416,256]{1,0:T(8,128)(2,1)S(1)}) custom-call(s32[4,8,128]{2,1,0:T(8,128)S(1)} %get-tuple-element.51.refs_0_, s32[4,8,128]{2,1,0:T(8,128)S(1)} %collective-permute-done.3.refs_0_.refs_1_, bf16[800,2048]{1,0:T(8,128)(2,1)S(1)} %get-tuple-element.70.refs_2_, f32[4,280,128]{2,1,0:T(8,128)S(1)} %get-tuple-element.66.refs_3_.refs_0_), custom_call_target="tpu_custom_call" | custom-call | flops 1800000000 | bytes 5400000 | tf_op jit(solution)/shard_map/target/pallas_call | solution.py:528
  45.6 2.3 %collective-permute-done.8.refs_1_ = s16[4,288,128]{2,1,0:T(8,128)(2,1)S(1)} collective-permute-done((s16[4,288,128]{2,1,0:T(8,128)(2,1)S(1)}, s16[4,288,128]{2,1,0:T(8,128)(2,1)S(1)}, u32[]{:S(2)}, u32[]{:S(2)}) %collective-permute-start.8) | collective-permute-done | bytes 294944 | tf_op jit(solution)/shard_map/ppermute | solution.py:187
  47.9 4.9 %collective-permute-done.9.refs_2_ = s16[4,288,128]{2,1,0:T(8,128)(2,1)S(1)} collective-permute-done((s16[4,288,128]{2,1,0:T(8,128)(2,1)S(1)}, s16[4,288,128]{2,1,0:T(8,128)(2,1)S(1)}, u32[]{:S(2)}, u32[]{:S(2)}) %collective-permute-start.9) | collective-permute-done | bytes 294944 | tf_op jit(solution)/shard_map/ppermute | solution.py:187
  54.6 2.3 %collective-permute-start.16 = (s16[416,256]{1,0:T(8,128)(2,1)S(1)}, s16[416,256]{1,0:T(8,128)(2,1)S(1)}, u32[]{:S(2)}, u32[]{:S(2)}) collective-permute-start(s16[416,256]{1,0:T(8,128)(2,1)S(1)} %get-tuple-element.78), channel_id=1, source_target_pairs={{0,1},{1,0},{2,3},{3,2},{4,5},{5,4},{6,7},{7,6},{8,9},{9,8},{10,11... | collective-permute-start | bytes 638984 | tf_op jit(solution)/shard_map/ppermute | solution.py:187
  57.0 2.5 %collective-permute-start.17 = (s16[416,128]{1,0:T(8,128)(2,1)S(1)}, s16[416,128]{1,0:T(8,128)(2,1)S(1)}, u32[]{:S(2)}, u32[]{:S(2)}) collective-permute-start(s16[416,128]{1,0:T(8,128)(2,1)S(1)} %get-tuple-element.80), channel_id=1, source_target_pairs={{0,2},{1,3},{2,0},{3,1},{4,6},{5,7},{6,4},{7,5},{8,10},{9,11},{10,... | collective-permute-start | bytes 319496 | tf_op jit(solution)/shard_map/ppermute | solution.py:187
  59.5 2.1 %collective-permute-start.14 = (s16[1,288,128]{2,1,0:T(8,128)(2,1)S(1)}, s16[1,288,128]{2,1,0:T(8,128)(2,1)S(1)}, u32[]{:S(2)}, u32[]{:S(2)}) collective-permute-start(s16[1,288,128]{2,1,0:T(8,128)(2,1)S(1)} %get-tuple-element.75), channel_id=1, source_target_pairs={{0,16},{1,17},{2,18},{3,19},{4,20},{5,21},{6,22},{7,23},{8,24},{9,... | collective-permute-start | bytes 221192 | tf_op jit(solution)/shard_map/ppermute | solution.py:187
  61.6 2.3 %collective-permute-start.15 = (s16[1,288,128]{2,1,0:T(8,128)(2,1)S(1)}, s16[1,288,128]{2,1,0:T(8,128)(2,1)S(1)}, u32[]{:S(2)}, u32[]{:S(2)}) collective-permute-start(s16[1,288,128]{2,1,0:T(8,128)(2,1)S(1)} %get-tuple-element.76), channel_id=1, source_target_pairs={{0,24},{1,25},{2,26},{3,27},{4,28},{5,29},{6,30},{7,31},{8,16},{9,... | collective-permute-start | bytes 221192 | tf_op jit(solution)/shard_map/ppermute | solution.py:187
  64.9 3.8 %collective-permute-done.14.refs_2_ = s16[1,288,128]{2,1,0:T(8,128)(2,1)S(1)} collective-permute-done((s16[1,288,128]{2,1,0:T(8,128)(2,1)S(1)}, s16[1,288,128]{2,1,0:T(8,128)(2,1)S(1)}, u32[]{:S(2)}, u32[]{:S(2)}) %collective-permute-start.14) | collective-permute-done | bytes 73760 | tf_op jit(solution)/shard_map/ppermute | solution.py:187
  70.5 2.2 %collective-permute-start.20 = (s16[1,288,128]{2,1,0:T(8,128)(2,1)S(1)}, s16[1,288,128]{2,1,0:T(8,128)(2,1)S(1)}, u32[]{:S(2)}, u32[]{:S(2)}) collective-permute-start(s16[1,288,128]{2,1,0:T(8,128)(2,1)S(1)} %get-tuple-element.81.refs_0_), channel_id=1, source_target_pairs={{0,24},{1,25},{2,26},{3,27},{4,28},{5,29},{6,30},{7,31},{8,16},{9,... | collective-permute-start | bytes 221192 | tf_op jit(solution)/shard_map/ppermute | solution.py:187
  74.9 2.2 %collective-permute-done.20.refs_3_ = s16[1,288,128]{2,1,0:T(8,128)(2,1)S(1)} collective-permute-done((s16[1,288,128]{2,1,0:T(8,128)(2,1)S(1)}, s16[1,288,128]{2,1,0:T(8,128)(2,1)S(1)}, u32[]{:S(2)}, u32[]{:S(2)}) %collective-permute-start.20) | collective-permute-done | bytes 73760 | tf_op jit(solution)/shard_map/ppermute | solution.py:187
  77.0 2.2 %collective-permute-done.19.refs_2_ = s16[1,288,128]{2,1,0:T(8,128)(2,1)S(1)} collective-permute-done((s16[1,288,128]{2,1,0:T(8,128)(2,1)S(1)}, s16[1,288,128]{2,1,0:T(8,128)(2,1)S(1)}, u32[]{:S(2)}, u32[]{:S(2)}) %collective-permute-start.19) | collective-permute-done | bytes 73760 | tf_op jit(solution)/shard_map/ppermute | solution.py:187
  79.9 1.6 %collective-permute-start.27 = (s16[4,288,128]{2,1,0:T(8,128)(2,1)S(1)}, s16[4,288,128]{2,1,0:T(8,128)(2,1)S(1)}, u32[]{:S(2)}, u32[]{:S(2)}) collective-permute-start(s16[4,288,128]{2,1,0:T(8,128)(2,1)S(1)} %get-tuple-element.86.refs_0_), channel_id=1, source_target_pairs={{0,2},{1,3},{2,0},{3,1},{4,6},{5,7},{6,4},{7,5},{8,10},{9,11},{10,... | collective-permute-start | bytes 884744 | tf_op jit(solution)/shard_map/ppermute | solution.py:187
  81.9 7.7 %collective-permute-done.24.refs_2_ = s16[416,128]{1,0:T(8,128)(2,1)S(1)} collective-permute-done((s16[416,128]{1,0:T(8,128)(2,1)S(1)}, s16[416,128]{1,0:T(8,128)(2,1)S(1)}, u32[]{:S(2)}, u32[]{:S(2)}) %collective-permute-start.24) | collective-permute-done | bytes 106528 | tf_op jit(solution)/shard_map/ppermute | solution.py:187
  89.6 1.7 %collective-permute-start.33 = (s16[2,288,128]{2,1,0:T(8,128)(2,1)S(1)}, s16[2,288,128]{2,1,0:T(8,128)(2,1)S(1)}, u32[]{:S(2)}, u32[]{:S(2)}) collective-permute-start(s16[2,288,128]{2,1,0:T(8,128)(2,1)S(1)} %slice.9), channel_id=1, source_target_pairs={{0,2},{1,3},{2,0},{3,1},{4,6},{5,7},{6,4},{7,5},{8,10},{9,11},{10,... | collective-permute-start | bytes 442376 | tf_op jit(solution)/shard_map/ppermute | solution.py:187
  (74 shorter events, 29.2 us)
Async XLA Ops:
  0.6 20.2 %collective-permute-start.5 = (bf16[400,512]{1,0:T(8,128)(2,1)}, bf16[400,512]{1,0:T(8,128)(2,1)S(1)}, u32[]{:S(2)}, u32[]{:S(2)}) collective-permute-start(bf16[400,512]{1,0:T(8,128)(2,1)} %bitcast.7), channel_id=1, source_target_pairs={{0,4},{1,5},{2,6},{3,7},{4,0},{5,1},{6,2},{7,3},{8,12},{9,13},{10,... | collective-permute-start | bytes 1228808 | tf_op jit(solution)/shard_map/ppermute | solution.py:187
  3.7 17.8 %collective-permute-start.4 = (bf16[400,512]{1,0:T(8,128)(2,1)}, bf16[400,512]{1,0:T(8,128)(2,1)S(1)}, u32[]{:S(2)}, u32[]{:S(2)}) collective-permute-start(bf16[400,512]{1,0:T(8,128)(2,1)} %bitcast.8), channel_id=1, source_target_pairs={{0,0},{1,17},{2,10},{3,27},{4,4},{5,21},{6,14},{7,31},{8,8},{9,25}... | collective-permute-start | bytes 1228808 | tf_op jit(solution)/shard_map/ppermute | solution.py:187
  6.8 7.0 %collective-permute-start = (s32[2,8,128]{2,1,0:T(8,128)}, s32[2,8,128]{2,1,0:T(8,128)S(1)}, u32[]{:S(2)}, u32[]{:S(2)}) collective-permute-start(s32[2,8,128]{2,1,0:T(8,128)} %get-tuple-element.48), channel_id=1, source_target_pairs={{0,1},{1,0},{2,3},{3,2},{4,5},{5,4},{6,7},{7,6},{8,9},{9,8},{10,11... | collective-permute-start | bytes 24584 | tf_op jit(solution)/shard_map/ppermute | solution.py:187
  38.0 9.9 %collective-permute-start.8 = (s16[4,288,128]{2,1,0:T(8,128)(2,1)S(1)}, s16[4,288,128]{2,1,0:T(8,128)(2,1)S(1)}, u32[]{:S(2)}, u32[]{:S(2)}) collective-permute-start(s16[4,288,128]{2,1,0:T(8,128)(2,1)S(1)} %get-tuple-element.67), channel_id=1, source_target_pairs={{0,2},{1,3},{2,0},{3,1},{4,6},{5,7},{6,4},{7,5},{8,10},{9,11},{10,... | collective-permute-start | bytes 884744 | tf_op jit(solution)/shard_map/ppermute | solution.py:187
  38.6 14.2 %collective-permute-start.9 = (s16[4,288,128]{2,1,0:T(8,128)(2,1)S(1)}, s16[4,288,128]{2,1,0:T(8,128)(2,1)S(1)}, u32[]{:S(2)}, u32[]{:S(2)}) collective-permute-start(s16[4,288,128]{2,1,0:T(8,128)(2,1)S(1)} %get-tuple-element.68), channel_id=1, source_target_pairs={{0,4},{1,5},{2,6},{3,7},{4,0},{5,1},{6,2},{7,3},{8,12},{9,13},{10,... | collective-permute-start | bytes 884744 | tf_op jit(solution)/shard_map/ppermute | solution.py:187
  40.0 14.1 %collective-permute-start.10 = (s16[4,288,128]{2,1,0:T(8,128)(2,1)S(1)}, s16[4,288,128]{2,1,0:T(8,128)(2,1)S(1)}, u32[]{:S(2)}, u32[]{:S(2)}) collective-permute-start(s16[4,288,128]{2,1,0:T(8,128)(2,1)S(1)} %get-tuple-element.69), channel_id=1, source_target_pairs={{0,6},{1,7},{2,4},{3,5},{4,2},{5,3},{6,0},{7,1},{8,14},{9,15},{10,... | collective-permute-start | bytes 884744 | tf_op jit(solution)/shard_map/ppermute | solution.py:187
  54.6 14.0 %collective-permute-start.16 = (s16[416,256]{1,0:T(8,128)(2,1)S(1)}, s16[416,256]{1,0:T(8,128)(2,1)S(1)}, u32[]{:S(2)}, u32[]{:S(2)}) collective-permute-start(s16[416,256]{1,0:T(8,128)(2,1)S(1)} %get-tuple-element.78), channel_id=1, source_target_pairs={{0,1},{1,0},{2,3},{3,2},{4,5},{5,4},{6,7},{7,6},{8,9},{9,8},{10,11... | collective-permute-start | bytes 638984 | tf_op jit(solution)/shard_map/ppermute | solution.py:187
  57.0 11.7 %collective-permute-start.17 = (s16[416,128]{1,0:T(8,128)(2,1)S(1)}, s16[416,128]{1,0:T(8,128)(2,1)S(1)}, u32[]{:S(2)}, u32[]{:S(2)}) collective-permute-start(s16[416,128]{1,0:T(8,128)(2,1)S(1)} %get-tuple-element.80), channel_id=1, source_target_pairs={{0,2},{1,3},{2,0},{3,1},{4,6},{5,7},{6,4},{7,5},{8,10},{9,11},{10,... | collective-permute-start | bytes 319496 | tf_op jit(solution)/shard_map/ppermute | solution.py:187
  59.5 9.2 %collective-permute-start.14 = (s16[1,288,128]{2,1,0:T(8,128)(2,1)S(1)}, s16[1,288,128]{2,1,0:T(8,128)(2,1)S(1)}, u32[]{:S(2)}, u32[]{:S(2)}) collective-permute-start(s16[1,288,128]{2,1,0:T(8,128)(2,1)S(1)} %get-tuple-element.75), channel_id=1, source_target_pairs={{0,16},{1,17},{2,18},{3,19},{4,20},{5,21},{6,22},{7,23},{8,24},{9,... | collective-permute-start | bytes 221192 | tf_op jit(solution)/shard_map/ppermute | solution.py:187
  61.6 7.1 %collective-permute-start.15 = (s16[1,288,128]{2,1,0:T(8,128)(2,1)S(1)}, s16[1,288,128]{2,1,0:T(8,128)(2,1)S(1)}, u32[]{:S(2)}, u32[]{:S(2)}) collective-permute-start(s16[1,288,128]{2,1,0:T(8,128)(2,1)S(1)} %get-tuple-element.76), channel_id=1, source_target_pairs={{0,24},{1,25},{2,26},{3,27},{4,28},{5,29},{6,30},{7,31},{8,16},{9,... | collective-permute-start | bytes 221192 | tf_op jit(solution)/shard_map/ppermute | solution.py:187
  68.9 10.3 %collective-permute-start.21 = (s16[416,128]{1,0:T(8,128)(2,1)S(1)}, s16[416,128]{1,0:T(8,128)(2,1)S(1)}, u32[]{:S(2)}, u32[]{:S(2)}) collective-permute-start(s16[416,128]{1,0:T(8,128)(2,1)S(1)} %get-tuple-element.83), channel_id=1, source_target_pairs={{0,2},{1,3},{2,0},{3,1},{4,6},{5,7},{6,4},{7,5},{8,10},{9,11},{10,... | collective-permute-start | bytes 319496 | tf_op jit(solution)/shard_map/ppermute | solution.py:187
  69.1 10.1 %collective-permute-start.22 = (s16[416,128]{1,0:T(8,128)(2,1)S(1)}, s16[416,128]{1,0:T(8,128)(2,1)S(1)}, u32[]{:S(2)}, u32[]{:S(2)}) collective-permute-start(s16[416,128]{1,0:T(8,128)(2,1)S(1)} %get-tuple-element.84), channel_id=1, source_target_pairs={{0,4},{1,5},{2,6},{3,7},{4,0},{5,1},{6,2},{7,3},{8,12},{9,13},{10,... | collective-permute-start | bytes 319496 | tf_op jit(solution)/shard_map/ppermute | solution.py:187
  70.5 6.6 %collective-permute-start.20 = (s16[1,288,128]{2,1,0:T(8,128)(2,1)S(1)}, s16[1,288,128]{2,1,0:T(8,128)(2,1)S(1)}, u32[]{:S(2)}, u32[]{:S(2)}) collective-permute-start(s16[1,288,128]{2,1,0:T(8,128)(2,1)S(1)} %get-tuple-element.81.refs_0_), channel_id=1, source_target_pairs={{0,24},{1,25},{2,26},{3,27},{4,28},{5,29},{6,30},{7,31},{8,16},{9,... | collective-permute-start | bytes 221192 | tf_op jit(solution)/shard_map/ppermute | solution.py:187
  72.6 6.6 %collective-permute-start.19 = (s16[1,288,128]{2,1,0:T(8,128)(2,1)S(1)}, s16[1,288,128]{2,1,0:T(8,128)(2,1)S(1)}, u32[]{:S(2)}, u32[]{:S(2)}) collective-permute-start(s16[1,288,128]{2,1,0:T(8,128)(2,1)S(1)} %get-tuple-element.81.refs_0_), channel_id=1, source_target_pairs={{0,16},{1,17},{2,18},{3,19},{4,20},{5,21},{6,22},{7,23},{8,24},{9,... | collective-permute-start | bytes 221192 | tf_op jit(solution)/shard_map/ppermute | solution.py:187
  73.4 5.8 %collective-permute-start.18 = (s16[1,288,128]{2,1,0:T(8,128)(2,1)S(1)}, s16[1,288,128]{2,1,0:T(8,128)(2,1)S(1)}, u32[]{:S(2)}, u32[]{:S(2)}) collective-permute-start(s16[1,288,128]{2,1,0:T(8,128)(2,1)S(1)} %get-tuple-element.81.refs_0_), channel_id=1, source_target_pairs={{0,8},{1,9},{2,10},{3,11},{4,12},{5,13},{6,14},{7,15},{8,0},{9,1},... | collective-permute-start | bytes 221192 | tf_op jit(solution)/shard_map/ppermute | solution.py:187
  79.4 10.2 %collective-permute-start.29 = (s16[4,288,128]{2,1,0:T(8,128)(2,1)S(1)}, s16[4,288,128]{2,1,0:T(8,128)(2,1)S(1)}, u32[]{:S(2)}, u32[]{:S(2)}) collective-permute-start(s16[4,288,128]{2,1,0:T(8,128)(2,1)S(1)} %get-tuple-element.86.refs_0_), channel_id=1, source_target_pairs={{0,4},{1,5},{2,6},{3,7},{4,0},{5,1},{6,2},{7,3},{8,12},{9,13},{10,... | collective-permute-start | bytes 884744 | tf_op jit(solution)/shard_map/ppermute | solution.py:187
  79.9 11.5 %collective-permute-start.27 = (s16[4,288,128]{2,1,0:T(8,128)(2,1)S(1)}, s16[4,288,128]{2,1,0:T(8,128)(2,1)S(1)}, u32[]{:S(2)}, u32[]{:S(2)}) collective-permute-start(s16[4,288,128]{2,1,0:T(8,128)(2,1)S(1)} %get-tuple-element.86.refs_0_), channel_id=1, source_target_pairs={{0,2},{1,3},{2,0},{3,1},{4,6},{5,7},{6,4},{7,5},{8,10},{9,11},{10,... | collective-permute-start | bytes 884744 | tf_op jit(solution)/shard_map/ppermute | solution.py:187
  81.5 8.1 %collective-permute-start.24 = (s16[416,128]{1,0:T(8,128)(2,1)S(1)}, s16[416,128]{1,0:T(8,128)(2,1)S(1)}, u32[]{:S(2)}, u32[]{:S(2)}) collective-permute-start(s16[416,128]{1,0:T(8,128)(2,1)S(1)} %get-tuple-element.85.refs_0_), channel_id=1, source_target_pairs={{0,2},{1,3},{2,0},{3,1},{4,6},{5,7},{6,4},{7,5},{8,10},{9,11},{10,... | collective-permute-start | bytes 319496 | tf_op jit(solution)/shard_map/ppermute | solution.py:187
  81.9 11.0 %collective-permute-start.23 = (s16[416,128]{1,0:T(8,128)(2,1)S(1)}, s16[416,128]{1,0:T(8,128)(2,1)S(1)}, u32[]{:S(2)}, u32[]{:S(2)}) collective-permute-start(s16[416,128]{1,0:T(8,128)(2,1)S(1)} %get-tuple-element.85.refs_0_), channel_id=1, source_target_pairs={{0,1},{1,0},{2,3},{3,2},{4,5},{5,4},{6,7},{7,6},{8,9},{9,8},{10,11... | collective-permute-start | bytes 319496 | tf_op jit(solution)/shard_map/ppermute | solution.py:187
  89.6 6.3 %collective-permute-start.33 = (s16[2,288,128]{2,1,0:T(8,128)(2,1)S(1)}, s16[2,288,128]{2,1,0:T(8,128)(2,1)S(1)}, u32[]{:S(2)}, u32[]{:S(2)}) collective-permute-start(s16[2,288,128]{2,1,0:T(8,128)(2,1)S(1)} %slice.9), channel_id=1, source_target_pairs={{0,2},{1,3},{2,0},{3,1},{4,6},{5,7},{6,4},{7,5},{8,10},{9,11},{10,... | collective-permute-start | bytes 442376 | tf_op jit(solution)/shard_map/ppermute | solution.py:187
  91.4 6.0 %collective-permute-start.31 = (s16[2,288,128]{2,1,0:T(8,128)(2,1)S(1)}, s16[2,288,128]{2,1,0:T(8,128)(2,1)S(1)}, u32[]{:S(2)}, u32[]{:S(2)}) collective-permute-start(s16[2,288,128]{2,1,0:T(8,128)(2,1)S(1)} %slice.8), channel_id=1, source_target_pairs={{0,4},{1,5},{2,6},{3,7},{4,0},{5,1},{6,2},{7,3},{8,12},{9,13},{10,... | collective-permute-start | bytes 442376 | tf_op jit(solution)/shard_map/ppermute | solution.py:187
  92.9 6.1 %collective-permute-start.26 = (s16[4,288,128]{2,1,0:T(8,128)(2,1)S(1)}, s16[4,288,128]{2,1,0:T(8,128)(2,1)S(1)}, u32[]{:S(2)}, u32[]{:S(2)}) collective-permute-start(s16[4,288,128]{2,1,0:T(8,128)(2,1)S(1)} %get-tuple-element.86.refs_0_), channel_id=1, source_target_pairs={{0,1},{1,0},{2,3},{3,2},{4,5},{5,4},{6,7},{7,6},{8,9},{9,8},{10,11... | collective-permute-start | bytes 884744 | tf_op jit(solution)/shard_map/ppermute | solution.py:187
  93.0 6.1 %collective-permute-start.30 = (s16[4,288,128]{2,1,0:T(8,128)(2,1)S(1)}, s16[4,288,128]{2,1,0:T(8,128)(2,1)S(1)}, u32[]{:S(2)}, u32[]{:S(2)}) collective-permute-start(s16[4,288,128]{2,1,0:T(8,128)(2,1)S(1)} %collective-permute-done.29.refs_2_), channel_id=1, source_target_pairs={{0,1},{1,0},{2,3},{3,2},{4,5},{5,4},{6,7},{7,6},{8,9},{9,8},{10,11... | collective-permute-start | bytes 884744 | tf_op jit(solution)/shard_map/ppermute | solution.py:187
  93.5 5.6 %collective-permute-start.28 = (s16[4,288,128]{2,1,0:T(8,128)(2,1)S(1)}, s16[4,288,128]{2,1,0:T(8,128)(2,1)S(1)}, u32[]{:S(2)}, u32[]{:S(2)}) collective-permute-start(s16[4,288,128]{2,1,0:T(8,128)(2,1)S(1)} %collective-permute-done.27.refs_1_), channel_id=1, source_target_pairs={{0,1},{1,0},{2,3},{3,2},{4,5},{5,4},{6,7},{7,6},{8,9},{9,8},{10,11... | collective-permute-start | bytes 884744 | tf_op jit(solution)/shard_map/ppermute | solution.py:187
  (14 other events, 43.9 us)
